TPU v7x, 32 devices: a whole 2x2x4 slice. The times are simulated.
32 devices in a mesh: slab: 16 (over z, y, x), tile: 2 (over core).
Axes of the slice: x: 2, y: 2, z: 4, core: 2. Of those that a mesh axis runs over, the one named last changes fastest.
Arguments:
- field: float32 [256, 256, 1024], P('slab', None, 'tile'), may hold values from -1 to 1
- tf_emission: float32 [3, 16], replicated, may hold values from 0 to 1
- tf_absorption: float32 [3, 16], replicated, may hold values from 0.05 to 1
Outputs:
- colour: float32 [3, 256, 1024], P(None, 'slab', 'tile')
- opacity: float32 [3, 256, 1024], P(None, 'slab', 'tile')
All inputs are finite; a program needn't handle non-finite values.
Results may differ from a plain program's by a relative error of at most 0.0003.
Values sent between devices are 32-bit elements; how exact they have to be, the bound alone decides.
No kernel may reach another device: no remote copies, remote signals or barrier semaphores. Data moves between devices by JAX's collectives and lax.ppermute only.
A program may use at most 128 MiB of HBM per device.

v0:
```python
import jax
import jax.numpy as jnp
from jax import lax
from jax.sharding import PartitionSpec as P

LIGHT_DIR = (0.2672612, 0.5345225, 0.8017837)


def extended(block, sides, width):
    for axis, dim in sides:
        count = lax.axis_size(axis)
        forward = [(i, i + 1) for i in range(count - 1)]
        backward = [(target, source) for source, target in forward]
        low = lax.ppermute(
            lax.slice_in_dim(block, block.shape[dim] - width, None, axis=dim), axis, forward
        )
        high = lax.ppermute(lax.slice_in_dim(block, 0, width, axis=dim), axis, backward)
        block = jnp.concatenate([low, block, high], axis=dim)
    return block


def from_partner(value, axis, distance):
    return lax.ppermute(value, axis, [(i, i ^ 1 << distance) for i in range(lax.axis_size(axis))])


def lookup_table(table, interval, fraction):
    count_breaks = table.shape[1]
    result = jnp.zeros((3,) + fraction.shape, jnp.float32)
    for k in range(count_breaks - 1):
        value = (
            table[:, k][:, None, None]
            + fraction[None] * (table[:, k + 1] - table[:, k])[:, None, None]
        )
        result = jnp.where((interval == k)[None], value, result)
    return result


def shade_plane(lower_plane, middle, upper_plane, tf_emission, tf_absorption, depth_total):
    centre = middle[:, 1:-1]
    grad_x = 0.5 * (middle[:, 2:] - middle[:, :-2])
    padded_rows = jnp.pad(centre, ((1, 1), (0, 0)))
    grad_y = 0.5 * (padded_rows[2:] - padded_rows[:-2])
    grad_z = 0.5 * (upper_plane[:, 1:-1] - lower_plane[:, 1:-1])
    squared = grad_x * grad_x + grad_y * grad_y + grad_z * grad_z
    facing = (LIGHT_DIR[0] * grad_x + LIGHT_DIR[1] * grad_y + LIGHT_DIR[2] * grad_z) * lax.rsqrt(
        squared + 0.25
    )
    shading = 0.1 + 0.9 * jnp.maximum(facing, 0.0)
    steepness = squared / (squared + 0.25)
    count_breaks = tf_emission.shape[1]
    scaled = (centre + 1.0) * (0.5 * (count_breaks - 1))
    lowest = jnp.clip(jnp.floor(scaled), 0.0, count_breaks - 2.0)
    fraction = scaled - lowest
    interval = lowest.astype(jnp.int32)
    emission = lookup_table(tf_emission, interval, fraction)
    absorption = lookup_table(tf_absorption, interval, fraction)
    opacity_step = absorption * (4.0 / depth_total) * (0.25 + 0.75 * steepness)[None]
    sample = emission * shading[None] * opacity_step
    return (sample, opacity_step)


def combine_pair(nearer, farther):
    return jnp.stack([nearer[0] + nearer[1] * farther[0], nearer[1] * farther[1]])


def per_device(field, tf_emission, tf_absorption):
    slab_count = lax.axis_size("slab")
    depth_total = field.shape[0] * slab_count
    height = field.shape[1]
    width = field.shape[2]
    padded = extended(field, (("slab", 0), ("tile", 2)), 1)

    def march(plane, running):
        colour, transmit = running
        lower_plane = lax.dynamic_index_in_dim(padded, plane, 0, keepdims=False)
        middle = lax.dynamic_index_in_dim(padded, plane + 1, 0, keepdims=False)
        upper_plane = lax.dynamic_index_in_dim(padded, plane + 2, 0, keepdims=False)
        sample, opacity_step = shade_plane(
            lower_plane, middle, upper_plane, tf_emission, tf_absorption, depth_total
        )
        return (colour + transmit * sample, transmit * (1.0 - opacity_step))

    start = (jnp.zeros((3, height, width), jnp.float32), jnp.ones((3, height, width), jnp.float32))
    colour, transmit = lax.fori_loop(0, field.shape[0], march, start)
    image = jnp.stack([colour, transmit])
    levels = slab_count.bit_length() - 1
    block_rows = height // slab_count
    slab_index = lax.axis_index("slab")
    result = image.reshape((2, 3) + (2,) * levels + (block_rows, width))
    for digit in range(levels):
        position = 2 + levels - 1 - digit
        own_bit = slab_index >> digit & 1
        kept = lax.dynamic_index_in_dim(result, own_bit, position, keepdims=False)
        given = lax.dynamic_index_in_dim(result, 1 - own_bit, position, keepdims=False)
        received = from_partner(given, "slab", digit)
        in_front = own_bit == 0
        nearer = jnp.where(in_front, kept, received)
        farther = jnp.where(in_front, received, kept)
        result = combine_pair(nearer, farther)
    return (result[0], 1.0 - result[1])


def solution(mesh):
    placed = (P("slab", None, "tile"), P(), P())
    return jax.shard_map(
        per_device,
        mesh=mesh,
        in_specs=placed,
        out_specs=(P(None, "slab", "tile"), P(None, "slab", "tile")),
        check_vma=False,
    )
```

profile of v0, /device:TPU:0, one launch (start us, length us, event | category | flops | bytes accessed | tf_op | source)
XLA Modules:
  0.0 521.2 jit_solution(8636225822388906028)
XLA Ops:
  0.6 9.3 %copy.9 = f32[16,256,512]{1,2,0:T(8,128)} copy(f32[16,256,512]{2,1,0:T(8,128)} %param.5) | data formatting | bytes 16777216 | tf_op args[0]
  11.2 4.9 collective-permute-start
  18.4 20.1 %collective-permute-done = f32[1,256,512]{1,2,0:T(8,128)S(1)} collective-permute-done((f32[1,256,512]{1,2,0:T(8,128)S(1)}, f32[1,256,512]{1,2,0:T(8,128)S(1)}, u32[]{:S(2)}, u32[]{:S(2)}) %collective-permute-start) | collective-permute-done | bytes 524320 | tf_op jit(solution)/shard_map/ppermute | solution.py:14
  38.4 1.9 collective-permute-done.1
  45.8 6.5 %pad_maximum_fusion = f32[18,256,514]{1,2,0:T(8,128)} fusion(f32[18,256,1]{1,2,0:T(1,128)S(1)} %collective-permute-done.3, f32[1,256,512]{1,2,0:T(8,128)S(1)} %collective-permute-done.1, f32[16,256,512]{1,2,0:T(8,128)} %copy.9, f32[1,256,512]{1,2,0:T(8,128)S(1)} %collective-permute-done, f32[18,256,1]{1,2,0:T(1,128)S(1)} %collective-permute-done.2), kind=kLoop, calls=%fused_computation.67 | loop fusion | flops 9474048 | bytes 18948096 | tf_op jit(solution)/shard_map/concatenate | solution.py:18
  52.3 11.6 %copy.12 = f32[18,256,514]{2,1,0:T(8,128)} copy(f32[18,256,514]{1,2,0:T(8,128)} %pad_maximum_fusion) | data formatting | bytes 18948096
  63.9 373.6 %while.18 = (s32[]{:T(128)}, f32[3,256,512]{2,1,0:T(8,128)}, f32[3,256,512]{2,1,0:T(8,128)S(1)}, f32[18,256,514]{2,1,0:T(8,128)}, f32[3,16]{0,1:T(8,128)S(1)}, /...) while((s32[]{:T(128)}, f32[3,256,512]{2,1,0:T(8,128)}, ...), condition=%wide.region_1.2_spmd.clone, body=%wide.region_0.1_spmd.clone.sunk | while | flops 64749576 | bytes 32129652 | solution.py:84
  66.5 2.7 convert_compare_fusion.16
  70.9 10.3 %select_add_fusion.2 = f32[3,256,512]{2,1,0:T(8,128)} fusion(f32[3,256,512]{2,1,0:T(8,128)} %get-tuple-element.1047, f32[3,256,512]{2,1,0:T(8,128)S(1)} %get-tuple-element.1048, f32[256,512]{1,0:T(8,128)S(1)} %get-tuple-element.957, f32[3]{0:T(128)} %bitcast.279, f32[3]{0:T(128)} %get-tuple-element.958, f32[3]{0:T(128)} %bitcast.307, ...), kind=kLoop, calls=%fused_computation.clone.1 | loop fusion | flops 38141952 | bytes 8258257 | tf_op jit(solution)/shard_map/while/body/eval_jaxpr/add | solution.py:81
  81.6 5.2 subtract_multiply_fusion.2
  89.4 2.7 convert_compare_fusion.16
  93.8 10.8 %select_add_fusion.2 = f32[3,256,512]{2,1,0:T(8,128)} fusion(f32[3,256,512]{2,1,0:T(8,128)} %get-tuple-element.1047, f32[3,256,512]{2,1,0:T(8,128)S(1)} %get-tuple-element.1048, f32[256,512]{1,0:T(8,128)S(1)} %get-tuple-element.957, f32[3]{0:T(128)} %bitcast.279, f32[3]{0:T(128)} %get-tuple-element.958, f32[3]{0:T(128)} %bitcast.307, ...), kind=kLoop, calls=%fused_computation.clone.1 | loop fusion | flops 38141952 | bytes 8258257 | tf_op jit(solution)/shard_map/while/body/eval_jaxpr/add | solution.py:81
  105.0 5.2 subtract_multiply_fusion.2
  112.8 2.7 convert_compare_fusion.16
  117.2 10.8 %select_add_fusion.2 = f32[3,256,512]{2,1,0:T(8,128)} fusion(f32[3,256,512]{2,1,0:T(8,128)} %get-tuple-element.1047, f32[3,256,512]{2,1,0:T(8,128)S(1)} %get-tuple-element.1048, f32[256,512]{1,0:T(8,128)S(1)} %get-tuple-element.957, f32[3]{0:T(128)} %bitcast.279, f32[3]{0:T(128)} %get-tuple-element.958, f32[3]{0:T(128)} %bitcast.307, ...), kind=kLoop, calls=%fused_computation.clone.1 | loop fusion | flops 38141952 | bytes 8258257 | tf_op jit(solution)/shard_map/while/body/eval_jaxpr/add | solution.py:81
  128.4 5.2 subtract_multiply_fusion.2
  136.1 2.7 convert_compare_fusion.16
  140.5 10.8 %select_add_fusion.2 = f32[3,256,512]{2,1,0:T(8,128)} fusion(f32[3,256,512]{2,1,0:T(8,128)} %get-tuple-element.1047, f32[3,256,512]{2,1,0:T(8,128)S(1)} %get-tuple-element.1048, f32[256,512]{1,0:T(8,128)S(1)} %get-tuple-element.957, f32[3]{0:T(128)} %bitcast.279, f32[3]{0:T(128)} %get-tuple-element.958, f32[3]{0:T(128)} %bitcast.307, ...), kind=kLoop, calls=%fused_computation.clone.1 | loop fusion | flops 38141952 | bytes 8258257 | tf_op jit(solution)/shard_map/while/body/eval_jaxpr/add | solution.py:81
  151.7 5.2 subtract_multiply_fusion.2
  159.5 2.7 convert_compare_fusion.16
  163.9 10.8 %select_add_fusion.2 = f32[3,256,512]{2,1,0:T(8,128)} fusion(f32[3,256,512]{2,1,0:T(8,128)} %get-tuple-element.1047, f32[3,256,512]{2,1,0:T(8,128)S(1)} %get-tuple-element.1048, f32[256,512]{1,0:T(8,128)S(1)} %get-tuple-element.957, f32[3]{0:T(128)} %bitcast.279, f32[3]{0:T(128)} %get-tuple-element.958, f32[3]{0:T(128)} %bitcast.307, ...), kind=kLoop, calls=%fused_computation.clone.1 | loop fusion | flops 38141952 | bytes 8258257 | tf_op jit(solution)/shard_map/while/body/eval_jaxpr/add | solution.py:81
  175.1 5.2 subtract_multiply_fusion.2
  182.9 2.7 convert_compare_fusion.16
  187.3 10.8 %select_add_fusion.2 = f32[3,256,512]{2,1,0:T(8,128)} fusion(f32[3,256,512]{2,1,0:T(8,128)} %get-tuple-element.1047, f32[3,256,512]{2,1,0:T(8,128)S(1)} %get-tuple-element.1048, f32[256,512]{1,0:T(8,128)S(1)} %get-tuple-element.957, f32[3]{0:T(128)} %bitcast.279, f32[3]{0:T(128)} %get-tuple-element.958, f32[3]{0:T(128)} %bitcast.307, ...), kind=kLoop, calls=%fused_computation.clone.1 | loop fusion | flops 38141952 | bytes 8258257 | tf_op jit(solution)/shard_map/while/body/eval_jaxpr/add | solution.py:81
  198.5 5.2 subtract_multiply_fusion.2
  206.3 2.7 convert_compare_fusion.16
  210.7 10.8 %select_add_fusion.2 = f32[3,256,512]{2,1,0:T(8,128)} fusion(f32[3,256,512]{2,1,0:T(8,128)} %get-tuple-element.1047, f32[3,256,512]{2,1,0:T(8,128)S(1)} %get-tuple-element.1048, f32[256,512]{1,0:T(8,128)S(1)} %get-tuple-element.957, f32[3]{0:T(128)} %bitcast.279, f32[3]{0:T(128)} %get-tuple-element.958, f32[3]{0:T(128)} %bitcast.307, ...), kind=kLoop, calls=%fused_computation.clone.1 | loop fusion | flops 38141952 | bytes 8258257 | tf_op jit(solution)/shard_map/while/body/eval_jaxpr/add | solution.py:81
  221.9 5.2 subtract_multiply_fusion.2
  229.7 2.7 convert_compare_fusion.16
  234.1 10.8 %select_add_fusion.2 = f32[3,256,512]{2,1,0:T(8,128)} fusion(f32[3,256,512]{2,1,0:T(8,128)} %get-tuple-element.1047, f32[3,256,512]{2,1,0:T(8,128)S(1)} %get-tuple-element.1048, f32[256,512]{1,0:T(8,128)S(1)} %get-tuple-element.957, f32[3]{0:T(128)} %bitcast.279, f32[3]{0:T(128)} %get-tuple-element.958, f32[3]{0:T(128)} %bitcast.307, ...), kind=kLoop, calls=%fused_computation.clone.1 | loop fusion | flops 38141952 | bytes 8258257 | tf_op jit(solution)/shard_map/while/body/eval_jaxpr/add | solution.py:81
  245.3 5.2 subtract_multiply_fusion.2
  253.1 2.7 convert_compare_fusion.16
  257.5 10.8 %select_add_fusion.2 = f32[3,256,512]{2,1,0:T(8,128)} fusion(f32[3,256,512]{2,1,0:T(8,128)} %get-tuple-element.1047, f32[3,256,512]{2,1,0:T(8,128)S(1)} %get-tuple-element.1048, f32[256,512]{1,0:T(8,128)S(1)} %get-tuple-element.957, f32[3]{0:T(128)} %bitcast.279, f32[3]{0:T(128)} %get-tuple-element.958, f32[3]{0:T(128)} %bitcast.307, ...), kind=kLoop, calls=%fused_computation.clone.1 | loop fusion | flops 38141952 | bytes 8258257 | tf_op jit(solution)/shard_map/while/body/eval_jaxpr/add | solution.py:81
  268.7 5.2 subtract_multiply_fusion.2
  276.4 2.7 convert_compare_fusion.16
  280.8 10.8 %select_add_fusion.2 = f32[3,256,512]{2,1,0:T(8,128)} fusion(f32[3,256,512]{2,1,0:T(8,128)} %get-tuple-element.1047, f32[3,256,512]{2,1,0:T(8,128)S(1)} %get-tuple-element.1048, f32[256,512]{1,0:T(8,128)S(1)} %get-tuple-element.957, f32[3]{0:T(128)} %bitcast.279, f32[3]{0:T(128)} %get-tuple-element.958, f32[3]{0:T(128)} %bitcast.307, ...), kind=kLoop, calls=%fused_computation.clone.1 | loop fusion | flops 38141952 | bytes 8258257 | tf_op jit(solution)/shard_map/while/body/eval_jaxpr/add | solution.py:81
  292.0 5.2 subtract_multiply_fusion.2
  299.8 2.7 convert_compare_fusion.16
  304.2 10.8 %select_add_fusion.2 = f32[3,256,512]{2,1,0:T(8,128)} fusion(f32[3,256,512]{2,1,0:T(8,128)} %get-tuple-element.1047, f32[3,256,512]{2,1,0:T(8,128)S(1)} %get-tuple-element.1048, f32[256,512]{1,0:T(8,128)S(1)} %get-tuple-element.957, f32[3]{0:T(128)} %bitcast.279, f32[3]{0:T(128)} %get-tuple-element.958, f32[3]{0:T(128)} %bitcast.307, ...), kind=kLoop, calls=%fused_computation.clone.1 | loop fusion | flops 38141952 | bytes 8258257 | tf_op jit(solution)/shard_map/while/body/eval_jaxpr/add | solution.py:81
  315.4 5.2 subtract_multiply_fusion.2
  323.2 2.7 convert_compare_fusion.16
  327.6 10.8 %select_add_fusion.2 = f32[3,256,512]{2,1,0:T(8,128)} fusion(f32[3,256,512]{2,1,0:T(8,128)} %get-tuple-element.1047, f32[3,256,512]{2,1,0:T(8,128)S(1)} %get-tuple-element.1048, f32[256,512]{1,0:T(8,128)S(1)} %get-tuple-element.957, f32[3]{0:T(128)} %bitcast.279, f32[3]{0:T(128)} %get-tuple-element.958, f32[3]{0:T(128)} %bitcast.307, ...), kind=kLoop, calls=%fused_computation.clone.1 | loop fusion | flops 38141952 | bytes 8258257 | tf_op jit(solution)/shard_map/while/body/eval_jaxpr/add | solution.py:81
  338.8 5.2 subtract_multiply_fusion.2
  346.6 2.7 convert_compare_fusion.16
  351.0 10.8 %select_add_fusion.2 = f32[3,256,512]{2,1,0:T(8,128)} fusion(f32[3,256,512]{2,1,0:T(8,128)} %get-tuple-element.1047, f32[3,256,512]{2,1,0:T(8,128)S(1)} %get-tuple-element.1048, f32[256,512]{1,0:T(8,128)S(1)} %get-tuple-element.957, f32[3]{0:T(128)} %bitcast.279, f32[3]{0:T(128)} %get-tuple-element.958, f32[3]{0:T(128)} %bitcast.307, ...), kind=kLoop, calls=%fused_computation.clone.1 | loop fusion | flops 38141952 | bytes 8258257 | tf_op jit(solution)/shard_map/while/body/eval_jaxpr/add | solution.py:81
  362.2 5.2 subtract_multiply_fusion.2
  370.0 2.7 convert_compare_fusion.16
  374.4 10.8 %select_add_fusion.2 = f32[3,256,512]{2,1,0:T(8,128)} fusion(f32[3,256,512]{2,1,0:T(8,128)} %get-tuple-element.1047, f32[3,256,512]{2,1,0:T(8,128)S(1)} %get-tuple-element.1048, f32[256,512]{1,0:T(8,128)S(1)} %get-tuple-element.957, f32[3]{0:T(128)} %bitcast.279, f32[3]{0:T(128)} %get-tuple-element.958, f32[3]{0:T(128)} %bitcast.307, ...), kind=kLoop, calls=%fused_computation.clone.1 | loop fusion | flops 38141952 | bytes 8258257 | tf_op jit(solution)/shard_map/while/body/eval_jaxpr/add | solution.py:81
  385.6 5.2 subtract_multiply_fusion.2
  390.8 1.6 dynamic-slice_bitcast_fusion.4
  393.4 2.7 convert_compare_fusion.16
  397.8 10.8 %select_add_fusion.2 = f32[3,256,512]{2,1,0:T(8,128)} fusion(f32[3,256,512]{2,1,0:T(8,128)} %get-tuple-element.1047, f32[3,256,512]{2,1,0:T(8,128)S(1)} %get-tuple-element.1048, f32[256,512]{1,0:T(8,128)S(1)} %get-tuple-element.957, f32[3]{0:T(128)} %bitcast.279, f32[3]{0:T(128)} %get-tuple-element.958, f32[3]{0:T(128)} %bitcast.307, ...), kind=kLoop, calls=%fused_computation.clone.1 | loop fusion | flops 38141952 | bytes 8258257 | tf_op jit(solution)/shard_map/while/body/eval_jaxpr/add | solution.py:81
  409.0 5.2 subtract_multiply_fusion.2
  416.7 2.7 convert_compare_fusion.16
  421.2 10.8 %select_add_fusion.2 = f32[3,256,512]{2,1,0:T(8,128)} fusion(f32[3,256,512]{2,1,0:T(8,128)} %get-tuple-element.1047, f32[3,256,512]{2,1,0:T(8,128)S(1)} %get-tuple-element.1048, f32[256,512]{1,0:T(8,128)S(1)} %get-tuple-element.957, f32[3]{0:T(128)} %bitcast.279, f32[3]{0:T(128)} %get-tuple-element.958, f32[3]{0:T(128)} %bitcast.307, ...), kind=kLoop, calls=%fused_computation.clone.1 | loop fusion | flops 38141952 | bytes 8258257 | tf_op jit(solution)/shard_map/while/body/eval_jaxpr/add | solution.py:81
  432.4 5.2 subtract_multiply_fusion.2
  437.5 2.6 fusion.9
  441.6 35.6 %collective-permute-done.4 = f32[2,3,2,2,2,16,512]{6,5,4,3,2,1,0:T(8,128)} collective-permute-done((f32[2,3,2,2,2,16,512]{6,5,4,3,2,1,0:T(8,128)}, f32[2,3,2,2,2,16,512]{6,5,4,3,2,1,0:T(8,128)}, u32[]{:S(2)}, u32[]{:S(2)}) %collective-permute-start.4) | collective-permute-done | bytes 1572896 | tf_op jit(solution)/shard_map/ppermute | solution.py:23
  477.3 1.8 broadcast_select_fusion.1
  479.8 19.2 %collective-permute-done.5 = f32[2,3,2,2,16,512]{5,4,1,0,2,3:T(8,128)S(1)} collective-permute-done((f32[2,3,2,2,16,512]{5,4,1,0,2,3:T(8,128)S(1)}, f32[2,3,2,2,16,512]{5,4,1,0,2,3:T(8,128)S(1)}, u32[]{:S(2)}, u32[]{:S(2)}) %collective-permute-start.5) | collective-permute-done | bytes 786464 | tf_op jit(solution)/shard_map/ppermute | solution.py:23
  499.5 1.9 collective-permute-start.6
  501.4 8.5 %collective-permute-done.6 = f32[2,3,2,16,512]{4,3,1,0,2:T(8,128)S(1)} collective-permute-done((f32[2,3,2,16,512]{4,3,1,0,2:T(8,128)S(1)}, f32[2,3,2,16,512]{4,3,1,0,2:T(8,128)S(1)}, u32[]{:S(2)}, u32[]{:S(2)}) %collective-permute-start.6) | collective-permute-done | bytes 393248 | tf_op jit(solution)/shard_map/ppermute | solution.py:23
  510.1 2.8 collective-permute-start.7
  512.9 7.6 %collective-permute-done.7 = f32[2,3,16,512]{3,2,1,0:T(8,128)S(1)} collective-permute-done((f32[2,3,16,512]{3,2,1,0:T(8,128)S(1)}, f32[2,3,16,512]{3,2,1,0:T(8,128)S(1)}, u32[]{:S(2)}, u32[]{:S(2)}) %collective-permute-start.7) | collective-permute-done | bytes 196640 | tf_op jit(solution)/shard_map/ppermute | solution.py:23
  (1391 shorter events, 75.0 us)
Async XLA Ops:
  11.2 27.2 %collective-permute-start = (f32[1,256,512]{1,2,0:T(8,128)S(1)}, f32[1,256,512]{1,2,0:T(8,128)S(1)}, u32[]{:S(2)}, u32[]{:S(2)}) collective-permute-start(f32[1,256,512]{1,2,0:T(8,128)S(1)} %get-tuple-element.654), channel_id=1, source_target_pairs={{0,2},{2,4},{4,6},{6,8},{8,10},{10,12},{12,14},{14,16},{16,18},{18... | collective-permute-start | bytes 1572872 | tf_op jit(solution)/shard_map/ppermute | solution.py:14
  16.1 24.3 %collective-permute-start.1 = (f32[1,256,512]{1,2,0:T(8,128)S(1)}, f32[1,256,512]{1,2,0:T(8,128)S(1)}, u32[]{:S(2)}, u32[]{:S(2)}) collective-permute-start(f32[1,256,512]{1,2,0:T(8,128)S(1)} %get-tuple-element.655), channel_id=1, source_target_pairs={{2,0},{4,2},{6,4},{8,6},{10,8},{12,10},{14,12},{16,14},{18,16},{20... | collective-permute-start | bytes 1572872 | tf_op jit(solution)/shard_map/ppermute | solution.py:17
  18.4 25.6 %copy-start.13 = (f32[3,16]{1,0:T(4,128)S(1)}, f32[3,16]{1,0:T(4,128)}, u32[]{:S(2)}) copy-start(f32[3,16]{1,0:T(4,128)} %param.6) | copy-start | bytes 580
  41.4 3.8 collective-permute-start.2
  42.7 3.1 collective-permute-start.3
  116.8 11.2 %copy-start.4 = (pred[256,512]{1,0:T(8,128)(4,1)S(1)}, pred[256,512]{1,0:T(8,128)(4,1)}, u32[]{:S(2)}) copy-start(pred[256,512]{1,0:T(8,128)(4,1)} %get-tuple-element.979) | copy-start | bytes 393220 | tf_op jit(solution)/shard_map/while
  116.8 11.2 %copy-start.5 = (pred[256,512]{1,0:T(8,128)(4,1)S(1)}, pred[256,512]{1,0:T(8,128)(4,1)}, u32[]{:S(2)}) copy-start(pred[256,512]{1,0:T(8,128)(4,1)} %get-tuple-element.980) | copy-start | bytes 393220 | tf_op jit(solution)/shard_map/while
  116.8 11.2 %copy-start.6 = (pred[256,512]{1,0:T(8,128)(4,1)S(1)}, pred[256,512]{1,0:T(8,128)(4,1)}, u32[]{:S(2)}) copy-start(pred[256,512]{1,0:T(8,128)(4,1)} %get-tuple-element.981) | copy-start | bytes 393220 | tf_op jit(solution)/shard_map/while
  116.8 11.2 %copy-start.7 = (pred[256,512]{1,0:T(8,128)(4,1)S(1)}, pred[256,512]{1,0:T(8,128)(4,1)}, u32[]{:S(2)}) copy-start(pred[256,512]{1,0:T(8,128)(4,1)} %get-tuple-element.982) | copy-start | bytes 393220 | tf_op jit(solution)/shard_map/while
  116.8 11.2 %copy-start.8 = (pred[256,512]{1,0:T(8,128)(4,1)S(1)}, pred[256,512]{1,0:T(8,128)(4,1)}, u32[]{:S(2)}) copy-start(pred[256,512]{1,0:T(8,128)(4,1)} %get-tuple-element.983) | copy-start | bytes 393220 | tf_op jit(solution)/shard_map/while
  116.8 11.2 %copy-start.9 = (pred[256,512]{1,0:T(8,128)(4,1)S(1)}, pred[256,512]{1,0:T(8,128)(4,1)}, u32[]{:S(2)}) copy-start(pred[256,512]{1,0:T(8,128)(4,1)} %get-tuple-element.984) | copy-start | bytes 393220 | tf_op jit(solution)/shard_map/while
  116.8 11.2 %copy-start.10 = (pred[256,512]{1,0:T(8,128)(4,1)S(1)}, pred[256,512]{1,0:T(8,128)(4,1)}, u32[]{:S(2)}) copy-start(pred[256,512]{1,0:T(8,128)(4,1)} %get-tuple-element.985) | copy-start | bytes 393220 | tf_op jit(solution)/shard_map/while
  116.9 11.2 %copy-start.11 = (pred[256,512]{1,0:T(8,128)(4,1)S(1)}, pred[256,512]{1,0:T(8,128)(4,1)}, u32[]{:S(2)}) copy-start(pred[256,512]{1,0:T(8,128)(4,1)} %get-tuple-element.986) | copy-start | bytes 393220 | tf_op jit(solution)/shard_map/while
  116.9 11.2 %copy-start.12 = (pred[256,512]{1,0:T(8,128)(4,1)S(1)}, pred[256,512]{1,0:T(8,128)(4,1)}, u32[]{:S(2)}) copy-start(pred[256,512]{1,0:T(8,128)(4,1)} %get-tuple-element.987) | copy-start | bytes 393220 | tf_op jit(solution)/shard_map/while
  116.9 11.2 %copy-start.15 = (f32[3]{0:T(128)S(1)}, f32[3]{0:T(128)}, u32[]{:S(2)}) copy-start(f32[3]{0:T(128)} %get-tuple-element.1004) | copy-start | bytes 40 | tf_op jit(solution)/shard_map/while
  116.9 11.2 %copy-start.16 = (f32[3]{0:T(128)S(1)}, f32[3]{0:T(128)}, u32[]{:S(2)}) copy-start(f32[3]{0:T(128)} %get-tuple-element.990) | copy-start | bytes 40 | tf_op jit(solution)/shard_map/while
  116.9 11.2 %copy-start.17 = (f32[3]{0:T(128)S(1)}, f32[3]{0:T(128)}, u32[]{:S(2)}) copy-start(f32[3]{0:T(128)} %get-tuple-element.991) | copy-start | bytes 40 | tf_op jit(solution)/shard_map/while
  116.9 11.2 %copy-start.18 = (f32[3]{0:T(128)S(1)}, f32[3]{0:T(128)}, u32[]{:S(2)}) copy-start(f32[3]{0:T(128)} %get-tuple-element.992) | copy-start | bytes 40 | tf_op jit(solution)/shard_map/while
  116.9 11.2 %copy-start.19 = (f32[3]{0:T(128)S(1)}, f32[3]{0:T(128)}, u32[]{:S(2)}) copy-start(f32[3]{0:T(128)} %get-tuple-element.993) | copy-start | bytes 40 | tf_op jit(solution)/shard_map/while
  116.9 11.2 %copy-start.20 = (f32[3]{0:T(128)S(1)}, f32[3]{0:T(128)}, u32[]{:S(2)}) copy-start(f32[3]{0:T(128)} %get-tuple-element.994) | copy-start | bytes 40 | tf_op jit(solution)/shard_map/while
  116.9 11.2 %copy-start.21 = (f32[3]{0:T(128)S(1)}, f32[3]{0:T(128)}, u32[]{:S(2)}) copy-start(f32[3]{0:T(128)} %get-tuple-element.995) | copy-start | bytes 40 | tf_op jit(solution)/shard_map/while
  116.9 11.2 %copy-start.22 = (f32[3]{0:T(128)S(1)}, f32[3]{0:T(128)}, u32[]{:S(2)}) copy-start(f32[3]{0:T(128)} %get-tuple-element.996) | copy-start | bytes 40 | tf_op jit(solution)/shard_map/while
  117.0 11.2 %copy-start.23 = (f32[3]{0:T(128)S(1)}, f32[3]{0:T(128)}, u32[]{:S(2)}) copy-start(f32[3]{0:T(128)} %get-tuple-element.997) | copy-start | bytes 40 | tf_op jit(solution)/shard_map/while
  117.0 11.2 %copy-start.24 = (f32[3]{0:T(128)S(1)}, f32[3]{0:T(128)}, u32[]{:S(2)}) copy-start(f32[3]{0:T(128)} %get-tuple-element.998) | copy-start | bytes 40 | tf_op jit(solution)/shard_map/while
  117.0 11.2 %copy-start.25 = (f32[3]{0:T(128)S(1)}, f32[3]{0:T(128)}, u32[]{:S(2)}) copy-start(f32[3]{0:T(128)} %get-tuple-element.999) | copy-start | bytes 40 | tf_op jit(solution)/shard_map/while
  117.0 11.2 %copy-start.26 = (f32[3]{0:T(128)S(1)}, f32[3]{0:T(128)}, u32[]{:S(2)}) copy-start(f32[3]{0:T(128)} %get-tuple-element.1000) | copy-start | bytes 40 | tf_op jit(solution)/shard_map/while
  117.0 11.2 %copy-start.27 = (f32[3]{0:T(128)S(1)}, f32[3]{0:T(128)}, u32[]{:S(2)}) copy-start(f32[3]{0:T(128)} %get-tuple-element.1001) | copy-start | bytes 40 | tf_op jit(solution)/shard_map/while
  117.0 11.2 %copy-start.28 = (f32[3]{0:T(128)S(1)}, f32[3]{0:T(128)}, u32[]{:S(2)}) copy-start(f32[3]{0:T(128)} %get-tuple-element.1002) | copy-start | bytes 40 | tf_op jit(solution)/shard_map/while
  117.0 11.2 %copy-start.29 = (f32[3]{0:T(128)S(1)}, f32[3]{0:T(128)}, u32[]{:S(2)}) copy-start(f32[3]{0:T(128)} %get-tuple-element.1003) | copy-start | bytes 40 | tf_op jit(solution)/shard_map/while
  117.0 11.2 %copy-start.30 = (f32[3,1,1]{0,2,1:T(1,128)S(1)}, f32[3,1,1]{0,2,1:T(1,128)}, u32[]{:S(2)}) copy-start(f32[3,1,1]{0,2,1:T(1,128)} %get-tuple-element.1122) | copy-start | bytes 40 | tf_op jit(solution)/shard_map/while
  117.0 11.2 %copy-start.31 = (f32[3,1,1]{0,2,1:T(1,128)S(1)}, f32[3,1,1]{0,2,1:T(1,128)}, u32[]{:S(2)}) copy-start(f32[3,1,1]{0,2,1:T(1,128)} %get-tuple-element.1120) | copy-start | bytes 40 | tf_op jit(solution)/shard_map/while
  117.0 11.2 %copy-start.32 = (f32[3,1,1]{0,2,1:T(1,128)S(1)}, f32[3,1,1]{0,2,1:T(1,128)}, u32[]{:S(2)}) copy-start(f32[3,1,1]{0,2,1:T(1,128)} %get-tuple-element.1119) | copy-start | bytes 40 | tf_op jit(solution)/shard_map/while
  117.1 11.2 %copy-start.33 = (f32[3,1,1]{0,2,1:T(1,128)S(1)}, f32[3,1,1]{0,2,1:T(1,128)}, u32[]{:S(2)}) copy-start(f32[3,1,1]{0,2,1:T(1,128)} %get-tuple-element.1118) | copy-start | bytes 40 | tf_op jit(solution)/shard_map/while
  117.1 11.2 %copy-start.34 = (f32[3,1,1]{0,2,1:T(1,128)S(1)}, f32[3,1,1]{0,2,1:T(1,128)}, u32[]{:S(2)}) copy-start(f32[3,1,1]{0,2,1:T(1,128)} %get-tuple-element.1117) | copy-start | bytes 40 | tf_op jit(solution)/shard_map/while
  117.1 11.2 %copy-start.35 = (f32[3,1,1]{0,2,1:T(1,128)S(1)}, f32[3,1,1]{0,2,1:T(1,128)}, u32[]{:S(2)}) copy-start(f32[3,1,1]{0,2,1:T(1,128)} %get-tuple-element.1116) | copy-start | bytes 40 | tf_op jit(solution)/shard_map/while
  117.1 11.2 %copy-start.36 = (f32[3,1,1]{0,2,1:T(1,128)S(1)}, f32[3,1,1]{0,2,1:T(1,128)}, u32[]{:S(2)}) copy-start(f32[3,1,1]{0,2,1:T(1,128)} %get-tuple-element.1115) | copy-start | bytes 40 | tf_op jit(solution)/shard_map/while
  117.1 11.2 %copy-start.37 = (f32[3,1,1]{0,2,1:T(1,128)S(1)}, f32[3,1,1]{0,2,1:T(1,128)}, u32[]{:S(2)}) copy-start(f32[3,1,1]{0,2,1:T(1,128)} %get-tuple-element.1114) | copy-start | bytes 40 | tf_op jit(solution)/shard_map/while
  117.1 11.2 %copy-start.38 = (f32[3,1,1]{0,2,1:T(1,128)S(1)}, f32[3,1,1]{0,2,1:T(1,128)}, u32[]{:S(2)}) copy-start(f32[3,1,1]{0,2,1:T(1,128)} %get-tuple-element.1113) | copy-start | bytes 40 | tf_op jit(solution)/shard_map/while
  117.1 11.2 %copy-start.39 = (f32[3,1,1]{0,2,1:T(1,128)S(1)}, f32[3,1,1]{0,2,1:T(1,128)}, u32[]{:S(2)}) copy-start(f32[3,1,1]{0,2,1:T(1,128)} %get-tuple-element.1108) | copy-start | bytes 40 | tf_op jit(solution)/shard_map/while
  117.1 11.2 %copy-start.40 = (f32[3,1,1]{0,2,1:T(1,128)S(1)}, f32[3,1,1]{0,2,1:T(1,128)}, u32[]{:S(2)}) copy-start(f32[3,1,1]{0,2,1:T(1,128)} %get-tuple-element.1109) | copy-start | bytes 40 | tf_op jit(solution)/shard_map/while
  117.1 11.2 %copy-start.41 = (f32[3,1,1]{0,2,1:T(1,128)S(1)}, f32[3,1,1]{0,2,1:T(1,128)}, u32[]{:S(2)}) copy-start(f32[3,1,1]{0,2,1:T(1,128)} %get-tuple-element.1110) | copy-start | bytes 40 | tf_op jit(solution)/shard_map/while
  117.1 11.2 %copy-start.42 = (f32[3,1,1]{0,2,1:T(1,128)S(1)}, f32[3,1,1]{0,2,1:T(1,128)}, u32[]{:S(2)}) copy-start(f32[3,1,1]{0,2,1:T(1,128)} %get-tuple-element.1111) | copy-start | bytes 40 | tf_op jit(solution)/shard_map/while
  163.6 11.2 %copy-start.4 = (pred[256,512]{1,0:T(8,128)(4,1)S(1)}, pred[256,512]{1,0:T(8,128)(4,1)}, u32[]{:S(2)}) copy-start(pred[256,512]{1,0:T(8,128)(4,1)} %get-tuple-element.979) | copy-start | bytes 393220 | tf_op jit(solution)/shard_map/while
  163.6 11.2 %copy-start.5 = (pred[256,512]{1,0:T(8,128)(4,1)S(1)}, pred[256,512]{1,0:T(8,128)(4,1)}, u32[]{:S(2)}) copy-start(pred[256,512]{1,0:T(8,128)(4,1)} %get-tuple-element.980) | copy-start | bytes 393220 | tf_op jit(solution)/shard_map/while
  163.6 11.2 %copy-start.6 = (pred[256,512]{1,0:T(8,128)(4,1)S(1)}, pred[256,512]{1,0:T(8,128)(4,1)}, u32[]{:S(2)}) copy-start(pred[256,512]{1,0:T(8,128)(4,1)} %get-tuple-element.981) | copy-start | bytes 393220 | tf_op jit(solution)/shard_map/while
  163.6 11.2 %copy-start.7 = (pred[256,512]{1,0:T(8,128)(4,1)S(1)}, pred[256,512]{1,0:T(8,128)(4,1)}, u32[]{:S(2)}) copy-start(pred[256,512]{1,0:T(8,128)(4,1)} %get-tuple-element.982) | copy-start | bytes 393220 | tf_op jit(solution)/shard_map/while
  163.6 11.2 %copy-start.8 = (pred[256,512]{1,0:T(8,128)(4,1)S(1)}, pred[256,512]{1,0:T(8,128)(4,1)}, u32[]{:S(2)}) copy-start(pred[256,512]{1,0:T(8,128)(4,1)} %get-tuple-element.983) | copy-start | bytes 393220 | tf_op jit(solution)/shard_map/while
  163.6 11.2 %copy-start.9 = (pred[256,512]{1,0:T(8,128)(4,1)S(1)}, pred[256,512]{1,0:T(8,128)(4,1)}, u32[]{:S(2)}) copy-start(pred[256,512]{1,0:T(8,128)(4,1)} %get-tuple-element.984) | copy-start | bytes 393220 | tf_op jit(solution)/shard_map/while
  163.6 11.2 %copy-start.10 = (pred[256,512]{1,0:T(8,128)(4,1)S(1)}, pred[256,512]{1,0:T(8,128)(4,1)}, u32[]{:S(2)}) copy-start(pred[256,512]{1,0:T(8,128)(4,1)} %get-tuple-element.985) | copy-start | bytes 393220 | tf_op jit(solution)/shard_map/while
  163.6 11.2 %copy-start.11 = (pred[256,512]{1,0:T(8,128)(4,1)S(1)}, pred[256,512]{1,0:T(8,128)(4,1)}, u32[]{:S(2)}) copy-start(pred[256,512]{1,0:T(8,128)(4,1)} %get-tuple-element.986) | copy-start | bytes 393220 | tf_op jit(solution)/shard_map/while
  163.6 11.2 %copy-start.12 = (pred[256,512]{1,0:T(8,128)(4,1)S(1)}, pred[256,512]{1,0:T(8,128)(4,1)}, u32[]{:S(2)}) copy-start(pred[256,512]{1,0:T(8,128)(4,1)} %get-tuple-element.987) | copy-start | bytes 393220 | tf_op jit(solution)/shard_map/while
  163.6 11.2 %copy-start.15 = (f32[3]{0:T(128)S(1)}, f32[3]{0:T(128)}, u32[]{:S(2)}) copy-start(f32[3]{0:T(128)} %get-tuple-element.1004) | copy-start | bytes 40 | tf_op jit(solution)/shard_map/while
  163.7 11.2 %copy-start.16 = (f32[3]{0:T(128)S(1)}, f32[3]{0:T(128)}, u32[]{:S(2)}) copy-start(f32[3]{0:T(128)} %get-tuple-element.990) | copy-start | bytes 40 | tf_op jit(solution)/shard_map/while
  163.7 11.2 %copy-start.17 = (f32[3]{0:T(128)S(1)}, f32[3]{0:T(128)}, u32[]{:S(2)}) copy-start(f32[3]{0:T(128)} %get-tuple-element.991) | copy-start | bytes 40 | tf_op jit(solution)/shard_map/while
  163.7 11.2 %copy-start.18 = (f32[3]{0:T(128)S(1)}, f32[3]{0:T(128)}, u32[]{:S(2)}) copy-start(f32[3]{0:T(128)} %get-tuple-element.992) | copy-start | bytes 40 | tf_op jit(solution)/shard_map/while
  163.7 11.2 %copy-start.19 = (f32[3]{0:T(128)S(1)}, f32[3]{0:T(128)}, u32[]{:S(2)}) copy-start(f32[3]{0:T(128)} %get-tuple-element.993) | copy-start | bytes 40 | tf_op jit(solution)/shard_map/while
  163.7 11.2 %copy-start.20 = (f32[3]{0:T(128)S(1)}, f32[3]{0:T(128)}, u32[]{:S(2)}) copy-start(f32[3]{0:T(128)} %get-tuple-element.994) | copy-start | bytes 40 | tf_op jit(solution)/shard_map/while
  163.7 11.2 %copy-start.21 = (f32[3]{0:T(128)S(1)}, f32[3]{0:T(128)}, u32[]{:S(2)}) copy-start(f32[3]{0:T(128)} %get-tuple-element.995) | copy-start | bytes 40 | tf_op jit(solution)/shard_map/while
  163.7 11.2 %copy-start.22 = (f32[3]{0:T(128)S(1)}, f32[3]{0:T(128)}, u32[]{:S(2)}) copy-start(f32[3]{0:T(128)} %get-tuple-element.996) | copy-start | bytes 40 | tf_op jit(solution)/shard_map/while
  437.5 39.7 %copy-start = (f32[3,256,512]{2,1,0:T(8,128)S(1)}, f32[3,256,512]{2,1,0:T(8,128)}, u32[]{:S(2)}) copy-start(f32[3,256,512]{2,1,0:T(8,128)} %get-tuple-element.314) | copy-start | bytes 4718596
  440.1 37.1 %collective-permute-start.4 = (f32[2,3,2,2,2,16,512]{6,5,4,3,2,1,0:T(8,128)}, f32[2,3,2,2,2,16,512]{6,5,4,3,2,1,0:T(8,128)}, u32[]{:S(2)}, u32[]{:S(2)}) collective-permute-start(f32[2,3,2,2,2,16,512]{6,5,4,3,2,1,0:T(8,128)} %fusion.9), channel_id=1, source_target_pairs={{0,2},{2,0},{4,6},{6,4},{8,10},{10,8},{12,14},{14,12},{16,18},{18,... | collective-permute-start | bytes 4718600 | tf_op jit(solution)/shard_map/ppermute | solution.py:23
  479.7 19.3 %collective-permute-start.5 = (f32[2,3,2,2,16,512]{5,4,1,0,2,3:T(8,128)S(1)}, f32[2,3,2,2,16,512]{5,4,1,0,2,3:T(8,128)S(1)}, u32[]{:S(2)}, u32[]{:S(2)}) collective-permute-start(f32[2,3,2,2,16,512]{5,4,1,0,2,3:T(8,128)S(1)} %bitcast.232), channel_id=1, source_target_pairs={{0,4},{2,6},{4,0},{6,2},{8,12},{10,14},{12,8},{14,10},{16,20},{18,... | collective-permute-start | bytes 2359304 | tf_op jit(solution)/shard_map/ppermute | solution.py:23
  499.5 10.4 %collective-permute-start.6 = (f32[2,3,2,16,512]{4,3,1,0,2:T(8,128)S(1)}, f32[2,3,2,16,512]{4,3,1,0,2:T(8,128)S(1)}, u32[]{:S(2)}, u32[]{:S(2)}) collective-permute-start(f32[2,3,2,16,512]{4,3,1,0,2:T(8,128)S(1)} %fusion.16), channel_id=1, source_target_pairs={{0,8},{2,10},{4,12},{6,14},{8,0},{10,2},{12,4},{14,6},{16,24},{18,... | collective-permute-start | bytes 1179656 | tf_op jit(solution)/shard_map/ppermute | solution.py:23
  510.1 10.4 %collective-permute-start.7 = (f32[2,3,16,512]{3,2,1,0:T(8,128)S(1)}, f32[2,3,16,512]{3,2,1,0:T(8,128)S(1)}, u32[]{:S(2)}, u32[]{:S(2)}) collective-permute-start(f32[2,3,16,512]{3,2,1,0:T(8,128)S(1)} %fusion.21), channel_id=1, source_target_pairs={{0,16},{2,18},{4,20},{6,22},{8,24},{10,26},{12,28},{14,30},{16,0},... | collective-permute-start | bytes 589832 | tf_op jit(solution)/shard_map/ppermute | solution.py:23
  (587 other events, 6552.7 us)
where the time goes:
time: 523 us; the launch traced here: 521 us
  other arithmetic  326 us (62%)
  waiting for transfers between devices  93.5 us (18%)
  local copies, waits for them, and re-layouts  74.7 us (14%)
  starting transfers between devices  15.1 us (3%)
  loops' own time  10.7 us (2%)
    add x16, other arithmetic, march(): return (colour + transmit * sample, transmit * (1.0 - opacity_step))  172 us
    mul x16, other arithmetic, march(): return (colour + transmit * sample, transmit * (1.0 - opacity_step))  82.7 us
    ppermute x4, waiting for transfers between devices, from_partner(): lax.ppermute(value, axis, [(i, i ^ 1 << distance) for i in range(lax.axis...  70.8 us
    eq x16, other arithmetic, lookup_table(): result = jnp.where((interval == k)[None], value, result)  43.8 us
    squeeze x16, local copies, waits for them, and re-layouts, march(): upper_plane = lax.dynamic_index_in_dim(padded, plane + 2, 0, keepdims=False)  25.9 us
    unnamed x10, local copies, waits for them, and re-layouts  21.1 us
    add x32, local copies, waits for them, and re-layouts, lookup_table(): table[:, k][:, None, None]  20.6 us
    ppermute x2, waiting for transfers between devices, extended(): lax.ppermute(lax.slice_in_dim(block, block.shape[dim] - width, None, axis...  20.1 us
  transfers between devices with their start and end apart: 8, of which 7 were waited for; matrix products, arithmetic and copies ran while one was open for 0% of the time, Pallas kernels for 0%

commit v1 on v0

v1 whole, which is shorter than its diff:
```python
import functools

import jax
import jax.numpy as jnp
from jax import lax
from jax.experimental import pallas as pl
from jax.experimental.pallas import tpu as pltpu
from jax.sharding import PartitionSpec as P

LIGHT_DIR = (0.2672612, 0.5345225, 0.8017837)
LANES = 128
SUBLANES = 8
PAD = 8


def segment_tables(tf_emission, tf_absorption, depth_total):
    count_breaks = tf_emission.shape[1]
    scale = 0.5 * (count_breaks - 1)
    tables = jnp.concatenate([tf_emission, tf_absorption * (4.0 / depth_total)], axis=0)
    rise = tables[:, 1:] - tables[:, :-1]
    knots = jnp.arange(count_breaks - 1, dtype=jnp.float32)
    intercept = tables[:, :-1] + rise * (scale - knots)
    slope = rise * scale
    both = jnp.concatenate([intercept, slope], axis=0)
    both = jnp.concatenate([both, both[:, -1:]], axis=1)
    both = jnp.pad(both, ((0, 0), (0, LANES - count_breaks)))
    return jnp.broadcast_to(both[:, None, :], (12, SUBLANES, LANES))


def lookup(table, index):
    return jnp.take_along_axis(table, index, axis=1, mode="promise_in_bounds")


def march_kernel(
    scale, tables, field, low, high, edges, image, cells, canvas, in_sems, out_sems
):
    planes, height, width = field.shape
    tiles = width // LANES
    stride = height // SUBLANES
    body_rows = pl.ds(PAD, height)

    def columns(tile):
        return pl.ds(tile * LANES, LANES)

    def incoming(slot):
        if slot in (0, tiles + 1):
            return [
                pltpu.make_async_copy(
                    edges, cells.at[slot, pl.ds(1, planes), body_rows, :], in_sems.at[slot, 0]
                )
            ]
        here = columns(slot - 1)
        return [
            pltpu.make_async_copy(
                field.at[:, :, here],
                cells.at[slot, pl.ds(1, planes), body_rows, :],
                in_sems.at[slot, 0],
            ),
            pltpu.make_async_copy(
                low.at[:, here], cells.at[slot, 0, body_rows, :], in_sems.at[slot, 1]
            ),
            pltpu.make_async_copy(
                high.at[:, here], cells.at[slot, planes + 1, body_rows, :], in_sems.at[slot, 2]
            ),
        ]

    def outgoing(tile):
        return pltpu.make_async_copy(
            canvas.at[tile], image.at[:, :, columns(tile)], out_sems.at[tile]
        )

    for slot in range(tiles + 2):
        for copy in incoming(slot):
            copy.start()
    zeros = jnp.zeros((planes, 1, LANES), jnp.float32)
    for slot in range(1, tiles + 1):
        cells[slot, pl.ds(1, planes), pl.ds(PAD - 1, 1), :] = zeros
        cells[slot, pl.ds(1, planes), pl.ds(PAD + height, 1), :] = zeros
    lane = lax.broadcasted_iota(jnp.int32, (SUBLANES, LANES), 1)
    first_lane = lane == 0
    last_lane = lane == LANES - 1

    def strip(slot, row):
        def rows(part, plane, offset):
            return cells[part, plane, pl.ds(PAD + row + offset, SUBLANES, stride=stride), :]

        table = [tables[k] for k in range(12)]
        colour = [None] * 3
        transmit = [None] * 3
        before = rows(slot, 0, 0)
        centre = rows(slot, 1, 0)
        for plane in range(1, planes + 1):
            after = rows(slot, plane + 1, 0)
            left = pltpu.roll(jnp.where(last_lane, rows(slot - 1, plane, 0), centre), 1, 1)
            right = pltpu.roll(
                jnp.where(first_lane, rows(slot + 1, plane, 0), centre), LANES - 1, 1
            )
            diff_x = right - left
            diff_y = rows(slot, plane, 1) - rows(slot, plane, -1)
            diff_z = after - before
            inverse = lax.rsqrt(diff_x * diff_x + diff_y * diff_y + diff_z * diff_z + 1.0)
            facing = (
                (0.9 * LIGHT_DIR[0]) * diff_x
                + (0.9 * LIGHT_DIR[1]) * diff_y
                + (0.9 * LIGHT_DIR[2]) * diff_z
            ) * inverse
            shading = jnp.maximum(facing, 0.0) + 0.1
            weight = 1.0 - 0.75 * (inverse * inverse)
            interval = (centre * scale + scale).astype(jnp.int32)
            values = [
                lookup(table[k], interval) + lookup(table[k + 6], interval) * centre
                for k in range(6)
            ]
            for ch in range(3):
                step = values[3 + ch] * weight
                glow = values[ch] * shading
                if plane == 1:
                    colour[ch] = step * glow
                    transmit[ch] = 1.0 - step
                else:
                    seen = transmit[ch] * step
                    colour[ch] = colour[ch] + seen * glow
                    transmit[ch] = transmit[ch] - seen
            before, centre = centre, after
        for ch in range(3):
            target = pl.ds(row, SUBLANES, stride=stride)
            canvas[slot - 1, ch, target, :] = colour[ch]
            canvas[slot - 1, 3 + ch, target, :] = transmit[ch]

    for copy in incoming(0) + incoming(1):
        copy.wait()
    for slot in range(1, tiles + 1):
        for copy in incoming(slot + 1):
            copy.wait()

        @pl.loop(0, stride)
        def _(row):
            strip(slot, row)

        outgoing(slot - 1).start()
    for tile in range(tiles):
        outgoing(tile).wait()


def march(tables, field, low, high, edges, count_breaks):
    planes, height, width = field.shape
    tiles = width // LANES
    anywhere = pl.BlockSpec(memory_space=pl.ANY)
    return pl.pallas_call(
        functools.partial(march_kernel, 0.5 * (count_breaks - 1)),
        out_shape=jax.ShapeDtypeStruct((6, height, width), jnp.float32),
        in_specs=[pl.BlockSpec(memory_space=pltpu.VMEM)] + [anywhere] * 4,
        out_specs=anywhere,
        scratch_shapes=[
            pltpu.VMEM((tiles + 2, planes + 2, height + 2 * PAD, LANES), jnp.float32),
            pltpu.VMEM((tiles, 6, height, LANES), jnp.float32),
            pltpu.SemaphoreType.DMA((tiles + 2, 3)),
            pltpu.SemaphoreType.DMA((tiles,)),
        ],
        compiler_params=pltpu.CompilerParams(vmem_limit_bytes=40 * 1024 * 1024),
        cost_estimate=pl.CostEstimate(
            flops=planes * height * width * 80,
            bytes_accessed=planes * height * width * 5,
            transcendentals=0,
        ),
    )(tables, field, low, high, edges)


def neighbours(first, last, axis):
    count = lax.axis_size(axis)
    forward = [(i, i + 1) for i in range(count - 1)]
    backward = [(i + 1, i) for i in range(count - 1)]
    return lax.ppermute(last, axis, forward), lax.ppermute(first, axis, backward)


def over(near, far):
    return (
        [near[0] + near[1] * far[0], near[1] * far[1]]
    )


def ordered(is_far, own, other):
    near = [jnp.where(is_far, b, a) for a, b in zip(own, other)]
    far = [jnp.where(is_far, a, b) for a, b in zip(own, other)]
    return over(near, far)


def exchange(image, slab_index, shift, bits):
    size = 1 << bits
    count = lax.axis_size("slab")
    own = (slab_index >> shift) & (size - 1)
    parts = []
    for change in range(size):
        part = lax.dynamic_index_in_dim(image, own ^ change, 2, keepdims=False)
        if change:
            part = lax.ppermute(part, "slab", [(i, i ^ change << shift) for i in range(count)])
        parts.append([part[:3], part[3:]])
    for digit in range(bits):
        is_far = (own >> digit & 1) == 1
        parts = [ordered(is_far, parts[k], parts[k + 1]) for k in range(0, len(parts), 2)]
    return parts[0]


def per_device(field, tf_emission, tf_absorption):
    slab_count = lax.axis_size("slab")
    planes, height, width = field.shape
    low, high = neighbours(field[0], field[-1], "slab")
    left, right = neighbours(field[:, :, 0], field[:, :, -1], "tile")
    edge_lane = lax.broadcasted_iota(jnp.int32, (1, 1, LANES), 2) == 0
    edges = jnp.where(edge_lane, right[:, :, None], left[:, :, None])
    tables = segment_tables(tf_emission, tf_absorption, planes * slab_count)
    image = march(tables, field, low, high, edges, tf_emission.shape[1])
    levels = slab_count.bit_length() - 1
    block_rows = height // slab_count
    slab_index = lax.axis_index("slab")
    for shift in range(0, levels, 2):
        bits = min(2, levels - shift)
        outer = slab_count >> (shift + bits)
        image = image.reshape((6, outer, 1 << bits, block_rows, width))
        pair = exchange(image, slab_index, shift, bits)
        if outer > 1:
            image = jnp.concatenate(pair, axis=0)
    colour, transmit = (part.reshape((3, block_rows, width)) for part in pair)
    return colour, 1.0 - transmit


def solution(mesh):
    placed = (P("slab", None, "tile"), P(), P())
    return jax.shard_map(
        per_device,
        mesh=mesh,
        in_specs=placed,
        out_specs=(P(None, "slab", "tile"), P(None, "slab", "tile")),
        check_vma=False,
    )
```

time: 523 us -> 166 us (0.32)
  other arithmetic: 326 us -> 4.13 us
  Pallas kernels: 0 us -> 59.5 us
  local copies, waits for them, and re-layouts: 74.7 us -> 15.2 us
  waiting for transfers between devices: 93.5 us -> 66.3 us
  loops' own time: 10.7 us -> 0 us
    add x16 -> x1, other arithmetic: 172 us -> 0.08 us  [segment_tables(): intercept = tables[:, :-1] + rise * (scale - knots)]
    mul x35 -> x2, other arithmetic: 95.1 us -> 1.99 us  [the longest x1 1.98 us: over(): return [near[0] + near[1] * far[0], near[1] * far[1]]]
    pallas_call x0 -> x1, Pallas kernels: none -> 59.5 us  [march(): pl.pallas_call(functools.partial(march_kernel, 0.5 * (count_breaks - 1)),...]
    eq x16 -> x1, other arithmetic: 43.8 us -> 0.01 us  [per_device(): edge_lane = lax.broadcasted_iota(jnp.int32, (1, 1, LANES), 2) == 0]
    ppermute x8 -> x10, waiting for transfers between devices: 93.5 us -> 66.3 us  [the longest x6 45.9 us: exchange(): lax.ppermute(part, 'slab', [(i, i ^ change << shift) for i in range(count)])]
    squeeze x16 -> x1, local copies, waits for them, and re-layouts: 25.9 us -> 1.27 us  [per_device(): low, high = neighbours(field[0], field[-1], 'slab')]
    add x32 -> x0, local copies, waits for them, and re-layouts: 20.6 us -> none  [lookup_table(): table[:, k][:, None, None]]
    unnamed x10 -> x14, local copies, waits for them, and re-layouts: 21.1 us -> 6.49 us
  transfers between devices with their start and end apart: 8 -> 10, of which waited for: 7 -> 6; matrix products, arithmetic and copies ran while one was open for 0% -> 3% of each run, Pallas kernels for 0% -> 0%
where the time goes in v1:
time: 166 us
  waiting for transfers between devices  66.3 us (40%)
  Pallas kernels  59.5 us (36%)
  starting transfers between devices  19.8 us (12%)
  local copies, waits for them, and re-layouts  15.2 us (9%)
  other arithmetic  4.13 us (2%)
    pallas_call x1, Pallas kernels, march(): pl.pallas_call(functools.partial(march_kernel, 0.5 * (count_breaks - 1)),...  59.5 us
    ppermute x6, waiting for transfers between devices, exchange(): lax.ppermute(part, 'slab', [(i, i ^ change << shift) for i in range(count)])  45.9 us
    ppermute x2, waiting for transfers between devices, neighbours(): lax.ppermute(last, axis, forward)  19.2 us
    ppermute x6, starting transfers between devices, exchange(): lax.ppermute(part, 'slab', [(i, i ^ change << shift) for i in range(count)])  9.33 us
    ppermute x2, starting transfers between devices, neighbours(): lax.ppermute(last, axis, forward)  7.9 us
    unnamed x14, local copies, waits for them, and re-layouts  6.49 us
    slice x1, local copies, waits for them, and re-layouts, per_device(): left, right = neighbours(field[:, :, 0], field[:, :, -1], 'tile')  4.29 us
  transfers between devices with their start and end apart: 10, of which 6 were waited for; matrix products, arithmetic and copies ran while one was open for 3% of the time, Pallas kernels for 0%

profile of v1, /device:TPU:0, one launch (start us, length us, event | category | flops | bytes accessed | tf_op | source)
XLA Modules:
  0.0 165.7 jit_solution(5295350352508631921)
XLA Ops:
  0.6 4.3 %fusion.6 = (f32[16,256,1]{2,1,0:T(8,128)}, f32[16,256,1]{2,1,0:T(8,128)S(1)}) fusion(f32[16,256,512]{2,1,0:T(8,128)} %field.1), kind=kLoop, calls=%fused_computation.49 | loop fusion | bytes 65536 | tf_op jit(solution)/shard_map/slice | solution.py:208
  4.9 2.2 %copy.15 = f32[16,256,1]{1,0,2:T(8,128)S(1)} copy(f32[16,256,1]{2,1,0:T(8,128)} %get-tuple-element.2) | data formatting | bytes 32768
  7.1 1.3 collective-permute-start.2
  8.4 0.0 copy-start.4
  8.4 0.0 copy-start.5
  8.4 0.6 copy.16
  9.0 3.0 %collective-permute-start.3 = (f32[16,256]{1,0:T(8,128)S(1)}, f32[16,256]{1,0:T(8,128)S(1)}, u32[]{:S(2)}, u32[]{:S(2)}) collective-permute-start(f32[16,256]{1,0:T(8,128)S(1)} %bitcast.41), channel_id=1, source_target_pairs={{0,1},{2,3},{4,5},{6,7},{8,9},{10,11},{12,13},{14,15},{16,17},{18,... | collective-permute-start | bytes 49160 | tf_op jit(solution)/shard_map/ppermute | solution.py:173
  12.1 1.3 slice_bitcast_fusion
  13.4 4.9 %collective-permute-start = (f32[256,512]{1,0:T(8,128)S(1)}, f32[256,512]{1,0:T(8,128)S(1)}, u32[]{:S(2)}, u32[]{:S(2)}) collective-permute-start(f32[256,512]{1,0:T(8,128)S(1)} %get-tuple-element.5), channel_id=1, source_target_pairs={{0,2},{2,4},{4,6},{6,8},{8,10},{10,12},{12,14},{14,16},{16,18},{18... | collective-permute-start | bytes 1572872 | tf_op jit(solution)/shard_map/ppermute | solution.py:173
  18.2 1.3 collective-permute-start.1
  19.6 0.0 copy-done.4
  19.6 0.0 copy-done.5
  19.6 0.1 multiply_add_fusion.1
  19.7 0.1 fusion.5
  19.8 0.0 collective-permute-done.2
  19.8 0.0 collective-permute-done.3
  19.8 1.1 broadcast_select_fusion.edges
  20.9 19.2 %collective-permute-done.low = f32[256,512]{1,0:T(8,128)S(1)} collective-permute-done((f32[256,512]{1,0:T(8,128)S(1)}, f32[256,512]{1,0:T(8,128)S(1)}, u32[]{:S(2)}, u32[]{:S(2)}) %collective-permute-start) | collective-permute-done | bytes 524320 | tf_op jit(solution)/shard_map/ppermute | solution.py:173
  40.2 0.0 copy-start
  40.2 0.8 copy-done
  41.0 1.1 collective-permute-done.1.high
  42.1 0.0 copy-start.2
  42.1 0.8 copy-done.2
  42.9 0.0 copy-start.1
  42.9 1.0 copy-done.1
  43.9 0.0 copy-start.3
  44.0 1.0 copy-done.3
  45.0 59.5 %shard_map.50 = f32[6,256,512]{2,1,0:T(8,128)S(1)} custom-call(f32[12,8,128]{2,1,0:T(8,128)S(1)} %broadcast_in_dim.33.tables, f32[16,256,512]{2,1,0:T(8,128)} %field.1, f32[256,512]{1,0:T(8,128)S(1)} %copy-done.1, f32[256,512]{1,0:T(8,128)S(1)} %copy-done.3, f32[16,256,128]{2,1,0:T(8,128)S(1)} %broadcast_select_fusion.edges), custom_call_target="tpu_custom_call" | custom-call | flops 167772160 | bytes 10485760 | tf_op jit(solution)/shard_map/pallas_call | solution.py:149
  104.5 0.2 constant_dynamic-slice_fusion.4
  104.7 1.0 copy.41
  105.6 0.0 collective-permute-start.4
  105.6 0.9 copy.40
  106.6 3.0 %collective-permute-start.5 = (f32[6,4,16,512]{3,2,0,1:T(8,128)}, f32[6,4,16,512]{3,2,0,1:T(8,128)}, u32[]{:S(2)}, u32[]{:S(2)}) collective-permute-start(f32[6,4,16,512]{3,2,0,1:T(8,128)} %bitcast.36), channel_id=1, source_target_pairs={{0,4},{2,6},{4,0},{6,2},{8,12},{10,14},{12,8},{14,10},{16,20},{18,... | collective-permute-start | bytes 2359304 | tf_op jit(solution)/shard_map/ppermute | solution.py:196
  109.5 1.0 copy.39
  110.5 0.5 collective-permute-start.6
  111.0 0.1 constant_dynamic-slice_fusion.1
  111.1 16.3 %collective-permute-done.4 = f32[6,4,16,512]{3,2,0,1:T(8,128)} collective-permute-done((f32[6,4,16,512]{3,2,0,1:T(8,128)}, f32[6,4,16,512]{3,2,0,1:T(8,128)}, u32[]{:S(2)}, u32[]{:S(2)}) %collective-permute-start.4) | collective-permute-done | bytes 786464 | tf_op jit(solution)/shard_map/ppermute | solution.py:196
  127.4 14.2 %collective-permute-done.5 = f32[6,4,16,512]{3,2,0,1:T(8,128)} collective-permute-done((f32[6,4,16,512]{3,2,0,1:T(8,128)}, f32[6,4,16,512]{3,2,0,1:T(8,128)}, u32[]{:S(2)}, u32[]{:S(2)}) %collective-permute-start.5) | collective-permute-done | bytes 786464 | tf_op jit(solution)/shard_map/ppermute | solution.py:196
  141.6 0.0 collective-permute-done.6
  141.6 2.0 %select_multiply_fusion = (f32[3,4,16,512]{3,2,0,1:T(8,128)S(1)}, f32[3,4,16,512]{3,2,0,1:T(8,128)S(1)}) fusion(pred[]{:T(512)S(6)} %eq.25, f32[3,4,1,16,512]{4,3,2,1,0:T(8,128)S(1)} %get-tuple-element.6, f32[6,4,16,512]{3,2,0,1:T(8,128)} %collective-permute-done.6, pred[]{:T(512)S(6)} %eq.26, f32[6,4,16,512]{3,2,0,1:T(8,128)} %collective-permute-done.5, ...), kind=kLoop, calls=%fused_computation.16 | loop fusion | flops 2064384 | bytes 3932162 | tf_op jit(solution)/shard_map/mul | solution.py:178
  143.6 0.1 fusion.2
  143.7 5.2 %collective-permute-start.7 = (f32[6,1,16,512]{3,2,0,1:T(8,128)S(1)}, f32[6,1,16,512]{3,2,0,1:T(8,128)S(1)}, u32[]{:S(2)}, u32[]{:S(2)}) collective-permute-start(f32[6,1,16,512]{3,2,0,1:T(8,128)S(1)} %get-tuple-element.15), channel_id=1, source_target_pairs={{0,24},{2,26},{4,28},{6,30},{8,16},{10,18},{12,20},{14,22},{16,8},... | collective-permute-start | bytes 589832 | tf_op jit(solution)/shard_map/ppermute | solution.py:196
  148.9 0.0 collective-permute-start.8
  148.9 0.6 collective-permute-start.9
  149.5 5.2 %collective-permute-done.7 = f32[6,1,16,512]{3,2,0,1:T(8,128)S(1)} collective-permute-done((f32[6,1,16,512]{3,2,0,1:T(8,128)S(1)}, f32[6,1,16,512]{3,2,0,1:T(8,128)S(1)}, u32[]{:S(2)}, u32[]{:S(2)}) %collective-permute-start.7) | collective-permute-done | bytes 196640 | tf_op jit(solution)/shard_map/ppermute | solution.py:196
  154.8 10.2 %collective-permute-done.8 = f32[6,1,16,512]{3,2,0,1:T(8,128)S(1)} collective-permute-done((f32[6,1,16,512]{3,2,0,1:T(8,128)S(1)}, f32[6,1,16,512]{3,2,0,1:T(8,128)S(1)}, u32[]{:S(2)}, u32[]{:S(2)}) %collective-permute-start.8) | collective-permute-done | bytes 196640 | tf_op jit(solution)/shard_map/ppermute | solution.py:196
  164.9 0.0 collective-permute-done.9
  164.9 0.8 subtract_bitcast_fusion
  (6 shorter events, 0.0 us)
Async XLA Ops:
  7.1 12.7 %collective-permute-start.2 = (f32[16,256]{1,0:T(8,128)S(1)}, f32[16,256]{1,0:T(8,128)S(1)}, u32[]{:S(2)}, u32[]{:S(2)}) collective-permute-start(f32[16,256]{1,0:T(8,128)S(1)} %bitcast.40), channel_id=1, source_target_pairs={{1,0},{3,2},{5,4},{7,6},{9,8},{11,10},{13,12},{15,14},{17,16},{19,... | collective-permute-start | bytes 49160 | tf_op jit(solution)/shard_map/ppermute | solution.py:173
  8.4 11.1 %copy-start.4 = (f32[3,16]{1,0:T(4,128)S(1)}, f32[3,16]{1,0:T(4,128)}, u32[]{:S(2)}) copy-start(f32[3,16]{1,0:T(4,128)} %param.5) | copy-start | bytes 580
  8.4 11.2 %copy-start.5 = (f32[3,16]{1,0:T(4,128)S(1)}, f32[3,16]{1,0:T(4,128)}, u32[]{:S(2)}) copy-start(f32[3,16]{1,0:T(4,128)} %param.4) | copy-start | bytes 580
  9.0 10.7 %collective-permute-start.3 = (f32[16,256]{1,0:T(8,128)S(1)}, f32[16,256]{1,0:T(8,128)S(1)}, u32[]{:S(2)}, u32[]{:S(2)}) collective-permute-start(f32[16,256]{1,0:T(8,128)S(1)} %bitcast.41), channel_id=1, source_target_pairs={{0,1},{2,3},{4,5},{6,7},{8,9},{10,11},{12,13},{14,15},{16,17},{18,... | collective-permute-start | bytes 49160 | tf_op jit(solution)/shard_map/ppermute | solution.py:173
  13.4 26.8 %collective-permute-start = (f32[256,512]{1,0:T(8,128)S(1)}, f32[256,512]{1,0:T(8,128)S(1)}, u32[]{:S(2)}, u32[]{:S(2)}) collective-permute-start(f32[256,512]{1,0:T(8,128)S(1)} %get-tuple-element.5), channel_id=1, source_target_pairs={{0,2},{2,4},{4,6},{6,8},{8,10},{10,12},{12,14},{14,16},{16,18},{18... | collective-permute-start | bytes 1572872 | tf_op jit(solution)/shard_map/ppermute | solution.py:173
  18.2 23.9 %collective-permute-start.1 = (f32[256,512]{1,0:T(8,128)S(1)}, f32[256,512]{1,0:T(8,128)S(1)}, u32[]{:S(2)}, u32[]{:S(2)}) collective-permute-start(f32[256,512]{1,0:T(8,128)S(1)} %get-tuple-element.4), channel_id=1, source_target_pairs={{2,0},{4,2},{6,4},{8,6},{10,8},{12,10},{14,12},{16,14},{18,16},{20... | collective-permute-start | bytes 1572872 | tf_op jit(solution)/shard_map/ppermute | solution.py:173
  40.2 0.8 copy-start
  42.1 0.8 copy-start.2
  42.9 1.0 copy-start.1
  43.9 1.0 copy-start.3
  105.6 21.7 %collective-permute-start.4 = (f32[6,4,16,512]{3,2,0,1:T(8,128)}, f32[6,4,16,512]{3,2,0,1:T(8,128)}, u32[]{:S(2)}, u32[]{:S(2)}) collective-permute-start(f32[6,4,16,512]{3,2,0,1:T(8,128)} %bitcast.37), channel_id=1, source_target_pairs={{0,6},{2,4},{4,2},{6,0},{8,14},{10,12},{12,10},{14,8},{16,22},{18,... | collective-permute-start | bytes 2359304 | tf_op jit(solution)/shard_map/ppermute | solution.py:196
  106.6 35.0 %collective-permute-start.5 = (f32[6,4,16,512]{3,2,0,1:T(8,128)}, f32[6,4,16,512]{3,2,0,1:T(8,128)}, u32[]{:S(2)}, u32[]{:S(2)}) collective-permute-start(f32[6,4,16,512]{3,2,0,1:T(8,128)} %bitcast.36), channel_id=1, source_target_pairs={{0,4},{2,6},{4,0},{6,2},{8,12},{10,14},{12,8},{14,10},{16,20},{18,... | collective-permute-start | bytes 2359304 | tf_op jit(solution)/shard_map/ppermute | solution.py:196
  110.5 31.1 %collective-permute-start.6 = (f32[6,4,16,512]{3,2,0,1:T(8,128)}, f32[6,4,16,512]{3,2,0,1:T(8,128)}, u32[]{:S(2)}, u32[]{:S(2)}) collective-permute-start(f32[6,4,16,512]{3,2,0,1:T(8,128)} %bitcast.35), channel_id=1, source_target_pairs={{0,2},{2,0},{4,6},{6,4},{8,10},{10,8},{12,14},{14,12},{16,18},{18,... | collective-permute-start | bytes 2359304 | tf_op jit(solution)/shard_map/ppermute | solution.py:196
  143.7 11.1 %collective-permute-start.7 = (f32[6,1,16,512]{3,2,0,1:T(8,128)S(1)}, f32[6,1,16,512]{3,2,0,1:T(8,128)S(1)}, u32[]{:S(2)}, u32[]{:S(2)}) collective-permute-start(f32[6,1,16,512]{3,2,0,1:T(8,128)S(1)} %get-tuple-element.15), channel_id=1, source_target_pairs={{0,24},{2,26},{4,28},{6,30},{8,16},{10,18},{12,20},{14,22},{16,8},... | collective-permute-start | bytes 589832 | tf_op jit(solution)/shard_map/ppermute | solution.py:196
  148.9 16.0 %collective-permute-start.8 = (f32[6,1,16,512]{3,2,0,1:T(8,128)S(1)}, f32[6,1,16,512]{3,2,0,1:T(8,128)S(1)}, u32[]{:S(2)}, u32[]{:S(2)}) collective-permute-start(f32[6,1,16,512]{3,2,0,1:T(8,128)S(1)} %get-tuple-element.16), channel_id=1, source_target_pairs={{0,16},{2,18},{4,20},{6,22},{8,24},{10,26},{12,28},{14,30},{16,0},... | collective-permute-start | bytes 589832 | tf_op jit(solution)/shard_map/ppermute | solution.py:196
  148.9 16.0 %collective-permute-start.9 = (f32[6,1,16,512]{3,2,0,1:T(8,128)S(1)}, f32[6,1,16,512]{3,2,0,1:T(8,128)S(1)}, u32[]{:S(2)}, u32[]{:S(2)}) collective-permute-start(f32[6,1,16,512]{3,2,0,1:T(8,128)S(1)} %get-tuple-element.17), channel_id=1, source_target_pairs={{0,8},{2,10},{4,12},{6,14},{8,0},{10,2},{12,4},{14,6},{16,24},{18,... | collective-permute-start | bytes 589832 | tf_op jit(solution)/shard_map/ppermute | solution.py:196

commit v2 on v1

--- a/solution.py
+++ b/solution.py
@@ -36,7 +36,7 @@
 ):
     planes, height, width = field.shape
     tiles = width // LANES
-    stride = height // SUBLANES
+    strips = height // SUBLANES
     body_rows = pl.ds(PAD, height)
 
     def columns(tile):
@@ -82,7 +82,7 @@
 
     def strip(slot, row):
         def rows(part, plane, offset):
-            return cells[part, plane, pl.ds(PAD + row + offset, SUBLANES, stride=stride), :]
+            return cells[part, plane, pl.ds(PAD + row * SUBLANES + offset, SUBLANES), :]
 
         table = [tables[k] for k in range(12)]
         colour = [None] * 3
@@ -123,7 +123,7 @@
                     transmit[ch] = transmit[ch] - seen
             before, centre = centre, after
         for ch in range(3):
-            target = pl.ds(row, SUBLANES, stride=stride)
+            target = pl.ds(row * SUBLANES, SUBLANES)
             canvas[slot - 1, ch, target, :] = colour[ch]
             canvas[slot - 1, 3 + ch, target, :] = transmit[ch]
 
@@ -133,7 +133,7 @@
         for copy in incoming(slot + 1):
             copy.wait()
 
-        @pl.loop(0, stride)
+        @pl.loop(0, strips)
         def _(row):
             strip(slot, row)
 

time: 166 us -> 160 us (0.964)
  Pallas kernels: 59.5 us -> 53.1 us
    pallas_call x1, Pallas kernels: 59.5 us -> 53.1 us  [march(): pl.pallas_call(functools.partial(march_kernel, 0.5 * (count_breaks - 1)),...]
where the time goes in v2:
time: 160 us; the launch traced here: 159 us
  waiting for transfers between devices  66.3 us (41%)
  Pallas kernels  53.1 us (33%)
  starting transfers between devices  19.8 us (12%)
  local copies, waits for them, and re-layouts  15.2 us (10%)
  other arithmetic  4.13 us (3%)
    pallas_call x1, Pallas kernels, march(): pl.pallas_call(functools.partial(march_kernel, 0.5 * (count_breaks - 1)),...  53.1 us
    ppermute x6, waiting for transfers between devices, exchange(): lax.ppermute(part, 'slab', [(i, i ^ change << shift) for i in range(count)])  45.9 us
    ppermute x2, waiting for transfers between devices, neighbours(): lax.ppermute(last, axis, forward)  19.2 us
    ppermute x6, starting transfers between devices, exchange(): lax.ppermute(part, 'slab', [(i, i ^ change << shift) for i in range(count)])  9.33 us
    ppermute x2, starting transfers between devices, neighbours(): lax.ppermute(last, axis, forward)  7.9 us
    unnamed x14, local copies, waits for them, and re-layouts  6.49 us
    slice x1, local copies, waits for them, and re-layouts, per_device(): left, right = neighbours(field[:, :, 0], field[:, :, -1], 'tile')  4.29 us
  transfers between devices with their start and end apart: 10, of which 6 were waited for; matrix products, arithmetic and copies ran while one was open for 3% of the time, Pallas kernels for 0%

profile of v2, /device:TPU:0, one launch (start us, length us, event | category | flops | bytes accessed | tf_op | source)
XLA Modules:
  0.0 159.3 jit_solution(7612184962864483389)
XLA Ops:
  0.6 4.3 %fusion.6 = (f32[16,256,1]{2,1,0:T(8,128)}, f32[16,256,1]{2,1,0:T(8,128)S(1)}) fusion(f32[16,256,512]{2,1,0:T(8,128)} %field.1), kind=kLoop, calls=%fused_computation.49 | loop fusion | bytes 65536 | tf_op jit(solution)/shard_map/slice | solution.py:208
  4.9 2.2 %copy.15 = f32[16,256,1]{1,0,2:T(8,128)S(1)} copy(f32[16,256,1]{2,1,0:T(8,128)} %get-tuple-element.2) | data formatting | bytes 32768
  7.1 1.3 collective-permute-start.2
  8.4 0.0 copy-start.4
  8.4 0.0 copy-start.5
  8.4 0.6 copy.16
  9.0 3.0 %collective-permute-start.3 = (f32[16,256]{1,0:T(8,128)S(1)}, f32[16,256]{1,0:T(8,128)S(1)}, u32[]{:S(2)}, u32[]{:S(2)}) collective-permute-start(f32[16,256]{1,0:T(8,128)S(1)} %bitcast.41), channel_id=1, source_target_pairs={{0,1},{2,3},{4,5},{6,7},{8,9},{10,11},{12,13},{14,15},{16,17},{18,... | collective-permute-start | bytes 49160 | tf_op jit(solution)/shard_map/ppermute | solution.py:173
  12.1 1.3 slice_bitcast_fusion
  13.4 4.9 %collective-permute-start = (f32[256,512]{1,0:T(8,128)S(1)}, f32[256,512]{1,0:T(8,128)S(1)}, u32[]{:S(2)}, u32[]{:S(2)}) collective-permute-start(f32[256,512]{1,0:T(8,128)S(1)} %get-tuple-element.5), channel_id=1, source_target_pairs={{0,2},{2,4},{4,6},{6,8},{8,10},{10,12},{12,14},{14,16},{16,18},{18... | collective-permute-start | bytes 1572872 | tf_op jit(solution)/shard_map/ppermute | solution.py:173
  18.2 1.3 collective-permute-start.1
  19.6 0.0 copy-done.4
  19.6 0.0 copy-done.5
  19.6 0.1 multiply_add_fusion.1
  19.7 0.1 fusion.5
  19.8 0.0 collective-permute-done.2
  19.8 0.0 collective-permute-done.3
  19.8 1.1 broadcast_select_fusion.edges
  20.9 19.2 %collective-permute-done.low = f32[256,512]{1,0:T(8,128)S(1)} collective-permute-done((f32[256,512]{1,0:T(8,128)S(1)}, f32[256,512]{1,0:T(8,128)S(1)}, u32[]{:S(2)}, u32[]{:S(2)}) %collective-permute-start) | collective-permute-done | bytes 524320 | tf_op jit(solution)/shard_map/ppermute | solution.py:173
  40.2 0.0 copy-start
  40.2 0.8 copy-done
  41.0 1.1 collective-permute-done.1.high
  42.1 0.0 copy-start.2
  42.1 0.8 copy-done.2
  42.9 0.0 copy-start.1
  42.9 1.0 copy-done.1
  43.9 0.0 copy-start.3
  44.0 1.0 copy-done.3
  45.0 53.1 %shard_map.50 = f32[6,256,512]{2,1,0:T(8,128)S(1)} custom-call(f32[12,8,128]{2,1,0:T(8,128)S(1)} %broadcast_in_dim.33.tables, f32[16,256,512]{2,1,0:T(8,128)} %field.1, f32[256,512]{1,0:T(8,128)S(1)} %copy-done.1, f32[256,512]{1,0:T(8,128)S(1)} %copy-done.3, f32[16,256,128]{2,1,0:T(8,128)S(1)} %broadcast_select_fusion.edges), custom_call_target="tpu_custom_call" | custom-call | flops 167772160 | bytes 10485760 | tf_op jit(solution)/shard_map/pallas_call | solution.py:149
  98.1 0.2 constant_dynamic-slice_fusion.4
  98.3 1.0 copy.41
  99.3 0.0 collective-permute-start.4
  99.3 0.9 copy.40
  100.2 3.0 %collective-permute-start.5 = (f32[6,4,16,512]{3,2,0,1:T(8,128)}, f32[6,4,16,512]{3,2,0,1:T(8,128)}, u32[]{:S(2)}, u32[]{:S(2)}) collective-permute-start(f32[6,4,16,512]{3,2,0,1:T(8,128)} %bitcast.36), channel_id=1, source_target_pairs={{0,4},{2,6},{4,0},{6,2},{8,12},{10,14},{12,8},{14,10},{16,20},{18,... | collective-permute-start | bytes 2359304 | tf_op jit(solution)/shard_map/ppermute | solution.py:196
  103.2 1.0 copy.39
  104.1 0.5 collective-permute-start.6
  104.6 0.1 constant_dynamic-slice_fusion.1
  104.7 16.3 %collective-permute-done.4 = f32[6,4,16,512]{3,2,0,1:T(8,128)} collective-permute-done((f32[6,4,16,512]{3,2,0,1:T(8,128)}, f32[6,4,16,512]{3,2,0,1:T(8,128)}, u32[]{:S(2)}, u32[]{:S(2)}) %collective-permute-start.4) | collective-permute-done | bytes 786464 | tf_op jit(solution)/shard_map/ppermute | solution.py:196
  121.0 14.2 %collective-permute-done.5 = f32[6,4,16,512]{3,2,0,1:T(8,128)} collective-permute-done((f32[6,4,16,512]{3,2,0,1:T(8,128)}, f32[6,4,16,512]{3,2,0,1:T(8,128)}, u32[]{:S(2)}, u32[]{:S(2)}) %collective-permute-start.5) | collective-permute-done | bytes 786464 | tf_op jit(solution)/shard_map/ppermute | solution.py:196
  135.2 0.0 collective-permute-done.6
  135.2 2.0 %select_multiply_fusion = (f32[3,4,16,512]{3,2,0,1:T(8,128)S(1)}, f32[3,4,16,512]{3,2,0,1:T(8,128)S(1)}) fusion(pred[]{:T(512)S(6)} %eq.25, f32[3,4,1,16,512]{4,3,2,1,0:T(8,128)S(1)} %get-tuple-element.6, f32[6,4,16,512]{3,2,0,1:T(8,128)} %collective-permute-done.6, pred[]{:T(512)S(6)} %eq.26, f32[6,4,16,512]{3,2,0,1:T(8,128)} %collective-permute-done.5, ...), kind=kLoop, calls=%fused_computation.16 | loop fusion | flops 2064384 | bytes 3932162 | tf_op jit(solution)/shard_map/mul | solution.py:178
  137.2 0.1 fusion.2
  137.3 5.2 %collective-permute-start.7 = (f32[6,1,16,512]{3,2,0,1:T(8,128)S(1)}, f32[6,1,16,512]{3,2,0,1:T(8,128)S(1)}, u32[]{:S(2)}, u32[]{:S(2)}) collective-permute-start(f32[6,1,16,512]{3,2,0,1:T(8,128)S(1)} %get-tuple-element.15), channel_id=1, source_target_pairs={{0,24},{2,26},{4,28},{6,30},{8,16},{10,18},{12,20},{14,22},{16,8},... | collective-permute-start | bytes 589832 | tf_op jit(solution)/shard_map/ppermute | solution.py:196
  142.5 0.0 collective-permute-start.8
  142.5 0.6 collective-permute-start.9
  143.1 5.2 %collective-permute-done.7 = f32[6,1,16,512]{3,2,0,1:T(8,128)S(1)} collective-permute-done((f32[6,1,16,512]{3,2,0,1:T(8,128)S(1)}, f32[6,1,16,512]{3,2,0,1:T(8,128)S(1)}, u32[]{:S(2)}, u32[]{:S(2)}) %collective-permute-start.7) | collective-permute-done | bytes 196640 | tf_op jit(solution)/shard_map/ppermute | solution.py:196
  148.4 10.2 %collective-permute-done.8 = f32[6,1,16,512]{3,2,0,1:T(8,128)S(1)} collective-permute-done((f32[6,1,16,512]{3,2,0,1:T(8,128)S(1)}, f32[6,1,16,512]{3,2,0,1:T(8,128)S(1)}, u32[]{:S(2)}, u32[]{:S(2)}) %collective-permute-start.8) | collective-permute-done | bytes 196640 | tf_op jit(solution)/shard_map/ppermute | solution.py:196
  158.5 0.0 collective-permute-done.9
  158.5 0.8 subtract_bitcast_fusion
  (6 shorter events, 0.0 us)
Async XLA Ops:
  7.1 12.7 %collective-permute-start.2 = (f32[16,256]{1,0:T(8,128)S(1)}, f32[16,256]{1,0:T(8,128)S(1)}, u32[]{:S(2)}, u32[]{:S(2)}) collective-permute-start(f32[16,256]{1,0:T(8,128)S(1)} %bitcast.40), channel_id=1, source_target_pairs={{1,0},{3,2},{5,4},{7,6},{9,8},{11,10},{13,12},{15,14},{17,16},{19,... | collective-permute-start | bytes 49160 | tf_op jit(solution)/shard_map/ppermute | solution.py:173
  8.4 11.1 %copy-start.4 = (f32[3,16]{1,0:T(4,128)S(1)}, f32[3,16]{1,0:T(4,128)}, u32[]{:S(2)}) copy-start(f32[3,16]{1,0:T(4,128)} %param.5) | copy-start | bytes 580
  8.4 11.2 %copy-start.5 = (f32[3,16]{1,0:T(4,128)S(1)}, f32[3,16]{1,0:T(4,128)}, u32[]{:S(2)}) copy-start(f32[3,16]{1,0:T(4,128)} %param.4) | copy-start | bytes 580
  9.0 10.7 %collective-permute-start.3 = (f32[16,256]{1,0:T(8,128)S(1)}, f32[16,256]{1,0:T(8,128)S(1)}, u32[]{:S(2)}, u32[]{:S(2)}) collective-permute-start(f32[16,256]{1,0:T(8,128)S(1)} %bitcast.41), channel_id=1, source_target_pairs={{0,1},{2,3},{4,5},{6,7},{8,9},{10,11},{12,13},{14,15},{16,17},{18,... | collective-permute-start | bytes 49160 | tf_op jit(solution)/shard_map/ppermute | solution.py:173
  13.4 26.8 %collective-permute-start = (f32[256,512]{1,0:T(8,128)S(1)}, f32[256,512]{1,0:T(8,128)S(1)}, u32[]{:S(2)}, u32[]{:S(2)}) collective-permute-start(f32[256,512]{1,0:T(8,128)S(1)} %get-tuple-element.5), channel_id=1, source_target_pairs={{0,2},{2,4},{4,6},{6,8},{8,10},{10,12},{12,14},{14,16},{16,18},{18... | collective-permute-start | bytes 1572872 | tf_op jit(solution)/shard_map/ppermute | solution.py:173
  18.2 23.9 %collective-permute-start.1 = (f32[256,512]{1,0:T(8,128)S(1)}, f32[256,512]{1,0:T(8,128)S(1)}, u32[]{:S(2)}, u32[]{:S(2)}) collective-permute-start(f32[256,512]{1,0:T(8,128)S(1)} %get-tuple-element.4), channel_id=1, source_target_pairs={{2,0},{4,2},{6,4},{8,6},{10,8},{12,10},{14,12},{16,14},{18,16},{20... | collective-permute-start | bytes 1572872 | tf_op jit(solution)/shard_map/ppermute | solution.py:173
  40.2 0.8 copy-start
  42.1 0.8 copy-start.2
  42.9 1.0 copy-start.1
  43.9 1.0 copy-start.3
  99.3 21.7 %collective-permute-start.4 = (f32[6,4,16,512]{3,2,0,1:T(8,128)}, f32[6,4,16,512]{3,2,0,1:T(8,128)}, u32[]{:S(2)}, u32[]{:S(2)}) collective-permute-start(f32[6,4,16,512]{3,2,0,1:T(8,128)} %bitcast.37), channel_id=1, source_target_pairs={{0,6},{2,4},{4,2},{6,0},{8,14},{10,12},{12,10},{14,8},{16,22},{18,... | collective-permute-start | bytes 2359304 | tf_op jit(solution)/shard_map/ppermute | solution.py:196
  100.2 35.0 %collective-permute-start.5 = (f32[6,4,16,512]{3,2,0,1:T(8,128)}, f32[6,4,16,512]{3,2,0,1:T(8,128)}, u32[]{:S(2)}, u32[]{:S(2)}) collective-permute-start(f32[6,4,16,512]{3,2,0,1:T(8,128)} %bitcast.36), channel_id=1, source_target_pairs={{0,4},{2,6},{4,0},{6,2},{8,12},{10,14},{12,8},{14,10},{16,20},{18,... | collective-permute-start | bytes 2359304 | tf_op jit(solution)/shard_map/ppermute | solution.py:196
  104.1 31.1 %collective-permute-start.6 = (f32[6,4,16,512]{3,2,0,1:T(8,128)}, f32[6,4,16,512]{3,2,0,1:T(8,128)}, u32[]{:S(2)}, u32[]{:S(2)}) collective-permute-start(f32[6,4,16,512]{3,2,0,1:T(8,128)} %bitcast.35), channel_id=1, source_target_pairs={{0,2},{2,0},{4,6},{6,4},{8,10},{10,8},{12,14},{14,12},{16,18},{18,... | collective-permute-start | bytes 2359304 | tf_op jit(solution)/shard_map/ppermute | solution.py:196
  137.3 11.1 %collective-permute-start.7 = (f32[6,1,16,512]{3,2,0,1:T(8,128)S(1)}, f32[6,1,16,512]{3,2,0,1:T(8,128)S(1)}, u32[]{:S(2)}, u32[]{:S(2)}) collective-permute-start(f32[6,1,16,512]{3,2,0,1:T(8,128)S(1)} %get-tuple-element.15), channel_id=1, source_target_pairs={{0,24},{2,26},{4,28},{6,30},{8,16},{10,18},{12,20},{14,22},{16,8},... | collective-permute-start | bytes 589832 | tf_op jit(solution)/shard_map/ppermute | solution.py:196
  142.5 16.0 %collective-permute-start.8 = (f32[6,1,16,512]{3,2,0,1:T(8,128)S(1)}, f32[6,1,16,512]{3,2,0,1:T(8,128)S(1)}, u32[]{:S(2)}, u32[]{:S(2)}) collective-permute-start(f32[6,1,16,512]{3,2,0,1:T(8,128)S(1)} %get-tuple-element.16), channel_id=1, source_target_pairs={{0,16},{2,18},{4,20},{6,22},{8,24},{10,26},{12,28},{14,30},{16,0},... | collective-permute-start | bytes 589832 | tf_op jit(solution)/shard_map/ppermute | solution.py:196
  142.5 16.0 %collective-permute-start.9 = (f32[6,1,16,512]{3,2,0,1:T(8,128)S(1)}, f32[6,1,16,512]{3,2,0,1:T(8,128)S(1)}, u32[]{:S(2)}, u32[]{:S(2)}) collective-permute-start(f32[6,1,16,512]{3,2,0,1:T(8,128)S(1)} %get-tuple-element.17), channel_id=1, source_target_pairs={{0,8},{2,10},{4,12},{6,14},{8,0},{10,2},{12,4},{14,6},{16,24},{18,... | collective-permute-start | bytes 589832 | tf_op jit(solution)/shard_map/ppermute | solution.py:196

commit v3 on v2

v3 whole, which is shorter than its diff:
```python
import functools

import jax
import jax.numpy as jnp
from jax import lax
from jax.experimental import pallas as pl
from jax.experimental.pallas import tpu as pltpu
from jax.sharding import PartitionSpec as P

LIGHT_DIR = (0.2672612, 0.5345225, 0.8017837)
LANES = 128
SUBLANES = 8
PAD = 8
WORD_SCALE = 2.0**31 - 2.0**17
HALF = 65536


def segment_words(tables):
    largest = jnp.maximum(jnp.max(tables), 1e-30)
    scaled = tables * (WORD_SCALE / largest)
    rise = jnp.round((scaled[:, 1:] - scaled[:, :-1]) * (1.0 / HALF))
    centre = 0.5 * (scaled[:, 1:] + scaled[:, :-1])
    rise = jnp.pad(rise, ((0, 0), (0, 1)))
    centre = jnp.concatenate([centre, scaled[:, -1:]], axis=1)
    upper = jnp.round((centre - rise) * (1.0 / HALF))
    return upper.astype(jnp.int32) * HALF + rise.astype(jnp.int32), largest / WORD_SCALE


def prepare_tables(tf_emission, tf_absorption, depth_total):
    emission, emission_unit = segment_words(tf_emission)
    absorption, absorption_unit = segment_words(tf_absorption)
    absorption_unit = absorption_unit * (4.0 / depth_total)
    words = jnp.concatenate([emission, absorption], axis=0)
    words = jnp.pad(words, ((0, 0), (0, LANES - words.shape[1])))
    words = jnp.broadcast_to(words[:, None, :], (6, SUBLANES, LANES))
    factors = jnp.stack(
        [(0.9 * part) * emission_unit for part in LIGHT_DIR]
        + [0.1 * emission_unit, absorption_unit, 0.75 * absorption_unit]
    )
    factors = jnp.broadcast_to(factors[:, None, None], (6, SUBLANES, LANES))
    return words, factors


def lookup(table, index):
    return jnp.take_along_axis(table, index, axis=1, mode="promise_in_bounds")


def march_kernel(mode, first_tile, tiles, scale, group, words, factors, *refs):
    refs = list(refs)
    field, side = refs.pop(0), refs.pop(0)
    low, high = (refs.pop(0), refs.pop(0)) if mode != "middle" else (None, None)
    middle = refs.pop(0) if mode == "rim" else None
    inner = refs.pop() if mode == "rim" else None
    cells, canvas, in_sems, out_sems = refs[-4:]
    outs = refs[:-4]
    planes, height, width = field.shape
    all_tiles = width // LANES
    body_rows = pl.ds(PAD, height)
    tile_index = lax.axis_index("tile")
    if mode == "full":
        blocks, marched = [(0, 1, planes)], range(planes)
    elif mode == "middle":
        blocks, marched = [(0, 1, planes)], range(1, planes - 1)
    else:
        blocks, marched = [(0, 1, 2), (planes - 2, 3, 2)], (0, planes - 1)
    place = {first + k: slot + k for first, slot, count in blocks for k in range(count)}
    place[-1] = 0
    place[planes] = max(place.values()) + 1

    def columns(tile):
        return pl.ds(tile * LANES, LANES)

    def incoming(slot):
        tile = first_tile + slot - 1
        copies = []
        for number, (first, where, count) in enumerate(blocks):
            if 0 <= tile < all_tiles:
                source = field.at[pl.ds(first, count), :, columns(tile)]
            else:
                source = side.at[pl.ds(first, count)]
            target = cells.at[slot, pl.ds(where, count), body_rows, :]
            copies.append(pltpu.make_async_copy(source, target, in_sems.at[slot, number]))
        if mode != "middle" and 1 <= slot <= tiles:
            here = columns(slot - 1)
            for number, (halo, plane) in enumerate(((low, -1), (high, planes))):
                target = cells.at[slot, place[plane], body_rows, :]
                copies.append(
                    pltpu.make_async_copy(halo.at[:, here], target, in_sems.at[slot, 2 + number])
                )
        if mode == "rim" and 1 <= slot <= tiles:
            copies.append(
                pltpu.make_async_copy(
                    middle.at[:, :, columns(slot - 1)], inner.at[slot - 1], in_sems.at[slot, 4]
                )
            )
        return copies

    def outgoing(tile):
        if len(outs) == 1:
            return [
                pltpu.make_async_copy(
                    canvas.at[tile], outs[0].at[:, :, columns(tile)], out_sems.at[tile, 0]
                )
            ]
        own = lax.axis_index("slab") & (group - 1)
        return [
            pltpu.make_async_copy(
                canvas.at[tile, :, :, own ^ change],
                outs[change].at[:, :, :, columns(tile)],
                out_sems.at[tile, change],
            )
            for change in range(group)
        ]

    for slot in range(tiles + 2):
        for copy in incoming(slot):
            copy.start()
    zeros = jnp.zeros((1, LANES), jnp.float32)
    for slot in range(1, tiles + 1):
        for plane in marched:
            cells[slot, place[plane], pl.ds(PAD - 1, 1), :] = zeros
            cells[slot, place[plane], pl.ds(PAD + height, 1), :] = zeros
    lane = lax.broadcasted_iota(jnp.int32, (SUBLANES, LANES), 1)
    first_lane = lane == 0
    last_lane = lane == LANES - 1
    has_left = (tile_index > 0).astype(jnp.float32)
    has_right = (tile_index < lax.axis_size("tile") - 1).astype(jnp.float32)

    def strip(slot, row):
        def rows(part, plane, offset=0):
            start = PAD + row * SUBLANES + offset
            return cells[part, place[plane], pl.ds(start, SUBLANES), :]

        colour = transmit = None
        for plane in marched:
            before, centre, after = (rows(slot, plane + k) for k in (-1, 0, 1))
            left_tile = rows(slot - 1, plane)
            right_tile = rows(slot + 1, plane)
            if first_tile + slot - 1 == 0:
                left_tile = left_tile * has_left
            if first_tile + slot == all_tiles:
                right_tile = right_tile * has_right
            left = pltpu.roll(jnp.where(last_lane, left_tile, centre), 1, 1)
            right = pltpu.roll(jnp.where(first_lane, right_tile, centre), LANES - 1, 1)
            diff_x = right - left
            diff_y = rows(slot, plane, 1) - rows(slot, plane, -1)
            diff_z = after - before
            inverse = lax.rsqrt(diff_x * diff_x + diff_y * diff_y + diff_z * diff_z + 1.0)
            facing = (factors[0] * diff_x + factors[1] * diff_y + factors[2] * diff_z) * inverse
            shading = jnp.maximum(facing, 0.0) + factors[3]
            weight = factors[4] - factors[5] * (inverse * inverse)
            middle_based = centre * scale + (scale - 0.5)
            interval = (middle_based + 0.5).astype(jnp.int32)
            offset = middle_based - interval.astype(jnp.float32)
            values = []
            for k in range(6):
                word = lookup(words[k], interval)
                rise = lax.shift_left(word, 16).astype(jnp.float32)
                values.append(word.astype(jnp.float32) + rise * offset)
            steps = [values[3 + ch] * weight for ch in range(3)]
            glows = [values[ch] * shading for ch in range(3)]
            if colour is None:
                colour = [step * glow for step, glow in zip(steps, glows)]
                transmit = [1.0 - step for step in steps]
            else:
                seen = [transmit[ch] * steps[ch] for ch in range(3)]
                colour = [colour[ch] + seen[ch] * glows[ch] for ch in range(3)]
                transmit = [transmit[ch] - seen[ch] for ch in range(3)]
            if mode == "rim" and plane == 0:
                here = pl.ds(row * SUBLANES, SUBLANES)
                held = [inner[slot - 1, k, here, :] for k in range(6)]
                colour = [colour[ch] + transmit[ch] * held[ch] for ch in range(3)]
                transmit = [transmit[ch] * held[3 + ch] for ch in range(3)]
        for k, value in enumerate(colour + transmit):
            if len(outs) == 1:
                canvas[slot - 1, k, pl.ds(row * SUBLANES, SUBLANES), :] = value
            else:
                block_rows = height // (canvas.shape[2] * group)
                block = (row * SUBLANES) // block_rows
                start = pl.multiple_of((row * SUBLANES) % block_rows, SUBLANES)
                canvas[
                    slot - 1, k, block // group, block % group, pl.ds(start, SUBLANES), :
                ] = value

    for copy in incoming(0) + incoming(1):
        copy.wait()
    for slot in range(1, tiles + 1):
        for copy in incoming(slot + 1):
            copy.wait()

        @pl.loop(0, height // SUBLANES)
        def _(row):
            strip(slot, row)

        for copy in outgoing(slot - 1):
            copy.start()
    for tile in range(tiles):
        for copy in outgoing(tile):
            copy.wait()


def march(mode, chunk, tables, field, side, halos, middle, count_breaks, part_shape):
    planes, height, width = field.shape
    first_tile, tiles = chunk
    extent = tiles * LANES
    held = 6 if mode == "rim" else planes + 2
    if part_shape is None:
        group = 1
        outs = [jax.ShapeDtypeStruct((6, height, extent), jnp.float32)]
        canvas = (tiles, 6, height, LANES)
    else:
        outer, group, rows = part_shape
        outs = [jax.ShapeDtypeStruct((6, outer, rows, extent), jnp.float32)] * group
        canvas = (tiles, 6, outer, group, rows, LANES)
    scratch = [
        pltpu.VMEM((tiles + 2, held, height + 2 * PAD, LANES), jnp.float32),
        pltpu.VMEM(canvas, jnp.float32),
        pltpu.SemaphoreType.DMA((tiles + 2, 5)),
        pltpu.SemaphoreType.DMA((tiles, group)),
    ]
    operands = [field, side]
    if mode != "middle":
        operands += list(halos)
    if mode == "rim":
        operands.append(middle)
        scratch.append(pltpu.VMEM((tiles, 6, height, LANES), jnp.float32))
    marched = {"full": planes, "middle": planes - 2, "rim": 2}[mode]
    anywhere = pl.BlockSpec(memory_space=pl.ANY)
    out = pl.pallas_call(
        functools.partial(
            march_kernel, mode, first_tile, tiles, 0.5 * (count_breaks - 1), group
        ),
        out_shape=outs,
        in_specs=[pl.BlockSpec(memory_space=pltpu.VMEM)] * 2 + [anywhere] * len(operands),
        out_specs=[anywhere] * len(outs),
        scratch_shapes=scratch,
        compiler_params=pltpu.CompilerParams(vmem_limit_bytes=24 * 1024 * 1024),
        cost_estimate=pl.CostEstimate(
            flops=marched * height * extent * 100,
            bytes_accessed=marched * height * extent * 6,
            transcendentals=0,
        ),
        name=f"march_{mode}_{first_tile}",
    )(*tables, *operands)
    return out[0] if part_shape is None else out


def plane_halos(first, last):
    count = lax.axis_size("slab")
    forward = [(i, i + 1) for i in range(count - 1)]
    backward = [(i + 1, i) for i in range(count - 1)]
    return lax.ppermute(last, "slab", forward), lax.ppermute(first, "slab", backward)


def edge_tile(field):
    first = lax.axis_index("tile") == 0
    planes, height, width = field.shape
    start = jnp.where(first, width - LANES, 0)
    own = lax.dynamic_slice_in_dim(field, start, LANES, axis=2)
    return lax.ppermute(own, "tile", [(0, 1), (1, 0)])


def ordered(is_far, own, other):
    near = [jnp.where(is_far, b, a) for a, b in zip(own, other)]
    far = [jnp.where(is_far, a, b) for a, b in zip(own, other)]
    return [near[0] + near[1] * far[0], near[1] * far[1]]


def take_parts(image, own, size):
    return [
        lax.dynamic_index_in_dim(image, own ^ change, 2, keepdims=False) for change in range(size)
    ]


def exchange(parts, own, shift):
    count = lax.axis_size("slab")
    merged = []
    for change, part in enumerate(parts):
        if change:
            part = lax.ppermute(part, "slab", [(i, i ^ change << shift) for i in range(count)])
        merged.append([part[:3], part[3:]])
    digit = 0
    while len(merged) > 1:
        is_far = (own >> digit & 1) == 1
        merged = [ordered(is_far, merged[k], merged[k + 1]) for k in range(0, len(merged), 2)]
        digit += 1
    return merged[0]


def reduce_image(image, parts, slab_index, block_rows):
    slab_count = lax.axis_size("slab")
    levels = slab_count.bit_length() - 1
    for shift in range(0, levels, 2):
        bits = min(2, levels - shift)
        own = (slab_index >> shift) & ((1 << bits) - 1)
        if parts is None:
            outer = slab_count >> (shift + bits)
            image = image.reshape((6, outer, 1 << bits, block_rows, image.shape[-1]))
            parts = take_parts(image, own, 1 << bits)
        colour, transmit = exchange(parts, own, shift)
        image, parts = jnp.concatenate([colour, transmit], axis=0), None
    return colour[:, 0], 1.0 - transmit[:, 0]


def per_device(field, tf_emission, tf_absorption):
    slab_count = lax.axis_size("slab")
    slab_index = lax.axis_index("slab")
    planes, height, width = field.shape
    count_breaks = tf_emission.shape[1]
    block_rows = height // slab_count
    tiles = width // LANES
    part_shape = None
    if slab_count >= 4 and block_rows % SUBLANES == 0:
        part_shape = (slab_count // 4, 4, block_rows)
    chunks = [(0, tiles // 2), (tiles // 2, tiles - tiles // 2)]
    tables = prepare_tables(tf_emission, tf_absorption, planes * slab_count)
    strips = [(first * LANES, (first + count) * LANES) for first, count in chunks]

    halos = []
    for begin, end in strips:
        first, last = field[0, :, begin:end], field[-1, :, begin:end]
        if halos:
            first, last, _ = lax.optimization_barrier((first, last, halos[-1]))
        halos.append(plane_halos(first, last))
        if len(halos) == 1:
            side = edge_tile(field)
    results = []
    for chunk, halo in zip(chunks, halos):
        if chunk[0] == 0:
            middle = march(
                "middle", chunk, tables, field, side, None, None, count_breaks, None
            )
            mode = "rim"
        else:
            middle, mode = None, "full"
        out = march(mode, chunk, tables, field, side, halo, middle, count_breaks, part_shape)
        image, parts = (out, None) if part_shape is None else (None, out)
        results.append(reduce_image(image, parts, slab_index, block_rows))
    return tuple(jnp.concatenate(pieces, axis=2) for pieces in zip(*results))


def solution(mesh):
    placed = (P("slab", None, "tile"), P(), P())
    return jax.shard_map(
        per_device,
        mesh=mesh,
        in_specs=placed,
        out_specs=(P(None, "slab", "tile"), P(None, "slab", "tile")),
        check_vma=False,
    )
```

time: 160 us -> 133 us (0.83)
  waiting for transfers between devices: 66.3 us -> 32.3 us
  starting transfers between devices: 19.8 us -> 29.1 us
  Pallas kernels: 53.1 us -> 46.2 us
  other arithmetic: 4.13 us -> 6.41 us
    ppermute x6 -> x12, waiting for transfers between devices: 45.9 us -> 13.3 us  [exchange(): lax.ppermute(part, 'slab', [(i, i ^ change << shift) for i in range(count)])]
    ppermute x6 -> x12, starting transfers between devices: 9.33 us -> 16.7 us  [exchange(): lax.ppermute(part, 'slab', [(i, i ^ change << shift) for i in range(count)])]
    pallas_call x1 -> x3, Pallas kernels: 53.1 us -> 46.2 us  [march(): pl.pallas_call(functools.partial(march_kernel, mode, first_tile, tiles, 0...]
    slice x2, local copies, waits for them, and re-layouts: 4.34 us -> 0.14 us  [segment_words(): centre = jnp.concatenate([centre, scaled[:, -1:]], axis=1)]
    unnamed x14 -> x16, local copies, waits for them, and re-layouts: 6.49 us -> 10.1 us
    ppermute x4 -> x5, starting transfers between devices: 10.5 us -> 12.4 us  [the longest x2 9.42 us: plane_halos(): lax.ppermute(last, 'slab', forward)]
    ppermute x4 -> x5, waiting for transfers between devices: 20.4 us -> 19 us  [the longest x2 16.5 us: plane_halos(): lax.ppermute(last, 'slab', forward)]
  transfers between devices with their start and end apart: 10 -> 17, of which waited for: 6 -> 7; matrix products, arithmetic and copies ran while one was open for 3% -> 6% of each run, Pallas kernels for 0% -> 19%
where the time goes in v3:
time: 133 us
  Pallas kernels  46.2 us (35%)
  waiting for transfers between devices  32.3 us (24%)
  starting transfers between devices  29.1 us (22%)
  local copies, waits for them, and re-layouts  16.5 us (12%)
  other arithmetic  6.41 us (5%)
  between operations  2.23 us (2%)
    pallas_call x3, Pallas kernels, march(): pl.pallas_call(functools.partial(march_kernel, mode, first_tile, tiles, 0...  46.2 us
    ppermute x12, starting transfers between devices, exchange(): lax.ppermute(part, 'slab', [(i, i ^ change << shift) for i in range(count)])  16.7 us
    ppermute x2, waiting for transfers between devices, plane_halos(): lax.ppermute(last, 'slab', forward)  16.5 us
    ppermute x12, waiting for transfers between devices, exchange(): lax.ppermute(part, 'slab', [(i, i ^ change << shift) for i in range(count)])  13.3 us
    unnamed x16, local copies, waits for them, and re-layouts  10.1 us
    ppermute x2, starting transfers between devices, plane_halos(): lax.ppermute(last, 'slab', forward)  9.42 us
    dynamic_slice x1, local copies, waits for them, and re-layouts, edge_tile(): own = lax.dynamic_slice_in_dim(field, start, LANES, axis=2)  3.16 us
  transfers between devices with their start and end apart: 17, of which 7 were waited for; matrix products, arithmetic and copies ran while one was open for 6% of the time, Pallas kernels for 19%

profile of v3, /device:TPU:0, one launch (start us, length us, event | category | flops | bytes accessed | tf_op | source)
XLA Modules:
  0.0 132.7 jit_solution(9389897922093731494)
XLA Ops:
  0.6 3.2 %constant_dynamic-slice_fusion = f32[16,256,128]{2,1,0:T(8,128)} fusion(f32[16,256,512]{2,1,0:T(8,128)} %refs_0_.5, s32[]{:T(128)S(6)} %select_n.230), kind=kLoop, calls=%fused_computation.71 | loop fusion | bytes 4194308 | tf_op jit(solution)/shard_map/dynamic_slice | solution.py:259
  3.8 0.5 collective-permute-start
  4.3 2.0 %slice_bitcast_fusion.2 = (f32[256,256]{1,0:T(8,128)S(1)}, f32[256,256]{1,0:T(8,128)S(1)}, f32[256,256]{1,0:T(8,128)S(1)}, f32[256,256]{1,0:T(8,128)}) fusion(f32[16,256,512]{2,1,0:T(8,128)} %refs_0_.5), kind=kLoop, calls=%fused_computation.18 | loop fusion | bytes 2097152 | tf_op jit(solution)/shard_map/squeeze | solution.py:321
  6.2 1.3 collective-permute-start.2
  7.5 5.1 %collective-permute-start.1 = (f32[256,256]{1,0:T(8,128)S(1)}, f32[256,256]{1,0:T(8,128)S(1)}, u32[]{:S(2)}, u32[]{:S(2)}) collective-permute-start(f32[256,256]{1,0:T(8,128)S(1)} %get-tuple-element.27), channel_id=1, source_target_pairs={{0,2},{2,4},{4,6},{6,8},{8,10},{10,12},{12,14},{14,16},{16,18},{18... | collective-permute-start | bytes 786440 | tf_op jit(solution)/shard_map/ppermute | solution.py:252
  12.6 0.0 copy-done.7
  12.6 0.6 reduce_max.19
  13.2 0.0 copy-done.6
  13.2 0.6 reduce_max.18
  15.2 0.1 multiply_round-nearest-even_fusion.1
  15.3 2.5 %collective-permute-done.2.refs_3_ = f32[256,256]{1,0:T(8,128)S(1)} collective-permute-done((f32[256,256]{1,0:T(8,128)S(1)}, f32[256,256]{1,0:T(8,128)S(1)}, u32[]{:S(2)}, u32[]{:S(2)}) %collective-permute-start.2) | collective-permute-done | bytes 262176 | tf_op jit(solution)/shard_map/ppermute | solution.py:252
  17.8 6.5 %collective-permute-done.1.refs_2_ = f32[256,256]{1,0:T(8,128)S(1)} collective-permute-done((f32[256,256]{1,0:T(8,128)S(1)}, f32[256,256]{1,0:T(8,128)S(1)}, u32[]{:S(2)}, u32[]{:S(2)}) %collective-permute-start.1) | collective-permute-done | bytes 262176 | tf_op jit(solution)/shard_map/ppermute | solution.py:252
  24.3 4.4 %collective-permute-start.9 = (f32[256,256]{1,0:T(8,128)}, f32[256,256]{1,0:T(8,128)S(1)}, u32[]{:S(2)}, u32[]{:S(2)}) collective-permute-start(f32[256,256]{1,0:T(8,128)} %get-tuple-element.16), channel_id=1, source_target_pairs={{0,2},{2,4},{4,6},{6,8},{8,10},{10,12},{12,14},{14,16},{16,18},{18... | collective-permute-start | bytes 786440 | tf_op jit(solution)/shard_map/ppermute | solution.py:252
  28.7 1.3 collective-permute-start.10
  30.0 0.1 multiply_round-nearest-even_fusion
  30.1 0.1 slice.137
  30.2 0.1 slice.134
  30.2 0.1 fusion.24
  30.3 0.1 stack.27
  30.4 10.0 %collective-permute-done.9.refs_2_ = f32[256,256]{1,0:T(8,128)S(1)} collective-permute-done((f32[256,256]{1,0:T(8,128)}, f32[256,256]{1,0:T(8,128)S(1)}, u32[]{:S(2)}, u32[]{:S(2)}) %collective-permute-start.9) | collective-permute-done | bytes 262176 | tf_op jit(solution)/shard_map/ppermute | solution.py:252
  40.4 0.7 copy-done.2
  41.1 0.0 collective-permute-done.10.refs_3_
  41.1 0.7 copy-done.4
  41.9 0.0 collective-permute-done.refs_1_
  41.9 0.1 broadcast_in_dim.5.factors
  41.9 3.4 %copy-done = f32[16,256,512]{2,1,0:T(8,128)S(1)} copy-done((f32[16,256,512]{2,1,0:T(8,128)S(1)}, f32[16,256,512]{2,1,0:T(8,128)}, u32[]{:S(2)}) %copy-start) | copy-done | bytes 8388632
  45.3 0.9 copy-done.3
  46.3 0.9 copy-done.5
  47.2 20.7 %march_full_2.1 = (f32[6,4,16,256]{3,2,1,0:T(8,128)S(1)}, f32[6,4,16,256]{3,2,1,0:T(8,128)S(1)}, f32[6,4,16,256]{3,2,1,0:T(8,128)S(1)}, f32[6,4,16,256]{3,2,1,0:T(8,128)}) custom-call(s32[6,8,128]{2,1,0:T(8,128)S(1)} %broadcast_in_dim.4.words, f32[6,8,128]{2,1,0:T(8,128)S(1)} %broadcast_in_dim.5.factors, f32[16,256,512]{2,1,0:T(8,128)S(1)} %copy-done, ...), custom_call_target="tpu_custom_call" | custom-call | flops 104857600 | bytes 6291456 | tf_op jit(solution)/shard_map/march_full_2/pallas_call | solution.py:229
  67.9 0.8 copy.11
  68.7 0.0 collective-permute-start.12
  68.7 3.8 %collective-permute-start.11 = (f32[6,4,16,256]{3,2,1,0:T(8,128)}, f32[6,4,16,256]{3,2,1,0:T(8,128)}, u32[]{:S(2)}, u32[]{:S(2)}) collective-permute-start(f32[6,4,16,256]{3,2,1,0:T(8,128)} %get-tuple-element.18), channel_id=1, source_target_pairs={{0,6},{2,4},{4,2},{6,0},{8,14},{10,12},{12,10},{14,8},{16,22},{18,... | collective-permute-start | bytes 1179656 | tf_op jit(solution)/shard_map/ppermute | solution.py:280
  72.6 0.1 collective-permute-start.13
  72.7 0.0 copy-start.1
  72.7 3.4 %copy-done.1 = f32[16,256,512]{2,1,0:T(8,128)S(1)} copy-done((f32[16,256,512]{2,1,0:T(8,128)S(1)}, f32[16,256,512]{2,1,0:T(8,128)}, u32[]{:S(2)}) %copy-start.1) | copy-done | bytes 8388632
  76.1 18.2 %march_middle_0.1.refs_4_ = f32[6,256,256]{2,1,0:T(8,128)S(1)} custom-call(s32[6,8,128]{2,1,0:T(8,128)S(1)} %broadcast_in_dim.4.words, f32[6,8,128]{2,1,0:T(8,128)S(1)} %broadcast_in_dim.5.factors, f32[16,256,512]{2,1,0:T(8,128)S(1)} %copy-done.1, f32[16,256,128]{2,1,0:T(8,128)S(1)} %collective-permute-done.refs_1_), custom_call_target="tpu_custom_call" | custom-call | flops 91750400 | bytes 5505024 | tf_op jit(solution)/shard_map/march_middle_0/pallas_call | solution.py:229
  94.3 7.3 %march_rim_0.1 = (f32[6,4,16,256]{3,2,1,0:T(8,128)S(1)}, f32[6,4,16,256]{3,2,1,0:T(8,128)S(1)}, f32[6,4,16,256]{3,2,1,0:T(8,128)S(1)}, f32[6,4,16,256]{3,2,1,0:T(8,128)S(1)}) custom-call(s32[6,8,128]{2,1,0:T(8,128)S(1)} %broadcast_in_dim.4.words, f32[6,8,128]{2,1,0:T(8,128)S(1)} %broadcast_in_dim.5.factors, f32[16,256,512]{2,1,0:T(8,128)S(1)} %copy-done.1, ...), custom_call_target="tpu_custom_call" | custom-call | flops 13107200 | bytes 786432 | tf_op jit(solution)/shard_map/march_rim_0/pallas_call | solution.py:229
  101.7 2.1 %collective-permute-start.5 = (f32[6,4,16,256]{3,2,0,1:T(8,128)S(1)}, f32[6,4,16,256]{3,2,0,1:T(8,128)S(1)}, u32[]{:S(2)}, u32[]{:S(2)}) collective-permute-start(f32[6,4,16,256]{3,2,0,1:T(8,128)S(1)} %copy.7), channel_id=1, source_target_pairs={{0,2},{2,0},{4,6},{6,4},{8,10},{10,8},{12,14},{14,12},{16,18},{18,... | collective-permute-start | bytes 1179656 | tf_op jit(solution)/shard_map/ppermute | solution.py:280
  103.8 0.0 collective-permute-start.4
  103.8 0.0 collective-permute-done.12
  103.8 1.5 %collective-permute-start.3 = (f32[6,4,16,256]{3,2,0,1:T(8,128)S(1)}, f32[6,4,16,256]{3,2,0,1:T(8,128)S(1)}, u32[]{:S(2)}, u32[]{:S(2)}) collective-permute-start(f32[6,4,16,256]{3,2,0,1:T(8,128)S(1)} %copy.5), channel_id=1, source_target_pairs={{0,6},{2,4},{4,2},{6,0},{8,14},{10,12},{12,10},{14,8},{16,22},{18,... | collective-permute-start | bytes 1179656 | tf_op jit(solution)/shard_map/ppermute | solution.py:280
  105.3 0.0 collective-permute-done.11
  105.3 1.1 fusion.30
  106.4 1.1 copy_multiply_fusion.1
  107.5 0.0 collective-permute-done.13
  107.5 1.1 multiply_add_fusion
  108.7 2.1 %collective-permute-start.14 = (f32[6,1,16,256]{3,2,0,1:T(8,128)S(1)}, f32[6,1,16,256]{3,2,0,1:T(8,128)S(1)}, u32[]{:S(2)}, u32[]{:S(2)}) collective-permute-start(f32[6,1,16,256]{3,2,0,1:T(8,128)S(1)} %get-tuple-element.37), channel_id=1, source_target_pairs={{0,24},{2,26},{4,28},{6,30},{8,16},{10,18},{12,20},{14,22},{16,8},... | collective-permute-start | bytes 294920 | tf_op jit(solution)/shard_map/ppermute | solution.py:280
  110.9 1.0 collective-permute-start.15
  111.8 2.0 %collective-permute-done.5 = f32[6,4,16,256]{3,2,0,1:T(8,128)S(1)} collective-permute-done((f32[6,4,16,256]{3,2,0,1:T(8,128)S(1)}, f32[6,4,16,256]{3,2,0,1:T(8,128)S(1)}, u32[]{:S(2)}, u32[]{:S(2)}) %collective-permute-start.5) | collective-permute-done | bytes 393248 | tf_op jit(solution)/shard_map/ppermute | solution.py:280
  113.8 1.6 %collective-permute-start.16 = (f32[6,1,16,256]{3,2,0,1:T(8,128)S(1)}, f32[6,1,16,256]{3,2,0,1:T(8,128)S(1)}, u32[]{:S(2)}, u32[]{:S(2)}) collective-permute-start(f32[6,1,16,256]{3,2,0,1:T(8,128)S(1)} %get-tuple-element.39), channel_id=1, source_target_pairs={{0,8},{2,10},{4,12},{6,14},{8,0},{10,2},{12,4},{14,6},{16,24},{18,... | collective-permute-start | bytes 294920 | tf_op jit(solution)/shard_map/ppermute | solution.py:280
  115.4 5.9 %collective-permute-done.4 = f32[6,4,16,256]{3,2,0,1:T(8,128)S(1)} collective-permute-done((f32[6,4,16,256]{3,2,0,1:T(8,128)S(1)}, f32[6,4,16,256]{3,2,0,1:T(8,128)S(1)}, u32[]{:S(2)}, u32[]{:S(2)}) %collective-permute-start.4) | collective-permute-done | bytes 393248 | tf_op jit(solution)/shard_map/ppermute | solution.py:280
  121.4 0.0 collective-permute-done.3
  121.4 0.2 select_multiply_fusion.1
  121.6 2.0 %collective-permute-start.6 = (f32[6,1,16,256]{3,2,0,1:T(8,128)S(1)}, f32[6,1,16,256]{3,2,0,1:T(8,128)S(1)}, u32[]{:S(2)}, u32[]{:S(2)}) collective-permute-start(f32[6,1,16,256]{3,2,0,1:T(8,128)S(1)} %get-tuple-element.33), channel_id=1, source_target_pairs={{0,24},{2,26},{4,28},{6,30},{8,16},{10,18},{12,20},{14,22},{16,8},... | collective-permute-start | bytes 294920 | tf_op jit(solution)/shard_map/ppermute | solution.py:280
  123.6 1.1 collective-permute-start.7
  124.7 0.0 collective-permute-done.14
  124.7 1.3 %collective-permute-start.8 = (f32[6,1,16,256]{3,2,0,1:T(8,128)S(1)}, f32[6,1,16,256]{3,2,0,1:T(8,128)S(1)}, u32[]{:S(2)}, u32[]{:S(2)}) collective-permute-start(f32[6,1,16,256]{3,2,0,1:T(8,128)S(1)} %get-tuple-element.35), channel_id=1, source_target_pairs={{0,8},{2,10},{4,12},{6,14},{8,0},{10,2},{12,4},{14,6},{16,24},{18,... | collective-permute-start | bytes 294920 | tf_op jit(solution)/shard_map/ppermute | solution.py:280
  126.0 0.0 collective-permute-done.15
  126.0 0.0 collective-permute-done.16
  126.1 2.7 %collective-permute-done.6 = f32[6,1,16,256]{3,2,0,1:T(8,128)S(1)} collective-permute-done((f32[6,1,16,256]{3,2,0,1:T(8,128)S(1)}, f32[6,1,16,256]{3,2,0,1:T(8,128)S(1)}, u32[]{:S(2)}, u32[]{:S(2)}) %collective-permute-start.6) | collective-permute-done | bytes 98336 | tf_op jit(solution)/shard_map/ppermute | solution.py:280
  128.8 2.6 %collective-permute-done.7 = f32[6,1,16,256]{3,2,0,1:T(8,128)S(1)} collective-permute-done((f32[6,1,16,256]{3,2,0,1:T(8,128)S(1)}, f32[6,1,16,256]{3,2,0,1:T(8,128)S(1)}, u32[]{:S(2)}, u32[]{:S(2)}) %collective-permute-start.7) | collective-permute-done | bytes 98336 | tf_op jit(solution)/shard_map/ppermute | solution.py:280
  131.3 0.0 collective-permute-done.8
  131.4 0.6 pad_maximum_fusion.1
  132.1 0.6 pad_maximum_fusion
  (22 shorter events, 0.4 us)
Async XLA Ops:
  3.8 8.8 %copy-start.7 = (f32[3,16]{1,0:T(4,128)S(1)}, f32[3,16]{1,0:T(4,128)}, u32[]{:S(2)}) copy-start(f32[3,16]{1,0:T(4,128)} %param.5) | copy-start | bytes 580
  3.8 9.4 %copy-start.6 = (f32[3,16]{1,0:T(4,128)S(1)}, f32[3,16]{1,0:T(4,128)}, u32[]{:S(2)}) copy-start(f32[3,16]{1,0:T(4,128)} %param.4) | copy-start | bytes 580
  3.8 38.1 %collective-permute-start = (f32[16,256,128]{2,1,0:T(8,128)}, f32[16,256,128]{2,1,0:T(8,128)S(1)}, u32[]{:S(2)}, u32[]{:S(2)}) collective-permute-start(f32[16,256,128]{2,1,0:T(8,128)} %constant_dynamic-slice_fusion), channel_id=1, source_target_pairs={{0,1},{1,0},{2,3},{3,2},{4,5},{5,4},{6,7},{7,6},{8,9},{9,8},{10,11... | collective-permute-start | bytes 6291464 | tf_op jit(solution)/shard_map/ppermute | solution.py:260
  6.2 11.6 %collective-permute-start.2 = (f32[256,256]{1,0:T(8,128)S(1)}, f32[256,256]{1,0:T(8,128)S(1)}, u32[]{:S(2)}, u32[]{:S(2)}) collective-permute-start(f32[256,256]{1,0:T(8,128)S(1)} %get-tuple-element.25), channel_id=1, source_target_pairs={{2,0},{4,2},{6,4},{8,6},{10,8},{12,10},{14,12},{16,14},{18,16},{20... | collective-permute-start | bytes 786440 | tf_op jit(solution)/shard_map/ppermute | solution.py:252
  7.5 16.8 %collective-permute-start.1 = (f32[256,256]{1,0:T(8,128)S(1)}, f32[256,256]{1,0:T(8,128)S(1)}, u32[]{:S(2)}, u32[]{:S(2)}) collective-permute-start(f32[256,256]{1,0:T(8,128)S(1)} %get-tuple-element.27), channel_id=1, source_target_pairs={{0,2},{2,4},{4,6},{6,8},{8,10},{10,12},{12,14},{14,16},{16,18},{18... | collective-permute-start | bytes 786440 | tf_op jit(solution)/shard_map/ppermute | solution.py:252
  24.3 16.1 %collective-permute-start.9 = (f32[256,256]{1,0:T(8,128)}, f32[256,256]{1,0:T(8,128)S(1)}, u32[]{:S(2)}, u32[]{:S(2)}) collective-permute-start(f32[256,256]{1,0:T(8,128)} %get-tuple-element.16), channel_id=1, source_target_pairs={{0,2},{2,4},{4,6},{6,8},{8,10},{10,12},{12,14},{14,16},{16,18},{18... | collective-permute-start | bytes 786440 | tf_op jit(solution)/shard_map/ppermute | solution.py:252
  28.7 12.4 %collective-permute-start.10 = (f32[256,256]{1,0:T(8,128)S(1)}, f32[256,256]{1,0:T(8,128)S(1)}, u32[]{:S(2)}, u32[]{:S(2)}) collective-permute-start(f32[256,256]{1,0:T(8,128)S(1)} %get-tuple-element.17), channel_id=1, source_target_pairs={{2,0},{4,2},{6,4},{8,6},{10,8},{12,10},{14,12},{16,14},{18,16},{20... | collective-permute-start | bytes 786440 | tf_op jit(solution)/shard_map/ppermute | solution.py:252
  40.4 0.7 copy-start.2
  41.1 0.7 copy-start.4
  41.9 3.4 %copy-start = (f32[16,256,512]{2,1,0:T(8,128)S(1)}, f32[16,256,512]{2,1,0:T(8,128)}, u32[]{:S(2)}) copy-start(f32[16,256,512]{2,1,0:T(8,128)} %refs_0_.5) | copy-start | bytes 25165828
  45.3 0.9 copy-start.3
  46.3 0.9 copy-start.5
  68.7 35.1 %collective-permute-start.12 = (f32[6,4,16,256]{3,2,0,1:T(8,128)}, f32[6,4,16,256]{3,2,0,1:T(8,128)}, u32[]{:S(2)}, u32[]{:S(2)}) collective-permute-start(f32[6,4,16,256]{3,2,0,1:T(8,128)} %copy.11), channel_id=1, source_target_pairs={{0,4},{2,6},{4,0},{6,2},{8,12},{10,14},{12,8},{14,10},{16,20},{18,... | collective-permute-start | bytes 1179656 | tf_op jit(solution)/shard_map/ppermute | solution.py:280
  68.7 36.6 %collective-permute-start.11 = (f32[6,4,16,256]{3,2,1,0:T(8,128)}, f32[6,4,16,256]{3,2,1,0:T(8,128)}, u32[]{:S(2)}, u32[]{:S(2)}) collective-permute-start(f32[6,4,16,256]{3,2,1,0:T(8,128)} %get-tuple-element.18), channel_id=1, source_target_pairs={{0,6},{2,4},{4,2},{6,0},{8,14},{10,12},{12,10},{14,8},{16,22},{18,... | collective-permute-start | bytes 1179656 | tf_op jit(solution)/shard_map/ppermute | solution.py:280
  72.6 34.9 %collective-permute-start.13 = (f32[6,4,16,256]{3,2,0,1:T(8,128)S(1)}, f32[6,4,16,256]{3,2,0,1:T(8,128)S(1)}, u32[]{:S(2)}, u32[]{:S(2)}) collective-permute-start(f32[6,4,16,256]{3,2,0,1:T(8,128)S(1)} %copy.13), channel_id=1, source_target_pairs={{0,2},{2,0},{4,6},{6,4},{8,10},{10,8},{12,14},{14,12},{16,18},{18,... | collective-permute-start | bytes 1179656 | tf_op jit(solution)/shard_map/ppermute | solution.py:280
  72.7 3.4 %copy-start.1 = (f32[16,256,512]{2,1,0:T(8,128)S(1)}, f32[16,256,512]{2,1,0:T(8,128)}, u32[]{:S(2)}) copy-start(f32[16,256,512]{2,1,0:T(8,128)} %refs_0_.5) | copy-start | bytes 25165828
  101.7 12.1 %collective-permute-start.5 = (f32[6,4,16,256]{3,2,0,1:T(8,128)S(1)}, f32[6,4,16,256]{3,2,0,1:T(8,128)S(1)}, u32[]{:S(2)}, u32[]{:S(2)}) collective-permute-start(f32[6,4,16,256]{3,2,0,1:T(8,128)S(1)} %copy.7), channel_id=1, source_target_pairs={{0,2},{2,0},{4,6},{6,4},{8,10},{10,8},{12,14},{14,12},{16,18},{18,... | collective-permute-start | bytes 1179656 | tf_op jit(solution)/shard_map/ppermute | solution.py:280
  103.8 17.6 %collective-permute-start.4 = (f32[6,4,16,256]{3,2,0,1:T(8,128)S(1)}, f32[6,4,16,256]{3,2,0,1:T(8,128)S(1)}, u32[]{:S(2)}, u32[]{:S(2)}) collective-permute-start(f32[6,4,16,256]{3,2,0,1:T(8,128)S(1)} %copy.6), channel_id=1, source_target_pairs={{0,4},{2,6},{4,0},{6,2},{8,12},{10,14},{12,8},{14,10},{16,20},{18,... | collective-permute-start | bytes 1179656 | tf_op jit(solution)/shard_map/ppermute | solution.py:280
  103.8 17.6 %collective-permute-start.3 = (f32[6,4,16,256]{3,2,0,1:T(8,128)S(1)}, f32[6,4,16,256]{3,2,0,1:T(8,128)S(1)}, u32[]{:S(2)}, u32[]{:S(2)}) collective-permute-start(f32[6,4,16,256]{3,2,0,1:T(8,128)S(1)} %copy.5), channel_id=1, source_target_pairs={{0,6},{2,4},{4,2},{6,0},{8,14},{10,12},{12,10},{14,8},{16,22},{18,... | collective-permute-start | bytes 1179656 | tf_op jit(solution)/shard_map/ppermute | solution.py:280
  108.7 16.0 %collective-permute-start.14 = (f32[6,1,16,256]{3,2,0,1:T(8,128)S(1)}, f32[6,1,16,256]{3,2,0,1:T(8,128)S(1)}, u32[]{:S(2)}, u32[]{:S(2)}) collective-permute-start(f32[6,1,16,256]{3,2,0,1:T(8,128)S(1)} %get-tuple-element.37), channel_id=1, source_target_pairs={{0,24},{2,26},{4,28},{6,30},{8,16},{10,18},{12,20},{14,22},{16,8},... | collective-permute-start | bytes 294920 | tf_op jit(solution)/shard_map/ppermute | solution.py:280
  110.9 15.2 %collective-permute-start.15 = (f32[6,1,16,256]{3,2,0,1:T(8,128)S(1)}, f32[6,1,16,256]{3,2,0,1:T(8,128)S(1)}, u32[]{:S(2)}, u32[]{:S(2)}) collective-permute-start(f32[6,1,16,256]{3,2,0,1:T(8,128)S(1)} %get-tuple-element.38), channel_id=1, source_target_pairs={{0,16},{2,18},{4,20},{6,22},{8,24},{10,26},{12,28},{14,30},{16,0},... | collective-permute-start | bytes 294920 | tf_op jit(solution)/shard_map/ppermute | solution.py:280
  113.8 12.2 %collective-permute-start.16 = (f32[6,1,16,256]{3,2,0,1:T(8,128)S(1)}, f32[6,1,16,256]{3,2,0,1:T(8,128)S(1)}, u32[]{:S(2)}, u32[]{:S(2)}) collective-permute-start(f32[6,1,16,256]{3,2,0,1:T(8,128)S(1)} %get-tuple-element.39), channel_id=1, source_target_pairs={{0,8},{2,10},{4,12},{6,14},{8,0},{10,2},{12,4},{14,6},{16,24},{18,... | collective-permute-start | bytes 294920 | tf_op jit(solution)/shard_map/ppermute | solution.py:280
  121.6 7.2 %collective-permute-start.6 = (f32[6,1,16,256]{3,2,0,1:T(8,128)S(1)}, f32[6,1,16,256]{3,2,0,1:T(8,128)S(1)}, u32[]{:S(2)}, u32[]{:S(2)}) collective-permute-start(f32[6,1,16,256]{3,2,0,1:T(8,128)S(1)} %get-tuple-element.33), channel_id=1, source_target_pairs={{0,24},{2,26},{4,28},{6,30},{8,16},{10,18},{12,20},{14,22},{16,8},... | collective-permute-start | bytes 294920 | tf_op jit(solution)/shard_map/ppermute | solution.py:280
  123.6 7.8 %collective-permute-start.7 = (f32[6,1,16,256]{3,2,0,1:T(8,128)S(1)}, f32[6,1,16,256]{3,2,0,1:T(8,128)S(1)}, u32[]{:S(2)}, u32[]{:S(2)}) collective-permute-start(f32[6,1,16,256]{3,2,0,1:T(8,128)S(1)} %get-tuple-element.34), channel_id=1, source_target_pairs={{0,16},{2,18},{4,20},{6,22},{8,24},{10,26},{12,28},{14,30},{16,0},... | collective-permute-start | bytes 294920 | tf_op jit(solution)/shard_map/ppermute | solution.py:280
  124.7 6.7 %collective-permute-start.8 = (f32[6,1,16,256]{3,2,0,1:T(8,128)S(1)}, f32[6,1,16,256]{3,2,0,1:T(8,128)S(1)}, u32[]{:S(2)}, u32[]{:S(2)}) collective-permute-start(f32[6,1,16,256]{3,2,0,1:T(8,128)S(1)} %get-tuple-element.35), channel_id=1, source_target_pairs={{0,8},{2,10},{4,12},{6,14},{8,0},{10,2},{12,4},{14,6},{16,24},{18,... | collective-permute-start | bytes 294920 | tf_op jit(solution)/shard_map/ppermute | solution.py:280

commit v4 on v3

--- a/solution.py
+++ b/solution.py
@@ -225,7 +225,7 @@
         operands.append(middle)
         scratch.append(pltpu.VMEM((tiles, 6, height, LANES), jnp.float32))
     marched = {"full": planes, "middle": planes - 2, "rim": 2}[mode]
-    anywhere = pl.BlockSpec(memory_space=pl.ANY)
+    anywhere = pl.BlockSpec(memory_space=pltpu.HBM)
     out = pl.pallas_call(
         functools.partial(
             march_kernel, mode, first_tile, tiles, 0.5 * (count_breaks - 1), group
@@ -252,10 +252,10 @@
     return lax.ppermute(last, "slab", forward), lax.ppermute(first, "slab", backward)
 
 
-def edge_tile(field):
+def edge_tile(field, earlier):
     first = lax.axis_index("tile") == 0
     planes, height, width = field.shape
-    start = jnp.where(first, width - LANES, 0)
+    start, _ = lax.optimization_barrier((jnp.where(first, width - LANES, 0), earlier))
     own = lax.dynamic_slice_in_dim(field, start, LANES, axis=2)
     return lax.ppermute(own, "tile", [(0, 1), (1, 0)])
 
@@ -316,16 +316,13 @@
     tables = prepare_tables(tf_emission, tf_absorption, planes * slab_count)
     strips = [(first * LANES, (first + count) * LANES) for first, count in chunks]
 
-    halos = []
-    for begin, end in strips:
-        first, last = field[0, :, begin:end], field[-1, :, begin:end]
-        if halos:
-            first, last, _ = lax.optimization_barrier((first, last, halos[-1]))
-        halos.append(plane_halos(first, last))
-        if len(halos) == 1:
-            side = edge_tile(field)
+    planes_out = [(field[0, :, begin:end], field[-1, :, begin:end]) for begin, end in strips]
+    halos = [plane_halos(first, last) for first, last in planes_out]
+    side = edge_tile(field, planes_out)
     results = []
     for chunk, halo in zip(chunks, halos):
+        if results:
+            halo, _ = lax.optimization_barrier((halo, out))
         if chunk[0] == 0:
             middle = march(
                 "middle", chunk, tables, field, side, None, None, count_breaks, None

time: 133 us -> 129 us (0.970)
  waiting for transfers between devices: 32.3 us -> 22.5 us
  starting transfers between devices: 29.1 us -> 36.4 us
    ppermute x2, waiting for transfers between devices: 16.5 us -> 0.01 us  [plane_halos(): lax.ppermute(last, 'slab', forward)]
    ppermute x12, waiting for transfers between devices: 13.3 us -> 22.5 us  [exchange(): lax.ppermute(part, 'slab', [(i, i ^ change << shift) for i in range(count)])]
    ppermute x12, starting transfers between devices: 16.7 us -> 22.6 us  [exchange(): lax.ppermute(part, 'slab', [(i, i ^ change << shift) for i in range(count)])]
    ppermute x2, waiting for transfers between devices: 2.5 us -> 0.01 us  [plane_halos(): lax.ppermute(first, 'slab', backward)]
    unnamed x16 -> x24, local copies, waits for them, and re-layouts: 10.1 us -> 8.13 us
  transfers between devices with their start and end apart: 17 -> 17, of which waited for: 7 -> 5; matrix products, arithmetic and copies ran while one was open for 6% -> 4% of each run, Pallas kernels for 19% -> 20%
where the time goes in v4:
time: 129 us
  Pallas kernels  46.9 us (36%)
  starting transfers between devices  36.4 us (28%)
  waiting for transfers between devices  22.5 us (17%)
  local copies, waits for them, and re-layouts  15.3 us (12%)
  other arithmetic  5.29 us (4%)
  between operations  2.28 us (2%)
    pallas_call x3, Pallas kernels, march(): pl.pallas_call(functools.partial(march_kernel, mode, first_tile, tiles, 0...  46.9 us
    ppermute x12, starting transfers between devices, exchange(): lax.ppermute(part, 'slab', [(i, i ^ change << shift) for i in range(count)])  22.6 us
    ppermute x12, waiting for transfers between devices, exchange(): lax.ppermute(part, 'slab', [(i, i ^ change << shift) for i in range(count)])  22.5 us
    ppermute x2, starting transfers between devices, plane_halos(): lax.ppermute(last, 'slab', forward)  10.1 us
    unnamed x24, local copies, waits for them, and re-layouts  8.13 us
    dynamic_slice x1, local copies, waits for them, and re-layouts, edge_tile(): own = lax.dynamic_slice_in_dim(field, start, LANES, axis=2)  3.57 us
    ppermute x2, starting transfers between devices, plane_halos(): lax.ppermute(first, 'slab', backward)  2.58 us
  transfers between devices with their start and end apart: 17, of which 5 were waited for; matrix products, arithmetic and copies ran while one was open for 4% of the time, Pallas kernels for 20%

profile of v4, /device:TPU:0, one launch (start us, length us, event | category | flops | bytes accessed | tf_op | source)
XLA Modules:
  0.0 128.6 jit_solution(10149165704664648647)
XLA Ops:
  0.6 2.1 %slice_bitcast_fusion = (f32[256,256]{1,0:T(8,128)}, f32[256,256]{1,0:T(8,128)}, f32[256,256]{1,0:T(8,128)}, f32[256,256]{1,0:T(8,128)S(1)}) fusion(f32[16,256,512]{2,1,0:T(8,128)} %refs_0_.5), kind=kLoop, calls=%fused_computation.16 | loop fusion | bytes 2097152 | tf_op jit(solution)/shard_map/squeeze | solution.py:319
  2.8 3.6 %constant_dynamic-slice_fusion = f32[16,256,128]{2,1,0:T(8,128)} fusion(f32[16,256,512]{2,1,0:T(8,128)} %refs_0_.5, s32[]{:T(128)S(6)} %select_n.233), kind=kLoop, calls=%fused_computation.71 | loop fusion | bytes 4194308 | tf_op jit(solution)/shard_map/dynamic_slice | solution.py:259
  6.3 1.0 collective-permute-start
  7.4 4.2 %collective-permute-start.1 = (f32[256,256]{1,0:T(8,128)}, f32[256,256]{1,0:T(8,128)S(1)}, u32[]{:S(2)}, u32[]{:S(2)}) collective-permute-start(f32[256,256]{1,0:T(8,128)} %get-tuple-element.29), channel_id=1, source_target_pairs={{0,2},{2,4},{4,6},{6,8},{8,10},{10,12},{12,14},{14,16},{16,18},{18... | collective-permute-start | bytes 786440 | tf_op jit(solution)/shard_map/ppermute | solution.py:252
  11.6 1.3 %collective-permute-start.2 = (f32[256,256]{1,0:T(8,128)S(1)}, f32[256,256]{1,0:T(8,128)S(1)}, u32[]{:S(2)}, u32[]{:S(2)}) collective-permute-start(f32[256,256]{1,0:T(8,128)S(1)} %get-tuple-element.30), channel_id=1, source_target_pairs={{2,0},{4,2},{6,4},{8,6},{10,8},{12,10},{14,12},{16,14},{18,16},{20... | collective-permute-start | bytes 786440 | tf_op jit(solution)/shard_map/ppermute | solution.py:252
  12.9 1.3 %collective-permute-start.10 = (f32[256,256]{1,0:T(8,128)}, f32[256,256]{1,0:T(8,128)S(1)}, u32[]{:S(2)}, u32[]{:S(2)}) collective-permute-start(f32[256,256]{1,0:T(8,128)} %get-tuple-element.28), channel_id=1, source_target_pairs={{2,0},{4,2},{6,4},{8,6},{10,8},{12,10},{14,12},{16,14},{18,16},{20... | collective-permute-start | bytes 786440 | tf_op jit(solution)/shard_map/ppermute | solution.py:252
  14.2 5.9 %collective-permute-start.9 = (f32[256,256]{1,0:T(8,128)}, f32[256,256]{1,0:T(8,128)}, u32[]{:S(2)}, u32[]{:S(2)}) collective-permute-start(f32[256,256]{1,0:T(8,128)} %get-tuple-element.27), channel_id=1, source_target_pairs={{0,2},{2,4},{4,6},{6,8},{8,10},{10,12},{12,14},{14,16},{16,18},{18... | collective-permute-start | bytes 786440 | tf_op jit(solution)/shard_map/ppermute | solution.py:252
  20.1 0.6 reduce_max.18
  20.7 0.6 reduce_max.19
  22.7 0.1 multiply_round-nearest-even_fusion.1
  22.8 0.1 multiply_round-nearest-even_fusion
  22.9 0.1 slice.134
  22.9 0.1 slice.137
  23.0 0.1 fusion.24
  23.1 0.1 stack.27
  23.2 0.0 collective-permute-done.refs_1_
  23.2 0.1 broadcast_in_dim.5.factors
  23.3 3.4 %copy-done = f32[16,256,512]{2,1,0:T(8,128)S(1)} copy-done((f32[16,256,512]{2,1,0:T(8,128)S(1)}, f32[16,256,512]{2,1,0:T(8,128)}, u32[]{:S(2)}) %copy-start) | copy-done | bytes 8388632
  26.7 18.2 %march_middle_0.1.refs_4_ = f32[6,256,256]{2,1,0:T(8,128)S(1)} custom-call(s32[6,8,128]{2,1,0:T(8,128)S(1)} %broadcast_in_dim.4.words, f32[6,8,128]{2,1,0:T(8,128)S(1)} %broadcast_in_dim.5.factors, f32[16,256,512]{2,1,0:T(8,128)S(1)} %copy-done, f32[16,256,128]{2,1,0:T(8,128)S(1)} %collective-permute-done.refs_1_), custom_call_target="tpu_custom_call" | custom-call | flops 91750400 | bytes 5505024 | tf_op jit(solution)/shard_map/march_middle_0/pallas_call | solution.py:229
  44.9 0.0 collective-permute-done.1.refs_2_
  44.9 0.7 copy-done.6
  45.6 0.0 collective-permute-done.2.refs_3_
  45.6 0.7 copy-done.8
  46.3 0.9 copy-done.7
  47.3 0.9 copy-done.9
  48.2 7.3 %march_rim_0.1 = (f32[6,4,16,256]{3,2,1,0:T(8,128)S(1)}, f32[6,4,16,256]{3,2,1,0:T(8,128)S(1)}, f32[6,4,16,256]{3,2,1,0:T(8,128)S(1)}, f32[6,4,16,256]{3,2,1,0:T(8,128)S(1)}) custom-call(s32[6,8,128]{2,1,0:T(8,128)S(1)} %broadcast_in_dim.4.words, f32[6,8,128]{2,1,0:T(8,128)S(1)} %broadcast_in_dim.5.factors, f32[16,256,512]{2,1,0:T(8,128)S(1)} %copy-done, ...), custom_call_target="tpu_custom_call" | custom-call | flops 13107200 | bytes 786432 | tf_op jit(solution)/shard_map/march_rim_0/pallas_call | solution.py:229
  55.5 0.0 collective-permute-done.10.refs_3_
  55.5 0.0 collective-permute-done.9.refs_2_
  55.6 21.4 %march_full_2.1 = (f32[6,4,16,256]{3,2,1,0:T(8,128)S(1)}, f32[6,4,16,256]{3,2,1,0:T(8,128)S(1)}, f32[6,4,16,256]{3,2,1,0:T(8,128)S(1)}, f32[6,4,16,256]{3,2,1,0:T(8,128)}) custom-call(s32[6,8,128]{2,1,0:T(8,128)S(1)} %broadcast_in_dim.4.words, f32[6,8,128]{2,1,0:T(8,128)S(1)} %broadcast_in_dim.5.factors, f32[16,256,512]{2,1,0:T(8,128)S(1)} %copy-done, ...), custom_call_target="tpu_custom_call" | custom-call | flops 104857600 | bytes 6291456 | tf_op jit(solution)/shard_map/march_full_2/pallas_call | solution.py:229
  77.0 0.0 copy-done.1
  77.0 0.0 copy-start.2
  77.0 0.7 copy-done.2
  77.8 0.7 copy-done.4
  78.5 2.2 %collective-permute-start.12 = (f32[6,4,16,256]{3,2,0,1:T(8,128)S(1)}, f32[6,4,16,256]{3,2,0,1:T(8,128)}, u32[]{:S(2)}, u32[]{:S(2)}) collective-permute-start(f32[6,4,16,256]{3,2,0,1:T(8,128)S(1)} %copy.11), channel_id=1, source_target_pairs={{0,4},{2,6},{4,0},{6,2},{8,12},{10,14},{12,8},{14,10},{16,20},{18,... | collective-permute-start | bytes 1179656 | tf_op jit(solution)/shard_map/ppermute | solution.py:280
  80.7 1.8 %collective-permute-start.11 = (f32[6,4,16,256]{3,2,1,0:T(8,128)}, f32[6,4,16,256]{3,2,1,0:T(8,128)S(1)}, u32[]{:S(2)}, u32[]{:S(2)}) collective-permute-start(f32[6,4,16,256]{3,2,1,0:T(8,128)} %get-tuple-element.20), channel_id=1, source_target_pairs={{0,6},{2,4},{4,2},{6,0},{8,14},{10,12},{12,10},{14,8},{16,22},{18,... | collective-permute-start | bytes 1179656 | tf_op jit(solution)/shard_map/ppermute | solution.py:280
  82.5 1.0 copy.5
  83.7 0.6 collective-permute-start.13
  84.3 2.9 %collective-permute-start.3 = (f32[6,4,16,256]{3,2,0,1:T(8,128)S(1)}, f32[6,4,16,256]{3,2,0,1:T(8,128)S(1)}, u32[]{:S(2)}, u32[]{:S(2)}) collective-permute-start(f32[6,4,16,256]{3,2,0,1:T(8,128)S(1)} %copy.5), channel_id=1, source_target_pairs={{0,6},{2,4},{4,2},{6,0},{8,14},{10,12},{12,10},{14,8},{16,22},{18,... | collective-permute-start | bytes 1179656 | tf_op jit(solution)/shard_map/ppermute | solution.py:280
  87.2 0.0 collective-permute-start.4
  87.2 13.5 %collective-permute-done.12 = f32[6,4,16,256]{3,2,0,1:T(8,128)} collective-permute-done((f32[6,4,16,256]{3,2,0,1:T(8,128)S(1)}, f32[6,4,16,256]{3,2,0,1:T(8,128)}, u32[]{:S(2)}, u32[]{:S(2)}) %collective-permute-start.12) | collective-permute-done | bytes 393248 | tf_op jit(solution)/shard_map/ppermute | solution.py:280
  100.7 2.4 %collective-permute-start.5 = (f32[6,4,16,256]{3,2,0,1:T(8,128)S(1)}, f32[6,4,16,256]{3,2,0,1:T(8,128)S(1)}, u32[]{:S(2)}, u32[]{:S(2)}) collective-permute-start(f32[6,4,16,256]{3,2,0,1:T(8,128)S(1)} %copy.7), channel_id=1, source_target_pairs={{0,2},{2,0},{4,6},{6,4},{8,10},{10,8},{12,14},{14,12},{16,18},{18,... | collective-permute-start | bytes 1179656 | tf_op jit(solution)/shard_map/ppermute | solution.py:280
  103.1 0.0 collective-permute-done.11
  103.1 1.0 fusion.30
  104.1 0.1 copy_multiply_fusion.1
  104.2 0.0 collective-permute-done.13
  104.2 1.1 multiply_add_fusion
  105.4 7.4 %collective-permute-start.14 = (f32[6,1,16,256]{3,2,0,1:T(8,128)S(1)}, f32[6,1,16,256]{3,2,0,1:T(8,128)S(1)}, u32[]{:S(2)}, u32[]{:S(2)}) collective-permute-start(f32[6,1,16,256]{3,2,0,1:T(8,128)S(1)} %get-tuple-element.39), channel_id=1, source_target_pairs={{0,24},{2,26},{4,28},{6,30},{8,16},{10,18},{12,20},{14,22},{16,8},... | collective-permute-start | bytes 294920 | tf_op jit(solution)/shard_map/ppermute | solution.py:280
  112.8 0.0 collective-permute-start.15
  112.8 0.0 collective-permute-done.3
  112.8 0.6 collective-permute-start.16
  113.5 0.7 collective-permute-done.4
  114.2 2.4 %collective-permute-done.5 = f32[6,4,16,256]{3,2,0,1:T(8,128)S(1)} collective-permute-done((f32[6,4,16,256]{3,2,0,1:T(8,128)S(1)}, f32[6,4,16,256]{3,2,0,1:T(8,128)S(1)}, u32[]{:S(2)}, u32[]{:S(2)}) %collective-permute-start.5) | collective-permute-done | bytes 393248 | tf_op jit(solution)/shard_map/ppermute | solution.py:280
  116.6 0.2 select_multiply_fusion.1
  116.9 3.8 %collective-permute-start.6 = (f32[6,1,16,256]{3,2,0,1:T(8,128)S(1)}, f32[6,1,16,256]{3,2,0,1:T(8,128)S(1)}, u32[]{:S(2)}, u32[]{:S(2)}) collective-permute-start(f32[6,1,16,256]{3,2,0,1:T(8,128)S(1)} %get-tuple-element.35), channel_id=1, source_target_pairs={{0,24},{2,26},{4,28},{6,30},{8,16},{10,18},{12,20},{14,22},{16,8},... | collective-permute-start | bytes 294920 | tf_op jit(solution)/shard_map/ppermute | solution.py:280
  120.7 0.0 collective-permute-start.7
  120.7 0.0 collective-permute-done.14
  120.7 0.6 collective-permute-start.8
  121.4 0.0 collective-permute-done.15
  121.4 0.0 collective-permute-done.16
  121.4 2.4 %collective-permute-done.6 = f32[6,1,16,256]{3,2,0,1:T(8,128)S(1)} collective-permute-done((f32[6,1,16,256]{3,2,0,1:T(8,128)S(1)}, f32[6,1,16,256]{3,2,0,1:T(8,128)S(1)}, u32[]{:S(2)}, u32[]{:S(2)}) %collective-permute-start.6) | collective-permute-done | bytes 98336 | tf_op jit(solution)/shard_map/ppermute | solution.py:280
  123.8 3.4 %collective-permute-done.7 = f32[6,1,16,256]{3,2,0,1:T(8,128)S(1)} collective-permute-done((f32[6,1,16,256]{3,2,0,1:T(8,128)S(1)}, f32[6,1,16,256]{3,2,0,1:T(8,128)S(1)}, u32[]{:S(2)}, u32[]{:S(2)}) %collective-permute-start.7) | collective-permute-done | bytes 98336 | tf_op jit(solution)/shard_map/ppermute | solution.py:280
  127.2 0.0 collective-permute-done.8
  127.2 0.6 pad_maximum_fusion.1
  127.9 0.6 pad_maximum_fusion
  (30 shorter events, 0.4 us)
Async XLA Ops:
  2.8 17.3 %copy-start.10 = (f32[3,16]{1,0:T(4,128)S(1)}, f32[3,16]{1,0:T(4,128)}, u32[]{:S(2)}) copy-start(f32[3,16]{1,0:T(4,128)} %param.4) | copy-start | bytes 580
  2.8 17.9 %copy-start.11 = (f32[3,16]{1,0:T(4,128)S(1)}, f32[3,16]{1,0:T(4,128)}, u32[]{:S(2)}) copy-start(f32[3,16]{1,0:T(4,128)} %param.5) | copy-start | bytes 580
  6.3 16.9 %collective-permute-start = (f32[16,256,128]{2,1,0:T(8,128)}, f32[16,256,128]{2,1,0:T(8,128)S(1)}, u32[]{:S(2)}, u32[]{:S(2)}) collective-permute-start(f32[16,256,128]{2,1,0:T(8,128)} %constant_dynamic-slice_fusion), channel_id=1, source_target_pairs={{0,1},{1,0},{2,3},{3,2},{4,5},{5,4},{6,7},{7,6},{8,9},{9,8},{10,11... | collective-permute-start | bytes 6291464 | tf_op jit(solution)/shard_map/ppermute | solution.py:260
  7.4 37.5 %collective-permute-start.1 = (f32[256,256]{1,0:T(8,128)}, f32[256,256]{1,0:T(8,128)S(1)}, u32[]{:S(2)}, u32[]{:S(2)}) collective-permute-start(f32[256,256]{1,0:T(8,128)} %get-tuple-element.29), channel_id=1, source_target_pairs={{0,2},{2,4},{4,6},{6,8},{8,10},{10,12},{12,14},{14,16},{16,18},{18... | collective-permute-start | bytes 786440 | tf_op jit(solution)/shard_map/ppermute | solution.py:252
  11.6 34.0 %collective-permute-start.2 = (f32[256,256]{1,0:T(8,128)S(1)}, f32[256,256]{1,0:T(8,128)S(1)}, u32[]{:S(2)}, u32[]{:S(2)}) collective-permute-start(f32[256,256]{1,0:T(8,128)S(1)} %get-tuple-element.30), channel_id=1, source_target_pairs={{2,0},{4,2},{6,4},{8,6},{10,8},{12,10},{14,12},{16,14},{18,16},{20... | collective-permute-start | bytes 786440 | tf_op jit(solution)/shard_map/ppermute | solution.py:252
  12.9 42.6 %collective-permute-start.10 = (f32[256,256]{1,0:T(8,128)}, f32[256,256]{1,0:T(8,128)S(1)}, u32[]{:S(2)}, u32[]{:S(2)}) collective-permute-start(f32[256,256]{1,0:T(8,128)} %get-tuple-element.28), channel_id=1, source_target_pairs={{2,0},{4,2},{6,4},{8,6},{10,8},{12,10},{14,12},{16,14},{18,16},{20... | collective-permute-start | bytes 786440 | tf_op jit(solution)/shard_map/ppermute | solution.py:252
  14.2 41.3 %collective-permute-start.9 = (f32[256,256]{1,0:T(8,128)}, f32[256,256]{1,0:T(8,128)}, u32[]{:S(2)}, u32[]{:S(2)}) collective-permute-start(f32[256,256]{1,0:T(8,128)} %get-tuple-element.27), channel_id=1, source_target_pairs={{0,2},{2,4},{4,6},{6,8},{8,10},{10,12},{12,14},{14,16},{16,18},{18... | collective-permute-start | bytes 786440 | tf_op jit(solution)/shard_map/ppermute | solution.py:252
  23.3 3.4 %copy-start = (f32[16,256,512]{2,1,0:T(8,128)S(1)}, f32[16,256,512]{2,1,0:T(8,128)}, u32[]{:S(2)}) copy-start(f32[16,256,512]{2,1,0:T(8,128)} %refs_0_.5) | copy-start | bytes 25165828
  44.9 0.7 copy-start.6
  45.6 0.7 copy-start.8
  46.3 0.9 copy-start.7
  47.3 0.9 copy-start.9
  55.5 21.5 %copy-start.1 = (f32[6,4,16,256]{3,2,1,0:T(8,128)}, f32[6,4,16,256]{3,2,1,0:T(8,128)S(1)}, u32[]{:S(2)}) copy-start(f32[6,4,16,256]{3,2,1,0:T(8,128)S(1)} %get-tuple-element.14) | copy-start | bytes 1179652
  77.0 0.7 copy-start.2
  77.7 0.7 copy-start.4
  77.7 5.9 %copy-start.3 = (f32[6,4,16,256]{3,2,1,0:T(8,128)S(1)}, f32[6,4,16,256]{3,2,1,0:T(8,128)}, u32[]{:S(2)}) copy-start(f32[6,4,16,256]{3,2,1,0:T(8,128)} %copy-done.2) | copy-start | bytes 1179652
  78.5 22.3 %collective-permute-start.12 = (f32[6,4,16,256]{3,2,0,1:T(8,128)S(1)}, f32[6,4,16,256]{3,2,0,1:T(8,128)}, u32[]{:S(2)}, u32[]{:S(2)}) collective-permute-start(f32[6,4,16,256]{3,2,0,1:T(8,128)S(1)} %copy.11), channel_id=1, source_target_pairs={{0,4},{2,6},{4,0},{6,2},{8,12},{10,14},{12,8},{14,10},{16,20},{18,... | collective-permute-start | bytes 1179656 | tf_op jit(solution)/shard_map/ppermute | solution.py:280
  80.7 22.4 %collective-permute-start.11 = (f32[6,4,16,256]{3,2,1,0:T(8,128)}, f32[6,4,16,256]{3,2,1,0:T(8,128)S(1)}, u32[]{:S(2)}, u32[]{:S(2)}) collective-permute-start(f32[6,4,16,256]{3,2,1,0:T(8,128)} %get-tuple-element.20), channel_id=1, source_target_pairs={{0,6},{2,4},{4,2},{6,0},{8,14},{10,12},{12,10},{14,8},{16,22},{18,... | collective-permute-start | bytes 1179656 | tf_op jit(solution)/shard_map/ppermute | solution.py:280
  83.6 20.6 %copy-start.5 = (f32[6,4,16,256]{3,2,1,0:T(8,128)S(1)}, f32[6,4,16,256]{3,2,1,0:T(8,128)}, u32[]{:S(2)}) copy-start(f32[6,4,16,256]{3,2,1,0:T(8,128)} %copy-done.4) | copy-start | bytes 1179652
  83.7 20.5 %collective-permute-start.13 = (f32[6,4,16,256]{3,2,0,1:T(8,128)S(1)}, f32[6,4,16,256]{3,2,0,1:T(8,128)S(1)}, u32[]{:S(2)}, u32[]{:S(2)}) collective-permute-start(f32[6,4,16,256]{3,2,0,1:T(8,128)S(1)} %copy.13), channel_id=1, source_target_pairs={{0,2},{2,0},{4,6},{6,4},{8,10},{10,8},{12,14},{14,12},{16,18},{18,... | collective-permute-start | bytes 1179656 | tf_op jit(solution)/shard_map/ppermute | solution.py:280
  84.3 28.5 %collective-permute-start.3 = (f32[6,4,16,256]{3,2,0,1:T(8,128)S(1)}, f32[6,4,16,256]{3,2,0,1:T(8,128)S(1)}, u32[]{:S(2)}, u32[]{:S(2)}) collective-permute-start(f32[6,4,16,256]{3,2,0,1:T(8,128)S(1)} %copy.5), channel_id=1, source_target_pairs={{0,6},{2,4},{4,2},{6,0},{8,14},{10,12},{12,10},{14,8},{16,22},{18,... | collective-permute-start | bytes 1179656 | tf_op jit(solution)/shard_map/ppermute | solution.py:280
  87.2 27.0 %collective-permute-start.4 = (f32[6,4,16,256]{3,2,0,1:T(8,128)S(1)}, f32[6,4,16,256]{3,2,0,1:T(8,128)S(1)}, u32[]{:S(2)}, u32[]{:S(2)}) collective-permute-start(f32[6,4,16,256]{3,2,0,1:T(8,128)S(1)} %copy.6), channel_id=1, source_target_pairs={{0,4},{2,6},{4,0},{6,2},{8,12},{10,14},{12,8},{14,10},{16,20},{18,... | collective-permute-start | bytes 1179656 | tf_op jit(solution)/shard_map/ppermute | solution.py:280
  100.7 15.9 %collective-permute-start.5 = (f32[6,4,16,256]{3,2,0,1:T(8,128)S(1)}, f32[6,4,16,256]{3,2,0,1:T(8,128)S(1)}, u32[]{:S(2)}, u32[]{:S(2)}) collective-permute-start(f32[6,4,16,256]{3,2,0,1:T(8,128)S(1)} %copy.7), channel_id=1, source_target_pairs={{0,2},{2,0},{4,6},{6,4},{8,10},{10,8},{12,14},{14,12},{16,18},{18,... | collective-permute-start | bytes 1179656 | tf_op jit(solution)/shard_map/ppermute | solution.py:280
  105.4 15.3 %collective-permute-start.14 = (f32[6,1,16,256]{3,2,0,1:T(8,128)S(1)}, f32[6,1,16,256]{3,2,0,1:T(8,128)S(1)}, u32[]{:S(2)}, u32[]{:S(2)}) collective-permute-start(f32[6,1,16,256]{3,2,0,1:T(8,128)S(1)} %get-tuple-element.39), channel_id=1, source_target_pairs={{0,24},{2,26},{4,28},{6,30},{8,16},{10,18},{12,20},{14,22},{16,8},... | collective-permute-start | bytes 294920 | tf_op jit(solution)/shard_map/ppermute | solution.py:280
  112.8 8.5 %collective-permute-start.15 = (f32[6,1,16,256]{3,2,0,1:T(8,128)S(1)}, f32[6,1,16,256]{3,2,0,1:T(8,128)S(1)}, u32[]{:S(2)}, u32[]{:S(2)}) collective-permute-start(f32[6,1,16,256]{3,2,0,1:T(8,128)S(1)} %get-tuple-element.40), channel_id=1, source_target_pairs={{0,16},{2,18},{4,20},{6,22},{8,24},{10,26},{12,28},{14,30},{16,0},... | collective-permute-start | bytes 294920 | tf_op jit(solution)/shard_map/ppermute | solution.py:280
  112.8 8.5 %collective-permute-start.16 = (f32[6,1,16,256]{3,2,0,1:T(8,128)S(1)}, f32[6,1,16,256]{3,2,0,1:T(8,128)S(1)}, u32[]{:S(2)}, u32[]{:S(2)}) collective-permute-start(f32[6,1,16,256]{3,2,0,1:T(8,128)S(1)} %get-tuple-element.41), channel_id=1, source_target_pairs={{0,8},{2,10},{4,12},{6,14},{8,0},{10,2},{12,4},{14,6},{16,24},{18,... | collective-permute-start | bytes 294920 | tf_op jit(solution)/shard_map/ppermute | solution.py:280
  116.9 7.0 %collective-permute-start.6 = (f32[6,1,16,256]{3,2,0,1:T(8,128)S(1)}, f32[6,1,16,256]{3,2,0,1:T(8,128)S(1)}, u32[]{:S(2)}, u32[]{:S(2)}) collective-permute-start(f32[6,1,16,256]{3,2,0,1:T(8,128)S(1)} %get-tuple-element.35), channel_id=1, source_target_pairs={{0,24},{2,26},{4,28},{6,30},{8,16},{10,18},{12,20},{14,22},{16,8},... | collective-permute-start | bytes 294920 | tf_op jit(solution)/shard_map/ppermute | solution.py:280
  120.7 6.5 %collective-permute-start.7 = (f32[6,1,16,256]{3,2,0,1:T(8,128)S(1)}, f32[6,1,16,256]{3,2,0,1:T(8,128)S(1)}, u32[]{:S(2)}, u32[]{:S(2)}) collective-permute-start(f32[6,1,16,256]{3,2,0,1:T(8,128)S(1)} %get-tuple-element.36), channel_id=1, source_target_pairs={{0,16},{2,18},{4,20},{6,22},{8,24},{10,26},{12,28},{14,30},{16,0},... | collective-permute-start | bytes 294920 | tf_op jit(solution)/shard_map/ppermute | solution.py:280
  120.7 6.5 %collective-permute-start.8 = (f32[6,1,16,256]{3,2,0,1:T(8,128)S(1)}, f32[6,1,16,256]{3,2,0,1:T(8,128)S(1)}, u32[]{:S(2)}, u32[]{:S(2)}) collective-permute-start(f32[6,1,16,256]{3,2,0,1:T(8,128)S(1)} %get-tuple-element.37), channel_id=1, source_target_pairs={{0,8},{2,10},{4,12},{6,14},{8,0},{10,2},{12,4},{14,6},{16,24},{18,... | collective-permute-start | bytes 294920 | tf_op jit(solution)/shard_map/ppermute | solution.py:280

commit v5 on v4

v5 whole, which is shorter than its diff:
```python
import functools

import jax
import jax.numpy as jnp
from jax import lax
from jax.experimental import pallas as pl
from jax.experimental.pallas import tpu as pltpu
from jax.sharding import PartitionSpec as P

LIGHT_DIR = (0.2672612, 0.5345225, 0.8017837)
LANES = 128
SUBLANES = 8
PAD = 8
WORD_SCALE = 2.0**31 - 2.0**17
HALF = 65536


def prepare_tables(emission, absorption, depth_total, table, words, factors):
    breaks = emission.shape[1]
    table[...] = jnp.zeros(table.shape, jnp.float32)
    table[0:3, 0:breaks] = emission[...]
    table[3:6, 0:breaks] = absorption[...]
    values = table[...]
    largest = [jnp.maximum(jnp.max(ref[...]), 1e-30) for ref in (emission, absorption)]
    row = lax.broadcasted_iota(jnp.int32, table.shape, 0)
    lane = lax.broadcasted_iota(jnp.int32, table.shape, 1)
    scaled = values * (WORD_SCALE / jnp.where(row < 3, largest[0], largest[1]))
    following = jnp.where(lane < breaks - 1, pltpu.roll(scaled, LANES - 1, 1), scaled)
    rise = jnp.floor((following - scaled) * (1.0 / HALF) + 0.5)
    upper = jnp.floor((0.5 * (following + scaled) - rise) * (1.0 / HALF) + 0.5)
    word = upper.astype(jnp.int32) * HALF + rise.astype(jnp.int32)
    units = [largest[0] / WORD_SCALE, largest[1] * (4.0 / depth_total) / WORD_SCALE]
    constants = [0.9 * part * units[0] for part in LIGHT_DIR]
    constants += [0.1 * units[0], units[1], 0.75 * units[1]]
    for k in range(6):
        words[k] = jnp.broadcast_to(word[k : k + 1, :], (SUBLANES, LANES))
        factors[k] = jnp.full((SUBLANES, LANES), constants[k], jnp.float32)


def lookup(table, index):
    return lax.gather(
        table,
        index.reshape(index.shape + (1,)),
        lax.GatherDimensionNumbers(
            offset_dims=(),
            collapsed_slice_dims=(1,),
            start_index_map=(1,),
            operand_batching_dims=(0,),
            start_indices_batching_dims=(0,),
        ),
        slice_sizes=(1, 1),
        mode=lax.GatherScatterMode.PROMISE_IN_BOUNDS,
    )


def march_kernel(mode, chunk, depth_total, group, emission, absorption, *refs):
    refs = list(refs)
    field = refs.pop(0)
    planes, height, width = field.shape
    all_tiles = width // LANES
    near = sorted({tile + k for tile in chunk for k in (-1, 0, 1)})
    side = refs.pop(0) if near[0] < 0 or near[-1] >= all_tiles else None
    low, high = (refs.pop(0), refs.pop(0)) if mode != "middle" else (None, None)
    middle = refs.pop(0) if mode == "rim" else None
    inner = refs.pop() if mode == "rim" else None
    cells, canvas, table, words, factors, in_sems, out_sems = refs[-7:]
    outs = refs[:-7]
    scale = 0.5 * (emission.shape[1] - 1)
    slot_of = {tile: slot for slot, tile in enumerate(near)}
    body_rows = pl.ds(PAD, height)
    tile_index = lax.axis_index("tile")
    if mode == "full":
        blocks, marched = [(0, 1, planes)], range(planes)
    elif mode == "middle":
        blocks, marched = [(0, 1, planes)], range(1, planes - 1)
    else:
        blocks, marched = [(0, 1, 2), (planes - 2, 3, 2)], (0, planes - 1)
    place = {first + k: slot + k for first, slot, count in blocks for k in range(count)}
    place[-1] = 0
    place[planes] = max(place.values()) + 1

    def columns(tile):
        return pl.ds(tile * LANES, LANES)

    def incoming(tile):
        slot = slot_of[tile]
        copies = []
        for number, (first, where, count) in enumerate(blocks):
            if 0 <= tile < all_tiles:
                source = field.at[pl.ds(first, count), :, columns(tile)]
            else:
                source = side.at[pl.ds(first, count)]
            target = cells.at[slot, pl.ds(where, count), body_rows, :]
            copies.append(pltpu.make_async_copy(source, target, in_sems.at[slot, number]))
        if mode != "middle" and tile in chunk:
            for number, (halo, plane) in enumerate(((low, -1), (high, planes))):
                target = cells.at[slot, place[plane], body_rows, :]
                source = halo.at[:, columns(tile)]
                copies.append(pltpu.make_async_copy(source, target, in_sems.at[slot, 2 + number]))
        if mode == "rim" and tile in chunk:
            at = chunk.index(tile)
            copies.append(
                pltpu.make_async_copy(
                    middle.at[:, :, columns(at)], inner.at[at], in_sems.at[slot, 4]
                )
            )
        return copies

    def outgoing(at):
        if len(outs) == 1:
            target = outs[0].at[:, :, columns(at)]
            return [pltpu.make_async_copy(canvas.at[at], target, out_sems.at[at, 0])]
        own = lax.axis_index("slab") & (group - 1)
        return [
            pltpu.make_async_copy(
                canvas.at[at, :, own ^ change],
                outs[change].at[:, :, :, columns(at)],
                out_sems.at[at, change],
            )
            for change in range(group)
        ]

    for tile in near:
        for copy in incoming(tile):
            copy.start()
    prepare_tables(emission, absorption, depth_total, table, words, factors)
    zeros = jnp.zeros((1, LANES), jnp.float32)
    for tile in chunk:
        for plane in marched:
            cells[slot_of[tile], place[plane], pl.ds(PAD - 1, 1), :] = zeros
            cells[slot_of[tile], place[plane], pl.ds(PAD + height, 1), :] = zeros
    lane = lax.broadcasted_iota(jnp.int32, (SUBLANES, LANES), 1)
    first_lane = lane == 0
    last_lane = lane == LANES - 1
    has_left = (tile_index > 0).astype(jnp.float32)
    has_right = (tile_index < lax.axis_size("tile") - 1).astype(jnp.float32)

    def strip(at, row):
        tile = chunk[at]

        def rows(of, plane, offset=0):
            start = PAD + row * SUBLANES + offset
            return cells[slot_of[of], place[plane], pl.ds(start, SUBLANES), :]

        colour = transmit = None
        for plane in marched:
            before, centre, after = (rows(tile, plane + k) for k in (-1, 0, 1))
            left_tile = rows(tile - 1, plane)
            right_tile = rows(tile + 1, plane)
            if tile == 0:
                left_tile = left_tile * has_left
            if tile == all_tiles - 1:
                right_tile = right_tile * has_right
            left = pltpu.roll(jnp.where(last_lane, left_tile, centre), 1, 1)
            right = pltpu.roll(jnp.where(first_lane, right_tile, centre), LANES - 1, 1)
            diff_x = right - left
            diff_y = rows(tile, plane, 1) - rows(tile, plane, -1)
            diff_z = after - before
            inverse = lax.rsqrt(diff_x * diff_x + diff_y * diff_y + diff_z * diff_z + 1.0)
            facing = (factors[0] * diff_x + factors[1] * diff_y + factors[2] * diff_z) * inverse
            shading = jnp.maximum(facing, 0.0) + factors[3]
            weight = factors[4] - factors[5] * (inverse * inverse)
            middle_based = centre * scale + (scale - 0.5)
            interval = (middle_based + 0.5).astype(jnp.int32)
            offset = middle_based - interval.astype(jnp.float32)
            values = []
            for k in range(6):
                word = lookup(words[k], interval)
                rise = lax.shift_left(word, 16).astype(jnp.float32)
                values.append(word.astype(jnp.float32) + rise * offset)
            steps = [values[3 + ch] * weight for ch in range(3)]
            glows = [values[ch] * shading for ch in range(3)]
            if colour is None:
                colour = [step * glow for step, glow in zip(steps, glows)]
                transmit = [1.0 - step for step in steps]
            else:
                seen = [transmit[ch] * steps[ch] for ch in range(3)]
                colour = [colour[ch] + seen[ch] * glows[ch] for ch in range(3)]
                transmit = [transmit[ch] - seen[ch] for ch in range(3)]
            if mode == "rim" and plane == 0:
                here = pl.ds(row * SUBLANES, SUBLANES)
                held = [inner[at, k, here, :] for k in range(6)]
                colour = [colour[ch] + transmit[ch] * held[ch] for ch in range(3)]
                transmit = [transmit[ch] * held[3 + ch] for ch in range(3)]
        for k, value in enumerate(colour + transmit):
            if len(outs) == 1:
                canvas[at, k, pl.ds(row * SUBLANES, SUBLANES), :] = value
            else:
                block_rows = canvas.shape[4]
                block = (row * SUBLANES) // block_rows
                start = pl.multiple_of((row * SUBLANES) % block_rows, SUBLANES)
                canvas[at, block // group, block % group, k, pl.ds(start, SUBLANES), :] = value

    arrived = set()
    for at, tile in enumerate(chunk):
        for other in (tile - 1, tile, tile + 1):
            if other not in arrived:
                for copy in incoming(other):
                    copy.wait()
                arrived.add(other)

        @pl.loop(0, height // SUBLANES, unroll=4 if mode == "rim" else 2)
        def _(row):
            strip(at, row)

        for copy in outgoing(at):
            copy.start()
    for at in range(len(chunk)):
        for copy in outgoing(at):
            copy.wait()


def march(mode, chunk, tables, field, side, halos, middle, depth_total, part_shape):
    planes, height, width = field.shape
    tiles = len(chunk)
    near = {tile + k for tile in chunk for k in (-1, 0, 1)}
    extent = tiles * LANES
    held = 6 if mode == "rim" else planes + 2
    if part_shape is None:
        group = 1
        outs = [jax.ShapeDtypeStruct((6, height, extent), jnp.float32)]
        canvas = (tiles, 6, height, LANES)
    else:
        outer, group, rows = part_shape
        outs = [jax.ShapeDtypeStruct((outer, 6, rows, extent), jnp.float32)] * group
        canvas = (tiles, outer, group, 6, rows, LANES)
    scratch = [
        pltpu.VMEM((len(near), held, height + 2 * PAD, LANES), jnp.float32),
        pltpu.VMEM(canvas, jnp.float32),
        pltpu.VMEM((SUBLANES, LANES), jnp.float32),
        pltpu.VMEM((6, SUBLANES, LANES), jnp.int32),
        pltpu.VMEM((6, SUBLANES, LANES), jnp.float32),
        pltpu.SemaphoreType.DMA((len(near), 5)),
        pltpu.SemaphoreType.DMA((tiles, group)),
    ]
    operands = [field]
    if min(near) < 0 or max(near) >= width // LANES:
        operands.append(side)
    if mode != "middle":
        operands += list(halos)
    if mode == "rim":
        operands.append(middle)
        scratch.append(pltpu.VMEM((tiles, 6, height, LANES), jnp.float32))
    marched = {"full": planes, "middle": planes - 2, "rim": 4}[mode]
    weight = 100 if mode == "middle" else 20000
    far = pl.BlockSpec(memory_space=pltpu.HBM)
    out = pl.pallas_call(
        functools.partial(march_kernel, mode, chunk, depth_total, group),
        out_shape=outs,
        in_specs=[pl.BlockSpec(memory_space=pltpu.VMEM)] * 2 + [far] * len(operands),
        out_specs=[far] * len(outs),
        scratch_shapes=scratch,
        compiler_params=pltpu.CompilerParams(vmem_limit_bytes=60 * 1024 * 1024),
        cost_estimate=pl.CostEstimate(
            flops=marched * height * extent * weight,
            bytes_accessed=marched * height * extent * 5,
            transcendentals=0,
        ),
        name=f"march_{mode}_{chunk[0]}",
    )(*tables, *operands)
    return out[0] if part_shape is None else out


def plane_halos(first, last):
    count = lax.axis_size("slab")
    forward = [(i, i + 1) for i in range(count - 1)]
    backward = [(i + 1, i) for i in range(count - 1)]
    return lax.ppermute(last, "slab", forward), lax.ppermute(first, "slab", backward)


def edge_tile(field, earlier):
    first = lax.axis_index("tile") == 0
    planes, height, width = field.shape
    start, _ = lax.optimization_barrier((jnp.where(first, width - LANES, 0), earlier))
    own = lax.dynamic_slice_in_dim(field, start, LANES, axis=2)
    return lax.ppermute(own, "tile", [(0, 1), (1, 0)])


def ordered(is_far, own, other):
    near = [jnp.where(is_far, b, a) for a, b in zip(own, other)]
    far = [jnp.where(is_far, a, b) for a, b in zip(own, other)]
    return [near[0] + near[1] * far[0], near[1] * far[1]]


def exchange(parts, own, shift):
    count = lax.axis_size("slab")
    merged = []
    for change, part in enumerate(parts):
        if change:
            part = lax.ppermute(part, "slab", [(i, i ^ change << shift) for i in range(count)])
        merged.append([part[:, :3], part[:, 3:]])
    digit = 0
    while len(merged) > 1:
        is_far = (own >> digit & 1) == 1
        merged = [ordered(is_far, merged[k], merged[k + 1]) for k in range(0, len(merged), 2)]
        digit += 1
    return merged[0]


def reduce_image(image, parts, slab_index, block_rows):
    slab_count = lax.axis_size("slab")
    levels = slab_count.bit_length() - 1
    if parts is None:
        image = image.reshape((6, slab_count, block_rows, image.shape[-1]))
        image = jnp.swapaxes(image, 0, 1)
    for shift in range(0, levels, 2):
        size = 1 << min(2, levels - shift)
        own = (slab_index >> shift) & (size - 1)
        if parts is None:
            image = image.reshape((-1, size) + image.shape[1:])
            parts = [
                lax.dynamic_index_in_dim(image, own ^ change, 1, keepdims=False)
                for change in range(size)
            ]
        colour, transmit = exchange(parts, own, shift)
        image, parts = jnp.concatenate([colour, transmit], axis=1), None
    return colour[0], 1.0 - transmit[0]


def per_device(field, tf_emission, tf_absorption):
    slab_count = lax.axis_size("slab")
    slab_index = lax.axis_index("slab")
    planes, height, width = field.shape
    depth_total = planes * slab_count
    block_rows = height // slab_count
    tiles = width // LANES
    part_shape = None
    if slab_count >= 4 and block_rows % SUBLANES == 0:
        part_shape = (slab_count // 4, 4, block_rows)
    chunks = [tuple(range(1, tiles - 1)), (0, tiles - 1)]
    tables = (tf_emission, tf_absorption)

    halo = plane_halos(field[0], field[-1])
    results = []
    for number, chunk in enumerate(chunks):
        if number == 0:
            middle = march(
                "middle", chunk, tables, field, None, None, None, depth_total, None
            )
            mode, side = "rim", None
        else:
            side = edge_tile(field, (halo, middle))
            halo, side, _ = lax.optimization_barrier((halo, side, out))
            middle, mode = None, "full"
        out = march(mode, chunk, tables, field, side, halo, middle, depth_total, part_shape)
        image, parts = (out, None) if part_shape is None else (None, out)
        results.append(reduce_image(image, parts, slab_index, block_rows))
    gathered = []
    for inner, outer in zip(*results):
        gathered.append(
            jnp.concatenate([outer[:, :, :LANES], inner, outer[:, :, LANES:]], axis=2)
        )
    return tuple(gathered)


def solution(mesh):
    placed = (P("slab", None, "tile"), P(), P())
    return jax.shard_map(
        per_device,
        mesh=mesh,
        in_specs=placed,
        out_specs=(P(None, "slab", "tile"), P(None, "slab", "tile")),
        check_vma=False,
    )
```

time: 129 us -> 98.1 us (0.76)
  starting transfers between devices: 36.4 us -> 22.8 us
  local copies, waits for them, and re-layouts: 15.3 us -> 3.68 us
  other arithmetic: 5.29 us -> 1.84 us
  between operations: 2.28 us -> 0.78 us
    unnamed x24 -> x8, local copies, waits for them, and re-layouts: 8.13 us -> 0.02 us
    ppermute x12, starting transfers between devices: 22.6 us -> 16.6 us  [exchange(): lax.ppermute(part, 'slab', [(i, i ^ change << shift) for i in range(count)])]
    ppermute x2 -> x1, starting transfers between devices: 10.1 us -> 4.88 us  [plane_halos(): lax.ppermute(last, 'slab', forward)]
    ppermute x12, waiting for transfers between devices: 22.5 us -> 17.7 us  [exchange(): lax.ppermute(part, 'slab', [(i, i ^ change << shift) for i in range(count)])]
    ppermute x2 -> x1, waiting for transfers between devices: 0.01 us -> 1.94 us  [plane_halos(): lax.ppermute(first, 'slab', backward)]
    ppermute x2 -> x1, waiting for transfers between devices: 0.01 us -> 1.86 us  [plane_halos(): lax.ppermute(last, 'slab', forward)]
    ppermute x2 -> x1, starting transfers between devices: 2.58 us -> 1.29 us  [plane_halos(): lax.ppermute(first, 'slab', backward)]
  transfers between devices with their start and end apart: 17 -> 15, of which waited for: 5 -> 6; matrix products, arithmetic and copies ran while one was open for 4% -> 1% of each run, Pallas kernels for 20% -> 48%
where the time goes in v5:
time: 98.1 us; the launch traced here: 97.8 us
  Pallas kernels  47.1 us (48%)
  starting transfers between devices  22.8 us (23%)
  waiting for transfers between devices  21.5 us (22%)
  local copies, waits for them, and re-layouts  3.68 us (4%)
  other arithmetic  1.84 us (2%)
    pallas_call x3, Pallas kernels, march(): pl.pallas_call(functools.partial(march_kernel, mode, chunk, depth_total,...  47.1 us
    ppermute x12, waiting for transfers between devices, exchange(): lax.ppermute(part, 'slab', [(i, i ^ change << shift) for i in range(count)])  17.7 us
    ppermute x12, starting transfers between devices, exchange(): lax.ppermute(part, 'slab', [(i, i ^ change << shift) for i in range(count)])  16.6 us
    ppermute x1, starting transfers between devices, plane_halos(): lax.ppermute(last, 'slab', forward)  4.88 us
    dynamic_slice x1, local copies, waits for them, and re-layouts, edge_tile(): own = lax.dynamic_slice_in_dim(field, start, LANES, axis=2)  2.38 us
  transfers between devices with their start and end apart: 15, of which 6 were waited for; matrix products, arithmetic and copies ran while one was open for 1% of the time, Pallas kernels for 48%

profile of v5, /device:TPU:0, one launch (start us, length us, event | category | flops | bytes accessed | tf_op | source)
XLA Modules:
  0.0 97.8 jit_solution(13802403717499037806)
XLA Ops:
  0.6 1.3 %slice_bitcast_fusion = (f32[256,512]{1,0:T(8,128)S(1)}, f32[256,512]{1,0:T(8,128)S(1)}) fusion(f32[16,256,512]{2,1,0:T(8,128)} %refs_0_.5), kind=kLoop, calls=%fused_computation.16 | loop fusion | bytes 2097152 | tf_op jit(solution)/shard_map/squeeze | solution.py:333
  1.9 4.9 %collective-permute-start = (f32[256,512]{1,0:T(8,128)S(1)}, f32[256,512]{1,0:T(8,128)S(1)}, u32[]{:S(2)}, u32[]{:S(2)}) collective-permute-start(f32[256,512]{1,0:T(8,128)S(1)} %get-tuple-element.27), channel_id=1, source_target_pairs={{0,2},{2,4},{4,6},{6,8},{8,10},{10,12},{12,14},{14,16},{16,18},{18... | collective-permute-start | bytes 1572872 | tf_op jit(solution)/shard_map/ppermute | solution.py:268
  6.8 1.3 %collective-permute-start.1 = (f32[256,512]{1,0:T(8,128)S(1)}, f32[256,512]{1,0:T(8,128)S(1)}, u32[]{:S(2)}, u32[]{:S(2)}) collective-permute-start(f32[256,512]{1,0:T(8,128)S(1)} %get-tuple-element.26), channel_id=1, source_target_pairs={{2,0},{4,2},{6,4},{8,6},{10,8},{12,10},{14,12},{16,14},{18,16},{20... | collective-permute-start | bytes 1572872 | tf_op jit(solution)/shard_map/ppermute | solution.py:268
  8.1 19.2 %march_middle_1.1.refs_3_ = f32[6,256,256]{2,1,0:T(8,128)} custom-call(f32[3,16]{1,0:T(4,128)} %emission.5, f32[3,16]{1,0:T(4,128)} %absorption.5, f32[16,256,512]{2,1,0:T(8,128)} %refs_0_.5), custom_call_target="tpu_custom_call" | custom-call | flops 91750400 | bytes 4587520 | tf_op jit(solution)/shard_map/march_middle_1/pallas_call | solution.py:247
  27.3 1.9 %collective-permute-done.refs_1_.refs_2_ = f32[256,512]{1,0:T(8,128)S(1)} collective-permute-done((f32[256,512]{1,0:T(8,128)S(1)}, f32[256,512]{1,0:T(8,128)S(1)}, u32[]{:S(2)}, u32[]{:S(2)}) %collective-permute-start) | collective-permute-done | bytes 524320 | tf_op jit(solution)/shard_map/ppermute | solution.py:268
  29.2 0.0 copy-start.2
  29.2 1.9 %collective-permute-done.1.refs_2_.refs_3_ = f32[256,512]{1,0:T(8,128)S(1)} collective-permute-done((f32[256,512]{1,0:T(8,128)S(1)}, f32[256,512]{1,0:T(8,128)S(1)}, u32[]{:S(2)}, u32[]{:S(2)}) %collective-permute-start.1) | collective-permute-done | bytes 524320 | tf_op jit(solution)/shard_map/ppermute | solution.py:268
  31.1 0.0 copy-start.3
  31.1 2.4 %constant_dynamic-slice_fusion = f32[16,256,128]{2,1,0:T(8,128)S(1)} fusion(f32[16,256,512]{2,1,0:T(8,128)} %refs_0_.5, s32[]{:T(128)S(6)} %select_n.233), kind=kLoop, calls=%fused_computation.56 | loop fusion | bytes 4194308 | tf_op jit(solution)/shard_map/dynamic_slice | solution.py:275
  33.5 0.0 copy-done.2
  33.5 0.0 copy-done.3
  33.5 0.1 collective-permute-start.2
  33.6 6.9 %march_rim_1.1 = (f32[4,6,16,256]{3,2,1,0:T(8,128)}, f32[4,6,16,256]{3,2,1,0:T(8,128)}, f32[4,6,16,256]{3,2,1,0:T(8,128)}, f32[4,6,16,256]{3,2,1,0:T(8,128)}) custom-call(f32[3,16]{1,0:T(4,128)} %emission.5, f32[3,16]{1,0:T(4,128)} %absorption.5, f32[16,256,512]{2,1,0:T(8,128)} %refs_0_.5, f32[256,512]{1,0:T(8,128)} %copy-done.2, f32[256,512]{1,0:T(8,128)} %copy-done.3, ...), custom_call_target="tpu_custom_call" | custom-call | flops 5242880000 | bytes 1310720 | tf_op jit(solution)/shard_map/march_rim_1/pallas_call | solution.py:247
  40.5 0.1 collective-permute-start.10
  40.6 2.9 %collective-permute-start.9 = (f32[4,6,16,256]{3,2,1,0:T(8,128)}, f32[4,6,16,256]{3,2,1,0:T(8,128)S(1)}, u32[]{:S(2)}, u32[]{:S(2)}) collective-permute-start(f32[4,6,16,256]{3,2,1,0:T(8,128)} %get-tuple-element.18), channel_id=1, source_target_pairs={{0,6},{2,4},{4,2},{6,0},{8,14},{10,12},{12,10},{14,8},{16,22},{18,... | collective-permute-start | bytes 1179656 | tf_op jit(solution)/shard_map/ppermute | solution.py:290
  43.5 0.5 collective-permute-start.11
  44.0 0.0 collective-permute-done.2.refs_1_
  44.0 0.0 copy-start.1
  44.0 21.0 %march_full_0.1 = (f32[4,6,16,256]{3,2,1,0:T(8,128)}, f32[4,6,16,256]{3,2,1,0:T(8,128)}, f32[4,6,16,256]{3,2,1,0:T(8,128)}, f32[4,6,16,256]{3,2,1,0:T(8,128)}) custom-call(f32[3,16]{1,0:T(4,128)} %emission.5, f32[3,16]{1,0:T(4,128)} %absorption.5, f32[16,256,512]{2,1,0:T(8,128)} %refs_0_.5, f32[16,256,128]{2,1,0:T(8,128)} %collective-permute-done.2.refs_1_, ...), custom_call_target="tpu_custom_call" | custom-call | flops 20971520000 | bytes 5242880 | tf_op jit(solution)/shard_map/march_full_0/pallas_call | solution.py:247
  65.1 0.0 copy-start
  65.1 0.1 collective-permute-start.4
  65.2 2.9 %collective-permute-start.3 = (f32[4,6,16,256]{3,2,1,0:T(8,128)}, f32[4,6,16,256]{3,2,1,0:T(8,128)S(1)}, u32[]{:S(2)}, u32[]{:S(2)}) collective-permute-start(f32[4,6,16,256]{3,2,1,0:T(8,128)} %get-tuple-element.22), channel_id=1, source_target_pairs={{0,6},{2,4},{4,2},{6,0},{8,14},{10,12},{12,10},{14,8},{16,22},{18,... | collective-permute-start | bytes 1179656 | tf_op jit(solution)/shard_map/ppermute | solution.py:290
  68.1 0.0 collective-permute-done.10
  68.1 0.5 collective-permute-start.5
  68.7 0.0 collective-permute-done.9
  68.7 0.0 collective-permute-done.11
  68.7 0.0 copy-done.1
  68.7 0.2 select_multiply_fusion
  68.9 2.7 %collective-permute-start.13 = (f32[1,6,16,256]{3,2,1,0:T(8,128)S(1)}, f32[1,6,16,256]{3,2,1,0:T(8,128)S(1)}, u32[]{:S(2)}, u32[]{:S(2)}) collective-permute-start(f32[1,6,16,256]{3,2,1,0:T(8,128)S(1)} %get-tuple-element.37), channel_id=1, source_target_pairs={{0,16},{2,18},{4,20},{6,22},{8,24},{10,26},{12,28},{14,30},{16,0},... | collective-permute-start | bytes 294920 | tf_op jit(solution)/shard_map/ppermute | solution.py:290
  71.6 1.3 %collective-permute-start.12 = (f32[1,6,16,256]{3,2,1,0:T(8,128)S(1)}, f32[1,6,16,256]{3,2,1,0:T(8,128)S(1)}, u32[]{:S(2)}, u32[]{:S(2)}) collective-permute-start(f32[1,6,16,256]{3,2,1,0:T(8,128)S(1)} %get-tuple-element.36), channel_id=1, source_target_pairs={{0,24},{2,26},{4,28},{6,30},{8,16},{10,18},{12,20},{14,22},{16,8},... | collective-permute-start | bytes 294920 | tf_op jit(solution)/shard_map/ppermute | solution.py:290
  73.0 11.5 %collective-permute-done.4 = f32[4,6,16,256]{3,2,1,0:T(8,128)S(1)} collective-permute-done((f32[4,6,16,256]{3,2,1,0:T(8,128)}, f32[4,6,16,256]{3,2,1,0:T(8,128)S(1)}, u32[]{:S(2)}, u32[]{:S(2)}) %collective-permute-start.4) | collective-permute-done | bytes 393248 | tf_op jit(solution)/shard_map/ppermute | solution.py:290
  84.5 1.6 %collective-permute-start.14 = (f32[1,6,16,256]{3,2,1,0:T(8,128)S(1)}, f32[1,6,16,256]{3,2,1,0:T(8,128)S(1)}, u32[]{:S(2)}, u32[]{:S(2)}) collective-permute-start(f32[1,6,16,256]{3,2,1,0:T(8,128)S(1)} %get-tuple-element.38), channel_id=1, source_target_pairs={{0,8},{2,10},{4,12},{6,14},{8,0},{10,2},{12,4},{14,6},{16,24},{18,... | collective-permute-start | bytes 294920 | tf_op jit(solution)/shard_map/ppermute | solution.py:290
  86.0 0.0 collective-permute-done.3
  86.0 0.0 collective-permute-done.5
  86.1 0.0 copy-done
  86.1 0.2 select_multiply_fusion.3
  86.3 2.7 %collective-permute-start.7 = (f32[1,6,16,256]{3,2,1,0:T(8,128)S(1)}, f32[1,6,16,256]{3,2,1,0:T(8,128)S(1)}, u32[]{:S(2)}, u32[]{:S(2)}) collective-permute-start(f32[1,6,16,256]{3,2,1,0:T(8,128)S(1)} %get-tuple-element.41), channel_id=1, source_target_pairs={{0,16},{2,18},{4,20},{6,22},{8,24},{10,26},{12,28},{14,30},{16,0},... | collective-permute-start | bytes 294920 | tf_op jit(solution)/shard_map/ppermute | solution.py:290
  89.0 1.0 %collective-permute-start.6 = (f32[1,6,16,256]{3,2,1,0:T(8,128)S(1)}, f32[1,6,16,256]{3,2,1,0:T(8,128)S(1)}, u32[]{:S(2)}, u32[]{:S(2)}) collective-permute-start(f32[1,6,16,256]{3,2,1,0:T(8,128)S(1)} %get-tuple-element.40), channel_id=1, source_target_pairs={{0,24},{2,26},{4,28},{6,30},{8,16},{10,18},{12,20},{14,22},{16,8},... | collective-permute-start | bytes 294920 | tf_op jit(solution)/shard_map/ppermute | solution.py:290
  89.9 0.0 collective-permute-done.13
  89.9 0.2 collective-permute-start.8
  90.2 0.0 collective-permute-done.12
  90.2 0.0 collective-permute-done.14
  90.2 4.6 %collective-permute-done.7 = f32[1,6,16,256]{3,2,1,0:T(8,128)S(1)} collective-permute-done((f32[1,6,16,256]{3,2,1,0:T(8,128)S(1)}, f32[1,6,16,256]{3,2,1,0:T(8,128)S(1)}, u32[]{:S(2)}, u32[]{:S(2)}) %collective-permute-start.7) | collective-permute-done | bytes 98336 | tf_op jit(solution)/shard_map/ppermute | solution.py:290
  94.8 1.0 %collective-permute-done.6 = f32[1,6,16,256]{3,2,1,0:T(8,128)S(1)} collective-permute-done((f32[1,6,16,256]{3,2,1,0:T(8,128)S(1)}, f32[1,6,16,256]{3,2,1,0:T(8,128)S(1)}, u32[]{:S(2)}, u32[]{:S(2)}) %collective-permute-start.6) | collective-permute-done | bytes 98336 | tf_op jit(solution)/shard_map/ppermute | solution.py:290
  95.9 0.5 collective-permute-done.8
  96.5 0.6 pad_maximum_fusion
  97.1 0.6 pad_maximum_fusion.1
  (5 shorter events, 0.2 us)
Async XLA Ops:
  1.9 27.2 %collective-permute-start = (f32[256,512]{1,0:T(8,128)S(1)}, f32[256,512]{1,0:T(8,128)S(1)}, u32[]{:S(2)}, u32[]{:S(2)}) collective-permute-start(f32[256,512]{1,0:T(8,128)S(1)} %get-tuple-element.27), channel_id=1, source_target_pairs={{0,2},{2,4},{4,6},{6,8},{8,10},{10,12},{12,14},{14,16},{16,18},{18... | collective-permute-start | bytes 1572872 | tf_op jit(solution)/shard_map/ppermute | solution.py:268
  6.8 24.3 %collective-permute-start.1 = (f32[256,512]{1,0:T(8,128)S(1)}, f32[256,512]{1,0:T(8,128)S(1)}, u32[]{:S(2)}, u32[]{:S(2)}) collective-permute-start(f32[256,512]{1,0:T(8,128)S(1)} %get-tuple-element.26), channel_id=1, source_target_pairs={{2,0},{4,2},{6,4},{8,6},{10,8},{12,10},{14,12},{16,14},{18,16},{20... | collective-permute-start | bytes 1572872 | tf_op jit(solution)/shard_map/ppermute | solution.py:268
  29.2 4.3 %copy-start.2 = (f32[256,512]{1,0:T(8,128)}, f32[256,512]{1,0:T(8,128)S(1)}, u32[]{:S(2)}) copy-start(f32[256,512]{1,0:T(8,128)S(1)} %collective-permute-done.refs_1_.refs_2_) | copy-start | bytes 1572868
  31.1 2.4 %copy-start.3 = (f32[256,512]{1,0:T(8,128)}, f32[256,512]{1,0:T(8,128)S(1)}, u32[]{:S(2)}) copy-start(f32[256,512]{1,0:T(8,128)S(1)} %collective-permute-done.1.refs_2_.refs_3_) | copy-start | bytes 1572868
  33.5 10.5 %collective-permute-start.2 = (f32[16,256,128]{2,1,0:T(8,128)S(1)}, f32[16,256,128]{2,1,0:T(8,128)}, u32[]{:S(2)}, u32[]{:S(2)}) collective-permute-start(f32[16,256,128]{2,1,0:T(8,128)S(1)} %constant_dynamic-slice_fusion), channel_id=1, source_target_pairs={{0,1},{1,0},{2,3},{3,2},{4,5},{5,4},{6,7},{7,6},{8,9},{9,8},{10,11... | collective-permute-start | bytes 6291464 | tf_op jit(solution)/shard_map/ppermute | solution.py:276
  40.5 27.6 %collective-permute-start.10 = (f32[4,6,16,256]{3,2,1,0:T(8,128)}, f32[4,6,16,256]{3,2,1,0:T(8,128)S(1)}, u32[]{:S(2)}, u32[]{:S(2)}) collective-permute-start(f32[4,6,16,256]{3,2,1,0:T(8,128)} %get-tuple-element.17), channel_id=1, source_target_pairs={{0,4},{2,6},{4,0},{6,2},{8,12},{10,14},{12,8},{14,10},{16,20},{18,... | collective-permute-start | bytes 1179656 | tf_op jit(solution)/shard_map/ppermute | solution.py:290
  40.6 28.1 %collective-permute-start.9 = (f32[4,6,16,256]{3,2,1,0:T(8,128)}, f32[4,6,16,256]{3,2,1,0:T(8,128)S(1)}, u32[]{:S(2)}, u32[]{:S(2)}) collective-permute-start(f32[4,6,16,256]{3,2,1,0:T(8,128)} %get-tuple-element.18), channel_id=1, source_target_pairs={{0,6},{2,4},{4,2},{6,0},{8,14},{10,12},{12,10},{14,8},{16,22},{18,... | collective-permute-start | bytes 1179656 | tf_op jit(solution)/shard_map/ppermute | solution.py:290
  43.5 25.2 %collective-permute-start.11 = (f32[4,6,16,256]{3,2,1,0:T(8,128)}, f32[4,6,16,256]{3,2,1,0:T(8,128)S(1)}, u32[]{:S(2)}, u32[]{:S(2)}) collective-permute-start(f32[4,6,16,256]{3,2,1,0:T(8,128)} %get-tuple-element.16), channel_id=1, source_target_pairs={{0,2},{2,0},{4,6},{6,4},{8,10},{10,8},{12,14},{14,12},{16,18},{18,... | collective-permute-start | bytes 1179656 | tf_op jit(solution)/shard_map/ppermute | solution.py:290
  44.0 24.6 %copy-start.1 = (f32[4,6,16,256]{3,2,1,0:T(8,128)S(1)}, f32[4,6,16,256]{3,2,1,0:T(8,128)}, u32[]{:S(2)}) copy-start(f32[4,6,16,256]{3,2,1,0:T(8,128)} %get-tuple-element.15) | copy-start | bytes 1179652
  65.1 21.0 %copy-start = (f32[4,6,16,256]{3,2,1,0:T(8,128)S(1)}, f32[4,6,16,256]{3,2,1,0:T(8,128)}, u32[]{:S(2)}) copy-start(f32[4,6,16,256]{3,2,1,0:T(8,128)} %get-tuple-element.25) | copy-start | bytes 1179652
  65.1 19.4 %collective-permute-start.4 = (f32[4,6,16,256]{3,2,1,0:T(8,128)}, f32[4,6,16,256]{3,2,1,0:T(8,128)S(1)}, u32[]{:S(2)}, u32[]{:S(2)}) collective-permute-start(f32[4,6,16,256]{3,2,1,0:T(8,128)} %get-tuple-element.23), channel_id=1, source_target_pairs={{0,4},{2,6},{4,0},{6,2},{8,12},{10,14},{12,8},{14,10},{16,20},{18,... | collective-permute-start | bytes 1179656 | tf_op jit(solution)/shard_map/ppermute | solution.py:290
  65.2 20.8 %collective-permute-start.3 = (f32[4,6,16,256]{3,2,1,0:T(8,128)}, f32[4,6,16,256]{3,2,1,0:T(8,128)S(1)}, u32[]{:S(2)}, u32[]{:S(2)}) collective-permute-start(f32[4,6,16,256]{3,2,1,0:T(8,128)} %get-tuple-element.22), channel_id=1, source_target_pairs={{0,6},{2,4},{4,2},{6,0},{8,14},{10,12},{12,10},{14,8},{16,22},{18,... | collective-permute-start | bytes 1179656 | tf_op jit(solution)/shard_map/ppermute | solution.py:290
  68.1 17.9 %collective-permute-start.5 = (f32[4,6,16,256]{3,2,1,0:T(8,128)}, f32[4,6,16,256]{3,2,1,0:T(8,128)S(1)}, u32[]{:S(2)}, u32[]{:S(2)}) collective-permute-start(f32[4,6,16,256]{3,2,1,0:T(8,128)} %get-tuple-element.24), channel_id=1, source_target_pairs={{0,2},{2,0},{4,6},{6,4},{8,10},{10,8},{12,14},{14,12},{16,18},{18,... | collective-permute-start | bytes 1179656 | tf_op jit(solution)/shard_map/ppermute | solution.py:290
  68.9 21.0 %collective-permute-start.13 = (f32[1,6,16,256]{3,2,1,0:T(8,128)S(1)}, f32[1,6,16,256]{3,2,1,0:T(8,128)S(1)}, u32[]{:S(2)}, u32[]{:S(2)}) collective-permute-start(f32[1,6,16,256]{3,2,1,0:T(8,128)S(1)} %get-tuple-element.37), channel_id=1, source_target_pairs={{0,16},{2,18},{4,20},{6,22},{8,24},{10,26},{12,28},{14,30},{16,0},... | collective-permute-start | bytes 294920 | tf_op jit(solution)/shard_map/ppermute | solution.py:290
  71.6 18.6 %collective-permute-start.12 = (f32[1,6,16,256]{3,2,1,0:T(8,128)S(1)}, f32[1,6,16,256]{3,2,1,0:T(8,128)S(1)}, u32[]{:S(2)}, u32[]{:S(2)}) collective-permute-start(f32[1,6,16,256]{3,2,1,0:T(8,128)S(1)} %get-tuple-element.36), channel_id=1, source_target_pairs={{0,24},{2,26},{4,28},{6,30},{8,16},{10,18},{12,20},{14,22},{16,8},... | collective-permute-start | bytes 294920 | tf_op jit(solution)/shard_map/ppermute | solution.py:290
  84.5 5.7 %collective-permute-start.14 = (f32[1,6,16,256]{3,2,1,0:T(8,128)S(1)}, f32[1,6,16,256]{3,2,1,0:T(8,128)S(1)}, u32[]{:S(2)}, u32[]{:S(2)}) collective-permute-start(f32[1,6,16,256]{3,2,1,0:T(8,128)S(1)} %get-tuple-element.38), channel_id=1, source_target_pairs={{0,8},{2,10},{4,12},{6,14},{8,0},{10,2},{12,4},{14,6},{16,24},{18,... | collective-permute-start | bytes 294920 | tf_op jit(solution)/shard_map/ppermute | solution.py:290
  86.3 8.6 %collective-permute-start.7 = (f32[1,6,16,256]{3,2,1,0:T(8,128)S(1)}, f32[1,6,16,256]{3,2,1,0:T(8,128)S(1)}, u32[]{:S(2)}, u32[]{:S(2)}) collective-permute-start(f32[1,6,16,256]{3,2,1,0:T(8,128)S(1)} %get-tuple-element.41), channel_id=1, source_target_pairs={{0,16},{2,18},{4,20},{6,22},{8,24},{10,26},{12,28},{14,30},{16,0},... | collective-permute-start | bytes 294920 | tf_op jit(solution)/shard_map/ppermute | solution.py:290
  89.0 6.9 %collective-permute-start.6 = (f32[1,6,16,256]{3,2,1,0:T(8,128)S(1)}, f32[1,6,16,256]{3,2,1,0:T(8,128)S(1)}, u32[]{:S(2)}, u32[]{:S(2)}) collective-permute-start(f32[1,6,16,256]{3,2,1,0:T(8,128)S(1)} %get-tuple-element.40), channel_id=1, source_target_pairs={{0,24},{2,26},{4,28},{6,30},{8,16},{10,18},{12,20},{14,22},{16,8},... | collective-permute-start | bytes 294920 | tf_op jit(solution)/shard_map/ppermute | solution.py:290
  89.9 6.5 %collective-permute-start.8 = (f32[1,6,16,256]{3,2,1,0:T(8,128)S(1)}, f32[1,6,16,256]{3,2,1,0:T(8,128)S(1)}, u32[]{:S(2)}, u32[]{:S(2)}) collective-permute-start(f32[1,6,16,256]{3,2,1,0:T(8,128)S(1)} %get-tuple-element.42), channel_id=1, source_target_pairs={{0,8},{2,10},{4,12},{6,14},{8,0},{10,2},{12,4},{14,6},{16,24},{18,... | collective-permute-start | bytes 294920 | tf_op jit(solution)/shard_map/ppermute | solution.py:290

commit v6 on v5

--- a/solution.py
+++ b/solution.py
@@ -63,11 +63,13 @@
     low, high = (refs.pop(0), refs.pop(0)) if mode != "middle" else (None, None)
     middle = refs.pop(0) if mode == "rim" else None
     inner = refs.pop() if mode == "rim" else None
-    cells, canvas, table, words, factors, in_sems, out_sems = refs[-7:]
-    outs = refs[:-7]
+    cells, shifted, canvas, table, words, factors, in_sems, out_sems = refs[-8:]
+    outs = refs[:-8]
+    edge = outs.pop() if mode == "middle" else None
     scale = 0.5 * (emission.shape[1] - 1)
     slot_of = {tile: slot for slot, tile in enumerate(near)}
-    body_rows = pl.ds(PAD, height)
+    piece_rows = height // in_sems.shape[0]
+    pieces = height // piece_rows
     tile_index = lax.axis_index("tile")
     if mode == "full":
         blocks, marched = [(0, 1, planes)], range(planes)
@@ -78,69 +80,104 @@
     place = {first + k: slot + k for first, slot, count in blocks for k in range(count)}
     place[-1] = 0
     place[planes] = max(place.values()) + 1
+    if mode == "rim":
+        shifted_blocks = [(0, 0, 1), (planes - 1, 1, 1)]
+    else:
+        shifted_blocks = [(marched[0], 0, len(marched))]
+    shifted_place = {plane: k for k, plane in enumerate(marched)}
 
     def columns(tile):
         return pl.ds(tile * LANES, LANES)
 
-    def incoming(tile):
-        slot = slot_of[tile]
+    def incoming(piece, below):
+        start = pl.multiple_of(piece * piece_rows, SUBLANES)
+        body = pl.ds(start, piece_rows)
         copies = []
-        for number, (first, where, count) in enumerate(blocks):
-            if 0 <= tile < all_tiles:
-                source = field.at[pl.ds(first, count), :, columns(tile)]
+
+        def copy(source, target):
+            slot = len(copies) + (0 if below else 2 * len(chunk))
+            copies.append(pltpu.make_async_copy(source, target, in_sems.at[piece, slot]))
+
+        if below:
+            for at, tile in enumerate(chunk):
+                for first, where, count in shifted_blocks:
+                    copy(
+                        field.at[pl.ds(first, count), body, columns(tile)],
+                        shifted.at[
+                            1, at, pl.ds(where, count), pl.ds(start + PAD - 1, piece_rows), :
+                        ],
+                    )
+            return copies
+        for tile in near:
+            for first, where, count in blocks:
+                if 0 <= tile < all_tiles:
+                    source = field.at[pl.ds(first, count), body, columns(tile)]
+                else:
+                    source = side.at[pl.ds(first, count), body]
+                copy(source, cells.at[slot_of[tile], pl.ds(where, count), body, :])
+        for at, tile in enumerate(chunk):
+            for first, where, count in shifted_blocks:
+                copy(
+                    field.at[pl.ds(first, count), body, columns(tile)],
+                    shifted.at[0, at, pl.ds(where, count), pl.ds(start + PAD + 1, piece_rows), :],
+                )
+            if mode != "middle":
+                for halo, plane in ((low, -1), (high, planes)):
+                    target = cells.at[slot_of[tile], place[plane], body, :]
+                    copy(halo.at[body, columns(tile)], target)
+            if mode == "rim":
+                copy(middle.at[:, body, columns(at)], inner.at[at, :, body, :])
+        return copies
+
+    def outgoing(piece):
+        body = pl.ds(pl.multiple_of(piece * piece_rows, SUBLANES), piece_rows)
+        copies = []
+        for at in range(len(chunk)):
+            if len(outs) == 1:
+                pairs = [(canvas.at[at, :, body, :], outs[0].at[:, body, columns(at)])]
             else:
-                source = side.at[pl.ds(first, count)]
-            target = cells.at[slot, pl.ds(where, count), body_rows, :]
-            copies.append(pltpu.make_async_copy(source, target, in_sems.at[slot, number]))
-        if mode != "middle" and tile in chunk:
-            for number, (halo, plane) in enumerate(((low, -1), (high, planes))):
-                target = cells.at[slot, place[plane], body_rows, :]
-                source = halo.at[:, columns(tile)]
-                copies.append(pltpu.make_async_copy(source, target, in_sems.at[slot, 2 + number]))
-        if mode == "rim" and tile in chunk:
-            at = chunk.index(tile)
-            copies.append(
-                pltpu.make_async_copy(
-                    middle.at[:, :, columns(at)], inner.at[at], in_sems.at[slot, 4]
-                )
-            )
+                own = lax.axis_index("slab") & (group - 1)
+                pairs = [
+                    (canvas.at[at, piece, own ^ k], outs[k].at[piece, :, :, columns(at)])
+                    for k in range(group)
+                ]
+            for k, (source, target) in enumerate(pairs):
+                copies.append(pltpu.make_async_copy(source, target, out_sems.at[piece, at, k]))
+        if edge is not None:
+            mine = jnp.where(tile_index == 0, slot_of[all_tiles - 1], slot_of[0])
+            source = cells.at[mine, pl.ds(1, planes), body, :]
+            sem = out_sems.at[piece, len(chunk), 0]
+            copies.append(pltpu.make_async_copy(source, edge.at[:, body, :], sem))
         return copies
 
-    def outgoing(at):
-        if len(outs) == 1:
-            target = outs[0].at[:, :, columns(at)]
-            return [pltpu.make_async_copy(canvas.at[at], target, out_sems.at[at, 0])]
-        own = lax.axis_index("slab") & (group - 1)
-        return [
-            pltpu.make_async_copy(
-                canvas.at[at, :, own ^ change],
-                outs[change].at[:, :, :, columns(at)],
-                out_sems.at[at, change],
-            )
-            for change in range(group)
-        ]
-
-    for tile in near:
-        for copy in incoming(tile):
-            copy.start()
+    def start(piece):
+        for below in (False, True):
+            for copy in incoming(piece, below):
+                copy.start()
+
+    start(0)
+    if pieces > 1:
+        start(1)
     prepare_tables(emission, absorption, depth_total, table, words, factors)
-    zeros = jnp.zeros((1, LANES), jnp.float32)
-    for tile in chunk:
-        for plane in marched:
-            cells[slot_of[tile], place[plane], pl.ds(PAD - 1, 1), :] = zeros
-            cells[slot_of[tile], place[plane], pl.ds(PAD + height, 1), :] = zeros
+    zeros = jnp.zeros((len(marched), 1, LANES), jnp.float32)
+    for at in range(len(chunk)):
+        shifted[0, at, :, pl.ds(PAD, 1), :] = zeros
     lane = lax.broadcasted_iota(jnp.int32, (SUBLANES, LANES), 1)
     first_lane = lane == 0
     last_lane = lane == LANES - 1
     has_left = (tile_index > 0).astype(jnp.float32)
     has_right = (tile_index < lax.axis_size("tile") - 1).astype(jnp.float32)
 
-    def strip(at, row):
+    def strip(at, piece, number):
         tile = chunk[at]
-
-        def rows(of, plane, offset=0):
-            start = PAD + row * SUBLANES + offset
-            return cells[slot_of[of], place[plane], pl.ds(start, SUBLANES), :]
+        row = pl.multiple_of(piece * piece_rows + number * SUBLANES, SUBLANES)
+        here = pl.ds(row, SUBLANES)
+
+        def rows(of, plane):
+            return cells[slot_of[of], place[plane], here, :]
+
+        def beside(which, plane):
+            return shifted[which, at, shifted_place[plane], pl.ds(row + PAD, SUBLANES), :]
 
         colour = transmit = None
         for plane in marched:
@@ -154,7 +191,7 @@
             left = pltpu.roll(jnp.where(last_lane, left_tile, centre), 1, 1)
             right = pltpu.roll(jnp.where(first_lane, right_tile, centre), LANES - 1, 1)
             diff_x = right - left
-            diff_y = rows(tile, plane, 1) - rows(tile, plane, -1)
+            diff_y = beside(1, plane) - beside(0, plane)
             diff_z = after - before
             inverse = lax.rsqrt(diff_x * diff_x + diff_y * diff_y + diff_z * diff_z + 1.0)
             facing = (factors[0] * diff_x + factors[1] * diff_y + factors[2] * diff_z) * inverse
@@ -178,35 +215,52 @@
                 colour = [colour[ch] + seen[ch] * glows[ch] for ch in range(3)]
                 transmit = [transmit[ch] - seen[ch] for ch in range(3)]
             if mode == "rim" and plane == 0:
-                here = pl.ds(row * SUBLANES, SUBLANES)
                 held = [inner[at, k, here, :] for k in range(6)]
                 colour = [colour[ch] + transmit[ch] * held[ch] for ch in range(3)]
                 transmit = [transmit[ch] * held[3 + ch] for ch in range(3)]
         for k, value in enumerate(colour + transmit):
             if len(outs) == 1:
-                canvas[at, k, pl.ds(row * SUBLANES, SUBLANES), :] = value
+                canvas[at, k, here, :] = value
             else:
                 block_rows = canvas.shape[4]
-                block = (row * SUBLANES) // block_rows
-                start = pl.multiple_of((row * SUBLANES) % block_rows, SUBLANES)
-                canvas[at, block // group, block % group, k, pl.ds(start, SUBLANES), :] = value
-
-    arrived = set()
-    for at, tile in enumerate(chunk):
-        for other in (tile - 1, tile, tile + 1):
-            if other not in arrived:
-                for copy in incoming(other):
-                    copy.wait()
-                arrived.add(other)
-
-        @pl.loop(0, height // SUBLANES, unroll=4 if mode == "rim" else 2)
-        def _(row):
-            strip(at, row)
-
-        for copy in outgoing(at):
+                block = (number * SUBLANES) // block_rows
+                first = pl.multiple_of((number * SUBLANES) % block_rows, SUBLANES)
+                canvas[at, piece, block, k, pl.ds(first, SUBLANES), :] = value
+
+    for copy in incoming(0, True):
+        copy.wait()
+
+    @pl.loop(0, pieces)
+    def _(piece):
+        @pl.when(piece + 2 < pieces)
+        def _():
+            start(piece + 2)
+
+        for copy in incoming(piece, False):
+            copy.wait()
+
+        @pl.when(piece + 1 < pieces)
+        def _():
+            for copy in incoming(piece + 1, True):
+                copy.wait()
+
+        @pl.when(piece + 1 == pieces)
+        def _():
+            for at in range(len(chunk)):
+                shifted[1, at, :, pl.ds(PAD + height - 1, 1), :] = zeros
+
+        for at in range(len(chunk)):
+
+            @pl.loop(0, piece_rows // SUBLANES, unroll=4 if mode == "rim" else 2)
+            def _(number):
+                strip(at, piece, number)
+
+        for copy in outgoing(piece):
             copy.start()
-    for at in range(len(chunk)):
-        for copy in outgoing(at):
+
+    @pl.loop(0, pieces)
+    def _(piece):
+        for copy in outgoing(piece):
             copy.wait()
 
 
@@ -215,23 +269,25 @@
     tiles = len(chunk)
     near = {tile + k for tile in chunk for k in (-1, 0, 1)}
     extent = tiles * LANES
+    marched = {"full": planes, "middle": planes - 2, "rim": 2}[mode]
     held = 6 if mode == "rim" else planes + 2
     if part_shape is None:
-        group = 1
+        group, pieces = 1, max(1, height // 64)
         outs = [jax.ShapeDtypeStruct((6, height, extent), jnp.float32)]
         canvas = (tiles, 6, height, LANES)
     else:
-        outer, group, rows = part_shape
-        outs = [jax.ShapeDtypeStruct((outer, 6, rows, extent), jnp.float32)] * group
-        canvas = (tiles, outer, group, 6, rows, LANES)
+        pieces, group, rows = part_shape
+        outs = [jax.ShapeDtypeStruct((pieces, 6, rows, extent), jnp.float32)] * group
+        canvas = (tiles, pieces, group, 6, rows, LANES)
     scratch = [
-        pltpu.VMEM((len(near), held, height + 2 * PAD, LANES), jnp.float32),
+        pltpu.VMEM((len(near), held, height, LANES), jnp.float32),
+        pltpu.VMEM((2, tiles, marched, height + 2 * PAD, LANES), jnp.float32),
         pltpu.VMEM(canvas, jnp.float32),
         pltpu.VMEM((SUBLANES, LANES), jnp.float32),
         pltpu.VMEM((6, SUBLANES, LANES), jnp.int32),
         pltpu.VMEM((6, SUBLANES, LANES), jnp.float32),
-        pltpu.SemaphoreType.DMA((len(near), 5)),
-        pltpu.SemaphoreType.DMA((tiles, group)),
+        pltpu.SemaphoreType.DMA((pieces, 2 * len(near) + 7 * tiles)),
+        pltpu.SemaphoreType.DMA((pieces, tiles + 1, group)),
     ]
     operands = [field]
     if min(near) < 0 or max(near) >= width // LANES:
@@ -241,7 +297,8 @@
     if mode == "rim":
         operands.append(middle)
         scratch.append(pltpu.VMEM((tiles, 6, height, LANES), jnp.float32))
-    marched = {"full": planes, "middle": planes - 2, "rim": 4}[mode]
+    if mode == "middle":
+        outs.append(jax.ShapeDtypeStruct((planes, height, LANES), jnp.float32))
     weight = 100 if mode == "middle" else 20000
     far = pl.BlockSpec(memory_space=pltpu.HBM)
     out = pl.pallas_call(
@@ -252,13 +309,13 @@
         scratch_shapes=scratch,
         compiler_params=pltpu.CompilerParams(vmem_limit_bytes=60 * 1024 * 1024),
         cost_estimate=pl.CostEstimate(
-            flops=marched * height * extent * weight,
-            bytes_accessed=marched * height * extent * 5,
+            flops=planes * height * extent * weight,
+            bytes_accessed=planes * height * extent * 5,
             transcendentals=0,
         ),
         name=f"march_{mode}_{chunk[0]}",
     )(*tables, *operands)
-    return out[0] if part_shape is None else out
+    return out[0] if len(out) == 1 else out
 
 
 def plane_halos(first, last):
@@ -266,14 +323,6 @@
     forward = [(i, i + 1) for i in range(count - 1)]
     backward = [(i + 1, i) for i in range(count - 1)]
     return lax.ppermute(last, "slab", forward), lax.ppermute(first, "slab", backward)
-
-
-def edge_tile(field, earlier):
-    first = lax.axis_index("tile") == 0
-    planes, height, width = field.shape
-    start, _ = lax.optimization_barrier((jnp.where(first, width - LANES, 0), earlier))
-    own = lax.dynamic_slice_in_dim(field, start, LANES, axis=2)
-    return lax.ppermute(own, "tile", [(0, 1), (1, 0)])
 
 
 def ordered(is_far, own, other):
@@ -334,12 +383,12 @@
     results = []
     for number, chunk in enumerate(chunks):
         if number == 0:
-            middle = march(
+            middle, edge = march(
                 "middle", chunk, tables, field, None, None, None, depth_total, None
             )
-            mode, side = "rim", None
+            side = lax.ppermute(edge, "tile", [(0, 1), (1, 0)])
+            mode = "rim"
         else:
-            side = edge_tile(field, (halo, middle))
             halo, side, _ = lax.optimization_barrier((halo, side, out))
             middle, mode = None, "full"
         out = march(mode, chunk, tables, field, side, halo, middle, depth_total, part_shape)

time: 98.1 us -> 100 us (1.019)
  Pallas kernels: 47.1 us -> 51.6 us
  waiting for transfers between devices: 21.5 us -> 19.3 us
  starting transfers between devices: 22.8 us -> 24.5 us
  local copies, waits for them, and re-layouts: 3.68 us -> 2.1 us
    pallas_call x3, Pallas kernels: 47.1 us -> 51.6 us  [march(): pl.pallas_call(functools.partial(march_kernel, mode, chunk, depth_total,...]
    dynamic_slice x1 -> x0, local copies, waits for them, and re-layouts: 2.38 us -> none  [edge_tile(): own = lax.dynamic_slice_in_dim(field, start, LANES, axis=2)]
    ppermute x12, starting transfers between devices: 16.6 us -> 18.2 us  [exchange(): lax.ppermute(part, 'slab', [(i, i ^ change << shift) for i in range(count)])]
    ppermute x1, waiting for transfers between devices: 1.86 us -> 0.56 us  [plane_halos(): lax.ppermute(last, 'slab', forward)]
  transfers between devices with their start and end apart: 15 -> 15, of which waited for: 6 -> 6; matrix products, arithmetic and copies ran while one was open for 1% -> 0% of each run, Pallas kernels for 48% -> 52%
where the time goes in v6:
time: 100 us
  Pallas kernels  51.6 us (52%)
  starting transfers between devices  24.5 us (24%)
  waiting for transfers between devices  19.3 us (19%)
  local copies, waits for them, and re-layouts  2.1 us (2%)
  other arithmetic  1.83 us (2%)
    pallas_call x3, Pallas kernels, march(): pl.pallas_call(functools.partial(march_kernel, mode, chunk, depth_total,...  51.6 us
    ppermute x12, starting transfers between devices, exchange(): lax.ppermute(part, 'slab', [(i, i ^ change << shift) for i in range(count)])  18.2 us
    ppermute x12, waiting for transfers between devices, exchange(): lax.ppermute(part, 'slab', [(i, i ^ change << shift) for i in range(count)])  16.7 us
    ppermute x1, starting transfers between devices, plane_halos(): lax.ppermute(last, 'slab', forward)  4.88 us
  transfers between devices with their start and end apart: 15, of which 6 were waited for; matrix products, arithmetic and copies ran while one was open for 0% of the time, Pallas kernels for 52%

profile of v6, /device:TPU:0, one launch (start us, length us, event | category | flops | bytes accessed | tf_op | source)
XLA Modules:
  0.0 100.0 jit_solution(6590975448431240959)
XLA Ops:
  0.6 1.3 %slice_bitcast_fusion = (f32[256,512]{1,0:T(8,128)S(1)}, f32[256,512]{1,0:T(8,128)S(1)}) fusion(f32[16,256,512]{2,1,0:T(8,128)} %refs_0_.5), kind=kLoop, calls=%fused_computation.16 | loop fusion | bytes 2097152 | tf_op jit(solution)/shard_map/squeeze | solution.py:382
  1.9 4.9 %collective-permute-start = (f32[256,512]{1,0:T(8,128)S(1)}, f32[256,512]{1,0:T(8,128)S(1)}, u32[]{:S(2)}, u32[]{:S(2)}) collective-permute-start(f32[256,512]{1,0:T(8,128)S(1)} %get-tuple-element.29), channel_id=1, source_target_pairs={{0,2},{2,4},{4,6},{6,8},{8,10},{10,12},{12,14},{14,16},{16,18},{18... | collective-permute-start | bytes 1572872 | tf_op jit(solution)/shard_map/ppermute | solution.py:325
  6.8 1.3 %collective-permute-start.1 = (f32[256,512]{1,0:T(8,128)S(1)}, f32[256,512]{1,0:T(8,128)S(1)}, u32[]{:S(2)}, u32[]{:S(2)}) collective-permute-start(f32[256,512]{1,0:T(8,128)S(1)} %get-tuple-element.28), channel_id=1, source_target_pairs={{2,0},{4,2},{6,4},{8,6},{10,8},{12,10},{14,12},{16,14},{18,16},{20... | collective-permute-start | bytes 1572872 | tf_op jit(solution)/shard_map/ppermute | solution.py:325
  8.1 20.4 %march_middle_1.1 = (f32[6,256,256]{2,1,0:T(8,128)}, f32[16,256,128]{2,1,0:T(8,128)}) custom-call(f32[3,16]{1,0:T(4,128)} %emission.5, f32[3,16]{1,0:T(4,128)} %absorption.5, f32[16,256,512]{2,1,0:T(8,128)} %refs_0_.5), custom_call_target="tpu_custom_call" | custom-call | flops 104857600 | bytes 5242880 | tf_op jit(solution)/shard_map/march_middle_1/pallas_call | solution.py:304
  28.5 0.1 collective-permute-start.2
  28.6 0.6 collective-permute-done.refs_1_.refs_2_
  29.2 0.0 copy-start.2
  29.2 1.9 %collective-permute-done.1.refs_2_.refs_3_ = f32[256,512]{1,0:T(8,128)S(1)} collective-permute-done((f32[256,512]{1,0:T(8,128)S(1)}, f32[256,512]{1,0:T(8,128)S(1)}, u32[]{:S(2)}, u32[]{:S(2)}) %collective-permute-start.1) | collective-permute-done | bytes 524320 | tf_op jit(solution)/shard_map/ppermute | solution.py:325
  31.1 0.0 copy-start.3
  31.1 0.0 copy-done.2
  31.1 0.8 copy-done.3
  31.9 8.0 %march_rim_1.1 = (f32[4,6,16,256]{3,2,1,0:T(8,128)}, f32[4,6,16,256]{3,2,1,0:T(8,128)}, f32[4,6,16,256]{3,2,1,0:T(8,128)}, f32[4,6,16,256]{3,2,1,0:T(8,128)}) custom-call(f32[3,16]{1,0:T(4,128)} %emission.5, f32[3,16]{1,0:T(4,128)} %absorption.5, f32[16,256,512]{2,1,0:T(8,128)} %refs_0_.5, f32[256,512]{1,0:T(8,128)} %copy-done.2, f32[256,512]{1,0:T(8,128)} %copy-done.3, ...), custom_call_target="tpu_custom_call" | custom-call | flops 20971520000 | bytes 5242880 | tf_op jit(solution)/shard_map/march_rim_1/pallas_call | solution.py:304
  39.9 1.3 %collective-permute-start.10 = (f32[4,6,16,256]{3,2,1,0:T(8,128)}, f32[4,6,16,256]{3,2,1,0:T(8,128)S(1)}, u32[]{:S(2)}, u32[]{:S(2)}) collective-permute-start(f32[4,6,16,256]{3,2,1,0:T(8,128)} %get-tuple-element.19), channel_id=1, source_target_pairs={{0,4},{2,6},{4,0},{6,2},{8,12},{10,14},{12,8},{14,10},{16,20},{18,... | collective-permute-start | bytes 1179656 | tf_op jit(solution)/shard_map/ppermute | solution.py:339
  41.2 1.7 %collective-permute-start.9 = (f32[4,6,16,256]{3,2,1,0:T(8,128)}, f32[4,6,16,256]{3,2,1,0:T(8,128)S(1)}, u32[]{:S(2)}, u32[]{:S(2)}) collective-permute-start(f32[4,6,16,256]{3,2,1,0:T(8,128)} %get-tuple-element.20), channel_id=1, source_target_pairs={{0,6},{2,4},{4,2},{6,0},{8,14},{10,12},{12,10},{14,8},{16,22},{18,... | collective-permute-start | bytes 1179656 | tf_op jit(solution)/shard_map/ppermute | solution.py:339
  42.9 0.5 collective-permute-start.11
  43.5 0.0 collective-permute-done.2.refs_1_
  43.5 0.0 copy-start.1
  43.5 23.2 %march_full_0.1 = (f32[4,6,16,256]{3,2,1,0:T(8,128)}, f32[4,6,16,256]{3,2,1,0:T(8,128)}, f32[4,6,16,256]{3,2,1,0:T(8,128)}, f32[4,6,16,256]{3,2,1,0:T(8,128)}) custom-call(f32[3,16]{1,0:T(4,128)} %emission.5, f32[3,16]{1,0:T(4,128)} %absorption.5, f32[16,256,512]{2,1,0:T(8,128)} %refs_0_.5, f32[16,256,128]{2,1,0:T(8,128)} %collective-permute-done.2.refs_1_, ...), custom_call_target="tpu_custom_call" | custom-call | flops 20971520000 | bytes 5242880 | tf_op jit(solution)/shard_map/march_full_0/pallas_call | solution.py:304
  66.7 0.0 copy-start
  66.7 1.3 %collective-permute-start.4 = (f32[4,6,16,256]{3,2,1,0:T(8,128)}, f32[4,6,16,256]{3,2,1,0:T(8,128)S(1)}, u32[]{:S(2)}, u32[]{:S(2)}) collective-permute-start(f32[4,6,16,256]{3,2,1,0:T(8,128)} %get-tuple-element.25), channel_id=1, source_target_pairs={{0,4},{2,6},{4,0},{6,2},{8,12},{10,14},{12,8},{14,10},{16,20},{18,... | collective-permute-start | bytes 1179656 | tf_op jit(solution)/shard_map/ppermute | solution.py:339
  68.0 1.7 %collective-permute-start.3 = (f32[4,6,16,256]{3,2,1,0:T(8,128)}, f32[4,6,16,256]{3,2,1,0:T(8,128)S(1)}, u32[]{:S(2)}, u32[]{:S(2)}) collective-permute-start(f32[4,6,16,256]{3,2,1,0:T(8,128)} %get-tuple-element.24), channel_id=1, source_target_pairs={{0,6},{2,4},{4,2},{6,0},{8,14},{10,12},{12,10},{14,8},{16,22},{18,... | collective-permute-start | bytes 1179656 | tf_op jit(solution)/shard_map/ppermute | solution.py:339
  69.7 0.0 collective-permute-done.10
  69.7 0.5 collective-permute-start.5
  70.3 0.0 collective-permute-done.9
  70.3 0.0 collective-permute-done.11
  70.3 0.0 copy-done.1
  70.3 0.2 select_multiply_fusion
  70.5 3.3 %collective-permute-start.13 = (f32[1,6,16,256]{3,2,1,0:T(8,128)S(1)}, f32[1,6,16,256]{3,2,1,0:T(8,128)S(1)}, u32[]{:S(2)}, u32[]{:S(2)}) collective-permute-start(f32[1,6,16,256]{3,2,1,0:T(8,128)S(1)} %get-tuple-element.39), channel_id=1, source_target_pairs={{0,16},{2,18},{4,20},{6,22},{8,24},{10,26},{12,28},{14,30},{16,0},... | collective-permute-start | bytes 294920 | tf_op jit(solution)/shard_map/ppermute | solution.py:339
  73.8 1.3 %collective-permute-start.12 = (f32[1,6,16,256]{3,2,1,0:T(8,128)S(1)}, f32[1,6,16,256]{3,2,1,0:T(8,128)S(1)}, u32[]{:S(2)}, u32[]{:S(2)}) collective-permute-start(f32[1,6,16,256]{3,2,1,0:T(8,128)S(1)} %get-tuple-element.38), channel_id=1, source_target_pairs={{0,24},{2,26},{4,28},{6,30},{8,16},{10,18},{12,20},{14,22},{16,8},... | collective-permute-start | bytes 294920 | tf_op jit(solution)/shard_map/ppermute | solution.py:339
  75.1 10.5 %collective-permute-done.4 = f32[4,6,16,256]{3,2,1,0:T(8,128)S(1)} collective-permute-done((f32[4,6,16,256]{3,2,1,0:T(8,128)}, f32[4,6,16,256]{3,2,1,0:T(8,128)S(1)}, u32[]{:S(2)}, u32[]{:S(2)}) %collective-permute-start.4) | collective-permute-done | bytes 393248 | tf_op jit(solution)/shard_map/ppermute | solution.py:339
  85.7 2.6 %collective-permute-start.14 = (f32[1,6,16,256]{3,2,1,0:T(8,128)S(1)}, f32[1,6,16,256]{3,2,1,0:T(8,128)S(1)}, u32[]{:S(2)}, u32[]{:S(2)}) collective-permute-start(f32[1,6,16,256]{3,2,1,0:T(8,128)S(1)} %get-tuple-element.40), channel_id=1, source_target_pairs={{0,8},{2,10},{4,12},{6,14},{8,0},{10,2},{12,4},{14,6},{16,24},{18,... | collective-permute-start | bytes 294920 | tf_op jit(solution)/shard_map/ppermute | solution.py:339
  88.3 0.0 collective-permute-done.3
  88.3 0.0 collective-permute-done.5
  88.3 0.0 copy-done
  88.3 0.2 select_multiply_fusion.3
  88.5 2.7 %collective-permute-start.7 = (f32[1,6,16,256]{3,2,1,0:T(8,128)S(1)}, f32[1,6,16,256]{3,2,1,0:T(8,128)S(1)}, u32[]{:S(2)}, u32[]{:S(2)}) collective-permute-start(f32[1,6,16,256]{3,2,1,0:T(8,128)S(1)} %get-tuple-element.43), channel_id=1, source_target_pairs={{0,16},{2,18},{4,20},{6,22},{8,24},{10,26},{12,28},{14,30},{16,0},... | collective-permute-start | bytes 294920 | tf_op jit(solution)/shard_map/ppermute | solution.py:339
  91.2 1.0 collective-permute-start.6
  92.2 0.0 collective-permute-done.13
  92.2 0.2 collective-permute-start.8
  92.4 0.0 collective-permute-done.12
  92.4 0.0 collective-permute-done.14
  92.5 4.8 %collective-permute-done.7 = f32[1,6,16,256]{3,2,1,0:T(8,128)S(1)} collective-permute-done((f32[1,6,16,256]{3,2,1,0:T(8,128)S(1)}, f32[1,6,16,256]{3,2,1,0:T(8,128)S(1)}, u32[]{:S(2)}, u32[]{:S(2)}) %collective-permute-start.7) | collective-permute-done | bytes 98336 | tf_op jit(solution)/shard_map/ppermute | solution.py:339
  97.2 0.9 collective-permute-done.6
  98.1 0.5 collective-permute-done.8
  98.7 0.6 pad_maximum_fusion
  99.4 0.6 pad_maximum_fusion.1
  (5 shorter events, 0.2 us)
Async XLA Ops:
  1.9 27.2 %collective-permute-start = (f32[256,512]{1,0:T(8,128)S(1)}, f32[256,512]{1,0:T(8,128)S(1)}, u32[]{:S(2)}, u32[]{:S(2)}) collective-permute-start(f32[256,512]{1,0:T(8,128)S(1)} %get-tuple-element.29), channel_id=1, source_target_pairs={{0,2},{2,4},{4,6},{6,8},{8,10},{10,12},{12,14},{14,16},{16,18},{18... | collective-permute-start | bytes 1572872 | tf_op jit(solution)/shard_map/ppermute | solution.py:325
  6.8 24.3 %collective-permute-start.1 = (f32[256,512]{1,0:T(8,128)S(1)}, f32[256,512]{1,0:T(8,128)S(1)}, u32[]{:S(2)}, u32[]{:S(2)}) collective-permute-start(f32[256,512]{1,0:T(8,128)S(1)} %get-tuple-element.28), channel_id=1, source_target_pairs={{2,0},{4,2},{6,4},{8,6},{10,8},{12,10},{14,12},{16,14},{18,16},{20... | collective-permute-start | bytes 1572872 | tf_op jit(solution)/shard_map/ppermute | solution.py:325
  28.5 15.0 %collective-permute-start.2 = (f32[16,256,128]{2,1,0:T(8,128)}, f32[16,256,128]{2,1,0:T(8,128)}, u32[]{:S(2)}, u32[]{:S(2)}) collective-permute-start(f32[16,256,128]{2,1,0:T(8,128)} %get-tuple-element.15), channel_id=1, source_target_pairs={{0,1},{1,0},{2,3},{3,2},{4,5},{5,4},{6,7},{7,6},{8,9},{9,8},{10,11... | collective-permute-start | bytes 6291464 | tf_op jit(solution)/shard_map/ppermute | solution.py:389
  29.2 2.0 %copy-start.2 = (f32[256,512]{1,0:T(8,128)}, f32[256,512]{1,0:T(8,128)S(1)}, u32[]{:S(2)}) copy-start(f32[256,512]{1,0:T(8,128)S(1)} %collective-permute-done.refs_1_.refs_2_) | copy-start | bytes 1572868
  31.1 0.8 copy-start.3
  39.9 29.8 %collective-permute-start.10 = (f32[4,6,16,256]{3,2,1,0:T(8,128)}, f32[4,6,16,256]{3,2,1,0:T(8,128)S(1)}, u32[]{:S(2)}, u32[]{:S(2)}) collective-permute-start(f32[4,6,16,256]{3,2,1,0:T(8,128)} %get-tuple-element.19), channel_id=1, source_target_pairs={{0,4},{2,6},{4,0},{6,2},{8,12},{10,14},{12,8},{14,10},{16,20},{18,... | collective-permute-start | bytes 1179656 | tf_op jit(solution)/shard_map/ppermute | solution.py:339
  41.2 29.1 %collective-permute-start.9 = (f32[4,6,16,256]{3,2,1,0:T(8,128)}, f32[4,6,16,256]{3,2,1,0:T(8,128)S(1)}, u32[]{:S(2)}, u32[]{:S(2)}) collective-permute-start(f32[4,6,16,256]{3,2,1,0:T(8,128)} %get-tuple-element.20), channel_id=1, source_target_pairs={{0,6},{2,4},{4,2},{6,0},{8,14},{10,12},{12,10},{14,8},{16,22},{18,... | collective-permute-start | bytes 1179656 | tf_op jit(solution)/shard_map/ppermute | solution.py:339
  42.9 27.4 %collective-permute-start.11 = (f32[4,6,16,256]{3,2,1,0:T(8,128)}, f32[4,6,16,256]{3,2,1,0:T(8,128)S(1)}, u32[]{:S(2)}, u32[]{:S(2)}) collective-permute-start(f32[4,6,16,256]{3,2,1,0:T(8,128)} %get-tuple-element.18), channel_id=1, source_target_pairs={{0,2},{2,0},{4,6},{6,4},{8,10},{10,8},{12,14},{14,12},{16,18},{18,... | collective-permute-start | bytes 1179656 | tf_op jit(solution)/shard_map/ppermute | solution.py:339
  43.5 26.8 %copy-start.1 = (f32[4,6,16,256]{3,2,1,0:T(8,128)S(1)}, f32[4,6,16,256]{3,2,1,0:T(8,128)}, u32[]{:S(2)}) copy-start(f32[4,6,16,256]{3,2,1,0:T(8,128)} %get-tuple-element.17) | copy-start | bytes 1179652
  66.7 21.6 %copy-start = (f32[4,6,16,256]{3,2,1,0:T(8,128)S(1)}, f32[4,6,16,256]{3,2,1,0:T(8,128)}, u32[]{:S(2)}) copy-start(f32[4,6,16,256]{3,2,1,0:T(8,128)} %get-tuple-element.27) | copy-start | bytes 1179652
  66.7 18.9 %collective-permute-start.4 = (f32[4,6,16,256]{3,2,1,0:T(8,128)}, f32[4,6,16,256]{3,2,1,0:T(8,128)S(1)}, u32[]{:S(2)}, u32[]{:S(2)}) collective-permute-start(f32[4,6,16,256]{3,2,1,0:T(8,128)} %get-tuple-element.25), channel_id=1, source_target_pairs={{0,4},{2,6},{4,0},{6,2},{8,12},{10,14},{12,8},{14,10},{16,20},{18,... | collective-permute-start | bytes 1179656 | tf_op jit(solution)/shard_map/ppermute | solution.py:339
  68.0 20.3 %collective-permute-start.3 = (f32[4,6,16,256]{3,2,1,0:T(8,128)}, f32[4,6,16,256]{3,2,1,0:T(8,128)S(1)}, u32[]{:S(2)}, u32[]{:S(2)}) collective-permute-start(f32[4,6,16,256]{3,2,1,0:T(8,128)} %get-tuple-element.24), channel_id=1, source_target_pairs={{0,6},{2,4},{4,2},{6,0},{8,14},{10,12},{12,10},{14,8},{16,22},{18,... | collective-permute-start | bytes 1179656 | tf_op jit(solution)/shard_map/ppermute | solution.py:339
  69.7 18.5 %collective-permute-start.5 = (f32[4,6,16,256]{3,2,1,0:T(8,128)}, f32[4,6,16,256]{3,2,1,0:T(8,128)S(1)}, u32[]{:S(2)}, u32[]{:S(2)}) collective-permute-start(f32[4,6,16,256]{3,2,1,0:T(8,128)} %get-tuple-element.26), channel_id=1, source_target_pairs={{0,2},{2,0},{4,6},{6,4},{8,10},{10,8},{12,14},{14,12},{16,18},{18,... | collective-permute-start | bytes 1179656 | tf_op jit(solution)/shard_map/ppermute | solution.py:339
  70.5 21.6 %collective-permute-start.13 = (f32[1,6,16,256]{3,2,1,0:T(8,128)S(1)}, f32[1,6,16,256]{3,2,1,0:T(8,128)S(1)}, u32[]{:S(2)}, u32[]{:S(2)}) collective-permute-start(f32[1,6,16,256]{3,2,1,0:T(8,128)S(1)} %get-tuple-element.39), channel_id=1, source_target_pairs={{0,16},{2,18},{4,20},{6,22},{8,24},{10,26},{12,28},{14,30},{16,0},... | collective-permute-start | bytes 294920 | tf_op jit(solution)/shard_map/ppermute | solution.py:339
  73.8 18.6 %collective-permute-start.12 = (f32[1,6,16,256]{3,2,1,0:T(8,128)S(1)}, f32[1,6,16,256]{3,2,1,0:T(8,128)S(1)}, u32[]{:S(2)}, u32[]{:S(2)}) collective-permute-start(f32[1,6,16,256]{3,2,1,0:T(8,128)S(1)} %get-tuple-element.38), channel_id=1, source_target_pairs={{0,24},{2,26},{4,28},{6,30},{8,16},{10,18},{12,20},{14,22},{16,8},... | collective-permute-start | bytes 294920 | tf_op jit(solution)/shard_map/ppermute | solution.py:339
  85.7 6.8 %collective-permute-start.14 = (f32[1,6,16,256]{3,2,1,0:T(8,128)S(1)}, f32[1,6,16,256]{3,2,1,0:T(8,128)S(1)}, u32[]{:S(2)}, u32[]{:S(2)}) collective-permute-start(f32[1,6,16,256]{3,2,1,0:T(8,128)S(1)} %get-tuple-element.40), channel_id=1, source_target_pairs={{0,8},{2,10},{4,12},{6,14},{8,0},{10,2},{12,4},{14,6},{16,24},{18,... | collective-permute-start | bytes 294920 | tf_op jit(solution)/shard_map/ppermute | solution.py:339
  88.5 8.7 %collective-permute-start.7 = (f32[1,6,16,256]{3,2,1,0:T(8,128)S(1)}, f32[1,6,16,256]{3,2,1,0:T(8,128)S(1)}, u32[]{:S(2)}, u32[]{:S(2)}) collective-permute-start(f32[1,6,16,256]{3,2,1,0:T(8,128)S(1)} %get-tuple-element.43), channel_id=1, source_target_pairs={{0,16},{2,18},{4,20},{6,22},{8,24},{10,26},{12,28},{14,30},{16,0},... | collective-permute-start | bytes 294920 | tf_op jit(solution)/shard_map/ppermute | solution.py:339
  91.2 6.9 %collective-permute-start.6 = (f32[1,6,16,256]{3,2,1,0:T(8,128)S(1)}, f32[1,6,16,256]{3,2,1,0:T(8,128)S(1)}, u32[]{:S(2)}, u32[]{:S(2)}) collective-permute-start(f32[1,6,16,256]{3,2,1,0:T(8,128)S(1)} %get-tuple-element.42), channel_id=1, source_target_pairs={{0,24},{2,26},{4,28},{6,30},{8,16},{10,18},{12,20},{14,22},{16,8},... | collective-permute-start | bytes 294920 | tf_op jit(solution)/shard_map/ppermute | solution.py:339
  92.2 6.5 %collective-permute-start.8 = (f32[1,6,16,256]{3,2,1,0:T(8,128)S(1)}, f32[1,6,16,256]{3,2,1,0:T(8,128)S(1)}, u32[]{:S(2)}, u32[]{:S(2)}) collective-permute-start(f32[1,6,16,256]{3,2,1,0:T(8,128)S(1)} %get-tuple-element.44), channel_id=1, source_target_pairs={{0,8},{2,10},{4,12},{6,14},{8,0},{10,2},{12,4},{14,6},{16,24},{18,... | collective-permute-start | bytes 294920 | tf_op jit(solution)/shard_map/ppermute | solution.py:339

commit v7 on v6

v7 whole, which is shorter than its diff:
```python
import functools

import jax
import jax.numpy as jnp
from jax import lax
from jax.experimental import pallas as pl
from jax.experimental.pallas import tpu as pltpu
from jax.sharding import PartitionSpec as P

LIGHT_DIR = (0.2672612, 0.5345225, 0.8017837)
LANES = 128
SUBLANES = 8
PAD = 8
WORD_SCALE = 2.0**31 - 2.0**17
HALF = 65536


def prepare_tables(emission, absorption, depth_total, table, words, factors):
    breaks = emission.shape[1]
    table[...] = jnp.zeros(table.shape, jnp.float32)
    table[0:3, 0:breaks] = emission[...]
    table[3:6, 0:breaks] = absorption[...]
    values = table[...]
    largest = [jnp.maximum(jnp.max(ref[...]), 1e-30) for ref in (emission, absorption)]
    row = lax.broadcasted_iota(jnp.int32, table.shape, 0)
    lane = lax.broadcasted_iota(jnp.int32, table.shape, 1)
    scaled = values * (WORD_SCALE / jnp.where(row < 3, largest[0], largest[1]))
    following = jnp.where(lane < breaks - 1, pltpu.roll(scaled, LANES - 1, 1), scaled)
    rise = jnp.floor((following - scaled) * (1.0 / HALF) + 0.5)
    upper = jnp.floor((0.5 * (following + scaled) - rise) * (1.0 / HALF) + 0.5)
    word = upper.astype(jnp.int32) * HALF + rise.astype(jnp.int32)
    units = [largest[0] / WORD_SCALE, largest[1] * (4.0 / depth_total) / WORD_SCALE]
    constants = [0.9 * part * units[0] for part in LIGHT_DIR]
    constants += [0.1 * units[0], units[1], 0.75 * units[1]]
    for k in range(6):
        words[k] = jnp.broadcast_to(word[k : k + 1, :], (SUBLANES, LANES))
        factors[k] = jnp.full((SUBLANES, LANES), constants[k], jnp.float32)


def lookup(table, index):
    return lax.gather(
        table,
        index.reshape(index.shape + (1,)),
        lax.GatherDimensionNumbers(
            offset_dims=(),
            collapsed_slice_dims=(1,),
            start_index_map=(1,),
            operand_batching_dims=(0,),
            start_indices_batching_dims=(0,),
        ),
        slice_sizes=(1, 1),
        mode=lax.GatherScatterMode.PROMISE_IN_BOUNDS,
    )


def march_kernel(mode, depth_total, group, emission, absorption, *refs):
    refs = list(refs)
    field = refs.pop(0)
    side = refs.pop(0) if mode == "outer" else None
    low, high = (refs.pop(0), refs.pop(0)) if mode != "middle" else (None, None)
    middle = refs.pop(0) if mode == "rim" else None
    inner = refs.pop() if mode == "rim" else None
    cells, canvas, table, words, factors, in_sems, out_sems = refs[-7:]
    outs = refs[:-7]
    edge = outs.pop() if mode == "middle" else None
    planes, height, width = field.shape
    scale = 0.5 * (emission.shape[1] - 1)
    piece_rows = height // in_sems.shape[0]
    pieces = height // piece_rows
    core = lax.axis_index("tile")
    tiles = cells.shape[0] - 2
    blocks = [(0, 1, planes)] if mode != "rim" else [(0, 1, 2), (planes - 2, 3, 2)]
    marched = {
        "outer": range(planes), "middle": range(1, planes - 1), "rim": (0, planes - 1)
    }[mode]
    place = {first + k: slot + k for first, slot, count in blocks for k in range(count)}
    place[-1] = 0
    place[planes] = max(place.values()) + 1
    far = (1 - core) * (tiles + 1)
    if mode == "outer":
        first_lane_taken, first_tile, taken = (1 - core) * (width - 2 * LANES), core, 2
    else:
        first_lane_taken, first_tile, taken = 0, 1 - core, width // LANES

    def incoming(piece):
        start = pl.multiple_of(piece * piece_rows, SUBLANES)
        body = pl.ds(start, piece_rows)
        padded = pl.ds(start + PAD, piece_rows)
        pairs = []
        for k in range(taken):
            lanes = pl.ds(pl.multiple_of(first_lane_taken + k * LANES, LANES), LANES)
            held = cells.at[first_tile + k]
            for first, where, count in blocks:
                target = held.at[pl.ds(where, count), padded, :]
                pairs.append((field.at[pl.ds(first, count), body, lanes], target))
            if mode != "middle":
                for halo, plane in ((low, -1), (high, planes)):
                    pairs.append((halo.at[body, lanes], held.at[place[plane], padded, :]))
        if mode == "rim":
            pairs.append((middle.at[:, body, :], inner.at[:, body, :]))
        if mode == "outer":
            pairs.append((side.at[:, body, :], cells.at[far, pl.ds(1, planes), padded, :]))
        return [
            pltpu.make_async_copy(source, target, in_sems.at[piece, k])
            for k, (source, target) in enumerate(pairs)
        ]

    def outgoing(piece):
        start = pl.multiple_of(piece * piece_rows, SUBLANES)
        body = pl.ds(start, piece_rows)
        if len(outs) == 1:
            pairs = [(canvas.at[:, body, :], outs[0].at[:, body, :])]
        else:
            own = lax.axis_index("slab") & (group - 1)
            pairs = [(canvas.at[piece, own ^ k], outs[k].at[piece]) for k in range(group)]
        if edge is not None:
            padded = pl.ds(start + PAD, piece_rows)
            pairs.append((cells.at[far, pl.ds(1, planes), padded, :], edge.at[:, body, :]))
        return [
            pltpu.make_async_copy(source, target, out_sems.at[piece, k])
            for k, (source, target) in enumerate(pairs)
        ]

    def start(piece):
        for copy in incoming(piece):
            copy.start()

    def await_piece(piece):
        for copy in incoming(piece):
            copy.wait()

    for piece in range(min(3, pieces)):
        start(piece)
    prepare_tables(emission, absorption, depth_total, table, words, factors)
    zeros = jnp.zeros((1, LANES), jnp.float32)
    for tile in range(1, tiles + 1):
        for plane in marched:
            cells[tile, place[plane], pl.ds(PAD - 1, 1), :] = zeros
            cells[tile, place[plane], pl.ds(PAD + height, 1), :] = zeros
    if mode != "outer":
        blank = jnp.zeros((height, LANES), jnp.float32)
        for plane in marched:
            cells[core * (tiles + 1), place[plane], pl.ds(PAD, height), :] = blank

    lane = lax.broadcasted_iota(jnp.int32, (SUBLANES, LANES), 1)
    first_lane = lane == 0
    last_lane = lane == LANES - 1

    def strip(at, piece, number):
        row = pl.multiple_of(piece * piece_rows + number * SUBLANES, SUBLANES)

        def rows(tile, plane, offset=0):
            here = pl.ds(row + PAD + offset, SUBLANES)
            return cells[tile + 1, place[plane], here, :]

        colour = transmit = None
        for plane in marched:
            before, centre, after = (rows(at, plane + k) for k in (-1, 0, 1))
            left = pltpu.roll(jnp.where(last_lane, rows(at - 1, plane), centre), 1, 1)
            right = pltpu.roll(jnp.where(first_lane, rows(at + 1, plane), centre), LANES - 1, 1)
            diff_x = right - left
            diff_y = rows(at, plane, 1) - rows(at, plane, -1)
            diff_z = after - before
            inverse = lax.rsqrt(diff_x * diff_x + diff_y * diff_y + diff_z * diff_z + 1.0)
            facing = (factors[0] * diff_x + factors[1] * diff_y + factors[2] * diff_z) * inverse
            shading = jnp.maximum(facing, 0.0) + factors[3]
            weight = factors[4] - factors[5] * (inverse * inverse)
            middle_based = centre * scale + (scale - 0.5)
            interval = (middle_based + 0.5).astype(jnp.int32)
            offset = middle_based - interval.astype(jnp.float32)
            values = []
            for k in range(6):
                word = lookup(words[k], interval)
                rise = lax.shift_left(word, 16).astype(jnp.float32)
                values.append(word.astype(jnp.float32) + rise * offset)
            steps = [values[3 + ch] * weight for ch in range(3)]
            glows = [values[ch] * shading for ch in range(3)]
            if colour is None:
                colour = [step * glow for step, glow in zip(steps, glows)]
                transmit = [1.0 - step for step in steps]
            else:
                seen = [transmit[ch] * steps[ch] for ch in range(3)]
                colour = [colour[ch] + seen[ch] * glows[ch] for ch in range(3)]
                transmit = [transmit[ch] - seen[ch] for ch in range(3)]
            if mode == "rim" and plane == 0:
                held = [
                    inner[k, pl.ds(row, SUBLANES), pl.ds(at * LANES, LANES)] for k in range(6)
                ]
                colour = [colour[ch] + transmit[ch] * held[ch] for ch in range(3)]
                transmit = [transmit[ch] * held[3 + ch] for ch in range(3)]
        here = pl.ds(at * LANES, LANES)
        for k, value in enumerate(colour + transmit):
            if len(outs) == 1:
                canvas[k, pl.ds(row, SUBLANES), here] = value
            else:
                block_rows = canvas.shape[3]
                block = (number * SUBLANES) // block_rows
                first = pl.multiple_of((number * SUBLANES) % block_rows, SUBLANES)
                canvas[piece, block, k, pl.ds(first, SUBLANES), here] = value

    await_piece(0)

    @pl.loop(0, pieces)
    def _(piece):
        @pl.when(piece + 3 < pieces)
        def _():
            start(piece + 3)

        @pl.when(piece + 1 < pieces)
        def _():
            await_piece(piece + 1)

        @pl.loop(0, piece_rows // SUBLANES)
        def _(number):
            for at in range(tiles):
                strip(at, piece, number)

        for copy in outgoing(piece):
            copy.start()

    @pl.loop(0, pieces)
    def _(piece):
        for copy in outgoing(piece):
            copy.wait()


def march(mode, tables, field, side, halos, middle, depth_total, part_shape):
    planes, height, width = field.shape
    extent = LANES if mode == "outer" else width - LANES
    marched = {"outer": planes, "middle": planes - 2, "rim": 2}[mode]
    held = 6 if mode == "rim" else planes + 2
    if part_shape is None:
        group, pieces = 1, max(1, height // 64)
        outs = [jax.ShapeDtypeStruct((6, height, extent), jnp.float32)]
        canvas = (6, height, extent)
    else:
        pieces, group, rows = part_shape
        outs = [jax.ShapeDtypeStruct((pieces, 6, rows, extent), jnp.float32)] * group
        canvas = (pieces, group, 6, rows, extent)
    scratch = [
        pltpu.VMEM((extent // LANES + 2, held, height + 2 * PAD, LANES), jnp.float32),
        pltpu.VMEM(canvas, jnp.float32),
        pltpu.VMEM((SUBLANES, LANES), jnp.float32),
        pltpu.VMEM((6, SUBLANES, LANES), jnp.int32),
        pltpu.VMEM((6, SUBLANES, LANES), jnp.float32),
        pltpu.SemaphoreType.DMA((pieces, 4 * (width // LANES) + 1)),
        pltpu.SemaphoreType.DMA((pieces, group + 1)),
    ]
    operands = [field]
    if mode == "outer":
        operands.append(side)
    if mode != "middle":
        operands += list(halos)
    if mode == "rim":
        operands.append(middle)
        scratch.append(pltpu.VMEM((6, height, extent), jnp.float32))
    if mode == "middle":
        outs.append(jax.ShapeDtypeStruct((planes, height, LANES), jnp.float32))
    weight = 100 if mode == "middle" else 20000
    distant = pl.BlockSpec(memory_space=pltpu.HBM)
    out = pl.pallas_call(
        functools.partial(march_kernel, mode, depth_total, group),
        out_shape=outs,
        in_specs=[pl.BlockSpec(memory_space=pltpu.VMEM)] * 2 + [distant] * len(operands),
        out_specs=[distant] * len(outs),
        scratch_shapes=scratch,
        compiler_params=pltpu.CompilerParams(vmem_limit_bytes=60 * 1024 * 1024),
        cost_estimate=pl.CostEstimate(
            flops=planes * height * 256 * weight,
            bytes_accessed=planes * height * 256 * 5,
            transcendentals=0,
        ),
        name=f"march_{mode}",
    )(*tables, *operands)
    return out[0] if len(out) == 1 else out


def plane_halos(first, last):
    count = lax.axis_size("slab")
    forward = [(i, i + 1) for i in range(count - 1)]
    backward = [(i + 1, i) for i in range(count - 1)]
    return lax.ppermute(last, "slab", forward), lax.ppermute(first, "slab", backward)


def ordered(is_far, own, other):
    near = [jnp.where(is_far, b, a) for a, b in zip(own, other)]
    far = [jnp.where(is_far, a, b) for a, b in zip(own, other)]
    return [near[0] + near[1] * far[0], near[1] * far[1]]


def exchange(parts, own, shift):
    count = lax.axis_size("slab")
    merged = []
    for change, part in enumerate(parts):
        if change:
            part = lax.ppermute(part, "slab", [(i, i ^ change << shift) for i in range(count)])
        merged.append([part[:, :3], part[:, 3:]])
    digit = 0
    while len(merged) > 1:
        is_far = (own >> digit & 1) == 1
        merged = [ordered(is_far, merged[k], merged[k + 1]) for k in range(0, len(merged), 2)]
        digit += 1
    return merged[0]


def reduce_image(image, parts, slab_index, block_rows):
    slab_count = lax.axis_size("slab")
    levels = slab_count.bit_length() - 1
    if parts is None:
        image = image.reshape((6, slab_count, block_rows, image.shape[-1]))
        image = jnp.swapaxes(image, 0, 1)
    for shift in range(0, levels, 2):
        size = 1 << min(2, levels - shift)
        own = (slab_index >> shift) & (size - 1)
        if parts is None:
            image = image.reshape((-1, size) + image.shape[1:])
            parts = [
                lax.dynamic_index_in_dim(image, own ^ change, 1, keepdims=False)
                for change in range(size)
            ]
        colour, transmit = exchange(parts, own, shift)
        image, parts = jnp.concatenate([colour, transmit], axis=1), None
    return colour[0], 1.0 - transmit[0]


def per_device(field, tf_emission, tf_absorption):
    slab_count = lax.axis_size("slab")
    slab_index = lax.axis_index("slab")
    planes, height, width = field.shape
    depth_total = planes * slab_count
    block_rows = height // slab_count
    part_shape = None
    if slab_count >= 4 and block_rows % SUBLANES == 0:
        part_shape = (slab_count // 4, 4, block_rows)
    tables = (tf_emission, tf_absorption)

    def reduced(out):
        image, parts = (out, None) if part_shape is None else (None, out)
        return reduce_image(image, parts, slab_index, block_rows)

    halo = plane_halos(field[0], field[-1])
    middle, edge = march("middle", tables, field, None, None, None, depth_total, None)
    side = lax.ppermute(edge, "tile", [(0, 1), (1, 0)])
    rim = march("rim", tables, field, None, halo, middle, depth_total, part_shape)
    halo, side, _ = lax.optimization_barrier((halo, side, rim))
    outer = march("outer", tables, field, side, halo, None, depth_total, part_shape)
    first_core = lax.axis_index("tile") == 0
    return tuple(
        jnp.where(
            first_core,
            jnp.concatenate([wide, narrow], axis=2),
            jnp.concatenate([narrow, wide], axis=2),
        )
        for wide, narrow in zip(reduced(rim), reduced(outer))
    )


def solution(mesh):
    placed = (P("slab", None, "tile"), P(), P())
    return jax.shard_map(
        per_device,
        mesh=mesh,
        in_specs=placed,
        out_specs=(P(None, "slab", "tile"), P(None, "slab", "tile")),
        check_vma=False,
    )
```

time: 100 us -> 96.5 us (0.965)
  starting transfers between devices: 24.5 us -> 29.3 us
  waiting for transfers between devices: 19.3 us -> 15 us
  Pallas kernels: 51.6 us -> 47.8 us
    ppermute x12, starting transfers between devices: 18.2 us -> 23.1 us  [exchange(): lax.ppermute(part, 'slab', [(i, i ^ change << shift) for i in range(count)])]
    pallas_call x3, Pallas kernels: 51.6 us -> 47.8 us  [march(): pl.pallas_call(functools.partial(march_kernel, mode, depth_total, group),...]
    ppermute x1, waiting for transfers between devices: 1.94 us -> 0.01 us  [plane_halos(): lax.ppermute(first, 'slab', backward)]
    ppermute x12, waiting for transfers between devices: 16.7 us -> 15 us  [exchange(): lax.ppermute(part, 'slab', [(i, i ^ change << shift) for i in range(count)])]
    concatenate x2 -> x0, other arithmetic: 1.3 us -> none  [per_device(): jnp.concatenate([outer[:, :, :LANES], inner, outer[:, :, LANES:]], axis=2)]
  transfers between devices with their start and end apart: 15 -> 15, of which waited for: 6 -> 5; matrix products, arithmetic and copies ran while one was open for 0% -> 0% of each run, Pallas kernels for 52% -> 50%
where the time goes in v7:
time: 96.5 us; the launch traced here: 96.3 us
  Pallas kernels  47.8 us (50%)
  starting transfers between devices  29.3 us (30%)
  waiting for transfers between devices  15 us (16%)
  local copies, waits for them, and re-layouts  2.21 us (2%)
  other arithmetic  1.15 us (1%)
    pallas_call x3, Pallas kernels, march(): pl.pallas_call(functools.partial(march_kernel, mode, depth_total, group),...  47.8 us
    ppermute x12, starting transfers between devices, exchange(): lax.ppermute(part, 'slab', [(i, i ^ change << shift) for i in range(count)])  23.1 us
    ppermute x12, waiting for transfers between devices, exchange(): lax.ppermute(part, 'slab', [(i, i ^ change << shift) for i in range(count)])  15 us
    ppermute x1, starting transfers between devices, plane_halos(): lax.ppermute(last, 'slab', forward)  4.88 us
  transfers between devices with their start and end apart: 15, of which 5 were waited for; matrix products, arithmetic and copies ran while one was open for 0% of the time, Pallas kernels for 50%

profile of v7, /device:TPU:0, one launch (start us, length us, event | category | flops | bytes accessed | tf_op | source)
XLA Modules:
  0.0 96.3 jit_solution(12734564129418033137)
XLA Ops:
  0.6 1.3 %slice_bitcast_fusion = (f32[256,512]{1,0:T(8,128)S(1)}, f32[256,512]{1,0:T(8,128)S(1)}) fusion(f32[16,256,512]{2,1,0:T(8,128)} %refs_0_.5), kind=kLoop, calls=%fused_computation.8 | loop fusion | bytes 2097152 | tf_op jit(solution)/shard_map/squeeze | solution.py:341
  1.9 4.9 %collective-permute-start = (f32[256,512]{1,0:T(8,128)S(1)}, f32[256,512]{1,0:T(8,128)S(1)}, u32[]{:S(2)}, u32[]{:S(2)}) collective-permute-start(f32[256,512]{1,0:T(8,128)S(1)} %get-tuple-element.29), channel_id=1, source_target_pairs={{0,2},{2,4},{4,6},{6,8},{8,10},{10,12},{12,14},{14,16},{16,18},{18... | collective-permute-start | bytes 1572872 | tf_op jit(solution)/shard_map/ppermute | solution.py:282
  6.8 1.3 %collective-permute-start.1 = (f32[256,512]{1,0:T(8,128)S(1)}, f32[256,512]{1,0:T(8,128)S(1)}, u32[]{:S(2)}, u32[]{:S(2)}) collective-permute-start(f32[256,512]{1,0:T(8,128)S(1)} %get-tuple-element.28), channel_id=1, source_target_pairs={{2,0},{4,2},{6,4},{8,6},{10,8},{12,10},{14,12},{16,14},{18,16},{20... | collective-permute-start | bytes 1572872 | tf_op jit(solution)/shard_map/ppermute | solution.py:282
  8.1 24.7 %march_middle.1 = (f32[6,256,384]{2,1,0:T(8,128)}, f32[16,256,128]{2,1,0:T(8,128)}) custom-call(f32[3,16]{1,0:T(4,128)} %emission.5, f32[3,16]{1,0:T(4,128)} %absorption.5, f32[16,256,512]{2,1,0:T(8,128)} %refs_0_.5), custom_call_target="tpu_custom_call" | custom-call | flops 104857600 | bytes 5242880 | tf_op jit(solution)/shard_map/march_middle/pallas_call | solution.py:261
  32.8 0.1 collective-permute-start.8
  32.9 0.0 collective-permute-done.refs_1_.refs_2_
  32.9 0.0 copy-start.2
  32.9 0.0 collective-permute-done.1.refs_2_.refs_3_
  32.9 0.0 copy-start.3
  33.0 0.8 copy-done.2
  33.7 0.2 copy-done.3
  33.9 9.4 %march_rim.1 = (f32[4,6,16,384]{3,2,1,0:T(8,128)}, f32[4,6,16,384]{3,2,1,0:T(8,128)}, f32[4,6,16,384]{3,2,1,0:T(8,128)}, f32[4,6,16,384]{3,2,1,0:T(8,128)}) custom-call(f32[3,16]{1,0:T(4,128)} %emission.5, f32[3,16]{1,0:T(4,128)} %absorption.5, f32[16,256,512]{2,1,0:T(8,128)} %refs_0_.5, f32[256,512]{1,0:T(8,128)} %copy-done.2, f32[256,512]{1,0:T(8,128)} %copy-done.3, ...), custom_call_target="tpu_custom_call" | custom-call | flops 20971520000 | bytes 5242880 | tf_op jit(solution)/shard_map/march_rim/pallas_call | solution.py:261
  43.3 3.6 %collective-permute-start.2 = (f32[4,6,16,384]{3,2,1,0:T(8,128)}, f32[4,6,16,384]{3,2,1,0:T(8,128)S(1)}, u32[]{:S(2)}, u32[]{:S(2)}) collective-permute-start(f32[4,6,16,384]{3,2,1,0:T(8,128)} %get-tuple-element.16), channel_id=1, source_target_pairs={{0,6},{2,4},{4,2},{6,0},{8,14},{10,12},{12,10},{14,8},{16,22},{18,... | collective-permute-start | bytes 1769480 | tf_op jit(solution)/shard_map/ppermute | solution.py:296
  46.9 0.5 collective-permute-start.3
  47.4 0.9 collective-permute-start.4
  48.3 0.0 collective-permute-done.8.refs_1_
  48.3 0.0 copy-start
  48.3 13.7 %march_outer.1 = (f32[4,6,16,128]{3,2,1,0:T(8,128)}, f32[4,6,16,128]{3,2,1,0:T(8,128)}, f32[4,6,16,128]{3,2,1,0:T(8,128)}, f32[4,6,16,128]{3,2,1,0:T(8,128)}) custom-call(f32[3,16]{1,0:T(4,128)} %emission.5, f32[3,16]{1,0:T(4,128)} %absorption.5, f32[16,256,512]{2,1,0:T(8,128)} %refs_0_.5, f32[16,256,128]{2,1,0:T(8,128)} %collective-permute-done.8.refs_1_, ...), custom_call_target="tpu_custom_call" | custom-call | flops 20971520000 | bytes 5242880 | tf_op jit(solution)/shard_map/march_outer/pallas_call | solution.py:261
  62.1 0.0 copy-start.1
  62.1 2.1 %collective-permute-start.10 = (f32[4,6,16,128]{3,2,1,0:T(8,128)}, f32[4,6,16,128]{3,2,1,0:T(8,128)S(1)}, u32[]{:S(2)}, u32[]{:S(2)}) collective-permute-start(f32[4,6,16,128]{3,2,1,0:T(8,128)} %get-tuple-element.25), channel_id=1, source_target_pairs={{0,4},{2,6},{4,0},{6,2},{8,12},{10,14},{12,8},{14,10},{16,20},{18,... | collective-permute-start | bytes 589832 | tf_op jit(solution)/shard_map/ppermute | solution.py:296
  64.2 0.6 collective-permute-start.11
  64.8 0.0 collective-permute-done.2
  64.8 0.9 collective-permute-start.9
  65.7 8.3 %collective-permute-done.3 = f32[4,6,16,384]{3,2,1,0:T(8,128)S(1)} collective-permute-done((f32[4,6,16,384]{3,2,1,0:T(8,128)}, f32[4,6,16,384]{3,2,1,0:T(8,128)S(1)}, u32[]{:S(2)}, u32[]{:S(2)}) %collective-permute-start.3) | collective-permute-done | bytes 589856 | tf_op jit(solution)/shard_map/ppermute | solution.py:296
  74.0 1.3 %collective-permute-done.4 = f32[4,6,16,384]{3,2,1,0:T(8,128)S(1)} collective-permute-done((f32[4,6,16,384]{3,2,1,0:T(8,128)}, f32[4,6,16,384]{3,2,1,0:T(8,128)S(1)}, u32[]{:S(2)}, u32[]{:S(2)}) %collective-permute-start.4) | collective-permute-done | bytes 589856 | tf_op jit(solution)/shard_map/ppermute | solution.py:296
  75.3 0.0 copy-done
  75.3 0.2 select_multiply_fusion
  75.5 0.1 fusion.1
  75.6 4.1 %collective-permute-start.5 = (f32[1,6,16,384]{3,2,1,0:T(8,128)S(1)}, f32[1,6,16,384]{3,2,1,0:T(8,128)S(1)}, u32[]{:S(2)}, u32[]{:S(2)}) collective-permute-start(f32[1,6,16,384]{3,2,1,0:T(8,128)S(1)} %get-tuple-element.36), channel_id=1, source_target_pairs={{0,24},{2,26},{4,28},{6,30},{8,16},{10,18},{12,20},{14,22},{16,8},... | collective-permute-start | bytes 442376 | tf_op jit(solution)/shard_map/ppermute | solution.py:296
  79.7 0.0 collective-permute-start.6
  79.7 0.0 collective-permute-done.10
  79.7 1.2 %collective-permute-start.7 = (f32[1,6,16,384]{3,2,1,0:T(8,128)S(1)}, f32[1,6,16,384]{3,2,1,0:T(8,128)S(1)}, u32[]{:S(2)}, u32[]{:S(2)}) collective-permute-start(f32[1,6,16,384]{3,2,1,0:T(8,128)S(1)} %get-tuple-element.38), channel_id=1, source_target_pairs={{0,8},{2,10},{4,12},{6,14},{8,0},{10,2},{12,4},{14,6},{16,24},{18,... | collective-permute-start | bytes 442376 | tf_op jit(solution)/shard_map/ppermute | solution.py:296
  80.9 0.0 collective-permute-done.11
  81.0 1.2 %collective-permute-done.9 = f32[4,6,16,128]{3,2,1,0:T(8,128)S(1)} collective-permute-done((f32[4,6,16,128]{3,2,1,0:T(8,128)}, f32[4,6,16,128]{3,2,1,0:T(8,128)S(1)}, u32[]{:S(2)}, u32[]{:S(2)}) %collective-permute-start.9) | collective-permute-done | bytes 196640 | tf_op jit(solution)/shard_map/ppermute | solution.py:296
  82.2 0.0 copy-done.1
  82.2 0.1 select_multiply_fusion.3
  82.3 5.7 %collective-permute-start.12 = (f32[1,6,16,128]{3,2,1,0:T(8,128)S(1)}, f32[1,6,16,128]{3,2,1,0:T(8,128)S(1)}, u32[]{:S(2)}, u32[]{:S(2)}) collective-permute-start(f32[1,6,16,128]{3,2,1,0:T(8,128)S(1)} %get-tuple-element.42), channel_id=1, source_target_pairs={{0,24},{2,26},{4,28},{6,30},{8,16},{10,18},{12,20},{14,22},{16,8},... | collective-permute-start | bytes 147464 | tf_op jit(solution)/shard_map/ppermute | solution.py:296
  87.9 0.0 collective-permute-start.13
  87.9 0.0 collective-permute-done.5
  87.9 3.4 %collective-permute-start.14 = (f32[1,6,16,128]{3,2,1,0:T(8,128)S(1)}, f32[1,6,16,128]{3,2,1,0:T(8,128)S(1)}, u32[]{:S(2)}, u32[]{:S(2)}) collective-permute-start(f32[1,6,16,128]{3,2,1,0:T(8,128)S(1)} %get-tuple-element.44), channel_id=1, source_target_pairs={{0,8},{2,10},{4,12},{6,14},{8,0},{10,2},{12,4},{14,6},{16,24},{18,... | collective-permute-start | bytes 147464 | tf_op jit(solution)/shard_map/ppermute | solution.py:296
  91.3 3.2 %collective-permute-done.6 = f32[1,6,16,384]{3,2,1,0:T(8,128)S(1)} collective-permute-done((f32[1,6,16,384]{3,2,1,0:T(8,128)S(1)}, f32[1,6,16,384]{3,2,1,0:T(8,128)S(1)}, u32[]{:S(2)}, u32[]{:S(2)}) %collective-permute-start.6) | collective-permute-done | bytes 147488 | tf_op jit(solution)/shard_map/ppermute | solution.py:296
  94.5 0.0 collective-permute-done.7
  94.5 0.1 subtract_bitcast_fusion
  94.6 0.0 collective-permute-done.12
  94.6 0.9 collective-permute-done.13
  95.5 0.0 collective-permute-done.14
  95.6 0.7 maximum_select_fusion
  (2 shorter events, 0.1 us)
Async XLA Ops:
  1.9 31.0 %collective-permute-start = (f32[256,512]{1,0:T(8,128)S(1)}, f32[256,512]{1,0:T(8,128)S(1)}, u32[]{:S(2)}, u32[]{:S(2)}) collective-permute-start(f32[256,512]{1,0:T(8,128)S(1)} %get-tuple-element.29), channel_id=1, source_target_pairs={{0,2},{2,4},{4,6},{6,8},{8,10},{10,12},{12,14},{14,16},{16,18},{18... | collective-permute-start | bytes 1572872 | tf_op jit(solution)/shard_map/ppermute | solution.py:282
  6.8 26.2 %collective-permute-start.1 = (f32[256,512]{1,0:T(8,128)S(1)}, f32[256,512]{1,0:T(8,128)S(1)}, u32[]{:S(2)}, u32[]{:S(2)}) collective-permute-start(f32[256,512]{1,0:T(8,128)S(1)} %get-tuple-element.28), channel_id=1, source_target_pairs={{2,0},{4,2},{6,4},{8,6},{10,8},{12,10},{14,12},{16,14},{18,16},{20... | collective-permute-start | bytes 1572872 | tf_op jit(solution)/shard_map/ppermute | solution.py:282
  32.8 15.5 %collective-permute-start.8 = (f32[16,256,128]{2,1,0:T(8,128)}, f32[16,256,128]{2,1,0:T(8,128)}, u32[]{:S(2)}, u32[]{:S(2)}) collective-permute-start(f32[16,256,128]{2,1,0:T(8,128)} %get-tuple-element.20), channel_id=1, source_target_pairs={{0,1},{1,0},{2,3},{3,2},{4,5},{5,4},{6,7},{7,6},{8,9},{9,8},{10,11... | collective-permute-start | bytes 6291464 | tf_op jit(solution)/shard_map/ppermute | solution.py:343
  32.9 0.8 copy-start.2
  32.9 0.9 copy-start.3
  43.3 21.5 %collective-permute-start.2 = (f32[4,6,16,384]{3,2,1,0:T(8,128)}, f32[4,6,16,384]{3,2,1,0:T(8,128)S(1)}, u32[]{:S(2)}, u32[]{:S(2)}) collective-permute-start(f32[4,6,16,384]{3,2,1,0:T(8,128)} %get-tuple-element.16), channel_id=1, source_target_pairs={{0,6},{2,4},{4,2},{6,0},{8,14},{10,12},{12,10},{14,8},{16,22},{18,... | collective-permute-start | bytes 1769480 | tf_op jit(solution)/shard_map/ppermute | solution.py:296
  46.9 27.1 %collective-permute-start.3 = (f32[4,6,16,384]{3,2,1,0:T(8,128)}, f32[4,6,16,384]{3,2,1,0:T(8,128)S(1)}, u32[]{:S(2)}, u32[]{:S(2)}) collective-permute-start(f32[4,6,16,384]{3,2,1,0:T(8,128)} %get-tuple-element.17), channel_id=1, source_target_pairs={{0,4},{2,6},{4,0},{6,2},{8,12},{10,14},{12,8},{14,10},{16,20},{18,... | collective-permute-start | bytes 1769480 | tf_op jit(solution)/shard_map/ppermute | solution.py:296
  47.4 27.9 %collective-permute-start.4 = (f32[4,6,16,384]{3,2,1,0:T(8,128)}, f32[4,6,16,384]{3,2,1,0:T(8,128)S(1)}, u32[]{:S(2)}, u32[]{:S(2)}) collective-permute-start(f32[4,6,16,384]{3,2,1,0:T(8,128)} %get-tuple-element.18), channel_id=1, source_target_pairs={{0,2},{2,0},{4,6},{6,4},{8,10},{10,8},{12,14},{14,12},{16,18},{18,... | collective-permute-start | bytes 1769480 | tf_op jit(solution)/shard_map/ppermute | solution.py:296
  48.3 27.0 %copy-start = (f32[4,6,16,384]{3,2,1,0:T(8,128)S(1)}, f32[4,6,16,384]{3,2,1,0:T(8,128)}, u32[]{:S(2)}) copy-start(f32[4,6,16,384]{3,2,1,0:T(8,128)} %get-tuple-element.19) | copy-start | bytes 1769476
  62.1 20.1 %copy-start.1 = (f32[4,6,16,128]{3,2,1,0:T(8,128)S(1)}, f32[4,6,16,128]{3,2,1,0:T(8,128)}, u32[]{:S(2)}) copy-start(f32[4,6,16,128]{3,2,1,0:T(8,128)} %get-tuple-element.27) | copy-start | bytes 589828
  62.1 17.6 %collective-permute-start.10 = (f32[4,6,16,128]{3,2,1,0:T(8,128)}, f32[4,6,16,128]{3,2,1,0:T(8,128)S(1)}, u32[]{:S(2)}, u32[]{:S(2)}) collective-permute-start(f32[4,6,16,128]{3,2,1,0:T(8,128)} %get-tuple-element.25), channel_id=1, source_target_pairs={{0,4},{2,6},{4,0},{6,2},{8,12},{10,14},{12,8},{14,10},{16,20},{18,... | collective-permute-start | bytes 589832 | tf_op jit(solution)/shard_map/ppermute | solution.py:296
  64.2 16.8 %collective-permute-start.11 = (f32[4,6,16,128]{3,2,1,0:T(8,128)}, f32[4,6,16,128]{3,2,1,0:T(8,128)S(1)}, u32[]{:S(2)}, u32[]{:S(2)}) collective-permute-start(f32[4,6,16,128]{3,2,1,0:T(8,128)} %get-tuple-element.26), channel_id=1, source_target_pairs={{0,2},{2,0},{4,6},{6,4},{8,10},{10,8},{12,14},{14,12},{16,18},{18,... | collective-permute-start | bytes 589832 | tf_op jit(solution)/shard_map/ppermute | solution.py:296
  64.8 17.4 %collective-permute-start.9 = (f32[4,6,16,128]{3,2,1,0:T(8,128)}, f32[4,6,16,128]{3,2,1,0:T(8,128)S(1)}, u32[]{:S(2)}, u32[]{:S(2)}) collective-permute-start(f32[4,6,16,128]{3,2,1,0:T(8,128)} %get-tuple-element.24), channel_id=1, source_target_pairs={{0,6},{2,4},{4,2},{6,0},{8,14},{10,12},{12,10},{14,8},{16,22},{18,... | collective-permute-start | bytes 589832 | tf_op jit(solution)/shard_map/ppermute | solution.py:296
  75.6 12.3 %collective-permute-start.5 = (f32[1,6,16,384]{3,2,1,0:T(8,128)S(1)}, f32[1,6,16,384]{3,2,1,0:T(8,128)S(1)}, u32[]{:S(2)}, u32[]{:S(2)}) collective-permute-start(f32[1,6,16,384]{3,2,1,0:T(8,128)S(1)} %get-tuple-element.36), channel_id=1, source_target_pairs={{0,24},{2,26},{4,28},{6,30},{8,16},{10,18},{12,20},{14,22},{16,8},... | collective-permute-start | bytes 442376 | tf_op jit(solution)/shard_map/ppermute | solution.py:296
  79.7 14.8 %collective-permute-start.6 = (f32[1,6,16,384]{3,2,1,0:T(8,128)S(1)}, f32[1,6,16,384]{3,2,1,0:T(8,128)S(1)}, u32[]{:S(2)}, u32[]{:S(2)}) collective-permute-start(f32[1,6,16,384]{3,2,1,0:T(8,128)S(1)} %get-tuple-element.37), channel_id=1, source_target_pairs={{0,16},{2,18},{4,20},{6,22},{8,24},{10,26},{12,28},{14,30},{16,0},... | collective-permute-start | bytes 442376 | tf_op jit(solution)/shard_map/ppermute | solution.py:296
  79.7 14.8 %collective-permute-start.7 = (f32[1,6,16,384]{3,2,1,0:T(8,128)S(1)}, f32[1,6,16,384]{3,2,1,0:T(8,128)S(1)}, u32[]{:S(2)}, u32[]{:S(2)}) collective-permute-start(f32[1,6,16,384]{3,2,1,0:T(8,128)S(1)} %get-tuple-element.38), channel_id=1, source_target_pairs={{0,8},{2,10},{4,12},{6,14},{8,0},{10,2},{12,4},{14,6},{16,24},{18,... | collective-permute-start | bytes 442376 | tf_op jit(solution)/shard_map/ppermute | solution.py:296
  82.3 12.3 %collective-permute-start.12 = (f32[1,6,16,128]{3,2,1,0:T(8,128)S(1)}, f32[1,6,16,128]{3,2,1,0:T(8,128)S(1)}, u32[]{:S(2)}, u32[]{:S(2)}) collective-permute-start(f32[1,6,16,128]{3,2,1,0:T(8,128)S(1)} %get-tuple-element.42), channel_id=1, source_target_pairs={{0,24},{2,26},{4,28},{6,30},{8,16},{10,18},{12,20},{14,22},{16,8},... | collective-permute-start | bytes 147464 | tf_op jit(solution)/shard_map/ppermute | solution.py:296
  87.9 7.6 %collective-permute-start.13 = (f32[1,6,16,128]{3,2,1,0:T(8,128)S(1)}, f32[1,6,16,128]{3,2,1,0:T(8,128)S(1)}, u32[]{:S(2)}, u32[]{:S(2)}) collective-permute-start(f32[1,6,16,128]{3,2,1,0:T(8,128)S(1)} %get-tuple-element.43), channel_id=1, source_target_pairs={{0,16},{2,18},{4,20},{6,22},{8,24},{10,26},{12,28},{14,30},{16,0},... | collective-permute-start | bytes 147464 | tf_op jit(solution)/shard_map/ppermute | solution.py:296
  87.9 7.6 %collective-permute-start.14 = (f32[1,6,16,128]{3,2,1,0:T(8,128)S(1)}, f32[1,6,16,128]{3,2,1,0:T(8,128)S(1)}, u32[]{:S(2)}, u32[]{:S(2)}) collective-permute-start(f32[1,6,16,128]{3,2,1,0:T(8,128)S(1)} %get-tuple-element.44), channel_id=1, source_target_pairs={{0,8},{2,10},{4,12},{6,14},{8,0},{10,2},{12,4},{14,6},{16,24},{18,... | collective-permute-start | bytes 147464 | tf_op jit(solution)/shard_map/ppermute | solution.py:296

commit v8 on v7

--- a/solution.py
+++ b/solution.py
@@ -58,8 +58,9 @@
     field = refs.pop(0)
     side = refs.pop(0) if mode == "outer" else None
     low, high = (refs.pop(0), refs.pop(0)) if mode != "middle" else (None, None)
-    middle = refs.pop(0) if mode == "rim" else None
-    inner = refs.pop() if mode == "rim" else None
+    rim = mode in ("rim", "inner rim")
+    middle = refs.pop(0) if rim else None
+    inner = refs.pop() if rim else None
     cells, canvas, table, words, factors, in_sems, out_sems = refs[-7:]
     outs = refs[:-7]
     edge = outs.pop() if mode == "middle" else None
@@ -69,16 +70,20 @@
     pieces = height // piece_rows
     core = lax.axis_index("tile")
     tiles = cells.shape[0] - 2
-    blocks = [(0, 1, planes)] if mode != "rim" else [(0, 1, 2), (planes - 2, 3, 2)]
-    marched = {
-        "outer": range(planes), "middle": range(1, planes - 1), "rim": (0, planes - 1)
-    }[mode]
+    computed = (1, tiles) if mode == "rim" else range(1, tiles + 1)
+    blocks = [(0, 1, 2), (planes - 2, 3, 2)] if rim else [(0, 1, planes)]
+    if rim:
+        marched = (0, planes - 1)
+    else:
+        marched = range(1, planes - 1) if mode == "middle" else range(planes)
     place = {first + k: slot + k for first, slot, count in blocks for k in range(count)}
     place[-1] = 0
     place[planes] = max(place.values()) + 1
     far = (1 - core) * (tiles + 1)
     if mode == "outer":
         first_lane_taken, first_tile, taken = (1 - core) * (width - 2 * LANES), core, 2
+    elif mode == "inner rim":
+        first_lane_taken, first_tile, taken = core * LANES, 0, tiles + 2
     else:
         first_lane_taken, first_tile, taken = 0, 1 - core, width // LANES
 
@@ -96,8 +101,12 @@
             if mode != "middle":
                 for halo, plane in ((low, -1), (high, planes)):
                     pairs.append((halo.at[body, lanes], held.at[place[plane], padded, :]))
-        if mode == "rim":
-            pairs.append((middle.at[:, body, :], inner.at[:, body, :]))
+        if rim:
+            skipped = 1 if mode == "inner rim" else 0
+            for at, tile in enumerate(computed):
+                lanes = pl.ds((tile - 1 + skipped) * LANES, LANES)
+                held = inner.at[:, body, pl.ds(at * LANES, LANES)]
+                pairs.append((middle.at[:, body, lanes], held))
         if mode == "outer":
             pairs.append((side.at[:, body, :], cells.at[far, pl.ds(1, planes), padded, :]))
         return [
@@ -108,11 +117,10 @@
     def outgoing(piece):
         start = pl.multiple_of(piece * piece_rows, SUBLANES)
         body = pl.ds(start, piece_rows)
-        if len(outs) == 1:
+        if not group:
             pairs = [(canvas.at[:, body, :], outs[0].at[:, body, :])]
         else:
-            own = lax.axis_index("slab") & (group - 1)
-            pairs = [(canvas.at[piece, own ^ k], outs[k].at[piece]) for k in range(group)]
+            pairs = [(canvas.at[piece], outs[0].at[:, piece])]
         if edge is not None:
             padded = pl.ds(start + PAD, piece_rows)
             pairs.append((cells.at[far, pl.ds(1, planes), padded, :], edge.at[:, body, :]))
@@ -129,15 +137,15 @@
         for copy in incoming(piece):
             copy.wait()
 
-    for piece in range(min(3, pieces)):
+    for piece in range(min(2, pieces)):
         start(piece)
     prepare_tables(emission, absorption, depth_total, table, words, factors)
     zeros = jnp.zeros((1, LANES), jnp.float32)
-    for tile in range(1, tiles + 1):
+    for tile in computed:
         for plane in marched:
             cells[tile, place[plane], pl.ds(PAD - 1, 1), :] = zeros
             cells[tile, place[plane], pl.ds(PAD + height, 1), :] = zeros
-    if mode != "outer":
+    if mode in ("middle", "rim"):
         blank = jnp.zeros((height, LANES), jnp.float32)
         for plane in marched:
             cells[core * (tiles + 1), place[plane], pl.ds(PAD, height), :] = blank
@@ -146,20 +154,20 @@
     first_lane = lane == 0
     last_lane = lane == LANES - 1
 
-    def strip(at, piece, number):
+    def strip(at, tile, piece, number):
         row = pl.multiple_of(piece * piece_rows + number * SUBLANES, SUBLANES)
 
         def rows(tile, plane, offset=0):
             here = pl.ds(row + PAD + offset, SUBLANES)
-            return cells[tile + 1, place[plane], here, :]
+            return cells[tile, place[plane], here, :]
 
         colour = transmit = None
         for plane in marched:
-            before, centre, after = (rows(at, plane + k) for k in (-1, 0, 1))
-            left = pltpu.roll(jnp.where(last_lane, rows(at - 1, plane), centre), 1, 1)
-            right = pltpu.roll(jnp.where(first_lane, rows(at + 1, plane), centre), LANES - 1, 1)
+            before, centre, after = (rows(tile, plane + k) for k in (-1, 0, 1))
+            left = pltpu.roll(jnp.where(last_lane, rows(tile - 1, plane), centre), 1, 1)
+            right = pltpu.roll(jnp.where(first_lane, rows(tile + 1, plane), centre), LANES - 1, 1)
             diff_x = right - left
-            diff_y = rows(at, plane, 1) - rows(at, plane, -1)
+            diff_y = rows(tile, plane, 1) - rows(tile, plane, -1)
             diff_z = after - before
             inverse = lax.rsqrt(diff_x * diff_x + diff_y * diff_y + diff_z * diff_z + 1.0)
             facing = (factors[0] * diff_x + factors[1] * diff_y + factors[2] * diff_z) * inverse
@@ -182,7 +190,7 @@
                 seen = [transmit[ch] * steps[ch] for ch in range(3)]
                 colour = [colour[ch] + seen[ch] * glows[ch] for ch in range(3)]
                 transmit = [transmit[ch] - seen[ch] for ch in range(3)]
-            if mode == "rim" and plane == 0:
+            if rim and plane == 0:
                 held = [
                     inner[k, pl.ds(row, SUBLANES), pl.ds(at * LANES, LANES)] for k in range(6)
                 ]
@@ -190,7 +198,7 @@
                 transmit = [transmit[ch] * held[3 + ch] for ch in range(3)]
         here = pl.ds(at * LANES, LANES)
         for k, value in enumerate(colour + transmit):
-            if len(outs) == 1:
+            if not group:
                 canvas[k, pl.ds(row, SUBLANES), here] = value
             else:
                 block_rows = canvas.shape[3]
@@ -202,18 +210,18 @@
 
     @pl.loop(0, pieces)
     def _(piece):
-        @pl.when(piece + 3 < pieces)
+        @pl.when(piece + 2 < pieces)
         def _():
-            start(piece + 3)
-
-        @pl.when(piece + 1 < pieces)
-        def _():
-            await_piece(piece + 1)
+            start(piece + 2)
 
         @pl.loop(0, piece_rows // SUBLANES)
         def _(number):
-            for at in range(tiles):
-                strip(at, piece, number)
+            @pl.when((number == piece_rows // SUBLANES - 1) & (piece + 1 < pieces))
+            def _():
+                await_piece(piece + 1)
+
+            for at, tile in enumerate(computed):
+                strip(at, tile, piece, number)
 
         for copy in outgoing(piece):
             copy.start()
@@ -226,51 +234,53 @@
 
 def march(mode, tables, field, side, halos, middle, depth_total, part_shape):
     planes, height, width = field.shape
-    extent = LANES if mode == "outer" else width - LANES
-    marched = {"outer": planes, "middle": planes - 2, "rim": 2}[mode]
-    held = 6 if mode == "rim" else planes + 2
+    rim = mode in ("rim", "inner rim")
+    tiles = width // LANES - 1
+    tiles_held = {"outer": 3, "inner rim": tiles}.get(mode, tiles + 2)
+    extent = {"outer": 1, "rim": 2, "inner rim": tiles - 2, "middle": tiles}[mode] * LANES
+    held = 6 if rim else planes + 2
     if part_shape is None:
-        group, pieces = 1, max(1, height // 64)
+        group, pieces = 0, max(1, height // 64)
         outs = [jax.ShapeDtypeStruct((6, height, extent), jnp.float32)]
         canvas = (6, height, extent)
     else:
         pieces, group, rows = part_shape
-        outs = [jax.ShapeDtypeStruct((pieces, 6, rows, extent), jnp.float32)] * group
+        outs = [jax.ShapeDtypeStruct((group, pieces, 6, rows, extent), jnp.float32)]
         canvas = (pieces, group, 6, rows, extent)
     scratch = [
-        pltpu.VMEM((extent // LANES + 2, held, height + 2 * PAD, LANES), jnp.float32),
+        pltpu.VMEM((tiles_held, held, height + 2 * PAD, LANES), jnp.float32),
         pltpu.VMEM(canvas, jnp.float32),
         pltpu.VMEM((SUBLANES, LANES), jnp.float32),
         pltpu.VMEM((6, SUBLANES, LANES), jnp.int32),
         pltpu.VMEM((6, SUBLANES, LANES), jnp.float32),
-        pltpu.SemaphoreType.DMA((pieces, 4 * (width // LANES) + 1)),
-        pltpu.SemaphoreType.DMA((pieces, group + 1)),
+        pltpu.SemaphoreType.DMA((pieces, 4 * tiles_held + 2)),
+        pltpu.SemaphoreType.DMA((pieces, 2)),
     ]
     operands = [field]
     if mode == "outer":
         operands.append(side)
     if mode != "middle":
         operands += list(halos)
-    if mode == "rim":
+    if rim:
         operands.append(middle)
         scratch.append(pltpu.VMEM((6, height, extent), jnp.float32))
     if mode == "middle":
         outs.append(jax.ShapeDtypeStruct((planes, height, LANES), jnp.float32))
     weight = 100 if mode == "middle" else 20000
-    distant = pl.BlockSpec(memory_space=pltpu.HBM)
+    distant = pl.BlockSpec(memory_space=pl.ANY)
     out = pl.pallas_call(
         functools.partial(march_kernel, mode, depth_total, group),
         out_shape=outs,
         in_specs=[pl.BlockSpec(memory_space=pltpu.VMEM)] * 2 + [distant] * len(operands),
         out_specs=[distant] * len(outs),
         scratch_shapes=scratch,
-        compiler_params=pltpu.CompilerParams(vmem_limit_bytes=60 * 1024 * 1024),
+        compiler_params=pltpu.CompilerParams(vmem_limit_bytes=56 * 1024 * 1024),
         cost_estimate=pl.CostEstimate(
             flops=planes * height * 256 * weight,
             bytes_accessed=planes * height * 256 * 5,
             transcendentals=0,
         ),
-        name=f"march_{mode}",
+        name="march_" + mode.replace(" ", "_"),
     )(*tables, *operands)
     return out[0] if len(out) == 1 else out
 
@@ -282,50 +292,39 @@
     return lax.ppermute(last, "slab", forward), lax.ppermute(first, "slab", backward)
 
 
-def ordered(is_far, own, other):
-    near = [jnp.where(is_far, b, a) for a, b in zip(own, other)]
-    far = [jnp.where(is_far, a, b) for a, b in zip(own, other)]
-    return [near[0] + near[1] * far[0], near[1] * far[1]]
-
-
-def exchange(parts, own, shift):
-    count = lax.axis_size("slab")
-    merged = []
-    for change, part in enumerate(parts):
-        if change:
-            part = lax.ppermute(part, "slab", [(i, i ^ change << shift) for i in range(count)])
-        merged.append([part[:, :3], part[:, 3:]])
-    digit = 0
-    while len(merged) > 1:
-        is_far = (own >> digit & 1) == 1
-        merged = [ordered(is_far, merged[k], merged[k + 1]) for k in range(0, len(merged), 2)]
-        digit += 1
-    return merged[0]
-
-
-def reduce_image(image, parts, slab_index, block_rows):
+def composite(parts):
+    total = parts[-1]
+    for k in range(parts.shape[0] - 2, -1, -1):
+        colour, transmit = parts[k, :, :3], parts[k, :, 3:]
+        total = jnp.concatenate(
+            [colour + transmit * total[:, :3], transmit * total[:, 3:]], axis=1
+        )
+    return total
+
+
+def reduce_image(image, split, block_rows):
     slab_count = lax.axis_size("slab")
     levels = slab_count.bit_length() - 1
-    if parts is None:
+    if not split:
         image = image.reshape((6, slab_count, block_rows, image.shape[-1]))
         image = jnp.swapaxes(image, 0, 1)
     for shift in range(0, levels, 2):
         size = 1 << min(2, levels - shift)
-        own = (slab_index >> shift) & (size - 1)
-        if parts is None:
+        if shift or not split:
             image = image.reshape((-1, size) + image.shape[1:])
-            parts = [
-                lax.dynamic_index_in_dim(image, own ^ change, 1, keepdims=False)
-                for change in range(size)
-            ]
-        colour, transmit = exchange(parts, own, shift)
-        image, parts = jnp.concatenate([colour, transmit], axis=1), None
-    return colour[0], 1.0 - transmit[0]
+            image = jnp.moveaxis(image, 1, 0)
+        groups = [
+            [i + (k << shift) for k in range(size)]
+            for i in range(slab_count)
+            if not i >> shift & (size - 1)
+        ]
+        image = lax.all_to_all(image, "slab", 0, 0, axis_index_groups=groups)
+        image = composite(image)
+    return image[0, :3], 1.0 - image[0, 3:]
 
 
 def per_device(field, tf_emission, tf_absorption):
     slab_count = lax.axis_size("slab")
-    slab_index = lax.axis_index("slab")
     planes, height, width = field.shape
     depth_total = planes * slab_count
     block_rows = height // slab_count
@@ -334,25 +333,27 @@
         part_shape = (slab_count // 4, 4, block_rows)
     tables = (tf_emission, tf_absorption)
 
-    def reduced(out):
-        image, parts = (out, None) if part_shape is None else (None, out)
-        return reduce_image(image, parts, slab_index, block_rows)
-
     halo = plane_halos(field[0], field[-1])
     middle, edge = march("middle", tables, field, None, None, None, depth_total, None)
     side = lax.ppermute(edge, "tile", [(0, 1), (1, 0)])
-    rim = march("rim", tables, field, None, halo, middle, depth_total, part_shape)
-    halo, side, _ = lax.optimization_barrier((halo, side, rim))
-    outer = march("outer", tables, field, side, halo, None, depth_total, part_shape)
+    results = []
+    for mode in ("inner rim", "rim", "outer"):
+        if results:
+            halo, side, _ = lax.optimization_barrier((halo, side, out))
+        out = march(mode, tables, field, side, halo, middle, depth_total, part_shape)
+        results.append(reduce_image(out, part_shape is not None, block_rows))
     first_core = lax.axis_index("tile") == 0
-    return tuple(
-        jnp.where(
-            first_core,
-            jnp.concatenate([wide, narrow], axis=2),
-            jnp.concatenate([narrow, wide], axis=2),
+    gathered = []
+    for inner, ends, outer in zip(*results):
+        wide = [ends[:, :, :LANES], inner, ends[:, :, LANES:]]
+        gathered.append(
+            jnp.where(
+                first_core,
+                jnp.concatenate(wide + [outer], axis=2),
+                jnp.concatenate([outer] + wide, axis=2),
+            )
         )
-        for wide, narrow in zip(reduced(rim), reduced(outer))
-    )
+    return tuple(gathered)
 
 
 def solution(mesh):

time: 96.5 us -> 146 us (1.51)
  blocking collectives: 0 us -> 31.1 us
  waiting for transfers between devices: 15 us -> 31.3 us
  starting transfers between devices: 29.3 us -> 24.1 us
  Pallas kernels: 47.8 us -> 52.6 us
  other arithmetic: 1.15 us -> 3.18 us
    all_to_all x0 -> x4, waiting for transfers between devices: none -> 31.3 us  [reduce_image(): image = lax.all_to_all(image, 'slab', 0, 0, axis_index_groups=groups)]
    all_to_all x0 -> x2, blocking collectives: none -> 31.1 us  [reduce_image(): image = lax.all_to_all(image, 'slab', 0, 0, axis_index_groups=groups)]
    ppermute x12 -> x0, starting transfers between devices: 23.1 us -> none  [exchange(): lax.ppermute(part, 'slab', [(i, i ^ change << shift) for i in range(count)])]
    all_to_all x0 -> x4, starting transfers between devices: none -> 17.9 us  [reduce_image(): image = lax.all_to_all(image, 'slab', 0, 0, axis_index_groups=groups)]
    ppermute x12 -> x0, waiting for transfers between devices: 15 us -> none  [exchange(): lax.ppermute(part, 'slab', [(i, i ^ change << shift) for i in range(count)])]
    pallas_call x3 -> x4, Pallas kernels: 47.8 us -> 52.6 us  [march(): pl.pallas_call(functools.partial(march_kernel, mode, depth_total, group),...]
    another operation x0 -> x3, other arithmetic: none -> 2.16 us  [reduce_image(): image = jnp.moveaxis(image, 1, 0)]
  transfers between devices with their start and end apart: 15 -> 7, of which waited for: 5 -> 3; matrix products, arithmetic and copies ran while one was open for 0% -> 2% of each run, Pallas kernels for 50% -> 36%
where the time goes in v8:
time: 146 us; the launch traced here: 145 us
  Pallas kernels  52.6 us (36%)
  waiting for transfers between devices  31.3 us (21%)
  blocking collectives  31.1 us (21%)
  starting transfers between devices  24.1 us (17%)
  other arithmetic  3.18 us (2%)
  local copies, waits for them, and re-layouts  2.33 us (2%)
    pallas_call x4, Pallas kernels, march(): pl.pallas_call(functools.partial(march_kernel, mode, depth_total, group),...  52.6 us
    all_to_all x4, waiting for transfers between devices, reduce_image(): image = lax.all_to_all(image, 'slab', 0, 0, axis_index_groups=groups)  31.3 us
    all_to_all x2, blocking collectives, reduce_image(): image = lax.all_to_all(image, 'slab', 0, 0, axis_index_groups=groups)  31.1 us
    all_to_all x4, starting transfers between devices, reduce_image(): image = lax.all_to_all(image, 'slab', 0, 0, axis_index_groups=groups)  17.9 us
    ppermute x1, starting transfers between devices, plane_halos(): lax.ppermute(last, 'slab', forward)  4.88 us
  transfers between devices with their start and end apart: 7, of which 3 were waited for; matrix products, arithmetic and copies ran while one was open for 2% of the time, Pallas kernels for 36%

profile of v8, /device:TPU:0, one launch (start us, length us, event | category | flops | bytes accessed | tf_op | source)
XLA Modules:
  0.0 145.4 jit_solution(14145688204134129542)
XLA Ops:
  0.6 1.3 slice_bitcast_fusion
  1.9 4.9 %collective-permute-start = (f32[256,512]{1,0:T(8,128)S(1)}, f32[256,512]{1,0:T(8,128)S(1)}, u32[]{:S(2)}, u32[]{:S(2)}) collective-permute-start(f32[256,512]{1,0:T(8,128)S(1)} %get-tuple-element.19), channel_id=1, source_target_pairs={{0,2},{2,4},{4,6},{6,8},{8,10},{10,12},{12,14},{14,16},{16,18},{18... | collective-permute-start | bytes 1572872 | tf_op jit(solution)/shard_map/ppermute | solution.py:292
  6.8 1.3 collective-permute-start.1
  8.1 24.2 %march_middle.1 = (f32[6,256,384]{2,1,0:T(8,128)}, f32[16,256,128]{2,1,0:T(8,128)}) custom-call(f32[3,16]{1,0:T(4,128)} %emission.7, f32[3,16]{1,0:T(4,128)} %absorption.7, f32[16,256,512]{2,1,0:T(8,128)} %refs_0_.7), custom_call_target="tpu_custom_call" | custom-call | flops 104857600 | bytes 5242880 | tf_op jit(solution)/shard_map/march_middle/pallas_call | solution.py:271
  32.3 0.1 collective-permute-start.2
  32.4 0.0 collective-permute-done.refs_1_.refs_2_
  32.4 0.0 copy-start.1
  32.4 0.0 collective-permute-done.1.refs_2_.refs_3_
  32.4 0.0 copy-start.2
  32.4 0.8 copy-done.1
  33.2 0.2 copy-done.2
  33.4 6.9 %march_inner_rim.1 = f32[4,4,6,16,128]{4,3,2,1,0:T(8,128)} custom-call(f32[3,16]{1,0:T(4,128)} %emission.7, f32[3,16]{1,0:T(4,128)} %absorption.7, f32[16,256,512]{2,1,0:T(8,128)} %refs_0_.7, f32[256,512]{1,0:T(8,128)} %copy-done.1, f32[256,512]{1,0:T(8,128)} %copy-done.2, f32[6,256,384]{2,1,0:T(8,128)} %get-tuple-element.11.refs_3_), custom_call_target="tpu_custom_call" | custom-call | flops 20971520000 | bytes 5242880 | tf_op jit(solution)/shard_map/march_inner_rim/pallas_call | solution.py:271
  40.3 17.0 %all_to_all.30 = f32[4,4,6,16,128]{4,3,2,1,0:T(8,128)S(1)} all-to-all(f32[4,4,6,16,128]{4,3,2,1,0:T(8,128)} %march_inner_rim.1), channel_id=1, replica_groups={{0,2,4,6},{8,10,12,14},{16,18,20,22},{24,26,28,30},{1,3,5,7},{9,11,13,1..., dimensions={0} | all-to-all | bytes 1572864 | tf_op jit(solution)/shard_map/all_to_all | solution.py:321
  57.3 0.1 fusion.20
  57.4 0.7 maximum_bitcast_fusion.1
  58.1 6.5 %all-to-all-start.3 = ((f32[4,1,6,16,128]{4,3,2,1,0:T(8,128)}), f32[4,1,6,16,128]{4,3,2,1,0:T(8,128)S(1)}, u32[]{:S(2)}, u32[]{:S(2)}) async-start(f32[4,1,6,16,128]{4,3,2,1,0:T(8,128)} %maximum_bitcast_fusion.1), calls=%async_computation.3 | async-start | bytes 393216 | tf_op jit(solution)/shard_map/all_to_all | solution.py:321
  64.6 0.0 collective-permute-done.2.refs_1_
  64.6 0.0 copy-start
  64.6 8.5 %march_rim.1 = f32[4,4,6,16,256]{4,3,2,1,0:T(8,128)} custom-call(f32[3,16]{1,0:T(4,128)} %emission.7, f32[3,16]{1,0:T(4,128)} %absorption.7, f32[16,256,512]{2,1,0:T(8,128)} %refs_0_.7, f32[256,512]{1,0:T(8,128)} %copy-done.1, f32[256,512]{1,0:T(8,128)} %copy-done.2, f32[6,256,384]{2,1,0:T(8,128)} %get-tuple-element.11.refs_3_), custom_call_target="tpu_custom_call" | custom-call | flops 20971520000 | bytes 5242880 | tf_op jit(solution)/shard_map/march_rim/pallas_call | solution.py:271
  73.1 0.0 copy-done
  73.1 12.9 %march_outer.1 = f32[4,4,6,16,128]{4,3,2,1,0:T(8,128)} custom-call(f32[3,16]{1,0:T(4,128)} %emission.7, f32[3,16]{1,0:T(4,128)} %absorption.7, f32[16,256,512]{2,1,0:T(8,128)} %refs_0_.7, f32[16,256,128]{2,1,0:T(8,128)} %copy-done, f32[256,512]{1,0:T(8,128)} %copy-done.1, f32[256,512]{1,0:T(8,128)} %copy-done.2), custom_call_target="tpu_custom_call" | custom-call | flops 20971520000 | bytes 5242880 | tf_op jit(solution)/shard_map/march_outer/pallas_call | solution.py:271
  86.1 0.0 all-to-all-done.3
  86.1 14.0 %all_to_all.31 = f32[4,4,6,16,128]{4,3,2,1,0:T(8,128)S(1)} all-to-all(f32[4,4,6,16,128]{4,3,2,1,0:T(8,128)} %march_outer.1), channel_id=1, replica_groups={{0,2,4,6},{8,10,12,14},{16,18,20,22},{24,26,28,30},{1,3,5,7},{9,11,13,1..., dimensions={0} | all-to-all | bytes 1572864 | tf_op jit(solution)/shard_map/all_to_all | solution.py:321
  100.1 3.6 %all-to-all-start = ((f32[4,4,6,16,256]{4,3,2,1,0:T(8,128)}), f32[4,4,6,16,256]{4,3,2,1,0:T(8,128)S(1)}, u32[]{:S(2)}, u32[]{:S(2)}) async-start(f32[4,4,6,16,256]{4,3,2,1,0:T(8,128)} %march_rim.1), calls=%async_computation | async-start | bytes 3145728 | tf_op jit(solution)/shard_map/all_to_all | solution.py:321
  103.7 0.1 fusion.13
  103.8 0.7 maximum_bitcast_fusion.2
  104.5 16.4 %all-to-all-done = f32[4,4,6,16,256]{4,3,2,1,0:T(8,128)S(1)} async-done(((f32[4,4,6,16,256]{4,3,2,1,0:T(8,128)}), f32[4,4,6,16,256]{4,3,2,1,0:T(8,128)S(1)}, u32[]{:S(2)}, u32[]{:S(2)}) %all-to-all-start) | async-done | bytes 1572896 | tf_op jit(solution)/shard_map/all_to_all | solution.py:321
  120.9 4.3 %all-to-all-start.5 = ((f32[4,1,6,16,128]{4,3,2,1,0:T(8,128)}), f32[4,1,6,16,128]{4,3,2,1,0:T(8,128)S(1)}, u32[]{:S(2)}, u32[]{:S(2)}) async-start(f32[4,1,6,16,128]{4,3,2,1,0:T(8,128)} %maximum_bitcast_fusion.2), calls=%async_computation.5 | async-start | bytes 393216 | tf_op jit(solution)/shard_map/all_to_all | solution.py:321
  125.2 0.2 fusion.6
  125.4 0.8 maximum_bitcast_fusion
  126.2 5.5 %all-to-all-done.5 = f32[4,1,6,16,128]{4,3,2,1,0:T(8,128)S(1)} async-done(((f32[4,1,6,16,128]{4,3,2,1,0:T(8,128)}), f32[4,1,6,16,128]{4,3,2,1,0:T(8,128)S(1)}, u32[]{:S(2)}, u32[]{:S(2)}) %all-to-all-start.5) | async-done | bytes 196640 | tf_op jit(solution)/shard_map/all_to_all | solution.py:321
  131.7 3.5 %all-to-all-start.1 = ((f32[4,1,6,16,256]{4,3,2,1,0:T(8,128)}), f32[4,1,6,16,256]{4,3,2,1,0:T(8,128)S(1)}, u32[]{:S(2)}, u32[]{:S(2)}) async-start(f32[4,1,6,16,256]{4,3,2,1,0:T(8,128)} %maximum_bitcast_fusion), calls=%async_computation.1 | async-start | bytes 786432 | tf_op jit(solution)/shard_map/all_to_all | solution.py:321
  135.2 9.4 %all-to-all-done.1 = f32[4,1,6,16,256]{4,3,2,1,0:T(8,128)S(1)} async-done(((f32[4,1,6,16,256]{4,3,2,1,0:T(8,128)}), f32[4,1,6,16,256]{4,3,2,1,0:T(8,128)S(1)}, u32[]{:S(2)}, u32[]{:S(2)}) %all-to-all-start.1) | async-done | bytes 393248 | tf_op jit(solution)/shard_map/all_to_all | solution.py:321
  144.7 0.7 maximum_select_fusion
  (11 shorter events, 0.1 us)
Async XLA Ops:
  1.9 30.5 %collective-permute-start = (f32[256,512]{1,0:T(8,128)S(1)}, f32[256,512]{1,0:T(8,128)S(1)}, u32[]{:S(2)}, u32[]{:S(2)}) collective-permute-start(f32[256,512]{1,0:T(8,128)S(1)} %get-tuple-element.19), channel_id=1, source_target_pairs={{0,2},{2,4},{4,6},{6,8},{8,10},{10,12},{12,14},{14,16},{16,18},{18... | collective-permute-start | bytes 1572872 | tf_op jit(solution)/shard_map/ppermute | solution.py:292
  6.8 25.6 %collective-permute-start.1 = (f32[256,512]{1,0:T(8,128)S(1)}, f32[256,512]{1,0:T(8,128)S(1)}, u32[]{:S(2)}, u32[]{:S(2)}) collective-permute-start(f32[256,512]{1,0:T(8,128)S(1)} %get-tuple-element.18), channel_id=1, source_target_pairs={{2,0},{4,2},{6,4},{8,6},{10,8},{12,10},{14,12},{16,14},{18,16},{20... | collective-permute-start | bytes 1572872 | tf_op jit(solution)/shard_map/ppermute | solution.py:292
  32.3 32.2 %collective-permute-start.2 = (f32[16,256,128]{2,1,0:T(8,128)}, f32[16,256,128]{2,1,0:T(8,128)S(1)}, u32[]{:S(2)}, u32[]{:S(2)}) collective-permute-start(f32[16,256,128]{2,1,0:T(8,128)} %get-tuple-element.10), channel_id=1, source_target_pairs={{0,1},{1,0},{2,3},{3,2},{4,5},{5,4},{6,7},{7,6},{8,9},{9,8},{10,11... | collective-permute-start | bytes 6291464 | tf_op jit(solution)/shard_map/ppermute | solution.py:338
  32.4 0.8 copy-start.1
  32.4 1.0 copy-start.2
  58.1 28.0 %all-to-all-start.3 = ((f32[4,1,6,16,128]{4,3,2,1,0:T(8,128)}), f32[4,1,6,16,128]{4,3,2,1,0:T(8,128)S(1)}, u32[]{:S(2)}, u32[]{:S(2)}) async-start(f32[4,1,6,16,128]{4,3,2,1,0:T(8,128)} %maximum_bitcast_fusion.1), calls=%async_computation.3 | async-start | bytes 393216 | tf_op jit(solution)/shard_map/all_to_all | solution.py:321
  64.6 8.6 %copy-start = (f32[16,256,128]{2,1,0:T(8,128)}, f32[16,256,128]{2,1,0:T(8,128)S(1)}, u32[]{:S(2)}) copy-start(f32[16,256,128]{2,1,0:T(8,128)S(1)} %collective-permute-done.2.refs_1_) | copy-start | bytes 6291460
  100.1 20.7 %all-to-all-start = ((f32[4,4,6,16,256]{4,3,2,1,0:T(8,128)}), f32[4,4,6,16,256]{4,3,2,1,0:T(8,128)S(1)}, u32[]{:S(2)}, u32[]{:S(2)}) async-start(f32[4,4,6,16,256]{4,3,2,1,0:T(8,128)} %march_rim.1), calls=%async_computation | async-start | bytes 3145728 | tf_op jit(solution)/shard_map/all_to_all | solution.py:321
  120.9 10.8 %all-to-all-start.5 = ((f32[4,1,6,16,128]{4,3,2,1,0:T(8,128)}), f32[4,1,6,16,128]{4,3,2,1,0:T(8,128)S(1)}, u32[]{:S(2)}, u32[]{:S(2)}) async-start(f32[4,1,6,16,128]{4,3,2,1,0:T(8,128)} %maximum_bitcast_fusion.2), calls=%async_computation.5 | async-start | bytes 393216 | tf_op jit(solution)/shard_map/all_to_all | solution.py:321
  131.7 12.9 %all-to-all-start.1 = ((f32[4,1,6,16,256]{4,3,2,1,0:T(8,128)}), f32[4,1,6,16,256]{4,3,2,1,0:T(8,128)S(1)}, u32[]{:S(2)}, u32[]{:S(2)}) async-start(f32[4,1,6,16,256]{4,3,2,1,0:T(8,128)} %maximum_bitcast_fusion), calls=%async_computation.1 | async-start | bytes 786432 | tf_op jit(solution)/shard_map/all_to_all | solution.py:321

commit v9 on v7

--- a/solution.py
+++ b/solution.py
@@ -53,26 +53,32 @@
     )
 
 
-def march_kernel(mode, depth_total, group, emission, absorption, *refs):
+def march_kernel(mode, depth_total, group, scale, unroll, pieces, tables_a, tables_b, *refs):
     refs = list(refs)
     field = refs.pop(0)
     side = refs.pop(0) if mode == "outer" else None
     low, high = (refs.pop(0), refs.pop(0)) if mode != "middle" else (None, None)
-    middle = refs.pop(0) if mode == "rim" else None
-    inner = refs.pop() if mode == "rim" else None
-    cells, canvas, table, words, factors, in_sems, out_sems = refs[-7:]
-    outs = refs[:-7]
-    edge = outs.pop() if mode == "middle" else None
+    rim = mode == "rim"
+    middle = refs.pop(0) if rim else None
+    inner = refs.pop() if rim else None
+    cells, canvas, table, in_sems, out_sems = refs[-5:]
+    outs = refs[:-5]
+    if mode == "middle":
+        edge, words, factors = outs[-3:]
+        outs = outs[:-3]
+    else:
+        edge, words, factors = None, tables_a, tables_b
     planes, height, width = field.shape
-    scale = 0.5 * (emission.shape[1] - 1)
-    piece_rows = height // in_sems.shape[0]
-    pieces = height // piece_rows
+    piece_rows = height // pieces
+    in_pieces = in_sems.shape[0]
     core = lax.axis_index("tile")
     tiles = cells.shape[0] - 2
-    blocks = [(0, 1, planes)] if mode != "rim" else [(0, 1, 2), (planes - 2, 3, 2)]
-    marched = {
-        "outer": range(planes), "middle": range(1, planes - 1), "rim": (0, planes - 1)
-    }[mode]
+    computed = range(1, tiles + 1)
+    blocks = [(0, 1, 2), (planes - 2, 3, 2)] if rim else [(0, 1, planes)]
+    if rim:
+        marched = (0, planes - 1)
+    else:
+        marched = range(1, planes - 1) if mode == "middle" else range(planes)
     place = {first + k: slot + k for first, slot, count in blocks for k in range(count)}
     place[-1] = 0
     place[planes] = max(place.values()) + 1
@@ -83,9 +89,10 @@
         first_lane_taken, first_tile, taken = 0, 1 - core, width // LANES
 
     def incoming(piece):
-        start = pl.multiple_of(piece * piece_rows, SUBLANES)
-        body = pl.ds(start, piece_rows)
-        padded = pl.ds(start + PAD, piece_rows)
+        in_rows = height // in_pieces
+        start = pl.multiple_of(piece * in_rows, SUBLANES)
+        body = pl.ds(start, in_rows)
+        padded = pl.ds(start + PAD, in_rows)
         pairs = []
         for k in range(taken):
             lanes = pl.ds(pl.multiple_of(first_lane_taken + k * LANES, LANES), LANES)
@@ -96,7 +103,7 @@
             if mode != "middle":
                 for halo, plane in ((low, -1), (high, planes)):
                     pairs.append((halo.at[body, lanes], held.at[place[plane], padded, :]))
-        if mode == "rim":
+        if rim:
             pairs.append((middle.at[:, body, :], inner.at[:, body, :]))
         if mode == "outer":
             pairs.append((side.at[:, body, :], cells.at[far, pl.ds(1, planes), padded, :]))
@@ -129,11 +136,12 @@
         for copy in incoming(piece):
             copy.wait()
 
-    for piece in range(min(3, pieces)):
+    for piece in range(min(2, in_pieces)):
         start(piece)
-    prepare_tables(emission, absorption, depth_total, table, words, factors)
+    if mode == "middle":
+        prepare_tables(tables_a, tables_b, depth_total, table, words, factors)
     zeros = jnp.zeros((1, LANES), jnp.float32)
-    for tile in range(1, tiles + 1):
+    for tile in computed:
         for plane in marched:
             cells[tile, place[plane], pl.ds(PAD - 1, 1), :] = zeros
             cells[tile, place[plane], pl.ds(PAD + height, 1), :] = zeros
@@ -146,20 +154,20 @@
     first_lane = lane == 0
     last_lane = lane == LANES - 1
 
-    def strip(at, piece, number):
+    def strip(at, tile, piece, number):
         row = pl.multiple_of(piece * piece_rows + number * SUBLANES, SUBLANES)
 
         def rows(tile, plane, offset=0):
             here = pl.ds(row + PAD + offset, SUBLANES)
-            return cells[tile + 1, place[plane], here, :]
+            return cells[tile, place[plane], here, :]
 
         colour = transmit = None
         for plane in marched:
-            before, centre, after = (rows(at, plane + k) for k in (-1, 0, 1))
-            left = pltpu.roll(jnp.where(last_lane, rows(at - 1, plane), centre), 1, 1)
-            right = pltpu.roll(jnp.where(first_lane, rows(at + 1, plane), centre), LANES - 1, 1)
+            before, centre, after = (rows(tile, plane + k) for k in (-1, 0, 1))
+            left = pltpu.roll(jnp.where(last_lane, rows(tile - 1, plane), centre), 1, 1)
+            right = pltpu.roll(jnp.where(first_lane, rows(tile + 1, plane), centre), LANES - 1, 1)
             diff_x = right - left
-            diff_y = rows(at, plane, 1) - rows(at, plane, -1)
+            diff_y = rows(tile, plane, 1) - rows(tile, plane, -1)
             diff_z = after - before
             inverse = lax.rsqrt(diff_x * diff_x + diff_y * diff_y + diff_z * diff_z + 1.0)
             facing = (factors[0] * diff_x + factors[1] * diff_y + factors[2] * diff_z) * inverse
@@ -182,7 +190,7 @@
                 seen = [transmit[ch] * steps[ch] for ch in range(3)]
                 colour = [colour[ch] + seen[ch] * glows[ch] for ch in range(3)]
                 transmit = [transmit[ch] - seen[ch] for ch in range(3)]
-            if mode == "rim" and plane == 0:
+            if rim and plane == 0:
                 held = [
                     inner[k, pl.ds(row, SUBLANES), pl.ds(at * LANES, LANES)] for k in range(6)
                 ]
@@ -202,18 +210,21 @@
 
     @pl.loop(0, pieces)
     def _(piece):
-        @pl.when(piece + 3 < pieces)
+        @pl.when(piece + 2 < in_pieces)
         def _():
-            start(piece + 3)
-
-        @pl.when(piece + 1 < pieces)
-        def _():
-            await_piece(piece + 1)
-
-        @pl.loop(0, piece_rows // SUBLANES)
-        def _(number):
-            for at in range(tiles):
-                strip(at, piece, number)
+            start(piece + 2)
+
+        @pl.loop(0, piece_rows // (SUBLANES * unroll))
+        def _(step):
+            last_step = step == piece_rows // (SUBLANES * unroll) - 1
+
+            @pl.when(last_step & (piece + 1 < in_pieces))
+            def _():
+                await_piece(piece + 1)
+
+            for k in range(unroll):
+                for at, tile in enumerate(computed):
+                    strip(at, tile, piece, step * unroll + k)
 
         for copy in outgoing(piece):
             copy.start()
@@ -224,11 +235,14 @@
             copy.wait()
 
 
-def march(mode, tables, field, side, halos, middle, depth_total, part_shape):
+def march(mode, tables, field, side, halos, middle, depth_total, scale, part_shape):
     planes, height, width = field.shape
-    extent = LANES if mode == "outer" else width - LANES
-    marched = {"outer": planes, "middle": planes - 2, "rim": 2}[mode]
-    held = 6 if mode == "rim" else planes + 2
+    rim = mode == "rim"
+    tiles = width // LANES - 1
+    if mode == "outer":
+        tiles = 1
+    tiles_held, extent = tiles + 2, tiles * LANES
+    held = 6 if rim else planes + 2
     if part_shape is None:
         group, pieces = 1, max(1, height // 64)
         outs = [jax.ShapeDtypeStruct((6, height, extent), jnp.float32)]
@@ -238,12 +252,10 @@
         outs = [jax.ShapeDtypeStruct((pieces, 6, rows, extent), jnp.float32)] * group
         canvas = (pieces, group, 6, rows, extent)
     scratch = [
-        pltpu.VMEM((extent // LANES + 2, held, height + 2 * PAD, LANES), jnp.float32),
+        pltpu.VMEM((tiles_held, held, height + 2 * PAD, LANES), jnp.float32),
         pltpu.VMEM(canvas, jnp.float32),
         pltpu.VMEM((SUBLANES, LANES), jnp.float32),
-        pltpu.VMEM((6, SUBLANES, LANES), jnp.int32),
-        pltpu.VMEM((6, SUBLANES, LANES), jnp.float32),
-        pltpu.SemaphoreType.DMA((pieces, 4 * (width // LANES) + 1)),
+        pltpu.SemaphoreType.DMA((1 if rim else pieces, 4 * tiles_held + 2)),
         pltpu.SemaphoreType.DMA((pieces, group + 1)),
     ]
     operands = [field]
@@ -251,20 +263,27 @@
         operands.append(side)
     if mode != "middle":
         operands += list(halos)
-    if mode == "rim":
+    if rim:
         operands.append(middle)
         scratch.append(pltpu.VMEM((6, height, extent), jnp.float32))
+    near = pl.BlockSpec(memory_space=pltpu.VMEM)
+    out_specs = [pl.BlockSpec(memory_space=pl.ANY)] * len(outs)
     if mode == "middle":
         outs.append(jax.ShapeDtypeStruct((planes, height, LANES), jnp.float32))
+        outs.append(jax.ShapeDtypeStruct((6, SUBLANES, LANES), jnp.int32))
+        outs.append(jax.ShapeDtypeStruct((6, SUBLANES, LANES), jnp.float32))
+        out_specs += [pl.BlockSpec(memory_space=pl.ANY), near, near]
+    strips = height // pieces // SUBLANES
+    unroll = min(strips, {"rim": 4, "outer": 4, "middle": 2}[mode])
     weight = 100 if mode == "middle" else 20000
-    distant = pl.BlockSpec(memory_space=pltpu.HBM)
+    distant = pl.BlockSpec(memory_space=pl.ANY)
     out = pl.pallas_call(
-        functools.partial(march_kernel, mode, depth_total, group),
+        functools.partial(march_kernel, mode, depth_total, group, scale, unroll, pieces),
         out_shape=outs,
-        in_specs=[pl.BlockSpec(memory_space=pltpu.VMEM)] * 2 + [distant] * len(operands),
-        out_specs=[distant] * len(outs),
+        in_specs=[near] * 2 + [distant] * len(operands),
+        out_specs=out_specs,
         scratch_shapes=scratch,
-        compiler_params=pltpu.CompilerParams(vmem_limit_bytes=60 * 1024 * 1024),
+        compiler_params=pltpu.CompilerParams(vmem_limit_bytes=56 * 1024 * 1024),
         cost_estimate=pl.CostEstimate(
             flops=planes * height * 256 * weight,
             bytes_accessed=planes * height * 256 * 5,
@@ -290,17 +309,18 @@
 
 def exchange(parts, own, shift):
     count = lax.axis_size("slab")
-    merged = []
+    merged, received = [], []
     for change, part in enumerate(parts):
         if change:
             part = lax.ppermute(part, "slab", [(i, i ^ change << shift) for i in range(count)])
+            received.append(part)
         merged.append([part[:, :3], part[:, 3:]])
     digit = 0
     while len(merged) > 1:
         is_far = (own >> digit & 1) == 1
         merged = [ordered(is_far, merged[k], merged[k + 1]) for k in range(0, len(merged), 2)]
         digit += 1
-    return merged[0]
+    return merged[0], received
 
 
 def reduce_image(image, parts, slab_index, block_rows):
@@ -318,9 +338,10 @@
                 lax.dynamic_index_in_dim(image, own ^ change, 1, keepdims=False)
                 for change in range(size)
             ]
-        colour, transmit = exchange(parts, own, shift)
+        (colour, transmit), received = exchange(parts, own, shift)
         image, parts = jnp.concatenate([colour, transmit], axis=1), None
-    return colour[0], 1.0 - transmit[0]
+        first = received if not shift else first
+    return (colour[0], 1.0 - transmit[0]), first
 
 
 def per_device(field, tf_emission, tf_absorption):
@@ -334,16 +355,23 @@
         part_shape = (slab_count // 4, 4, block_rows)
     tables = (tf_emission, tf_absorption)
 
-    def reduced(out):
+    halo = plane_halos(field[0], field[-1])
+    scale = 0.5 * (tf_emission.shape[1] - 1)
+    middle, edge, *tables = march(
+        "middle", tables, field, None, None, None, depth_total, scale, None
+    )
+    side = lax.ppermute(edge, "tile", [(0, 1), (1, 0)])
+    arrived = None
+    results = []
+    for mode in ("rim", "outer"):
+        if arrived is not None:
+            halo, side, _ = lax.optimization_barrier((halo, side, out))
+        out = march(mode, tables, field, side, halo, middle, depth_total, scale, part_shape)
+        if arrived is not None:
+            out, _ = lax.optimization_barrier((out, arrived))
         image, parts = (out, None) if part_shape is None else (None, out)
-        return reduce_image(image, parts, slab_index, block_rows)
-
-    halo = plane_halos(field[0], field[-1])
-    middle, edge = march("middle", tables, field, None, None, None, depth_total, None)
-    side = lax.ppermute(edge, "tile", [(0, 1), (1, 0)])
-    rim = march("rim", tables, field, None, halo, middle, depth_total, part_shape)
-    halo, side, _ = lax.optimization_barrier((halo, side, rim))
-    outer = march("outer", tables, field, side, halo, None, depth_total, part_shape)
+        result, arrived = reduce_image(image, parts, slab_index, block_rows)
+        results.append(result)
     first_core = lax.axis_index("tile") == 0
     return tuple(
         jnp.where(
@@ -351,7 +379,7 @@
             jnp.concatenate([wide, narrow], axis=2),
             jnp.concatenate([narrow, wide], axis=2),
         )
-        for wide, narrow in zip(reduced(rim), reduced(outer))
+        for wide, narrow in zip(*results)
     )
 
 

time: 96.5 us -> 94.5 us (0.979)
  waiting for transfers between devices: 15 us -> 23.7 us
  Pallas kernels: 47.8 us -> 42 us
  starting transfers between devices: 29.3 us -> 23.9 us
    ppermute x12, waiting for transfers between devices: 15 us -> 23.7 us  [exchange(): lax.ppermute(part, 'slab', [(i, i ^ change << shift) for i in range(count)])]
    ppermute x12, starting transfers between devices: 23.1 us -> 16.9 us  [exchange(): lax.ppermute(part, 'slab', [(i, i ^ change << shift) for i in range(count)])]
    pallas_call x3, Pallas kernels: 47.8 us -> 42 us  [march(): pl.pallas_call(functools.partial(march_kernel, mode, depth_total, group,...]
  transfers between devices with their start and end apart: 15 -> 15, of which waited for: 5 -> 6; matrix products, arithmetic and copies ran while one was open for 0% -> 0% of each run, Pallas kernels for 50% -> 45%
where the time goes in v9:
time: 94.5 us; the launch traced here: 94.2 us
  Pallas kernels  42 us (44%)
  starting transfers between devices  23.9 us (25%)
  waiting for transfers between devices  23.7 us (25%)
  local copies, waits for them, and re-layouts  2.61 us (3%)
  other arithmetic  1.15 us (1%)
    pallas_call x3, Pallas kernels, march(): pl.pallas_call(functools.partial(march_kernel, mode, depth_total, group,...  42 us
    ppermute x12, waiting for transfers between devices, exchange(): lax.ppermute(part, 'slab', [(i, i ^ change << shift) for i in range(count)])  23.7 us
    ppermute x12, starting transfers between devices, exchange(): lax.ppermute(part, 'slab', [(i, i ^ change << shift) for i in range(count)])  16.9 us
    ppermute x1, starting transfers between devices, plane_halos(): lax.ppermute(last, 'slab', forward)  5.64 us
  transfers between devices with their start and end apart: 15, of which 6 were waited for; matrix products, arithmetic and copies ran while one was open for 0% of the time, Pallas kernels for 45%

profile of v9, /device:TPU:0, one launch (start us, length us, event | category | flops | bytes accessed | tf_op | source)
XLA Modules:
  0.0 94.2 jit_solution(1786143407173033777)
XLA Ops:
  0.6 1.3 %slice_bitcast_fusion = (f32[256,512]{1,0:T(8,128)S(1)}, f32[256,512]{1,0:T(8,128)S(1)}) fusion(f32[16,256,512]{2,1,0:T(8,128)} %refs_0_.5), kind=kLoop, calls=%fused_computation.8 | loop fusion | bytes 2097152 | tf_op jit(solution)/shard_map/squeeze | solution.py:358
  1.9 5.6 %collective-permute-start = (f32[256,512]{1,0:T(8,128)S(1)}, f32[256,512]{1,0:T(8,128)}, u32[]{:S(2)}, u32[]{:S(2)}) collective-permute-start(f32[256,512]{1,0:T(8,128)S(1)} %get-tuple-element.41), channel_id=1, source_target_pairs={{0,2},{2,4},{4,6},{6,8},{8,10},{10,12},{12,14},{14,16},{16,18},{18... | collective-permute-start | bytes 1572872 | tf_op jit(solution)/shard_map/ppermute | solution.py:301
  7.5 1.3 %collective-permute-start.1 = (f32[256,512]{1,0:T(8,128)S(1)}, f32[256,512]{1,0:T(8,128)}, u32[]{:S(2)}, u32[]{:S(2)}) collective-permute-start(f32[256,512]{1,0:T(8,128)S(1)} %get-tuple-element.40), channel_id=1, source_target_pairs={{2,0},{4,2},{6,4},{8,6},{10,8},{12,10},{14,12},{16,14},{18,16},{20... | collective-permute-start | bytes 1572872 | tf_op jit(solution)/shard_map/ppermute | solution.py:301
  8.8 23.1 %march_middle.1 = (f32[6,256,384]{2,1,0:T(8,128)}, f32[16,256,128]{2,1,0:T(8,128)}, s32[6,8,128]{2,1,0:T(8,128)}, f32[6,8,128]{2,1,0:T(8,128)}) custom-call(f32[3,16]{1,0:T(4,128)} %tables_a.1, f32[3,16]{1,0:T(4,128)} %tables_b.1, f32[16,256,512]{2,1,0:T(8,128)} %refs_0_.5), custom_call_target="tpu_custom_call" | custom-call | flops 104857600 | bytes 5242880 | tf_op jit(solution)/shard_map/march_middle/pallas_call | solution.py:280
  31.9 0.1 collective-permute-start.8
  32.0 0.0 collective-permute-done.refs_1_.refs_2_
  32.0 0.0 collective-permute-done.1.refs_2_.refs_3_
  32.0 8.0 %march_rim.1 = (f32[4,6,16,384]{3,2,1,0:T(8,128)}, f32[4,6,16,384]{3,2,1,0:T(8,128)}, f32[4,6,16,384]{3,2,1,0:T(8,128)}, f32[4,6,16,384]{3,2,1,0:T(8,128)}) custom-call(s32[6,8,128]{2,1,0:T(8,128)} %get-tuple-element.21.tables_a, f32[6,8,128]{2,1,0:T(8,128)} %get-tuple-element.22.tables_b, f32[16,256,512]{2,1,0:T(8,128)} %refs_0_.5, ...), custom_call_target="tpu_custom_call" | custom-call | flops 20971520000 | bytes 5242880 | tf_op jit(solution)/shard_map/march_rim/pallas_call | solution.py:280
  40.0 2.7 %collective-permute-start.4 = (f32[4,6,16,384]{3,2,1,0:T(8,128)}, f32[4,6,16,384]{3,2,1,0:T(8,128)S(1)}, u32[]{:S(2)}, u32[]{:S(2)}) collective-permute-start(f32[4,6,16,384]{3,2,1,0:T(8,128)} %get-tuple-element.26), channel_id=1, source_target_pairs={{0,2},{2,0},{4,6},{6,4},{8,10},{10,8},{12,14},{14,12},{16,18},{18,... | collective-permute-start | bytes 1769480 | tf_op jit(solution)/shard_map/ppermute | solution.py:315
  42.7 0.7 collective-permute-start.3
  43.5 0.9 collective-permute-start.2
  44.4 0.0 collective-permute-done.8.refs_1_
  44.4 0.0 copy-start.2
  44.4 1.3 %copy-done.2 = f32[16,256,128]{2,1,0:T(8,128)} copy-done((f32[16,256,128]{2,1,0:T(8,128)}, f32[16,256,128]{2,1,0:T(8,128)S(1)}, u32[]{:S(2)}) %copy-start.2) | copy-done | bytes 2097176
  45.7 0.0 copy-start
  45.7 10.9 %march_outer.1 = (f32[4,6,16,128]{3,2,1,0:T(8,128)}, f32[4,6,16,128]{3,2,1,0:T(8,128)}, f32[4,6,16,128]{3,2,1,0:T(8,128)}, f32[4,6,16,128]{3,2,1,0:T(8,128)}) custom-call(s32[6,8,128]{2,1,0:T(8,128)} %get-tuple-element.21.tables_a, f32[6,8,128]{2,1,0:T(8,128)} %get-tuple-element.22.tables_b, f32[16,256,512]{2,1,0:T(8,128)} %refs_0_.5, ...), custom_call_target="tpu_custom_call" | custom-call | flops 20971520000 | bytes 5242880 | tf_op jit(solution)/shard_map/march_outer/pallas_call | solution.py:280
  56.6 0.0 copy-start.1
  56.6 0.5 collective-permute-done.4
  57.1 13.9 %collective-permute-done.3 = f32[4,6,16,384]{3,2,1,0:T(8,128)S(1)} collective-permute-done((f32[4,6,16,384]{3,2,1,0:T(8,128)}, f32[4,6,16,384]{3,2,1,0:T(8,128)S(1)}, u32[]{:S(2)}, u32[]{:S(2)}) %collective-permute-start.3) | collective-permute-done | bytes 589856 | tf_op jit(solution)/shard_map/ppermute | solution.py:315
  71.0 0.0 collective-permute-done.2
  71.0 0.7 collective-permute-start.10
  71.7 1.2 %collective-permute-start.9 = (f32[4,6,16,128]{3,2,1,0:T(8,128)}, f32[4,6,16,128]{3,2,1,0:T(8,128)S(1)}, u32[]{:S(2)}, u32[]{:S(2)}) collective-permute-start(f32[4,6,16,128]{3,2,1,0:T(8,128)} %get-tuple-element.36), channel_id=1, source_target_pairs={{0,6},{2,4},{4,2},{6,0},{8,14},{10,12},{12,10},{14,8},{16,22},{18,... | collective-permute-start | bytes 589832 | tf_op jit(solution)/shard_map/ppermute | solution.py:315
  72.9 1.6 %collective-permute-start.11 = (f32[4,6,16,128]{3,2,1,0:T(8,128)}, f32[4,6,16,128]{3,2,1,0:T(8,128)S(1)}, u32[]{:S(2)}, u32[]{:S(2)}) collective-permute-start(f32[4,6,16,128]{3,2,1,0:T(8,128)} %get-tuple-element.38), channel_id=1, source_target_pairs={{0,2},{2,0},{4,6},{6,4},{8,10},{10,8},{12,14},{14,12},{16,18},{18,... | collective-permute-start | bytes 589832 | tf_op jit(solution)/shard_map/ppermute | solution.py:315
  74.5 0.0 copy-done
  74.5 0.2 select_multiply_fusion
  74.7 0.1 fusion.1
  74.8 2.5 %collective-permute-start.6 = (f32[1,6,16,384]{3,2,1,0:T(8,128)S(1)}, f32[1,6,16,384]{3,2,1,0:T(8,128)S(1)}, u32[]{:S(2)}, u32[]{:S(2)}) collective-permute-start(f32[1,6,16,384]{3,2,1,0:T(8,128)S(1)} %get-tuple-element.49), channel_id=1, source_target_pairs={{0,16},{2,18},{4,20},{6,22},{8,24},{10,26},{12,28},{14,30},{16,0},... | collective-permute-start | bytes 442376 | tf_op jit(solution)/shard_map/ppermute | solution.py:315
  77.3 1.3 %collective-permute-start.5 = (f32[1,6,16,384]{3,2,1,0:T(8,128)S(1)}, f32[1,6,16,384]{3,2,1,0:T(8,128)S(1)}, u32[]{:S(2)}, u32[]{:S(2)}) collective-permute-start(f32[1,6,16,384]{3,2,1,0:T(8,128)S(1)} %get-tuple-element.48), channel_id=1, source_target_pairs={{0,24},{2,26},{4,28},{6,30},{8,16},{10,18},{12,20},{14,22},{16,8},... | collective-permute-start | bytes 442376 | tf_op jit(solution)/shard_map/ppermute | solution.py:315
  78.6 3.1 %collective-permute-done.10 = f32[4,6,16,128]{3,2,1,0:T(8,128)S(1)} collective-permute-done((f32[4,6,16,128]{3,2,1,0:T(8,128)}, f32[4,6,16,128]{3,2,1,0:T(8,128)S(1)}, u32[]{:S(2)}, u32[]{:S(2)}) %collective-permute-start.10) | collective-permute-done | bytes 196640 | tf_op jit(solution)/shard_map/ppermute | solution.py:315
  81.8 1.5 %collective-permute-start.7 = (f32[1,6,16,384]{3,2,1,0:T(8,128)S(1)}, f32[1,6,16,384]{3,2,1,0:T(8,128)S(1)}, u32[]{:S(2)}, u32[]{:S(2)}) collective-permute-start(f32[1,6,16,384]{3,2,1,0:T(8,128)S(1)} %get-tuple-element.50), channel_id=1, source_target_pairs={{0,8},{2,10},{4,12},{6,14},{8,0},{10,2},{12,4},{14,6},{16,24},{18,... | collective-permute-start | bytes 442376 | tf_op jit(solution)/shard_map/ppermute | solution.py:315
  83.3 0.0 collective-permute-done.9
  83.3 0.0 collective-permute-done.11
  83.3 0.0 copy-done.1
  83.3 0.1 select_multiply_fusion.3
  83.5 2.7 %collective-permute-start.13 = (f32[1,6,16,128]{3,2,1,0:T(8,128)S(1)}, f32[1,6,16,128]{3,2,1,0:T(8,128)S(1)}, u32[]{:S(2)}, u32[]{:S(2)}) collective-permute-start(f32[1,6,16,128]{3,2,1,0:T(8,128)S(1)} %get-tuple-element.55), channel_id=1, source_target_pairs={{0,16},{2,18},{4,20},{6,22},{8,24},{10,26},{12,28},{14,30},{16,0},... | collective-permute-start | bytes 147464 | tf_op jit(solution)/shard_map/ppermute | solution.py:315
  86.1 1.0 %collective-permute-start.12 = (f32[1,6,16,128]{3,2,1,0:T(8,128)S(1)}, f32[1,6,16,128]{3,2,1,0:T(8,128)S(1)}, u32[]{:S(2)}, u32[]{:S(2)}) collective-permute-start(f32[1,6,16,128]{3,2,1,0:T(8,128)S(1)} %get-tuple-element.54), channel_id=1, source_target_pairs={{0,24},{2,26},{4,28},{6,30},{8,16},{10,18},{12,20},{14,22},{16,8},... | collective-permute-start | bytes 147464 | tf_op jit(solution)/shard_map/ppermute | solution.py:315
  87.1 1.1 %collective-permute-done.6 = f32[1,6,16,384]{3,2,1,0:T(8,128)S(1)} collective-permute-done((f32[1,6,16,384]{3,2,1,0:T(8,128)S(1)}, f32[1,6,16,384]{3,2,1,0:T(8,128)S(1)}, u32[]{:S(2)}, u32[]{:S(2)}) %collective-permute-start.6) | collective-permute-done | bytes 147488 | tf_op jit(solution)/shard_map/ppermute | solution.py:315
  88.2 0.1 collective-permute-start.14
  88.3 0.0 collective-permute-done.5
  88.3 2.2 %collective-permute-done.7 = f32[1,6,16,384]{3,2,1,0:T(8,128)S(1)} collective-permute-done((f32[1,6,16,384]{3,2,1,0:T(8,128)S(1)}, f32[1,6,16,384]{3,2,1,0:T(8,128)S(1)}, u32[]{:S(2)}, u32[]{:S(2)}) %collective-permute-start.7) | collective-permute-done | bytes 147488 | tf_op jit(solution)/shard_map/ppermute | solution.py:315
  90.4 0.1 subtract_bitcast_fusion
  90.5 2.9 %collective-permute-done.13 = f32[1,6,16,128]{3,2,1,0:T(8,128)S(1)} collective-permute-done((f32[1,6,16,128]{3,2,1,0:T(8,128)S(1)}, f32[1,6,16,128]{3,2,1,0:T(8,128)S(1)}, u32[]{:S(2)}, u32[]{:S(2)}) %collective-permute-start.13) | collective-permute-done | bytes 49184 | tf_op jit(solution)/shard_map/ppermute | solution.py:315
  93.4 0.0 collective-permute-done.12
  93.4 0.0 collective-permute-done.14
  93.5 0.7 maximum_select_fusion
  (2 shorter events, 0.1 us)
Async XLA Ops:
  1.9 30.1 %collective-permute-start = (f32[256,512]{1,0:T(8,128)S(1)}, f32[256,512]{1,0:T(8,128)}, u32[]{:S(2)}, u32[]{:S(2)}) collective-permute-start(f32[256,512]{1,0:T(8,128)S(1)} %get-tuple-element.41), channel_id=1, source_target_pairs={{0,2},{2,4},{4,6},{6,8},{8,10},{10,12},{12,14},{14,16},{16,18},{18... | collective-permute-start | bytes 1572872 | tf_op jit(solution)/shard_map/ppermute | solution.py:301
  7.5 24.5 %collective-permute-start.1 = (f32[256,512]{1,0:T(8,128)S(1)}, f32[256,512]{1,0:T(8,128)}, u32[]{:S(2)}, u32[]{:S(2)}) collective-permute-start(f32[256,512]{1,0:T(8,128)S(1)} %get-tuple-element.40), channel_id=1, source_target_pairs={{2,0},{4,2},{6,4},{8,6},{10,8},{12,10},{14,12},{16,14},{18,16},{20... | collective-permute-start | bytes 1572872 | tf_op jit(solution)/shard_map/ppermute | solution.py:301
  31.9 12.4 %collective-permute-start.8 = (f32[16,256,128]{2,1,0:T(8,128)}, f32[16,256,128]{2,1,0:T(8,128)S(1)}, u32[]{:S(2)}, u32[]{:S(2)}) collective-permute-start(f32[16,256,128]{2,1,0:T(8,128)} %get-tuple-element.28), channel_id=1, source_target_pairs={{0,1},{1,0},{2,3},{3,2},{4,5},{5,4},{6,7},{7,6},{8,9},{9,8},{10,11... | collective-permute-start | bytes 6291464 | tf_op jit(solution)/shard_map/ppermute | solution.py:363
  40.0 17.1 %collective-permute-start.4 = (f32[4,6,16,384]{3,2,1,0:T(8,128)}, f32[4,6,16,384]{3,2,1,0:T(8,128)S(1)}, u32[]{:S(2)}, u32[]{:S(2)}) collective-permute-start(f32[4,6,16,384]{3,2,1,0:T(8,128)} %get-tuple-element.26), channel_id=1, source_target_pairs={{0,2},{2,0},{4,6},{6,4},{8,10},{10,8},{12,14},{14,12},{16,18},{18,... | collective-permute-start | bytes 1769480 | tf_op jit(solution)/shard_map/ppermute | solution.py:315
  42.7 28.3 %collective-permute-start.3 = (f32[4,6,16,384]{3,2,1,0:T(8,128)}, f32[4,6,16,384]{3,2,1,0:T(8,128)S(1)}, u32[]{:S(2)}, u32[]{:S(2)}) collective-permute-start(f32[4,6,16,384]{3,2,1,0:T(8,128)} %get-tuple-element.25), channel_id=1, source_target_pairs={{0,4},{2,6},{4,0},{6,2},{8,12},{10,14},{12,8},{14,10},{16,20},{18,... | collective-permute-start | bytes 1769480 | tf_op jit(solution)/shard_map/ppermute | solution.py:315
  43.5 27.5 %collective-permute-start.2 = (f32[4,6,16,384]{3,2,1,0:T(8,128)}, f32[4,6,16,384]{3,2,1,0:T(8,128)S(1)}, u32[]{:S(2)}, u32[]{:S(2)}) collective-permute-start(f32[4,6,16,384]{3,2,1,0:T(8,128)} %get-tuple-element.24), channel_id=1, source_target_pairs={{0,6},{2,4},{4,2},{6,0},{8,14},{10,12},{12,10},{14,8},{16,22},{18,... | collective-permute-start | bytes 1769480 | tf_op jit(solution)/shard_map/ppermute | solution.py:315
  44.4 1.3 %copy-start.2 = (f32[16,256,128]{2,1,0:T(8,128)}, f32[16,256,128]{2,1,0:T(8,128)S(1)}, u32[]{:S(2)}) copy-start(f32[16,256,128]{2,1,0:T(8,128)S(1)} %collective-permute-done.8.refs_1_) | copy-start | bytes 6291460
  45.7 28.8 %copy-start = (f32[4,6,16,384]{3,2,1,0:T(8,128)S(1)}, f32[4,6,16,384]{3,2,1,0:T(8,128)}, u32[]{:S(2)}) copy-start(f32[4,6,16,384]{3,2,1,0:T(8,128)} %get-tuple-element.27) | copy-start | bytes 1769476
  56.6 26.7 %copy-start.1 = (f32[4,6,16,128]{3,2,1,0:T(8,128)S(1)}, f32[4,6,16,128]{3,2,1,0:T(8,128)}, u32[]{:S(2)}) copy-start(f32[4,6,16,128]{3,2,1,0:T(8,128)} %get-tuple-element.39) | copy-start | bytes 589828
  71.0 10.8 %collective-permute-start.10 = (f32[4,6,16,128]{3,2,1,0:T(8,128)}, f32[4,6,16,128]{3,2,1,0:T(8,128)S(1)}, u32[]{:S(2)}, u32[]{:S(2)}) collective-permute-start(f32[4,6,16,128]{3,2,1,0:T(8,128)} %get-tuple-element.37), channel_id=1, source_target_pairs={{0,4},{2,6},{4,0},{6,2},{8,12},{10,14},{12,8},{14,10},{16,20},{18,... | collective-permute-start | bytes 589832 | tf_op jit(solution)/shard_map/ppermute | solution.py:315
  71.7 11.6 %collective-permute-start.9 = (f32[4,6,16,128]{3,2,1,0:T(8,128)}, f32[4,6,16,128]{3,2,1,0:T(8,128)S(1)}, u32[]{:S(2)}, u32[]{:S(2)}) collective-permute-start(f32[4,6,16,128]{3,2,1,0:T(8,128)} %get-tuple-element.36), channel_id=1, source_target_pairs={{0,6},{2,4},{4,2},{6,0},{8,14},{10,12},{12,10},{14,8},{16,22},{18,... | collective-permute-start | bytes 589832 | tf_op jit(solution)/shard_map/ppermute | solution.py:315
  72.9 10.4 %collective-permute-start.11 = (f32[4,6,16,128]{3,2,1,0:T(8,128)}, f32[4,6,16,128]{3,2,1,0:T(8,128)S(1)}, u32[]{:S(2)}, u32[]{:S(2)}) collective-permute-start(f32[4,6,16,128]{3,2,1,0:T(8,128)} %get-tuple-element.38), channel_id=1, source_target_pairs={{0,2},{2,0},{4,6},{6,4},{8,10},{10,8},{12,14},{14,12},{16,18},{18,... | collective-permute-start | bytes 589832 | tf_op jit(solution)/shard_map/ppermute | solution.py:315
  74.8 13.5 %collective-permute-start.6 = (f32[1,6,16,384]{3,2,1,0:T(8,128)S(1)}, f32[1,6,16,384]{3,2,1,0:T(8,128)S(1)}, u32[]{:S(2)}, u32[]{:S(2)}) collective-permute-start(f32[1,6,16,384]{3,2,1,0:T(8,128)S(1)} %get-tuple-element.49), channel_id=1, source_target_pairs={{0,16},{2,18},{4,20},{6,22},{8,24},{10,26},{12,28},{14,30},{16,0},... | collective-permute-start | bytes 442376 | tf_op jit(solution)/shard_map/ppermute | solution.py:315
  77.3 11.0 %collective-permute-start.5 = (f32[1,6,16,384]{3,2,1,0:T(8,128)S(1)}, f32[1,6,16,384]{3,2,1,0:T(8,128)S(1)}, u32[]{:S(2)}, u32[]{:S(2)}) collective-permute-start(f32[1,6,16,384]{3,2,1,0:T(8,128)S(1)} %get-tuple-element.48), channel_id=1, source_target_pairs={{0,24},{2,26},{4,28},{6,30},{8,16},{10,18},{12,20},{14,22},{16,8},... | collective-permute-start | bytes 442376 | tf_op jit(solution)/shard_map/ppermute | solution.py:315
  81.8 8.7 %collective-permute-start.7 = (f32[1,6,16,384]{3,2,1,0:T(8,128)S(1)}, f32[1,6,16,384]{3,2,1,0:T(8,128)S(1)}, u32[]{:S(2)}, u32[]{:S(2)}) collective-permute-start(f32[1,6,16,384]{3,2,1,0:T(8,128)S(1)} %get-tuple-element.50), channel_id=1, source_target_pairs={{0,8},{2,10},{4,12},{6,14},{8,0},{10,2},{12,4},{14,6},{16,24},{18,... | collective-permute-start | bytes 442376 | tf_op jit(solution)/shard_map/ppermute | solution.py:315
  83.5 10.0 %collective-permute-start.13 = (f32[1,6,16,128]{3,2,1,0:T(8,128)S(1)}, f32[1,6,16,128]{3,2,1,0:T(8,128)S(1)}, u32[]{:S(2)}, u32[]{:S(2)}) collective-permute-start(f32[1,6,16,128]{3,2,1,0:T(8,128)S(1)} %get-tuple-element.55), channel_id=1, source_target_pairs={{0,16},{2,18},{4,20},{6,22},{8,24},{10,26},{12,28},{14,30},{16,0},... | collective-permute-start | bytes 147464 | tf_op jit(solution)/shard_map/ppermute | solution.py:315
  86.1 7.3 %collective-permute-start.12 = (f32[1,6,16,128]{3,2,1,0:T(8,128)S(1)}, f32[1,6,16,128]{3,2,1,0:T(8,128)S(1)}, u32[]{:S(2)}, u32[]{:S(2)}) collective-permute-start(f32[1,6,16,128]{3,2,1,0:T(8,128)S(1)} %get-tuple-element.54), channel_id=1, source_target_pairs={{0,24},{2,26},{4,28},{6,30},{8,16},{10,18},{12,20},{14,22},{16,8},... | collective-permute-start | bytes 147464 | tf_op jit(solution)/shard_map/ppermute | solution.py:315
  88.2 5.2 %collective-permute-start.14 = (f32[1,6,16,128]{3,2,1,0:T(8,128)S(1)}, f32[1,6,16,128]{3,2,1,0:T(8,128)S(1)}, u32[]{:S(2)}, u32[]{:S(2)}) collective-permute-start(f32[1,6,16,128]{3,2,1,0:T(8,128)S(1)} %get-tuple-element.56), channel_id=1, source_target_pairs={{0,8},{2,10},{4,12},{6,14},{8,0},{10,2},{12,4},{14,6},{16,24},{18,... | collective-permute-start | bytes 147464 | tf_op jit(solution)/shard_map/ppermute | solution.py:315

commit v10 on v9

--- a/solution.py
+++ b/solution.py
@@ -83,10 +83,8 @@
     place[-1] = 0
     place[planes] = max(place.values()) + 1
     far = (1 - core) * (tiles + 1)
-    if mode == "outer":
-        first_lane_taken, first_tile, taken = (1 - core) * (width - 2 * LANES), core, 2
-    else:
-        first_lane_taken, first_tile, taken = 0, 1 - core, width // LANES
+    nearer = core if mode == "outer" else 1 - core
+    first_lane_taken, first_tile = (1 - nearer) * (width // 2 - LANES), nearer
 
     def incoming(piece):
         in_rows = height // in_pieces
@@ -94,15 +92,18 @@
         body = pl.ds(start, in_rows)
         padded = pl.ds(start + PAD, in_rows)
         pairs = []
-        for k in range(taken):
+        for k in range(tiles + 1):
             lanes = pl.ds(pl.multiple_of(first_lane_taken + k * LANES, LANES), LANES)
             held = cells.at[first_tile + k]
             for first, where, count in blocks:
                 target = held.at[pl.ds(where, count), padded, :]
                 pairs.append((field.at[pl.ds(first, count), body, lanes], target))
-            if mode != "middle":
+        if mode != "middle":
+            for tile in computed:
+                lanes = pl.ds((tile - 1) * LANES, LANES)
                 for halo, plane in ((low, -1), (high, planes)):
-                    pairs.append((halo.at[body, lanes], held.at[place[plane], padded, :]))
+                    target = cells.at[tile, place[plane], padded, :]
+                    pairs.append((halo.at[body, lanes], target))
         if rim:
             pairs.append((middle.at[:, body, :], inner.at[:, body, :]))
         if mode == "outer":
@@ -120,9 +121,6 @@
         else:
             own = lax.axis_index("slab") & (group - 1)
             pairs = [(canvas.at[piece, own ^ k], outs[k].at[piece]) for k in range(group)]
-        if edge is not None:
-            padded = pl.ds(start + PAD, piece_rows)
-            pairs.append((cells.at[far, pl.ds(1, planes), padded, :], edge.at[:, body, :]))
         return [
             pltpu.make_async_copy(source, target, out_sems.at[piece, k])
             for k, (source, target) in enumerate(pairs)
@@ -139,6 +137,11 @@
     for piece in range(min(2, in_pieces)):
         start(piece)
     if mode == "middle":
+        first = pl.multiple_of((1 - core) * (width - LANES), LANES)
+        edge_copy = pltpu.make_async_copy(
+            field.at[:, :, pl.ds(first, LANES)], edge, out_sems.at[0, group]
+        )
+        edge_copy.start()
         prepare_tables(tables_a, tables_b, depth_total, table, words, factors)
     zeros = jnp.zeros((1, LANES), jnp.float32)
     for tile in computed:
@@ -234,17 +237,18 @@
         for copy in outgoing(piece):
             copy.wait()
 
+    if mode == "middle":
+        edge_copy.wait()
+
 
 def march(mode, tables, field, side, halos, middle, depth_total, scale, part_shape):
     planes, height, width = field.shape
     rim = mode == "rim"
-    tiles = width // LANES - 1
-    if mode == "outer":
-        tiles = 1
+    tiles = width // LANES // 2
     tiles_held, extent = tiles + 2, tiles * LANES
     held = 6 if rim else planes + 2
     if part_shape is None:
-        group, pieces = 1, max(1, height // 64)
+        group, pieces = 1, max(1, height // (32 if mode == "middle" else 64))
         outs = [jax.ShapeDtypeStruct((6, height, extent), jnp.float32)]
         canvas = (6, height, extent)
     else:
@@ -275,7 +279,7 @@
         out_specs += [pl.BlockSpec(memory_space=pl.ANY), near, near]
     strips = height // pieces // SUBLANES
     unroll = min(strips, {"rim": 4, "outer": 4, "middle": 2}[mode])
-    weight = 100 if mode == "middle" else 20000
+    weight = 20000 if mode == "outer" else 100
     distant = pl.BlockSpec(memory_space=pl.ANY)
     out = pl.pallas_call(
         functools.partial(march_kernel, mode, depth_total, group, scale, unroll, pieces),
@@ -355,24 +359,31 @@
         part_shape = (slab_count // 4, 4, block_rows)
     tables = (tf_emission, tf_absorption)
 
-    halo = plane_halos(field[0], field[-1])
+    core = lax.axis_index("tile")
+    half = width // 2
+    halos = []
+    for start in (core * half, (1 - core) * half):
+        first, last = (
+            lax.dynamic_slice_in_dim(field[plane], start, half, axis=1) for plane in (0, -1)
+        )
+        halos.append(plane_halos(first, last))
     scale = 0.5 * (tf_emission.shape[1] - 1)
     middle, edge, *tables = march(
         "middle", tables, field, None, None, None, depth_total, scale, None
     )
+    edge, _ = lax.optimization_barrier((edge, halos[0]))
     side = lax.ppermute(edge, "tile", [(0, 1), (1, 0)])
     arrived = None
     results = []
-    for mode in ("rim", "outer"):
+    for mode, halo in zip(("rim", "outer"), halos):
         if arrived is not None:
             halo, side, _ = lax.optimization_barrier((halo, side, out))
         out = march(mode, tables, field, side, halo, middle, depth_total, scale, part_shape)
-        if arrived is not None:
-            out, _ = lax.optimization_barrier((out, arrived))
+        out, _ = lax.optimization_barrier((out, halos[1] if arrived is None else arrived))
         image, parts = (out, None) if part_shape is None else (None, out)
         result, arrived = reduce_image(image, parts, slab_index, block_rows)
         results.append(result)
-    first_core = lax.axis_index("tile") == 0
+    first_core = core == 0
     return tuple(
         jnp.where(
             first_core,

time: 94.5 us -> 150 us (1.59)
  Pallas kernels: 42 us -> 91.3 us
  starting transfers between devices: 23.9 us -> 29.9 us
    pallas_call x3, Pallas kernels: 42 us -> 91.3 us  [march(): pl.pallas_call(functools.partial(march_kernel, mode, depth_total, group,...]
    ppermute x12, waiting for transfers between devices: 23.7 us -> 16.5 us  [exchange(): lax.ppermute(part, 'slab', [(i, i ^ change << shift) for i in range(count)])]
    ppermute x1 -> x2, waiting for transfers between devices: 0.01 us -> 6.81 us  [plane_halos(): lax.ppermute(first, 'slab', backward)]
    ppermute x1 -> x2, starting transfers between devices: 5.64 us -> 9.42 us  [plane_halos(): lax.ppermute(last, 'slab', forward)]
  transfers between devices with their start and end apart: 15 -> 17, of which waited for: 6 -> 5; matrix products, arithmetic and copies ran while one was open for 0% -> 0% of each run, Pallas kernels for 45% -> 61%
where the time goes in v10:
time: 150 us; the launch traced here: 149 us
  Pallas kernels  91.3 us (61%)
  starting transfers between devices  29.9 us (20%)
  waiting for transfers between devices  23.3 us (16%)
  local copies, waits for them, and re-layouts  2.73 us (2%)
    pallas_call x3, Pallas kernels, march(): pl.pallas_call(functools.partial(march_kernel, mode, depth_total, group,...  91.3 us
    ppermute x12, starting transfers between devices, exchange(): lax.ppermute(part, 'slab', [(i, i ^ change << shift) for i in range(count)])  17.8 us
    ppermute x12, waiting for transfers between devices, exchange(): lax.ppermute(part, 'slab', [(i, i ^ change << shift) for i in range(count)])  16.5 us
    ppermute x2, starting transfers between devices, plane_halos(): lax.ppermute(last, 'slab', forward)  9.42 us
    ppermute x2, waiting for transfers between devices, plane_halos(): lax.ppermute(first, 'slab', backward)  6.81 us
  transfers between devices with their start and end apart: 17, of which 5 were waited for; matrix products, arithmetic and copies ran while one was open for 0% of the time, Pallas kernels for 61%

profile of v10, /device:TPU:0, one launch (start us, length us, event | category | flops | bytes accessed | tf_op | source)
XLA Modules:
  0.0 149.4 jit_solution(9432892572103071112)
XLA Ops:
  0.6 1.3 fusion.8
  2.0 4.9 %collective-permute-start = (f32[256,256]{1,0:T(8,128)S(1)}, f32[256,256]{1,0:T(8,128)S(1)}, u32[]{:S(2)}, u32[]{:S(2)}) collective-permute-start(f32[256,256]{1,0:T(8,128)S(1)} %get-tuple-element.58), channel_id=1, source_target_pairs={{0,2},{2,4},{4,6},{6,8},{8,10},{10,12},{12,14},{14,16},{16,18},{18... | collective-permute-start | bytes 786440 | tf_op jit(solution)/shard_map/ppermute | solution.py:305
  6.9 1.3 collective-permute-start.1
  8.2 67.4 %march_middle.1 = (f32[6,256,256]{2,1,0:T(8,128)}, f32[16,256,128]{2,1,0:T(8,128)}, s32[6,8,128]{2,1,0:T(8,128)}, f32[6,8,128]{2,1,0:T(8,128)}) custom-call(f32[3,16]{1,0:T(4,128)} %tables_a.1, f32[3,16]{1,0:T(4,128)} %tables_b.1, f32[16,256,512]{2,1,0:T(8,128)} %refs_0_.5), custom_call_target="tpu_custom_call" | custom-call | flops 104857600 | bytes 5242880 | tf_op jit(solution)/shard_map/march_middle/pallas_call | solution.py:284
  75.6 0.0 collective-permute-done.refs_1_
  75.6 0.0 copy-start.2
  75.6 0.0 collective-permute-done.1.refs_2_
  75.6 0.0 copy-start.3
  75.6 0.1 collective-permute-start.10
  75.7 4.6 %collective-permute-start.2 = (f32[256,256]{1,0:T(8,128)S(1)}, f32[256,256]{1,0:T(8,128)S(1)}, u32[]{:S(2)}, u32[]{:S(2)}) collective-permute-start(f32[256,256]{1,0:T(8,128)S(1)} %get-tuple-element.59), channel_id=1, source_target_pairs={{0,2},{2,4},{4,6},{6,8},{8,10},{10,12},{12,14},{14,16},{16,18},{18... | collective-permute-start | bytes 786440 | tf_op jit(solution)/shard_map/ppermute | solution.py:305
  80.3 1.3 collective-permute-start.3
  81.6 0.0 copy-done.2
  81.6 0.0 copy-done.3
  81.6 6.5 %march_rim.1 = (f32[4,6,16,256]{3,2,1,0:T(8,128)}, f32[4,6,16,256]{3,2,1,0:T(8,128)}, f32[4,6,16,256]{3,2,1,0:T(8,128)}, f32[4,6,16,256]{3,2,1,0:T(8,128)}) custom-call(s32[6,8,128]{2,1,0:T(8,128)} %get-tuple-element.26.tables_a, f32[6,8,128]{2,1,0:T(8,128)} %get-tuple-element.27.tables_b, f32[16,256,512]{2,1,0:T(8,128)} %refs_0_.5, f32[256,256]{1,0:T(8,128)} %copy-done.2, ...), custom_call_target="tpu_custom_call" | custom-call | flops 104857600 | bytes 5242880 | tf_op jit(solution)/shard_map/march_rim/pallas_call | solution.py:284
  88.1 0.0 collective-permute-done.2.refs_2_
  88.1 0.0 copy-start.5
  88.1 6.8 %collective-permute-done.3.refs_3_ = f32[256,256]{1,0:T(8,128)S(1)} collective-permute-done((f32[256,256]{1,0:T(8,128)S(1)}, f32[256,256]{1,0:T(8,128)S(1)}, u32[]{:S(2)}, u32[]{:S(2)}) %collective-permute-start.3) | collective-permute-done | bytes 262176 | tf_op jit(solution)/shard_map/ppermute | solution.py:305
  94.9 0.0 copy-start.6
  94.9 0.0 copy-start.1
  94.9 0.6 collective-permute-start.6
  95.5 1.7 %collective-permute-start.5 = (f32[4,6,16,256]{3,2,1,0:T(8,128)}, f32[4,6,16,256]{3,2,1,0:T(8,128)S(1)}, u32[]{:S(2)}, u32[]{:S(2)}) collective-permute-start(f32[4,6,16,256]{3,2,1,0:T(8,128)} %get-tuple-element.34), channel_id=1, source_target_pairs={{0,4},{2,6},{4,0},{6,2},{8,12},{10,14},{12,8},{14,10},{16,20},{18,... | collective-permute-start | bytes 1179656 | tf_op jit(solution)/shard_map/ppermute | solution.py:319
  97.2 1.2 collective-permute-start.4
  98.4 0.0 collective-permute-done.10.refs_1_
  98.4 0.0 copy-done.5
  98.4 0.0 copy-done.6
  98.4 0.0 copy-start.4
  98.4 1.3 copy-done.4
  99.7 17.4 %march_outer.1 = (f32[4,6,16,256]{3,2,1,0:T(8,128)}, f32[4,6,16,256]{3,2,1,0:T(8,128)}, f32[4,6,16,256]{3,2,1,0:T(8,128)}, f32[4,6,16,256]{3,2,1,0:T(8,128)}) custom-call(s32[6,8,128]{2,1,0:T(8,128)} %get-tuple-element.26.tables_a, f32[6,8,128]{2,1,0:T(8,128)} %get-tuple-element.27.tables_b, f32[16,256,512]{2,1,0:T(8,128)} %refs_0_.5, ...), custom_call_target="tpu_custom_call" | custom-call | flops 20971520000 | bytes 5242880 | tf_op jit(solution)/shard_map/march_outer/pallas_call | solution.py:284
  117.2 0.0 copy-start
  117.2 0.0 collective-permute-done.6
  117.2 0.0 collective-permute-done.5
  117.2 0.0 collective-permute-done.4
  117.2 0.4 collective-permute-start.12
  117.6 1.8 %collective-permute-start.11 = (f32[4,6,16,256]{3,2,1,0:T(8,128)}, f32[4,6,16,256]{3,2,1,0:T(8,128)S(1)}, u32[]{:S(2)}, u32[]{:S(2)}) collective-permute-start(f32[4,6,16,256]{3,2,1,0:T(8,128)} %get-tuple-element.46), channel_id=1, source_target_pairs={{0,6},{2,4},{4,2},{6,0},{8,14},{10,12},{12,10},{14,8},{16,22},{18,... | collective-permute-start | bytes 1179656 | tf_op jit(solution)/shard_map/ppermute | solution.py:319
  119.4 1.4 collective-permute-start.13
  120.8 0.0 copy-done.1
  120.8 0.2 select_multiply_fusion.3
  121.0 3.0 %collective-permute-start.8 = (f32[1,6,16,256]{3,2,1,0:T(8,128)S(1)}, f32[1,6,16,256]{3,2,1,0:T(8,128)S(1)}, u32[]{:S(2)}, u32[]{:S(2)}) collective-permute-start(f32[1,6,16,256]{3,2,1,0:T(8,128)S(1)} %get-tuple-element.65), channel_id=1, source_target_pairs={{0,16},{2,18},{4,20},{6,22},{8,24},{10,26},{12,28},{14,30},{16,0},... | collective-permute-start | bytes 294920 | tf_op jit(solution)/shard_map/ppermute | solution.py:319
  124.0 1.3 collective-permute-start.7
  125.4 10.4 %collective-permute-done.12 = f32[4,6,16,256]{3,2,1,0:T(8,128)S(1)} collective-permute-done((f32[4,6,16,256]{3,2,1,0:T(8,128)}, f32[4,6,16,256]{3,2,1,0:T(8,128)S(1)}, u32[]{:S(2)}, u32[]{:S(2)}) %collective-permute-start.12) | collective-permute-done | bytes 393248 | tf_op jit(solution)/shard_map/ppermute | solution.py:319
  135.8 2.5 %collective-permute-start.9 = (f32[1,6,16,256]{3,2,1,0:T(8,128)S(1)}, f32[1,6,16,256]{3,2,1,0:T(8,128)S(1)}, u32[]{:S(2)}, u32[]{:S(2)}) collective-permute-start(f32[1,6,16,256]{3,2,1,0:T(8,128)S(1)} %get-tuple-element.66), channel_id=1, source_target_pairs={{0,8},{2,10},{4,12},{6,14},{8,0},{10,2},{12,4},{14,6},{16,24},{18,... | collective-permute-start | bytes 294920 | tf_op jit(solution)/shard_map/ppermute | solution.py:319
  138.3 0.0 collective-permute-done.11
  138.3 0.0 collective-permute-done.13
  138.3 0.0 copy-done
  138.3 0.2 select_multiply_fusion
  138.6 2.6 %collective-permute-start.15 = (f32[1,6,16,256]{3,2,1,0:T(8,128)S(1)}, f32[1,6,16,256]{3,2,1,0:T(8,128)S(1)}, u32[]{:S(2)}, u32[]{:S(2)}) collective-permute-start(f32[1,6,16,256]{3,2,1,0:T(8,128)S(1)} %get-tuple-element.69), channel_id=1, source_target_pairs={{0,16},{2,18},{4,20},{6,22},{8,24},{10,26},{12,28},{14,30},{16,0},... | collective-permute-start | bytes 294920 | tf_op jit(solution)/shard_map/ppermute | solution.py:319
  141.2 1.1 collective-permute-start.14
  142.3 0.0 collective-permute-done.8
  142.3 0.2 collective-permute-start.16
  142.5 0.0 collective-permute-done.7
  142.5 0.0 collective-permute-done.9
  142.6 4.4 %collective-permute-done.15 = f32[1,6,16,256]{3,2,1,0:T(8,128)S(1)} collective-permute-done((f32[1,6,16,256]{3,2,1,0:T(8,128)S(1)}, f32[1,6,16,256]{3,2,1,0:T(8,128)S(1)}, u32[]{:S(2)}, u32[]{:S(2)}) %collective-permute-start.15) | collective-permute-done | bytes 98336 | tf_op jit(solution)/shard_map/ppermute | solution.py:319
  147.0 1.0 collective-permute-done.14
  148.0 0.6 collective-permute-done.16
  148.7 0.7 maximum_select_fusion
  (6 shorter events, 0.3 us)
Async XLA Ops:
  2.0 73.6 %collective-permute-start = (f32[256,256]{1,0:T(8,128)S(1)}, f32[256,256]{1,0:T(8,128)S(1)}, u32[]{:S(2)}, u32[]{:S(2)}) collective-permute-start(f32[256,256]{1,0:T(8,128)S(1)} %get-tuple-element.58), channel_id=1, source_target_pairs={{0,2},{2,4},{4,6},{6,8},{8,10},{10,12},{12,14},{14,16},{16,18},{18... | collective-permute-start | bytes 786440 | tf_op jit(solution)/shard_map/ppermute | solution.py:305
  6.9 68.7 %collective-permute-start.1 = (f32[256,256]{1,0:T(8,128)S(1)}, f32[256,256]{1,0:T(8,128)S(1)}, u32[]{:S(2)}, u32[]{:S(2)}) collective-permute-start(f32[256,256]{1,0:T(8,128)S(1)} %get-tuple-element.56), channel_id=1, source_target_pairs={{2,0},{4,2},{6,4},{8,6},{10,8},{12,10},{14,12},{16,14},{18,16},{20... | collective-permute-start | bytes 786440 | tf_op jit(solution)/shard_map/ppermute | solution.py:305
  75.6 6.0 %copy-start.2 = (f32[256,256]{1,0:T(8,128)}, f32[256,256]{1,0:T(8,128)S(1)}, u32[]{:S(2)}) copy-start(f32[256,256]{1,0:T(8,128)S(1)} %collective-permute-done.refs_1_) | copy-start | bytes 786436
  75.6 6.0 %copy-start.3 = (f32[256,256]{1,0:T(8,128)}, f32[256,256]{1,0:T(8,128)S(1)}, u32[]{:S(2)}) copy-start(f32[256,256]{1,0:T(8,128)S(1)} %collective-permute-done.1.refs_2_) | copy-start | bytes 786436
  75.6 22.8 %collective-permute-start.10 = (f32[16,256,128]{2,1,0:T(8,128)}, f32[16,256,128]{2,1,0:T(8,128)S(1)}, u32[]{:S(2)}, u32[]{:S(2)}) collective-permute-start(f32[16,256,128]{2,1,0:T(8,128)} %get-tuple-element.38), channel_id=1, source_target_pairs={{0,1},{1,0},{2,3},{3,2},{4,5},{5,4},{6,7},{7,6},{8,9},{9,8},{10,11... | collective-permute-start | bytes 6291464 | tf_op jit(solution)/shard_map/ppermute | solution.py:375
  75.7 12.4 %collective-permute-start.2 = (f32[256,256]{1,0:T(8,128)S(1)}, f32[256,256]{1,0:T(8,128)S(1)}, u32[]{:S(2)}, u32[]{:S(2)}) collective-permute-start(f32[256,256]{1,0:T(8,128)S(1)} %get-tuple-element.59), channel_id=1, source_target_pairs={{0,2},{2,4},{4,6},{6,8},{8,10},{10,12},{12,14},{14,16},{16,18},{18... | collective-permute-start | bytes 786440 | tf_op jit(solution)/shard_map/ppermute | solution.py:305
  80.3 14.6 %collective-permute-start.3 = (f32[256,256]{1,0:T(8,128)S(1)}, f32[256,256]{1,0:T(8,128)S(1)}, u32[]{:S(2)}, u32[]{:S(2)}) collective-permute-start(f32[256,256]{1,0:T(8,128)S(1)} %get-tuple-element.57), channel_id=1, source_target_pairs={{2,0},{4,2},{6,4},{8,6},{10,8},{12,10},{14,12},{16,14},{18,16},{20... | collective-permute-start | bytes 786440 | tf_op jit(solution)/shard_map/ppermute | solution.py:305
  88.1 10.3 %copy-start.5 = (f32[256,256]{1,0:T(8,128)}, f32[256,256]{1,0:T(8,128)S(1)}, u32[]{:S(2)}) copy-start(f32[256,256]{1,0:T(8,128)S(1)} %collective-permute-done.2.refs_2_) | copy-start | bytes 786436
  94.9 3.5 %copy-start.6 = (f32[256,256]{1,0:T(8,128)}, f32[256,256]{1,0:T(8,128)S(1)}, u32[]{:S(2)}) copy-start(f32[256,256]{1,0:T(8,128)S(1)} %collective-permute-done.3.refs_3_) | copy-start | bytes 786436
  94.9 25.9 %copy-start.1 = (f32[4,6,16,256]{3,2,1,0:T(8,128)S(1)}, f32[4,6,16,256]{3,2,1,0:T(8,128)}, u32[]{:S(2)}) copy-start(f32[4,6,16,256]{3,2,1,0:T(8,128)} %get-tuple-element.36) | copy-start | bytes 1179652
  94.9 22.3 %collective-permute-start.6 = (f32[4,6,16,256]{3,2,1,0:T(8,128)}, f32[4,6,16,256]{3,2,1,0:T(8,128)S(1)}, u32[]{:S(2)}, u32[]{:S(2)}) collective-permute-start(f32[4,6,16,256]{3,2,1,0:T(8,128)} %get-tuple-element.35), channel_id=1, source_target_pairs={{0,2},{2,0},{4,6},{6,4},{8,10},{10,8},{12,14},{14,12},{16,18},{18,... | collective-permute-start | bytes 1179656 | tf_op jit(solution)/shard_map/ppermute | solution.py:319
  95.5 21.7 %collective-permute-start.5 = (f32[4,6,16,256]{3,2,1,0:T(8,128)}, f32[4,6,16,256]{3,2,1,0:T(8,128)S(1)}, u32[]{:S(2)}, u32[]{:S(2)}) collective-permute-start(f32[4,6,16,256]{3,2,1,0:T(8,128)} %get-tuple-element.34), channel_id=1, source_target_pairs={{0,4},{2,6},{4,0},{6,2},{8,12},{10,14},{12,8},{14,10},{16,20},{18,... | collective-permute-start | bytes 1179656 | tf_op jit(solution)/shard_map/ppermute | solution.py:319
  97.2 20.1 %collective-permute-start.4 = (f32[4,6,16,256]{3,2,1,0:T(8,128)}, f32[4,6,16,256]{3,2,1,0:T(8,128)S(1)}, u32[]{:S(2)}, u32[]{:S(2)}) collective-permute-start(f32[4,6,16,256]{3,2,1,0:T(8,128)} %get-tuple-element.33), channel_id=1, source_target_pairs={{0,6},{2,4},{4,2},{6,0},{8,14},{10,12},{12,10},{14,8},{16,22},{18,... | collective-permute-start | bytes 1179656 | tf_op jit(solution)/shard_map/ppermute | solution.py:319
  98.4 1.3 copy-start.4
  117.2 21.1 %copy-start = (f32[4,6,16,256]{3,2,1,0:T(8,128)S(1)}, f32[4,6,16,256]{3,2,1,0:T(8,128)}, u32[]{:S(2)}) copy-start(f32[4,6,16,256]{3,2,1,0:T(8,128)} %get-tuple-element.49) | copy-start | bytes 1179652
  117.2 18.6 %collective-permute-start.12 = (f32[4,6,16,256]{3,2,1,0:T(8,128)}, f32[4,6,16,256]{3,2,1,0:T(8,128)S(1)}, u32[]{:S(2)}, u32[]{:S(2)}) collective-permute-start(f32[4,6,16,256]{3,2,1,0:T(8,128)} %get-tuple-element.47), channel_id=1, source_target_pairs={{0,4},{2,6},{4,0},{6,2},{8,12},{10,14},{12,8},{14,10},{16,20},{18,... | collective-permute-start | bytes 1179656 | tf_op jit(solution)/shard_map/ppermute | solution.py:319
  117.6 20.7 %collective-permute-start.11 = (f32[4,6,16,256]{3,2,1,0:T(8,128)}, f32[4,6,16,256]{3,2,1,0:T(8,128)S(1)}, u32[]{:S(2)}, u32[]{:S(2)}) collective-permute-start(f32[4,6,16,256]{3,2,1,0:T(8,128)} %get-tuple-element.46), channel_id=1, source_target_pairs={{0,6},{2,4},{4,2},{6,0},{8,14},{10,12},{12,10},{14,8},{16,22},{18,... | collective-permute-start | bytes 1179656 | tf_op jit(solution)/shard_map/ppermute | solution.py:319
  119.4 19.0 %collective-permute-start.13 = (f32[4,6,16,256]{3,2,1,0:T(8,128)}, f32[4,6,16,256]{3,2,1,0:T(8,128)S(1)}, u32[]{:S(2)}, u32[]{:S(2)}) collective-permute-start(f32[4,6,16,256]{3,2,1,0:T(8,128)} %get-tuple-element.48), channel_id=1, source_target_pairs={{0,2},{2,0},{4,6},{6,4},{8,10},{10,8},{12,14},{14,12},{16,18},{18,... | collective-permute-start | bytes 1179656 | tf_op jit(solution)/shard_map/ppermute | solution.py:319
  121.0 21.3 %collective-permute-start.8 = (f32[1,6,16,256]{3,2,1,0:T(8,128)S(1)}, f32[1,6,16,256]{3,2,1,0:T(8,128)S(1)}, u32[]{:S(2)}, u32[]{:S(2)}) collective-permute-start(f32[1,6,16,256]{3,2,1,0:T(8,128)S(1)} %get-tuple-element.65), channel_id=1, source_target_pairs={{0,16},{2,18},{4,20},{6,22},{8,24},{10,26},{12,28},{14,30},{16,0},... | collective-permute-start | bytes 294920 | tf_op jit(solution)/shard_map/ppermute | solution.py:319
  124.0 18.5 %collective-permute-start.7 = (f32[1,6,16,256]{3,2,1,0:T(8,128)S(1)}, f32[1,6,16,256]{3,2,1,0:T(8,128)S(1)}, u32[]{:S(2)}, u32[]{:S(2)}) collective-permute-start(f32[1,6,16,256]{3,2,1,0:T(8,128)S(1)} %get-tuple-element.64), channel_id=1, source_target_pairs={{0,24},{2,26},{4,28},{6,30},{8,16},{10,18},{12,20},{14,22},{16,8},... | collective-permute-start | bytes 294920 | tf_op jit(solution)/shard_map/ppermute | solution.py:319
  135.8 6.7 %collective-permute-start.9 = (f32[1,6,16,256]{3,2,1,0:T(8,128)S(1)}, f32[1,6,16,256]{3,2,1,0:T(8,128)S(1)}, u32[]{:S(2)}, u32[]{:S(2)}) collective-permute-start(f32[1,6,16,256]{3,2,1,0:T(8,128)S(1)} %get-tuple-element.66), channel_id=1, source_target_pairs={{0,8},{2,10},{4,12},{6,14},{8,0},{10,2},{12,4},{14,6},{16,24},{18,... | collective-permute-start | bytes 294920 | tf_op jit(solution)/shard_map/ppermute | solution.py:319
  138.6 8.4 %collective-permute-start.15 = (f32[1,6,16,256]{3,2,1,0:T(8,128)S(1)}, f32[1,6,16,256]{3,2,1,0:T(8,128)S(1)}, u32[]{:S(2)}, u32[]{:S(2)}) collective-permute-start(f32[1,6,16,256]{3,2,1,0:T(8,128)S(1)} %get-tuple-element.69), channel_id=1, source_target_pairs={{0,16},{2,18},{4,20},{6,22},{8,24},{10,26},{12,28},{14,30},{16,0},... | collective-permute-start | bytes 294920 | tf_op jit(solution)/shard_map/ppermute | solution.py:319
  141.2 6.8 %collective-permute-start.14 = (f32[1,6,16,256]{3,2,1,0:T(8,128)S(1)}, f32[1,6,16,256]{3,2,1,0:T(8,128)S(1)}, u32[]{:S(2)}, u32[]{:S(2)}) collective-permute-start(f32[1,6,16,256]{3,2,1,0:T(8,128)S(1)} %get-tuple-element.68), channel_id=1, source_target_pairs={{0,24},{2,26},{4,28},{6,30},{8,16},{10,18},{12,20},{14,22},{16,8},... | collective-permute-start | bytes 294920 | tf_op jit(solution)/shard_map/ppermute | solution.py:319
  142.3 6.3 %collective-permute-start.16 = (f32[1,6,16,256]{3,2,1,0:T(8,128)S(1)}, f32[1,6,16,256]{3,2,1,0:T(8,128)S(1)}, u32[]{:S(2)}, u32[]{:S(2)}) collective-permute-start(f32[1,6,16,256]{3,2,1,0:T(8,128)S(1)} %get-tuple-element.70), channel_id=1, source_target_pairs={{0,8},{2,10},{4,12},{6,14},{8,0},{10,2},{12,4},{14,6},{16,24},{18,... | collective-permute-start | bytes 294920 | tf_op jit(solution)/shard_map/ppermute | solution.py:319

commit v11 on v10

--- a/solution.py
+++ b/solution.py
@@ -60,7 +60,7 @@
     low, high = (refs.pop(0), refs.pop(0)) if mode != "middle" else (None, None)
     rim = mode == "rim"
     middle = refs.pop(0) if rim else None
-    inner = refs.pop() if rim else None
+    inner = refs.pop() if mode != "outer" else None
     cells, canvas, table, in_sems, out_sems = refs[-5:]
     outs = refs[:-5]
     if mode == "middle":
@@ -100,7 +100,8 @@
                 pairs.append((field.at[pl.ds(first, count), body, lanes], target))
         if mode != "middle":
             for tile in computed:
-                lanes = pl.ds((tile - 1) * LANES, LANES)
+                lane = (1 - nearer) * (width // 2) + (tile - 1) * LANES
+                lanes = pl.ds(pl.multiple_of(lane, LANES), LANES)
                 for halo, plane in ((low, -1), (high, planes)):
                     target = cells.at[tile, place[plane], padded, :]
                     pairs.append((halo.at[body, lanes], target))
@@ -138,10 +139,11 @@
         start(piece)
     if mode == "middle":
         first = pl.multiple_of((1 - core) * (width - LANES), LANES)
-        edge_copy = pltpu.make_async_copy(
-            field.at[:, :, pl.ds(first, LANES)], edge, out_sems.at[0, group]
+        edge_in = pltpu.make_async_copy(
+            field.at[:, :, pl.ds(first, LANES)], inner, out_sems.at[0, group]
         )
-        edge_copy.start()
+        edge_out = pltpu.make_async_copy(inner, edge, out_sems.at[1, group])
+        edge_in.start()
         prepare_tables(tables_a, tables_b, depth_total, table, words, factors)
     zeros = jnp.zeros((1, LANES), jnp.float32)
     for tile in computed:
@@ -231,6 +233,12 @@
 
         for copy in outgoing(piece):
             copy.start()
+        if mode == "middle":
+
+            @pl.when(piece == pieces // 2)
+            def _():
+                edge_in.wait()
+                edge_out.start()
 
     @pl.loop(0, pieces)
     def _(piece):
@@ -238,7 +246,7 @@
             copy.wait()
 
     if mode == "middle":
-        edge_copy.wait()
+        edge_out.wait()
 
 
 def march(mode, tables, field, side, halos, middle, depth_total, scale, part_shape):
@@ -270,6 +278,8 @@
     if rim:
         operands.append(middle)
         scratch.append(pltpu.VMEM((6, height, extent), jnp.float32))
+    if mode == "middle":
+        scratch.append(pltpu.VMEM((planes, height, LANES), jnp.float32))
     near = pl.BlockSpec(memory_space=pltpu.VMEM)
     out_specs = [pl.BlockSpec(memory_space=pl.ANY)] * len(outs)
     if mode == "middle":
@@ -279,7 +289,7 @@
         out_specs += [pl.BlockSpec(memory_space=pl.ANY), near, near]
     strips = height // pieces // SUBLANES
     unroll = min(strips, {"rim": 4, "outer": 4, "middle": 2}[mode])
-    weight = 20000 if mode == "outer" else 100
+    weight = 20000 if mode == "outer" else 0
     distant = pl.BlockSpec(memory_space=pl.ANY)
     out = pl.pallas_call(
         functools.partial(march_kernel, mode, depth_total, group, scale, unroll, pieces),
@@ -290,7 +300,7 @@
         compiler_params=pltpu.CompilerParams(vmem_limit_bytes=56 * 1024 * 1024),
         cost_estimate=pl.CostEstimate(
             flops=planes * height * 256 * weight,
-            bytes_accessed=planes * height * 256 * 5,
+            bytes_accessed=planes * height * 4 * weight,
             transcendentals=0,
         ),
         name=f"march_{mode}",
@@ -360,26 +370,21 @@
     tables = (tf_emission, tf_absorption)
 
     core = lax.axis_index("tile")
-    half = width // 2
-    halos = []
-    for start in (core * half, (1 - core) * half):
-        first, last = (
-            lax.dynamic_slice_in_dim(field[plane], start, half, axis=1) for plane in (0, -1)
-        )
-        halos.append(plane_halos(first, last))
+    halo = plane_halos(field[0], field[-1])
     scale = 0.5 * (tf_emission.shape[1] - 1)
     middle, edge, *tables = march(
         "middle", tables, field, None, None, None, depth_total, scale, None
     )
-    edge, _ = lax.optimization_barrier((edge, halos[0]))
+    edge, _ = lax.optimization_barrier((edge, halo))
     side = lax.ppermute(edge, "tile", [(0, 1), (1, 0)])
     arrived = None
     results = []
-    for mode, halo in zip(("rim", "outer"), halos):
+    for mode in ("rim", "outer"):
         if arrived is not None:
             halo, side, _ = lax.optimization_barrier((halo, side, out))
         out = march(mode, tables, field, side, halo, middle, depth_total, scale, part_shape)
-        out, _ = lax.optimization_barrier((out, halos[1] if arrived is None else arrived))
+        if arrived is not None:
+            out, _ = lax.optimization_barrier((out, arrived))
         image, parts = (out, None) if part_shape is None else (None, out)
         result, arrived = reduce_image(image, parts, slab_index, block_rows)
         results.append(result)

time: 150 us -> 92.2 us (0.61)
  Pallas kernels: 91.3 us -> 41.4 us
  starting transfers between devices: 29.9 us -> 22.8 us
    pallas_call x3, Pallas kernels: 91.3 us -> 41.4 us  [march(): pl.pallas_call(functools.partial(march_kernel, mode, depth_total, group,...]
    ppermute x2 -> x1, waiting for transfers between devices: 6.81 us -> 1.94 us  [plane_halos(): lax.ppermute(first, 'slab', backward)]
    ppermute x2 -> x1, starting transfers between devices: 9.42 us -> 4.88 us  [plane_halos(): lax.ppermute(last, 'slab', forward)]
    ppermute x2 -> x1, waiting for transfers between devices: 0.01 us -> 3.48 us  [plane_halos(): lax.ppermute(last, 'slab', forward)]
  transfers between devices with their start and end apart: 17 -> 15, of which waited for: 5 -> 6; matrix products, arithmetic and copies ran while one was open for 0% -> 1% of each run, Pallas kernels for 61% -> 45%
where the time goes in v11:
time: 92.2 us; the launch traced here: 91.9 us
  Pallas kernels  41.4 us (45%)
  starting transfers between devices  22.8 us (25%)
  waiting for transfers between devices  22.3 us (24%)
  local copies, waits for them, and re-layouts  3.42 us (4%)
  other arithmetic  1.23 us (1%)
    pallas_call x3, Pallas kernels, march(): pl.pallas_call(functools.partial(march_kernel, mode, depth_total, group,...  41.4 us
    ppermute x12, waiting for transfers between devices, exchange(): lax.ppermute(part, 'slab', [(i, i ^ change << shift) for i in range(count)])  16.8 us
    ppermute x12, starting transfers between devices, exchange(): lax.ppermute(part, 'slab', [(i, i ^ change << shift) for i in range(count)])  16.6 us
    ppermute x1, starting transfers between devices, plane_halos(): lax.ppermute(last, 'slab', forward)  4.88 us
    ppermute x1, waiting for transfers between devices, plane_halos(): lax.ppermute(last, 'slab', forward)  3.48 us
    unnamed x10, local copies, waits for them, and re-layouts  2.15 us
    ppermute x1, waiting for transfers between devices, plane_halos(): lax.ppermute(first, 'slab', backward)  1.94 us
  transfers between devices with their start and end apart: 15, of which 6 were waited for; matrix products, arithmetic and copies ran while one was open for 1% of the time, Pallas kernels for 45%

profile of v11, /device:TPU:0, one launch (start us, length us, event | category | flops | bytes accessed | tf_op | source)
XLA Modules:
  0.0 91.9 jit_solution(18203070350940204845)
XLA Ops:
  0.6 1.3 %slice_bitcast_fusion = (f32[256,512]{1,0:T(8,128)S(1)}, f32[256,512]{1,0:T(8,128)S(1)}) fusion(f32[16,256,512]{2,1,0:T(8,128)} %refs_0_.5), kind=kLoop, calls=%fused_computation.16 | loop fusion | bytes 2097152 | tf_op jit(solution)/shard_map/squeeze | solution.py:373
  1.9 4.9 %collective-permute-start = (f32[256,512]{1,0:T(8,128)S(1)}, f32[256,512]{1,0:T(8,128)S(1)}, u32[]{:S(2)}, u32[]{:S(2)}) collective-permute-start(f32[256,512]{1,0:T(8,128)S(1)} %get-tuple-element.43), channel_id=1, source_target_pairs={{0,2},{2,4},{4,6},{6,8},{8,10},{10,12},{12,14},{14,16},{16,18},{18... | collective-permute-start | bytes 1572872 | tf_op jit(solution)/shard_map/ppermute | solution.py:315
  6.8 1.3 %collective-permute-start.1 = (f32[256,512]{1,0:T(8,128)S(1)}, f32[256,512]{1,0:T(8,128)S(1)}, u32[]{:S(2)}, u32[]{:S(2)}) collective-permute-start(f32[256,512]{1,0:T(8,128)S(1)} %get-tuple-element.42), channel_id=1, source_target_pairs={{2,0},{4,2},{6,4},{8,6},{10,8},{12,10},{14,12},{16,14},{18,16},{20... | collective-permute-start | bytes 1572872 | tf_op jit(solution)/shard_map/ppermute | solution.py:315
  8.1 17.6 %march_middle.1 = (f32[6,256,256]{2,1,0:T(8,128)}, f32[16,256,128]{2,1,0:T(8,128)}, s32[6,8,128]{2,1,0:T(8,128)}, f32[6,8,128]{2,1,0:T(8,128)}) custom-call(f32[3,16]{1,0:T(4,128)} %tables_a.1, f32[3,16]{1,0:T(4,128)} %tables_b.1, f32[16,256,512]{2,1,0:T(8,128)} %refs_0_.5), custom_call_target="tpu_custom_call" | custom-call | tf_op jit(solution)/shard_map/march_middle/pallas_call | solution.py:294
  25.7 3.5 %collective-permute-done.refs_1_.refs_2_ = f32[256,512]{1,0:T(8,128)S(1)} collective-permute-done((f32[256,512]{1,0:T(8,128)S(1)}, f32[256,512]{1,0:T(8,128)S(1)}, u32[]{:S(2)}, u32[]{:S(2)}) %collective-permute-start) | collective-permute-done | bytes 524320 | tf_op jit(solution)/shard_map/ppermute | solution.py:315
  29.2 0.0 copy-start
  29.2 1.9 %collective-permute-done.1.refs_2_.refs_3_ = f32[256,512]{1,0:T(8,128)S(1)} collective-permute-done((f32[256,512]{1,0:T(8,128)S(1)}, f32[256,512]{1,0:T(8,128)S(1)}, u32[]{:S(2)}, u32[]{:S(2)}) %collective-permute-start.1) | collective-permute-done | bytes 524320 | tf_op jit(solution)/shard_map/ppermute | solution.py:315
  31.1 0.0 copy-start.1
  31.1 0.0 collective-permute-start.8
  31.1 0.0 copy-done
  31.1 0.8 copy-done.1
  31.9 6.4 %march_rim.1 = (f32[4,6,16,256]{3,2,1,0:T(8,128)}, f32[4,6,16,256]{3,2,1,0:T(8,128)}, f32[4,6,16,256]{3,2,1,0:T(8,128)}, f32[4,6,16,256]{3,2,1,0:T(8,128)}) custom-call(s32[6,8,128]{2,1,0:T(8,128)} %get-tuple-element.22.tables_a, f32[6,8,128]{2,1,0:T(8,128)} %get-tuple-element.23.tables_b, f32[16,256,512]{2,1,0:T(8,128)} %refs_0_.5, f32[256,512]{1,0:T(8,128)} %copy-done, ...), custom_call_target="tpu_custom_call" | custom-call | tf_op jit(solution)/shard_map/march_rim/pallas_call | solution.py:294
  38.3 1.6 %collective-permute-start.4 = (f32[4,6,16,256]{3,2,1,0:T(8,128)}, f32[4,6,16,256]{3,2,1,0:T(8,128)S(1)}, u32[]{:S(2)}, u32[]{:S(2)}) collective-permute-start(f32[4,6,16,256]{3,2,1,0:T(8,128)} %get-tuple-element.27), channel_id=1, source_target_pairs={{0,2},{2,0},{4,6},{6,4},{8,10},{10,8},{12,14},{14,12},{16,18},{18,... | collective-permute-start | bytes 1179656 | tf_op jit(solution)/shard_map/ppermute | solution.py:329
  39.9 0.0 collective-permute-start.3
  39.9 2.0 %collective-permute-start.2 = (f32[4,6,16,256]{3,2,1,0:T(8,128)}, f32[4,6,16,256]{3,2,1,0:T(8,128)S(1)}, u32[]{:S(2)}, u32[]{:S(2)}) collective-permute-start(f32[4,6,16,256]{3,2,1,0:T(8,128)} %get-tuple-element.25), channel_id=1, source_target_pairs={{0,6},{2,4},{4,2},{6,0},{8,14},{10,12},{12,10},{14,8},{16,22},{18,... | collective-permute-start | bytes 1179656 | tf_op jit(solution)/shard_map/ppermute | solution.py:329
  41.9 0.0 collective-permute-done.8.refs_1_
  41.9 0.0 copy-start.4
  41.9 1.3 %copy-done.4 = f32[16,256,128]{2,1,0:T(8,128)} copy-done((f32[16,256,128]{2,1,0:T(8,128)}, f32[16,256,128]{2,1,0:T(8,128)S(1)}, u32[]{:S(2)}) %copy-start.4) | copy-done | bytes 2097176
  43.2 0.0 copy-start.3
  43.2 17.5 %march_outer.1 = (f32[4,6,16,256]{3,2,1,0:T(8,128)}, f32[4,6,16,256]{3,2,1,0:T(8,128)}, f32[4,6,16,256]{3,2,1,0:T(8,128)}, f32[4,6,16,256]{3,2,1,0:T(8,128)}) custom-call(s32[6,8,128]{2,1,0:T(8,128)} %get-tuple-element.22.tables_a, f32[6,8,128]{2,1,0:T(8,128)} %get-tuple-element.23.tables_b, f32[16,256,512]{2,1,0:T(8,128)} %refs_0_.5, ...), custom_call_target="tpu_custom_call" | custom-call | flops 20971520000 | bytes 327680000 | tf_op jit(solution)/shard_map/march_outer/pallas_call | solution.py:294
  60.7 0.0 copy-start.2
  60.7 0.0 collective-permute-done.4
  60.7 0.0 collective-permute-done.3
  60.7 0.0 collective-permute-done.2
  60.7 0.1 collective-permute-start.10
  60.8 2.9 %collective-permute-start.9 = (f32[4,6,16,256]{3,2,1,0:T(8,128)}, f32[4,6,16,256]{3,2,1,0:T(8,128)S(1)}, u32[]{:S(2)}, u32[]{:S(2)}) collective-permute-start(f32[4,6,16,256]{3,2,1,0:T(8,128)} %get-tuple-element.38), channel_id=1, source_target_pairs={{0,6},{2,4},{4,2},{6,0},{8,14},{10,12},{12,10},{14,8},{16,22},{18,... | collective-permute-start | bytes 1179656 | tf_op jit(solution)/shard_map/ppermute | solution.py:329
  63.7 0.5 collective-permute-start.11
  64.3 0.0 copy-done.3
  64.3 0.2 select_multiply_fusion.3
  64.5 2.7 %collective-permute-start.6 = (f32[1,6,16,256]{3,2,1,0:T(8,128)S(1)}, f32[1,6,16,256]{3,2,1,0:T(8,128)S(1)}, u32[]{:S(2)}, u32[]{:S(2)}) collective-permute-start(f32[1,6,16,256]{3,2,1,0:T(8,128)S(1)} %get-tuple-element.53), channel_id=1, source_target_pairs={{0,16},{2,18},{4,20},{6,22},{8,24},{10,26},{12,28},{14,30},{16,0},... | collective-permute-start | bytes 294920 | tf_op jit(solution)/shard_map/ppermute | solution.py:329
  67.2 1.3 %collective-permute-start.5 = (f32[1,6,16,256]{3,2,1,0:T(8,128)S(1)}, f32[1,6,16,256]{3,2,1,0:T(8,128)S(1)}, u32[]{:S(2)}, u32[]{:S(2)}) collective-permute-start(f32[1,6,16,256]{3,2,1,0:T(8,128)S(1)} %get-tuple-element.52), channel_id=1, source_target_pairs={{0,24},{2,26},{4,28},{6,30},{8,16},{10,18},{12,20},{14,22},{16,8},... | collective-permute-start | bytes 294920 | tf_op jit(solution)/shard_map/ppermute | solution.py:329
  68.5 10.8 %collective-permute-done.10 = f32[4,6,16,256]{3,2,1,0:T(8,128)S(1)} collective-permute-done((f32[4,6,16,256]{3,2,1,0:T(8,128)}, f32[4,6,16,256]{3,2,1,0:T(8,128)S(1)}, u32[]{:S(2)}, u32[]{:S(2)}) %collective-permute-start.10) | collective-permute-done | bytes 393248 | tf_op jit(solution)/shard_map/ppermute | solution.py:329
  79.3 1.6 %collective-permute-start.7 = (f32[1,6,16,256]{3,2,1,0:T(8,128)S(1)}, f32[1,6,16,256]{3,2,1,0:T(8,128)S(1)}, u32[]{:S(2)}, u32[]{:S(2)}) collective-permute-start(f32[1,6,16,256]{3,2,1,0:T(8,128)S(1)} %get-tuple-element.54), channel_id=1, source_target_pairs={{0,8},{2,10},{4,12},{6,14},{8,0},{10,2},{12,4},{14,6},{16,24},{18,... | collective-permute-start | bytes 294920 | tf_op jit(solution)/shard_map/ppermute | solution.py:329
  80.9 0.0 collective-permute-done.9
  80.9 0.0 collective-permute-done.11
  80.9 0.0 copy-done.2
  80.9 0.2 select_multiply_fusion
  81.1 2.7 %collective-permute-start.13 = (f32[1,6,16,256]{3,2,1,0:T(8,128)S(1)}, f32[1,6,16,256]{3,2,1,0:T(8,128)S(1)}, u32[]{:S(2)}, u32[]{:S(2)}) collective-permute-start(f32[1,6,16,256]{3,2,1,0:T(8,128)S(1)} %get-tuple-element.57), channel_id=1, source_target_pairs={{0,16},{2,18},{4,20},{6,22},{8,24},{10,26},{12,28},{14,30},{16,0},... | collective-permute-start | bytes 294920 | tf_op jit(solution)/shard_map/ppermute | solution.py:329
  83.8 1.0 %collective-permute-start.12 = (f32[1,6,16,256]{3,2,1,0:T(8,128)S(1)}, f32[1,6,16,256]{3,2,1,0:T(8,128)S(1)}, u32[]{:S(2)}, u32[]{:S(2)}) collective-permute-start(f32[1,6,16,256]{3,2,1,0:T(8,128)S(1)} %get-tuple-element.56), channel_id=1, source_target_pairs={{0,24},{2,26},{4,28},{6,30},{8,16},{10,18},{12,20},{14,22},{16,8},... | collective-permute-start | bytes 294920 | tf_op jit(solution)/shard_map/ppermute | solution.py:329
  84.8 0.0 collective-permute-done.6
  84.8 0.2 collective-permute-start.14
  85.0 0.0 collective-permute-done.5
  85.1 0.0 collective-permute-done.7
  85.1 4.0 %collective-permute-done.13 = f32[1,6,16,256]{3,2,1,0:T(8,128)S(1)} collective-permute-done((f32[1,6,16,256]{3,2,1,0:T(8,128)S(1)}, f32[1,6,16,256]{3,2,1,0:T(8,128)S(1)}, u32[]{:S(2)}, u32[]{:S(2)}) %collective-permute-start.13) | collective-permute-done | bytes 98336 | tf_op jit(solution)/shard_map/ppermute | solution.py:329
  89.1 1.3 %collective-permute-done.12 = f32[1,6,16,256]{3,2,1,0:T(8,128)S(1)} collective-permute-done((f32[1,6,16,256]{3,2,1,0:T(8,128)S(1)}, f32[1,6,16,256]{3,2,1,0:T(8,128)S(1)}, u32[]{:S(2)}, u32[]{:S(2)}) %collective-permute-start.12) | collective-permute-done | bytes 98336 | tf_op jit(solution)/shard_map/ppermute | solution.py:329
  90.4 0.8 collective-permute-done.14
  91.2 0.7 maximum_select_fusion
  (4 shorter events, 0.2 us)
Async XLA Ops:
  1.9 27.2 %collective-permute-start = (f32[256,512]{1,0:T(8,128)S(1)}, f32[256,512]{1,0:T(8,128)S(1)}, u32[]{:S(2)}, u32[]{:S(2)}) collective-permute-start(f32[256,512]{1,0:T(8,128)S(1)} %get-tuple-element.43), channel_id=1, source_target_pairs={{0,2},{2,4},{4,6},{6,8},{8,10},{10,12},{12,14},{14,16},{16,18},{18... | collective-permute-start | bytes 1572872 | tf_op jit(solution)/shard_map/ppermute | solution.py:315
  6.8 24.3 %collective-permute-start.1 = (f32[256,512]{1,0:T(8,128)S(1)}, f32[256,512]{1,0:T(8,128)S(1)}, u32[]{:S(2)}, u32[]{:S(2)}) collective-permute-start(f32[256,512]{1,0:T(8,128)S(1)} %get-tuple-element.42), channel_id=1, source_target_pairs={{2,0},{4,2},{6,4},{8,6},{10,8},{12,10},{14,12},{16,14},{18,16},{20... | collective-permute-start | bytes 1572872 | tf_op jit(solution)/shard_map/ppermute | solution.py:315
  29.2 2.0 %copy-start = (f32[256,512]{1,0:T(8,128)}, f32[256,512]{1,0:T(8,128)S(1)}, u32[]{:S(2)}) copy-start(f32[256,512]{1,0:T(8,128)S(1)} %collective-permute-done.refs_1_.refs_2_) | copy-start | bytes 1572868
  31.1 0.8 copy-start.1
  31.1 10.8 %collective-permute-start.8 = (f32[16,256,128]{2,1,0:T(8,128)}, f32[16,256,128]{2,1,0:T(8,128)S(1)}, u32[]{:S(2)}, u32[]{:S(2)}) collective-permute-start(f32[16,256,128]{2,1,0:T(8,128)} %get-tuple-element.30), channel_id=1, source_target_pairs={{0,1},{1,0},{2,3},{3,2},{4,5},{5,4},{6,7},{7,6},{8,9},{9,8},{10,11... | collective-permute-start | bytes 6291464 | tf_op jit(solution)/shard_map/ppermute | solution.py:379
  38.3 22.4 %collective-permute-start.4 = (f32[4,6,16,256]{3,2,1,0:T(8,128)}, f32[4,6,16,256]{3,2,1,0:T(8,128)S(1)}, u32[]{:S(2)}, u32[]{:S(2)}) collective-permute-start(f32[4,6,16,256]{3,2,1,0:T(8,128)} %get-tuple-element.27), channel_id=1, source_target_pairs={{0,2},{2,0},{4,6},{6,4},{8,10},{10,8},{12,14},{14,12},{16,18},{18,... | collective-permute-start | bytes 1179656 | tf_op jit(solution)/shard_map/ppermute | solution.py:329
  39.9 20.8 %collective-permute-start.3 = (f32[4,6,16,256]{3,2,1,0:T(8,128)}, f32[4,6,16,256]{3,2,1,0:T(8,128)S(1)}, u32[]{:S(2)}, u32[]{:S(2)}) collective-permute-start(f32[4,6,16,256]{3,2,1,0:T(8,128)} %get-tuple-element.26), channel_id=1, source_target_pairs={{0,4},{2,6},{4,0},{6,2},{8,12},{10,14},{12,8},{14,10},{16,20},{18,... | collective-permute-start | bytes 1179656 | tf_op jit(solution)/shard_map/ppermute | solution.py:329
  39.9 20.8 %collective-permute-start.2 = (f32[4,6,16,256]{3,2,1,0:T(8,128)}, f32[4,6,16,256]{3,2,1,0:T(8,128)S(1)}, u32[]{:S(2)}, u32[]{:S(2)}) collective-permute-start(f32[4,6,16,256]{3,2,1,0:T(8,128)} %get-tuple-element.25), channel_id=1, source_target_pairs={{0,6},{2,4},{4,2},{6,0},{8,14},{10,12},{12,10},{14,8},{16,22},{18,... | collective-permute-start | bytes 1179656 | tf_op jit(solution)/shard_map/ppermute | solution.py:329
  41.9 1.3 %copy-start.4 = (f32[16,256,128]{2,1,0:T(8,128)}, f32[16,256,128]{2,1,0:T(8,128)S(1)}, u32[]{:S(2)}) copy-start(f32[16,256,128]{2,1,0:T(8,128)S(1)} %collective-permute-done.8.refs_1_) | copy-start | bytes 6291460
  43.2 21.1 %copy-start.3 = (f32[4,6,16,256]{3,2,1,0:T(8,128)S(1)}, f32[4,6,16,256]{3,2,1,0:T(8,128)}, u32[]{:S(2)}) copy-start(f32[4,6,16,256]{3,2,1,0:T(8,128)} %get-tuple-element.28) | copy-start | bytes 1179652
  60.7 20.2 %copy-start.2 = (f32[4,6,16,256]{3,2,1,0:T(8,128)S(1)}, f32[4,6,16,256]{3,2,1,0:T(8,128)}, u32[]{:S(2)}) copy-start(f32[4,6,16,256]{3,2,1,0:T(8,128)} %get-tuple-element.41) | copy-start | bytes 1179652
  60.7 18.6 %collective-permute-start.10 = (f32[4,6,16,256]{3,2,1,0:T(8,128)}, f32[4,6,16,256]{3,2,1,0:T(8,128)S(1)}, u32[]{:S(2)}, u32[]{:S(2)}) collective-permute-start(f32[4,6,16,256]{3,2,1,0:T(8,128)} %get-tuple-element.39), channel_id=1, source_target_pairs={{0,4},{2,6},{4,0},{6,2},{8,12},{10,14},{12,8},{14,10},{16,20},{18,... | collective-permute-start | bytes 1179656 | tf_op jit(solution)/shard_map/ppermute | solution.py:329
  60.8 20.1 %collective-permute-start.9 = (f32[4,6,16,256]{3,2,1,0:T(8,128)}, f32[4,6,16,256]{3,2,1,0:T(8,128)S(1)}, u32[]{:S(2)}, u32[]{:S(2)}) collective-permute-start(f32[4,6,16,256]{3,2,1,0:T(8,128)} %get-tuple-element.38), channel_id=1, source_target_pairs={{0,6},{2,4},{4,2},{6,0},{8,14},{10,12},{12,10},{14,8},{16,22},{18,... | collective-permute-start | bytes 1179656 | tf_op jit(solution)/shard_map/ppermute | solution.py:329
  63.7 17.2 %collective-permute-start.11 = (f32[4,6,16,256]{3,2,1,0:T(8,128)}, f32[4,6,16,256]{3,2,1,0:T(8,128)S(1)}, u32[]{:S(2)}, u32[]{:S(2)}) collective-permute-start(f32[4,6,16,256]{3,2,1,0:T(8,128)} %get-tuple-element.40), channel_id=1, source_target_pairs={{0,2},{2,0},{4,6},{6,4},{8,10},{10,8},{12,14},{14,12},{16,18},{18,... | collective-permute-start | bytes 1179656 | tf_op jit(solution)/shard_map/ppermute | solution.py:329
  64.5 20.3 %collective-permute-start.6 = (f32[1,6,16,256]{3,2,1,0:T(8,128)S(1)}, f32[1,6,16,256]{3,2,1,0:T(8,128)S(1)}, u32[]{:S(2)}, u32[]{:S(2)}) collective-permute-start(f32[1,6,16,256]{3,2,1,0:T(8,128)S(1)} %get-tuple-element.53), channel_id=1, source_target_pairs={{0,16},{2,18},{4,20},{6,22},{8,24},{10,26},{12,28},{14,30},{16,0},... | collective-permute-start | bytes 294920 | tf_op jit(solution)/shard_map/ppermute | solution.py:329
  67.2 17.9 %collective-permute-start.5 = (f32[1,6,16,256]{3,2,1,0:T(8,128)S(1)}, f32[1,6,16,256]{3,2,1,0:T(8,128)S(1)}, u32[]{:S(2)}, u32[]{:S(2)}) collective-permute-start(f32[1,6,16,256]{3,2,1,0:T(8,128)S(1)} %get-tuple-element.52), channel_id=1, source_target_pairs={{0,24},{2,26},{4,28},{6,30},{8,16},{10,18},{12,20},{14,22},{16,8},... | collective-permute-start | bytes 294920 | tf_op jit(solution)/shard_map/ppermute | solution.py:329
  79.3 5.8 %collective-permute-start.7 = (f32[1,6,16,256]{3,2,1,0:T(8,128)S(1)}, f32[1,6,16,256]{3,2,1,0:T(8,128)S(1)}, u32[]{:S(2)}, u32[]{:S(2)}) collective-permute-start(f32[1,6,16,256]{3,2,1,0:T(8,128)S(1)} %get-tuple-element.54), channel_id=1, source_target_pairs={{0,8},{2,10},{4,12},{6,14},{8,0},{10,2},{12,4},{14,6},{16,24},{18,... | collective-permute-start | bytes 294920 | tf_op jit(solution)/shard_map/ppermute | solution.py:329
  81.1 8.0 %collective-permute-start.13 = (f32[1,6,16,256]{3,2,1,0:T(8,128)S(1)}, f32[1,6,16,256]{3,2,1,0:T(8,128)S(1)}, u32[]{:S(2)}, u32[]{:S(2)}) collective-permute-start(f32[1,6,16,256]{3,2,1,0:T(8,128)S(1)} %get-tuple-element.57), channel_id=1, source_target_pairs={{0,16},{2,18},{4,20},{6,22},{8,24},{10,26},{12,28},{14,30},{16,0},... | collective-permute-start | bytes 294920 | tf_op jit(solution)/shard_map/ppermute | solution.py:329
  83.8 6.6 %collective-permute-start.12 = (f32[1,6,16,256]{3,2,1,0:T(8,128)S(1)}, f32[1,6,16,256]{3,2,1,0:T(8,128)S(1)}, u32[]{:S(2)}, u32[]{:S(2)}) collective-permute-start(f32[1,6,16,256]{3,2,1,0:T(8,128)S(1)} %get-tuple-element.56), channel_id=1, source_target_pairs={{0,24},{2,26},{4,28},{6,30},{8,16},{10,18},{12,20},{14,22},{16,8},... | collective-permute-start | bytes 294920 | tf_op jit(solution)/shard_map/ppermute | solution.py:329
  84.8 6.3 %collective-permute-start.14 = (f32[1,6,16,256]{3,2,1,0:T(8,128)S(1)}, f32[1,6,16,256]{3,2,1,0:T(8,128)S(1)}, u32[]{:S(2)}, u32[]{:S(2)}) collective-permute-start(f32[1,6,16,256]{3,2,1,0:T(8,128)S(1)} %get-tuple-element.58), channel_id=1, source_target_pairs={{0,8},{2,10},{4,12},{6,14},{8,0},{10,2},{12,4},{14,6},{16,24},{18,... | collective-permute-start | bytes 294920 | tf_op jit(solution)/shard_map/ppermute | solution.py:329

commit v12 on v11

--- a/solution.py
+++ b/solution.py
@@ -288,7 +288,7 @@
         outs.append(jax.ShapeDtypeStruct((6, SUBLANES, LANES), jnp.float32))
         out_specs += [pl.BlockSpec(memory_space=pl.ANY), near, near]
     strips = height // pieces // SUBLANES
-    unroll = min(strips, {"rim": 4, "outer": 4, "middle": 2}[mode])
+    unroll = min(strips, {"rim": 8, "outer": 4, "middle": 2}[mode])
     weight = 20000 if mode == "outer" else 0
     distant = pl.BlockSpec(memory_space=pl.ANY)
     out = pl.pallas_call(
@@ -297,7 +297,7 @@
         in_specs=[near] * 2 + [distant] * len(operands),
         out_specs=out_specs,
         scratch_shapes=scratch,
-        compiler_params=pltpu.CompilerParams(vmem_limit_bytes=56 * 1024 * 1024),
+        compiler_params=pltpu.CompilerParams(vmem_limit_bytes=44 * 1024 * 1024),
         cost_estimate=pl.CostEstimate(
             flops=planes * height * 256 * weight,
             bytes_accessed=planes * height * 4 * weight,

time: 92.2 us -> 91.8 us (level)
  local copies, waits for them, and re-layouts: 3.42 us -> 1.29 us
  other arithmetic: 1.23 us -> 3.27 us
  Pallas kernels: 41.4 us -> 40 us
  waiting for transfers between devices: 22.3 us -> 23.4 us
    unnamed x10 -> x6, local copies, waits for them, and re-layouts: 2.15 us -> 0.01 us
    mul x2, other arithmetic: 0.37 us -> 2.41 us  [ordered(): return [near[0] + near[1] * far[0], near[1] * far[1]]]
    pallas_call x3, Pallas kernels: 41.4 us -> 40 us  [march(): pl.pallas_call(functools.partial(march_kernel, mode, depth_total, group,...]
    ppermute x1, waiting for transfers between devices: 3.48 us -> 4.81 us  [plane_halos(): lax.ppermute(last, 'slab', forward)]
  transfers between devices with their start and end apart: 15 -> 15, of which waited for: 6 -> 5; matrix products, arithmetic and copies ran while one was open for 1% -> 3% of each run, Pallas kernels for 45% -> 44%
where the time goes in v12:
time: 91.8 us; the launch traced here: 91.5 us
  Pallas kernels  40 us (44%)
  waiting for transfers between devices  23.4 us (25%)
  starting transfers between devices  22.8 us (25%)
  other arithmetic  3.27 us (4%)
  local copies, waits for them, and re-layouts  1.29 us (1%)
    pallas_call x3, Pallas kernels, march(): pl.pallas_call(functools.partial(march_kernel, mode, depth_total, group,...  40 us
    ppermute x12, starting transfers between devices, exchange(): lax.ppermute(part, 'slab', [(i, i ^ change << shift) for i in range(count)])  16.7 us
    ppermute x12, waiting for transfers between devices, exchange(): lax.ppermute(part, 'slab', [(i, i ^ change << shift) for i in range(count)])  16.6 us
    ppermute x1, starting transfers between devices, plane_halos(): lax.ppermute(last, 'slab', forward)  4.88 us
    ppermute x1, waiting for transfers between devices, plane_halos(): lax.ppermute(last, 'slab', forward)  4.81 us
    mul x2, other arithmetic, ordered(): return [near[0] + near[1] * far[0], near[1] * far[1]]  2.41 us
    ppermute x1, waiting for transfers between devices, plane_halos(): lax.ppermute(first, 'slab', backward)  1.95 us
  transfers between devices with their start and end apart: 15, of which 5 were waited for; matrix products, arithmetic and copies ran while one was open for 3% of the time, Pallas kernels for 44%

profile of v12, /device:TPU:0, one launch (start us, length us, event | category | flops | bytes accessed | tf_op | source)
XLA Modules:
  0.0 91.5 jit_solution(5639420219404167262)
XLA Ops:
  0.6 0.0 copy-start
  0.6 0.0 copy-start.1
  0.6 1.3 %slice_bitcast_fusion = (f32[256,512]{1,0:T(8,128)S(1)}, f32[256,512]{1,0:T(8,128)S(1)}) fusion(f32[16,256,512]{2,1,0:T(8,128)} %refs_0_.5), kind=kLoop, calls=%fused_computation.16 | loop fusion | bytes 2097152 | tf_op jit(solution)/shard_map/squeeze | solution.py:373
  1.9 4.9 %collective-permute-start = (f32[256,512]{1,0:T(8,128)S(1)}, f32[256,512]{1,0:T(8,128)S(1)}, u32[]{:S(2)}, u32[]{:S(2)}) collective-permute-start(f32[256,512]{1,0:T(8,128)S(1)} %get-tuple-element.43), channel_id=1, source_target_pairs={{0,2},{2,4},{4,6},{6,8},{8,10},{10,12},{12,14},{14,16},{16,18},{18... | collective-permute-start | bytes 1572872 | tf_op jit(solution)/shard_map/ppermute | solution.py:315
  6.8 1.3 %collective-permute-start.1 = (f32[256,512]{1,0:T(8,128)S(1)}, f32[256,512]{1,0:T(8,128)S(1)}, u32[]{:S(2)}, u32[]{:S(2)}) collective-permute-start(f32[256,512]{1,0:T(8,128)S(1)} %get-tuple-element.42), channel_id=1, source_target_pairs={{2,0},{4,2},{6,4},{8,6},{10,8},{12,10},{14,12},{16,14},{18,16},{20... | collective-permute-start | bytes 1572872 | tf_op jit(solution)/shard_map/ppermute | solution.py:315
  8.1 0.0 copy-done
  8.1 0.0 copy-done.1
  8.1 16.2 %march_middle.1 = (f32[6,256,256]{2,1,0:T(8,128)S(1)}, f32[16,256,128]{2,1,0:T(8,128)S(1)}, s32[6,8,128]{2,1,0:T(8,128)S(1)}, f32[6,8,128]{2,1,0:T(8,128)S(1)}) custom-call(f32[3,16]{1,0:T(4,128)S(1)} %copy-done, f32[3,16]{1,0:T(4,128)S(1)} %copy-done.1, f32[16,256,512]{2,1,0:T(8,128)} %refs_0_.5), custom_call_target="tpu_custom_call" | custom-call | tf_op jit(solution)/shard_map/march_middle/pallas_call | solution.py:294
  24.4 4.8 %collective-permute-done.refs_1_.refs_2_ = f32[256,512]{1,0:T(8,128)S(1)} collective-permute-done((f32[256,512]{1,0:T(8,128)S(1)}, f32[256,512]{1,0:T(8,128)S(1)}, u32[]{:S(2)}, u32[]{:S(2)}) %collective-permute-start) | collective-permute-done | bytes 524320 | tf_op jit(solution)/shard_map/ppermute | solution.py:315
  29.2 1.9 %collective-permute-done.1.refs_2_.refs_3_ = f32[256,512]{1,0:T(8,128)S(1)} collective-permute-done((f32[256,512]{1,0:T(8,128)S(1)}, f32[256,512]{1,0:T(8,128)S(1)}, u32[]{:S(2)}, u32[]{:S(2)}) %collective-permute-start.1) | collective-permute-done | bytes 524320 | tf_op jit(solution)/shard_map/ppermute | solution.py:315
  31.1 0.0 collective-permute-start.8
  31.1 5.8 %march_rim.1 = (f32[4,6,16,256]{3,2,1,0:T(8,128)S(1)}, f32[4,6,16,256]{3,2,1,0:T(8,128)S(1)}, f32[4,6,16,256]{3,2,1,0:T(8,128)S(1)}, f32[4,6,16,256]{3,2,1,0:T(8,128)S(1)}) custom-call(s32[6,8,128]{2,1,0:T(8,128)S(1)} %get-tuple-element.22.tables_a, f32[6,8,128]{2,1,0:T(8,128)S(1)} %get-tuple-element.23.tables_b, f32[16,256,512]{2,1,0:T(8,128)} %refs_0_.5, ...), custom_call_target="tpu_custom_call" | custom-call | tf_op jit(solution)/shard_map/march_rim/pallas_call | solution.py:294
  37.0 1.6 %collective-permute-start.4 = (f32[4,6,16,256]{3,2,1,0:T(8,128)S(1)}, f32[4,6,16,256]{3,2,1,0:T(8,128)S(1)}, u32[]{:S(2)}, u32[]{:S(2)}) collective-permute-start(f32[4,6,16,256]{3,2,1,0:T(8,128)S(1)} %get-tuple-element.27), channel_id=1, source_target_pairs={{0,2},{2,0},{4,6},{6,4},{8,10},{10,8},{12,14},{14,12},{16,18},{18,... | collective-permute-start | bytes 1179656 | tf_op jit(solution)/shard_map/ppermute | solution.py:329
  38.5 0.0 collective-permute-start.3
  38.5 2.0 %collective-permute-start.2 = (f32[4,6,16,256]{3,2,1,0:T(8,128)S(1)}, f32[4,6,16,256]{3,2,1,0:T(8,128)S(1)}, u32[]{:S(2)}, u32[]{:S(2)}) collective-permute-start(f32[4,6,16,256]{3,2,1,0:T(8,128)S(1)} %get-tuple-element.25), channel_id=1, source_target_pairs={{0,6},{2,4},{4,2},{6,0},{8,14},{10,12},{12,10},{14,8},{16,22},{18,... | collective-permute-start | bytes 1179656 | tf_op jit(solution)/shard_map/ppermute | solution.py:329
  40.5 0.0 collective-permute-done.8.refs_1_
  40.5 17.9 %march_outer.1 = (f32[4,6,16,256]{3,2,1,0:T(8,128)S(1)}, f32[4,6,16,256]{3,2,1,0:T(8,128)S(1)}, f32[4,6,16,256]{3,2,1,0:T(8,128)S(1)}, f32[4,6,16,256]{3,2,1,0:T(8,128)S(1)}) custom-call(s32[6,8,128]{2,1,0:T(8,128)S(1)} %get-tuple-element.22.tables_a, f32[6,8,128]{2,1,0:T(8,128)S(1)} %get-tuple-element.23.tables_b, f32[16,256,512]{2,1,0:T(8,128)} %refs_0_.5, ...), custom_call_target="tpu_custom_call" | custom-call | flops 20971520000 | bytes 327680000 | tf_op jit(solution)/shard_map/march_outer/pallas_call | solution.py:294
  58.5 0.0 collective-permute-done.4
  58.5 0.0 collective-permute-done.3
  58.5 0.0 collective-permute-done.2
  58.5 0.0 copy-start.2
  58.5 0.1 collective-permute-start.10
  58.6 2.9 %collective-permute-start.9 = (f32[4,6,16,256]{3,2,1,0:T(8,128)S(1)}, f32[4,6,16,256]{3,2,1,0:T(8,128)S(1)}, u32[]{:S(2)}, u32[]{:S(2)}) collective-permute-start(f32[4,6,16,256]{3,2,1,0:T(8,128)S(1)} %get-tuple-element.38), channel_id=1, source_target_pairs={{0,6},{2,4},{4,2},{6,0},{8,14},{10,12},{12,10},{14,8},{16,22},{18,... | collective-permute-start | bytes 1179656 | tf_op jit(solution)/shard_map/ppermute | solution.py:329
  61.5 0.5 collective-permute-start.11
  62.1 0.0 copy-done.2
  62.1 1.2 %select_multiply_fusion.3 = (f32[4,3,16,256]{3,2,1,0:T(8,128)S(1)}, f32[4,3,16,256]{3,2,1,0:T(8,128)S(1)}) fusion(pred[]{:T(512)S(6)} %eq.22, f32[4,6,16,256]{3,2,1,0:T(8,128)S(1)} %collective-permute-done.3, f32[4,6,16,256]{3,2,1,0:T(8,128)} %copy-done.2, pred[]{:T(512)S(6)} %eq.23, f32[4,6,16,256]{3,2,1,0:T(8,128)S(1)} %get-tuple-element.28, ...), kind=kLoop, calls=%fused_computation.22 | loop fusion | flops 1032192 | bytes 1966082 | tf_op jit(solution)/shard_map/mul | solution.py:321
  63.3 2.7 %collective-permute-start.6 = (f32[1,6,16,256]{3,2,1,0:T(8,128)S(1)}, f32[1,6,16,256]{3,2,1,0:T(8,128)S(1)}, u32[]{:S(2)}, u32[]{:S(2)}) collective-permute-start(f32[1,6,16,256]{3,2,1,0:T(8,128)S(1)} %get-tuple-element.53), channel_id=1, source_target_pairs={{0,16},{2,18},{4,20},{6,22},{8,24},{10,26},{12,28},{14,30},{16,0},... | collective-permute-start | bytes 294920 | tf_op jit(solution)/shard_map/ppermute | solution.py:329
  66.0 1.3 %collective-permute-start.5 = (f32[1,6,16,256]{3,2,1,0:T(8,128)S(1)}, f32[1,6,16,256]{3,2,1,0:T(8,128)S(1)}, u32[]{:S(2)}, u32[]{:S(2)}) collective-permute-start(f32[1,6,16,256]{3,2,1,0:T(8,128)S(1)} %get-tuple-element.52), channel_id=1, source_target_pairs={{0,24},{2,26},{4,28},{6,30},{8,16},{10,18},{12,20},{14,22},{16,8},... | collective-permute-start | bytes 294920 | tf_op jit(solution)/shard_map/ppermute | solution.py:329
  67.3 10.4 %collective-permute-done.10 = f32[4,6,16,256]{3,2,1,0:T(8,128)S(1)} collective-permute-done((f32[4,6,16,256]{3,2,1,0:T(8,128)S(1)}, f32[4,6,16,256]{3,2,1,0:T(8,128)S(1)}, u32[]{:S(2)}, u32[]{:S(2)}) %collective-permute-start.10) | collective-permute-done | bytes 393248 | tf_op jit(solution)/shard_map/ppermute | solution.py:329
  77.7 1.6 %collective-permute-start.7 = (f32[1,6,16,256]{3,2,1,0:T(8,128)S(1)}, f32[1,6,16,256]{3,2,1,0:T(8,128)S(1)}, u32[]{:S(2)}, u32[]{:S(2)}) collective-permute-start(f32[1,6,16,256]{3,2,1,0:T(8,128)S(1)} %get-tuple-element.54), channel_id=1, source_target_pairs={{0,8},{2,10},{4,12},{6,14},{8,0},{10,2},{12,4},{14,6},{16,24},{18,... | collective-permute-start | bytes 294920 | tf_op jit(solution)/shard_map/ppermute | solution.py:329
  79.3 0.0 collective-permute-done.9
  79.3 0.0 collective-permute-done.11
  79.3 1.2 %select_multiply_fusion = (f32[4,3,16,256]{3,2,1,0:T(8,128)S(1)}, f32[4,3,16,256]{3,2,1,0:T(8,128)S(1)}) fusion(pred[]{:T(512)S(6)} %eq.22, f32[4,6,16,256]{3,2,1,0:T(8,128)S(1)} %collective-permute-done.10, f32[4,6,16,256]{3,2,1,0:T(8,128)S(1)} %collective-permute-done.9, pred[]{:T(512)S(6)} %eq.23, f32[4,6,16,256]{3,2,1,0:T(8,128)S(1)} %get-tuple-element.41, ...), kind=kLoop, calls=%fused_computation.18 | loop fusion | flops 1032192 | bytes 1966082 | tf_op jit(solution)/shard_map/mul | solution.py:321
  80.5 2.7 %collective-permute-start.13 = (f32[1,6,16,256]{3,2,1,0:T(8,128)S(1)}, f32[1,6,16,256]{3,2,1,0:T(8,128)S(1)}, u32[]{:S(2)}, u32[]{:S(2)}) collective-permute-start(f32[1,6,16,256]{3,2,1,0:T(8,128)S(1)} %get-tuple-element.57), channel_id=1, source_target_pairs={{0,16},{2,18},{4,20},{6,22},{8,24},{10,26},{12,28},{14,30},{16,0},... | collective-permute-start | bytes 294920 | tf_op jit(solution)/shard_map/ppermute | solution.py:329
  83.2 1.1 %collective-permute-start.12 = (f32[1,6,16,256]{3,2,1,0:T(8,128)S(1)}, f32[1,6,16,256]{3,2,1,0:T(8,128)S(1)}, u32[]{:S(2)}, u32[]{:S(2)}) collective-permute-start(f32[1,6,16,256]{3,2,1,0:T(8,128)S(1)} %get-tuple-element.56), channel_id=1, source_target_pairs={{0,24},{2,26},{4,28},{6,30},{8,16},{10,18},{12,20},{14,22},{16,8},... | collective-permute-start | bytes 294920 | tf_op jit(solution)/shard_map/ppermute | solution.py:329
  84.3 0.0 collective-permute-done.6
  84.3 0.2 collective-permute-start.14
  84.5 0.0 collective-permute-done.5
  84.5 0.0 collective-permute-done.7
  84.6 5.8 %collective-permute-done.13 = f32[1,6,16,256]{3,2,1,0:T(8,128)S(1)} collective-permute-done((f32[1,6,16,256]{3,2,1,0:T(8,128)S(1)}, f32[1,6,16,256]{3,2,1,0:T(8,128)S(1)}, u32[]{:S(2)}, u32[]{:S(2)}) %collective-permute-start.13) | collective-permute-done | bytes 98336 | tf_op jit(solution)/shard_map/ppermute | solution.py:329
  90.4 0.0 collective-permute-done.12
  90.4 0.4 collective-permute-done.14
  90.9 0.7 maximum_select_fusion
  (4 shorter events, 0.2 us)
Async XLA Ops:
  0.6 7.5 %copy-start = (f32[3,16]{1,0:T(4,128)S(1)}, f32[3,16]{1,0:T(4,128)}, u32[]{:S(2)}) copy-start(f32[3,16]{1,0:T(4,128)} %tables_a.1) | copy-start | bytes 580
  0.6 7.5 %copy-start.1 = (f32[3,16]{1,0:T(4,128)S(1)}, f32[3,16]{1,0:T(4,128)}, u32[]{:S(2)}) copy-start(f32[3,16]{1,0:T(4,128)} %tables_b.1) | copy-start | bytes 580
  1.9 27.2 %collective-permute-start = (f32[256,512]{1,0:T(8,128)S(1)}, f32[256,512]{1,0:T(8,128)S(1)}, u32[]{:S(2)}, u32[]{:S(2)}) collective-permute-start(f32[256,512]{1,0:T(8,128)S(1)} %get-tuple-element.43), channel_id=1, source_target_pairs={{0,2},{2,4},{4,6},{6,8},{8,10},{10,12},{12,14},{14,16},{16,18},{18... | collective-permute-start | bytes 1572872 | tf_op jit(solution)/shard_map/ppermute | solution.py:315
  6.8 24.3 %collective-permute-start.1 = (f32[256,512]{1,0:T(8,128)S(1)}, f32[256,512]{1,0:T(8,128)S(1)}, u32[]{:S(2)}, u32[]{:S(2)}) collective-permute-start(f32[256,512]{1,0:T(8,128)S(1)} %get-tuple-element.42), channel_id=1, source_target_pairs={{2,0},{4,2},{6,4},{8,6},{10,8},{12,10},{14,12},{16,14},{18,16},{20... | collective-permute-start | bytes 1572872 | tf_op jit(solution)/shard_map/ppermute | solution.py:315
  31.1 9.4 %collective-permute-start.8 = (f32[16,256,128]{2,1,0:T(8,128)S(1)}, f32[16,256,128]{2,1,0:T(8,128)S(1)}, u32[]{:S(2)}, u32[]{:S(2)}) collective-permute-start(f32[16,256,128]{2,1,0:T(8,128)S(1)} %get-tuple-element.30), channel_id=1, source_target_pairs={{0,1},{1,0},{2,3},{3,2},{4,5},{5,4},{6,7},{7,6},{8,9},{9,8},{10,11... | collective-permute-start | bytes 6291464 | tf_op jit(solution)/shard_map/ppermute | solution.py:379
  37.0 21.5 %collective-permute-start.4 = (f32[4,6,16,256]{3,2,1,0:T(8,128)S(1)}, f32[4,6,16,256]{3,2,1,0:T(8,128)S(1)}, u32[]{:S(2)}, u32[]{:S(2)}) collective-permute-start(f32[4,6,16,256]{3,2,1,0:T(8,128)S(1)} %get-tuple-element.27), channel_id=1, source_target_pairs={{0,2},{2,0},{4,6},{6,4},{8,10},{10,8},{12,14},{14,12},{16,18},{18,... | collective-permute-start | bytes 1179656 | tf_op jit(solution)/shard_map/ppermute | solution.py:329
  38.5 19.9 %collective-permute-start.3 = (f32[4,6,16,256]{3,2,1,0:T(8,128)S(1)}, f32[4,6,16,256]{3,2,1,0:T(8,128)S(1)}, u32[]{:S(2)}, u32[]{:S(2)}) collective-permute-start(f32[4,6,16,256]{3,2,1,0:T(8,128)S(1)} %get-tuple-element.26), channel_id=1, source_target_pairs={{0,4},{2,6},{4,0},{6,2},{8,12},{10,14},{12,8},{14,10},{16,20},{18,... | collective-permute-start | bytes 1179656 | tf_op jit(solution)/shard_map/ppermute | solution.py:329
  38.5 20.0 %collective-permute-start.2 = (f32[4,6,16,256]{3,2,1,0:T(8,128)S(1)}, f32[4,6,16,256]{3,2,1,0:T(8,128)S(1)}, u32[]{:S(2)}, u32[]{:S(2)}) collective-permute-start(f32[4,6,16,256]{3,2,1,0:T(8,128)S(1)} %get-tuple-element.25), channel_id=1, source_target_pairs={{0,6},{2,4},{4,2},{6,0},{8,14},{10,12},{12,10},{14,8},{16,22},{18,... | collective-permute-start | bytes 1179656 | tf_op jit(solution)/shard_map/ppermute | solution.py:329
  58.5 3.6 %copy-start.2 = (f32[4,6,16,256]{3,2,1,0:T(8,128)}, f32[4,6,16,256]{3,2,1,0:T(8,128)S(1)}, u32[]{:S(2)}) copy-start(f32[4,6,16,256]{3,2,1,0:T(8,128)S(1)} %collective-permute-done.2) | copy-start | bytes 1179652
  58.5 19.2 %collective-permute-start.10 = (f32[4,6,16,256]{3,2,1,0:T(8,128)S(1)}, f32[4,6,16,256]{3,2,1,0:T(8,128)S(1)}, u32[]{:S(2)}, u32[]{:S(2)}) collective-permute-start(f32[4,6,16,256]{3,2,1,0:T(8,128)S(1)} %get-tuple-element.39), channel_id=1, source_target_pairs={{0,4},{2,6},{4,0},{6,2},{8,12},{10,14},{12,8},{14,10},{16,20},{18,... | collective-permute-start | bytes 1179656 | tf_op jit(solution)/shard_map/ppermute | solution.py:329
  58.6 20.7 %collective-permute-start.9 = (f32[4,6,16,256]{3,2,1,0:T(8,128)S(1)}, f32[4,6,16,256]{3,2,1,0:T(8,128)S(1)}, u32[]{:S(2)}, u32[]{:S(2)}) collective-permute-start(f32[4,6,16,256]{3,2,1,0:T(8,128)S(1)} %get-tuple-element.38), channel_id=1, source_target_pairs={{0,6},{2,4},{4,2},{6,0},{8,14},{10,12},{12,10},{14,8},{16,22},{18,... | collective-permute-start | bytes 1179656 | tf_op jit(solution)/shard_map/ppermute | solution.py:329
  61.5 17.7 %collective-permute-start.11 = (f32[4,6,16,256]{3,2,1,0:T(8,128)S(1)}, f32[4,6,16,256]{3,2,1,0:T(8,128)}, u32[]{:S(2)}, u32[]{:S(2)}) collective-permute-start(f32[4,6,16,256]{3,2,1,0:T(8,128)S(1)} %get-tuple-element.40), channel_id=1, source_target_pairs={{0,2},{2,0},{4,6},{6,4},{8,10},{10,8},{12,14},{14,12},{16,18},{18,... | collective-permute-start | bytes 1179656 | tf_op jit(solution)/shard_map/ppermute | solution.py:329
  63.3 21.0 %collective-permute-start.6 = (f32[1,6,16,256]{3,2,1,0:T(8,128)S(1)}, f32[1,6,16,256]{3,2,1,0:T(8,128)S(1)}, u32[]{:S(2)}, u32[]{:S(2)}) collective-permute-start(f32[1,6,16,256]{3,2,1,0:T(8,128)S(1)} %get-tuple-element.53), channel_id=1, source_target_pairs={{0,16},{2,18},{4,20},{6,22},{8,24},{10,26},{12,28},{14,30},{16,0},... | collective-permute-start | bytes 294920 | tf_op jit(solution)/shard_map/ppermute | solution.py:329
  66.0 18.5 %collective-permute-start.5 = (f32[1,6,16,256]{3,2,1,0:T(8,128)S(1)}, f32[1,6,16,256]{3,2,1,0:T(8,128)S(1)}, u32[]{:S(2)}, u32[]{:S(2)}) collective-permute-start(f32[1,6,16,256]{3,2,1,0:T(8,128)S(1)} %get-tuple-element.52), channel_id=1, source_target_pairs={{0,24},{2,26},{4,28},{6,30},{8,16},{10,18},{12,20},{14,22},{16,8},... | collective-permute-start | bytes 294920 | tf_op jit(solution)/shard_map/ppermute | solution.py:329
  77.7 6.8 %collective-permute-start.7 = (f32[1,6,16,256]{3,2,1,0:T(8,128)S(1)}, f32[1,6,16,256]{3,2,1,0:T(8,128)S(1)}, u32[]{:S(2)}, u32[]{:S(2)}) collective-permute-start(f32[1,6,16,256]{3,2,1,0:T(8,128)S(1)} %get-tuple-element.54), channel_id=1, source_target_pairs={{0,8},{2,10},{4,12},{6,14},{8,0},{10,2},{12,4},{14,6},{16,24},{18,... | collective-permute-start | bytes 294920 | tf_op jit(solution)/shard_map/ppermute | solution.py:329
  80.5 9.9 %collective-permute-start.13 = (f32[1,6,16,256]{3,2,1,0:T(8,128)S(1)}, f32[1,6,16,256]{3,2,1,0:T(8,128)S(1)}, u32[]{:S(2)}, u32[]{:S(2)}) collective-permute-start(f32[1,6,16,256]{3,2,1,0:T(8,128)S(1)} %get-tuple-element.57), channel_id=1, source_target_pairs={{0,16},{2,18},{4,20},{6,22},{8,24},{10,26},{12,28},{14,30},{16,0},... | collective-permute-start | bytes 294920 | tf_op jit(solution)/shard_map/ppermute | solution.py:329
  83.2 7.2 %collective-permute-start.12 = (f32[1,6,16,256]{3,2,1,0:T(8,128)S(1)}, f32[1,6,16,256]{3,2,1,0:T(8,128)S(1)}, u32[]{:S(2)}, u32[]{:S(2)}) collective-permute-start(f32[1,6,16,256]{3,2,1,0:T(8,128)S(1)} %get-tuple-element.56), channel_id=1, source_target_pairs={{0,24},{2,26},{4,28},{6,30},{8,16},{10,18},{12,20},{14,22},{16,8},... | collective-permute-start | bytes 294920 | tf_op jit(solution)/shard_map/ppermute | solution.py:329
  84.3 6.5 %collective-permute-start.14 = (f32[1,6,16,256]{3,2,1,0:T(8,128)S(1)}, f32[1,6,16,256]{3,2,1,0:T(8,128)S(1)}, u32[]{:S(2)}, u32[]{:S(2)}) collective-permute-start(f32[1,6,16,256]{3,2,1,0:T(8,128)S(1)} %get-tuple-element.58), channel_id=1, source_target_pairs={{0,8},{2,10},{4,12},{6,14},{8,0},{10,2},{12,4},{14,6},{16,24},{18,... | collective-permute-start | bytes 294920 | tf_op jit(solution)/shard_map/ppermute | solution.py:329

commit v13 on v12

--- a/solution.py
+++ b/solution.py
@@ -135,8 +135,7 @@
         for copy in incoming(piece):
             copy.wait()
 
-    for piece in range(min(2, in_pieces)):
-        start(piece)
+    start(0)
     if mode == "middle":
         first = pl.multiple_of((1 - core) * (width - LANES), LANES)
         edge_in = pltpu.make_async_copy(
@@ -215,9 +214,9 @@
 
     @pl.loop(0, pieces)
     def _(piece):
-        @pl.when(piece + 2 < in_pieces)
+        @pl.when(piece + 1 < in_pieces)
         def _():
-            start(piece + 2)
+            start(piece + 1)
 
         @pl.loop(0, piece_rows // (SUBLANES * unroll))
         def _(step):
@@ -288,7 +287,7 @@
         outs.append(jax.ShapeDtypeStruct((6, SUBLANES, LANES), jnp.float32))
         out_specs += [pl.BlockSpec(memory_space=pl.ANY), near, near]
     strips = height // pieces // SUBLANES
-    unroll = min(strips, {"rim": 8, "outer": 4, "middle": 2}[mode])
+    unroll = min(strips, {"rim": 8, "outer": 8, "middle": 2}[mode])
     weight = 20000 if mode == "outer" else 0
     distant = pl.BlockSpec(memory_space=pl.ANY)
     out = pl.pallas_call(

time: 91.8 us -> 95.4 us (1.039)
  Pallas kernels: 40 us -> 45.6 us
  waiting for transfers between devices: 23.4 us -> 21.1 us
    pallas_call x3, Pallas kernels: 40 us -> 45.6 us  [march(): pl.pallas_call(functools.partial(march_kernel, mode, depth_total, group,...]
    ppermute x1, waiting for transfers between devices: 4.81 us -> 2.5 us  [plane_halos(): lax.ppermute(last, 'slab', forward)]
  transfers between devices with their start and end apart: 15 -> 15, of which waited for: 5 -> 5; matrix products, arithmetic and copies ran while one was open for 3% -> 3% of each run, Pallas kernels for 44% -> 48%
where the time goes in v13:
time: 95.4 us; the launch traced here: 94.9 us
  Pallas kernels  45.6 us (48%)
  starting transfers between devices  22.8 us (24%)
  waiting for transfers between devices  21.1 us (22%)
  other arithmetic  3.27 us (3%)
  local copies, waits for them, and re-layouts  1.29 us (1%)
    pallas_call x3, Pallas kernels, march(): pl.pallas_call(functools.partial(march_kernel, mode, depth_total, group,...  45.6 us
    ppermute x12, starting transfers between devices, exchange(): lax.ppermute(part, 'slab', [(i, i ^ change << shift) for i in range(count)])  16.7 us
    ppermute x12, waiting for transfers between devices, exchange(): lax.ppermute(part, 'slab', [(i, i ^ change << shift) for i in range(count)])  16.6 us
    ppermute x1, starting transfers between devices, plane_halos(): lax.ppermute(last, 'slab', forward)  4.88 us
    ppermute x1, waiting for transfers between devices, plane_halos(): lax.ppermute(last, 'slab', forward)  2.5 us
    mul x2, other arithmetic, ordered(): return [near[0] + near[1] * far[0], near[1] * far[1]]  2.41 us
    ppermute x1, waiting for transfers between devices, plane_halos(): lax.ppermute(first, 'slab', backward)  1.95 us
  transfers between devices with their start and end apart: 15, of which 5 were waited for; matrix products, arithmetic and copies ran while one was open for 3% of the time, Pallas kernels for 48%

profile of v13, /device:TPU:0, one launch (start us, length us, event | category | flops | bytes accessed | tf_op | source)
XLA Modules:
  0.0 94.9 jit_solution(3298478445416275700)
XLA Ops:
  0.6 0.0 copy-start
  0.6 0.0 copy-start.1
  0.6 1.3 %slice_bitcast_fusion = (f32[256,512]{1,0:T(8,128)S(1)}, f32[256,512]{1,0:T(8,128)S(1)}) fusion(f32[16,256,512]{2,1,0:T(8,128)} %refs_0_.5), kind=kLoop, calls=%fused_computation.16 | loop fusion | bytes 2097152 | tf_op jit(solution)/shard_map/squeeze | solution.py:372
  1.9 4.9 %collective-permute-start = (f32[256,512]{1,0:T(8,128)S(1)}, f32[256,512]{1,0:T(8,128)S(1)}, u32[]{:S(2)}, u32[]{:S(2)}) collective-permute-start(f32[256,512]{1,0:T(8,128)S(1)} %get-tuple-element.43), channel_id=1, source_target_pairs={{0,2},{2,4},{4,6},{6,8},{8,10},{10,12},{12,14},{14,16},{16,18},{18... | collective-permute-start | bytes 1572872 | tf_op jit(solution)/shard_map/ppermute | solution.py:314
  6.8 1.3 %collective-permute-start.1 = (f32[256,512]{1,0:T(8,128)S(1)}, f32[256,512]{1,0:T(8,128)S(1)}, u32[]{:S(2)}, u32[]{:S(2)}) collective-permute-start(f32[256,512]{1,0:T(8,128)S(1)} %get-tuple-element.42), channel_id=1, source_target_pairs={{2,0},{4,2},{6,4},{8,6},{10,8},{12,10},{14,12},{16,14},{18,16},{20... | collective-permute-start | bytes 1572872 | tf_op jit(solution)/shard_map/ppermute | solution.py:314
  8.1 0.0 copy-done
  8.1 0.0 copy-done.1
  8.1 18.5 %march_middle.1 = (f32[6,256,256]{2,1,0:T(8,128)S(1)}, f32[16,256,128]{2,1,0:T(8,128)S(1)}, s32[6,8,128]{2,1,0:T(8,128)S(1)}, f32[6,8,128]{2,1,0:T(8,128)S(1)}) custom-call(f32[3,16]{1,0:T(4,128)S(1)} %copy-done, f32[3,16]{1,0:T(4,128)S(1)} %copy-done.1, f32[16,256,512]{2,1,0:T(8,128)} %refs_0_.5), custom_call_target="tpu_custom_call" | custom-call | tf_op jit(solution)/shard_map/march_middle/pallas_call | solution.py:293
  26.7 2.5 %collective-permute-done.refs_1_.refs_2_ = f32[256,512]{1,0:T(8,128)S(1)} collective-permute-done((f32[256,512]{1,0:T(8,128)S(1)}, f32[256,512]{1,0:T(8,128)S(1)}, u32[]{:S(2)}, u32[]{:S(2)}) %collective-permute-start) | collective-permute-done | bytes 524320 | tf_op jit(solution)/shard_map/ppermute | solution.py:314
  29.2 1.9 %collective-permute-done.1.refs_2_.refs_3_ = f32[256,512]{1,0:T(8,128)S(1)} collective-permute-done((f32[256,512]{1,0:T(8,128)S(1)}, f32[256,512]{1,0:T(8,128)S(1)}, u32[]{:S(2)}, u32[]{:S(2)}) %collective-permute-start.1) | collective-permute-done | bytes 524320 | tf_op jit(solution)/shard_map/ppermute | solution.py:314
  31.1 0.0 collective-permute-start.8
  31.1 5.8 %march_rim.1 = (f32[4,6,16,256]{3,2,1,0:T(8,128)S(1)}, f32[4,6,16,256]{3,2,1,0:T(8,128)S(1)}, f32[4,6,16,256]{3,2,1,0:T(8,128)S(1)}, f32[4,6,16,256]{3,2,1,0:T(8,128)S(1)}) custom-call(s32[6,8,128]{2,1,0:T(8,128)S(1)} %get-tuple-element.22.tables_a, f32[6,8,128]{2,1,0:T(8,128)S(1)} %get-tuple-element.23.tables_b, f32[16,256,512]{2,1,0:T(8,128)} %refs_0_.5, ...), custom_call_target="tpu_custom_call" | custom-call | tf_op jit(solution)/shard_map/march_rim/pallas_call | solution.py:293
  36.9 1.6 %collective-permute-start.4 = (f32[4,6,16,256]{3,2,1,0:T(8,128)S(1)}, f32[4,6,16,256]{3,2,1,0:T(8,128)S(1)}, u32[]{:S(2)}, u32[]{:S(2)}) collective-permute-start(f32[4,6,16,256]{3,2,1,0:T(8,128)S(1)} %get-tuple-element.27), channel_id=1, source_target_pairs={{0,2},{2,0},{4,6},{6,4},{8,10},{10,8},{12,14},{14,12},{16,18},{18,... | collective-permute-start | bytes 1179656 | tf_op jit(solution)/shard_map/ppermute | solution.py:328
  38.5 0.0 collective-permute-start.3
  38.5 2.0 %collective-permute-start.2 = (f32[4,6,16,256]{3,2,1,0:T(8,128)S(1)}, f32[4,6,16,256]{3,2,1,0:T(8,128)S(1)}, u32[]{:S(2)}, u32[]{:S(2)}) collective-permute-start(f32[4,6,16,256]{3,2,1,0:T(8,128)S(1)} %get-tuple-element.25), channel_id=1, source_target_pairs={{0,6},{2,4},{4,2},{6,0},{8,14},{10,12},{12,10},{14,8},{16,22},{18,... | collective-permute-start | bytes 1179656 | tf_op jit(solution)/shard_map/ppermute | solution.py:328
  40.5 0.0 collective-permute-done.8.refs_1_
  40.5 21.3 %march_outer.1 = (f32[4,6,16,256]{3,2,1,0:T(8,128)S(1)}, f32[4,6,16,256]{3,2,1,0:T(8,128)S(1)}, f32[4,6,16,256]{3,2,1,0:T(8,128)S(1)}, f32[4,6,16,256]{3,2,1,0:T(8,128)S(1)}) custom-call(s32[6,8,128]{2,1,0:T(8,128)S(1)} %get-tuple-element.22.tables_a, f32[6,8,128]{2,1,0:T(8,128)S(1)} %get-tuple-element.23.tables_b, f32[16,256,512]{2,1,0:T(8,128)} %refs_0_.5, ...), custom_call_target="tpu_custom_call" | custom-call | flops 20971520000 | bytes 327680000 | tf_op jit(solution)/shard_map/march_outer/pallas_call | solution.py:293
  61.8 0.0 collective-permute-done.4
  61.8 0.0 collective-permute-done.3
  61.8 0.0 collective-permute-done.2
  61.8 0.0 copy-start.2
  61.8 0.1 collective-permute-start.10
  61.9 2.9 %collective-permute-start.9 = (f32[4,6,16,256]{3,2,1,0:T(8,128)S(1)}, f32[4,6,16,256]{3,2,1,0:T(8,128)S(1)}, u32[]{:S(2)}, u32[]{:S(2)}) collective-permute-start(f32[4,6,16,256]{3,2,1,0:T(8,128)S(1)} %get-tuple-element.38), channel_id=1, source_target_pairs={{0,6},{2,4},{4,2},{6,0},{8,14},{10,12},{12,10},{14,8},{16,22},{18,... | collective-permute-start | bytes 1179656 | tf_op jit(solution)/shard_map/ppermute | solution.py:328
  64.9 0.5 collective-permute-start.11
  65.4 0.0 copy-done.2
  65.4 1.2 %select_multiply_fusion.3 = (f32[4,3,16,256]{3,2,1,0:T(8,128)S(1)}, f32[4,3,16,256]{3,2,1,0:T(8,128)S(1)}) fusion(pred[]{:T(512)S(6)} %eq.22, f32[4,6,16,256]{3,2,1,0:T(8,128)S(1)} %collective-permute-done.3, f32[4,6,16,256]{3,2,1,0:T(8,128)} %copy-done.2, pred[]{:T(512)S(6)} %eq.23, f32[4,6,16,256]{3,2,1,0:T(8,128)S(1)} %get-tuple-element.28, ...), kind=kLoop, calls=%fused_computation.22 | loop fusion | flops 1032192 | bytes 1966082 | tf_op jit(solution)/shard_map/mul | solution.py:320
  66.7 2.7 %collective-permute-start.6 = (f32[1,6,16,256]{3,2,1,0:T(8,128)S(1)}, f32[1,6,16,256]{3,2,1,0:T(8,128)S(1)}, u32[]{:S(2)}, u32[]{:S(2)}) collective-permute-start(f32[1,6,16,256]{3,2,1,0:T(8,128)S(1)} %get-tuple-element.53), channel_id=1, source_target_pairs={{0,16},{2,18},{4,20},{6,22},{8,24},{10,26},{12,28},{14,30},{16,0},... | collective-permute-start | bytes 294920 | tf_op jit(solution)/shard_map/ppermute | solution.py:328
  69.3 1.3 %collective-permute-start.5 = (f32[1,6,16,256]{3,2,1,0:T(8,128)S(1)}, f32[1,6,16,256]{3,2,1,0:T(8,128)S(1)}, u32[]{:S(2)}, u32[]{:S(2)}) collective-permute-start(f32[1,6,16,256]{3,2,1,0:T(8,128)S(1)} %get-tuple-element.52), channel_id=1, source_target_pairs={{0,24},{2,26},{4,28},{6,30},{8,16},{10,18},{12,20},{14,22},{16,8},... | collective-permute-start | bytes 294920 | tf_op jit(solution)/shard_map/ppermute | solution.py:328
  70.7 10.4 %collective-permute-done.10 = f32[4,6,16,256]{3,2,1,0:T(8,128)S(1)} collective-permute-done((f32[4,6,16,256]{3,2,1,0:T(8,128)S(1)}, f32[4,6,16,256]{3,2,1,0:T(8,128)S(1)}, u32[]{:S(2)}, u32[]{:S(2)}) %collective-permute-start.10) | collective-permute-done | bytes 393248 | tf_op jit(solution)/shard_map/ppermute | solution.py:328
  81.0 1.6 %collective-permute-start.7 = (f32[1,6,16,256]{3,2,1,0:T(8,128)S(1)}, f32[1,6,16,256]{3,2,1,0:T(8,128)S(1)}, u32[]{:S(2)}, u32[]{:S(2)}) collective-permute-start(f32[1,6,16,256]{3,2,1,0:T(8,128)S(1)} %get-tuple-element.54), channel_id=1, source_target_pairs={{0,8},{2,10},{4,12},{6,14},{8,0},{10,2},{12,4},{14,6},{16,24},{18,... | collective-permute-start | bytes 294920 | tf_op jit(solution)/shard_map/ppermute | solution.py:328
  82.6 0.0 collective-permute-done.9
  82.6 0.0 collective-permute-done.11
  82.6 1.2 %select_multiply_fusion = (f32[4,3,16,256]{3,2,1,0:T(8,128)S(1)}, f32[4,3,16,256]{3,2,1,0:T(8,128)S(1)}) fusion(pred[]{:T(512)S(6)} %eq.22, f32[4,6,16,256]{3,2,1,0:T(8,128)S(1)} %collective-permute-done.10, f32[4,6,16,256]{3,2,1,0:T(8,128)S(1)} %collective-permute-done.9, pred[]{:T(512)S(6)} %eq.23, f32[4,6,16,256]{3,2,1,0:T(8,128)S(1)} %get-tuple-element.41, ...), kind=kLoop, calls=%fused_computation.18 | loop fusion | flops 1032192 | bytes 1966082 | tf_op jit(solution)/shard_map/mul | solution.py:320
  83.9 2.7 %collective-permute-start.13 = (f32[1,6,16,256]{3,2,1,0:T(8,128)S(1)}, f32[1,6,16,256]{3,2,1,0:T(8,128)S(1)}, u32[]{:S(2)}, u32[]{:S(2)}) collective-permute-start(f32[1,6,16,256]{3,2,1,0:T(8,128)S(1)} %get-tuple-element.57), channel_id=1, source_target_pairs={{0,16},{2,18},{4,20},{6,22},{8,24},{10,26},{12,28},{14,30},{16,0},... | collective-permute-start | bytes 294920 | tf_op jit(solution)/shard_map/ppermute | solution.py:328
  86.5 1.1 %collective-permute-start.12 = (f32[1,6,16,256]{3,2,1,0:T(8,128)S(1)}, f32[1,6,16,256]{3,2,1,0:T(8,128)S(1)}, u32[]{:S(2)}, u32[]{:S(2)}) collective-permute-start(f32[1,6,16,256]{3,2,1,0:T(8,128)S(1)} %get-tuple-element.56), channel_id=1, source_target_pairs={{0,24},{2,26},{4,28},{6,30},{8,16},{10,18},{12,20},{14,22},{16,8},... | collective-permute-start | bytes 294920 | tf_op jit(solution)/shard_map/ppermute | solution.py:328
  87.6 0.0 collective-permute-done.6
  87.6 0.2 collective-permute-start.14
  87.8 0.0 collective-permute-done.5
  87.8 0.0 collective-permute-done.7
  87.9 5.8 %collective-permute-done.13 = f32[1,6,16,256]{3,2,1,0:T(8,128)S(1)} collective-permute-done((f32[1,6,16,256]{3,2,1,0:T(8,128)S(1)}, f32[1,6,16,256]{3,2,1,0:T(8,128)S(1)}, u32[]{:S(2)}, u32[]{:S(2)}) %collective-permute-start.13) | collective-permute-done | bytes 98336 | tf_op jit(solution)/shard_map/ppermute | solution.py:328
  93.7 0.0 collective-permute-done.12
  93.7 0.4 collective-permute-done.14
  94.2 0.7 maximum_select_fusion
  (4 shorter events, 0.2 us)
Async XLA Ops:
  0.6 7.5 %copy-start = (f32[3,16]{1,0:T(4,128)S(1)}, f32[3,16]{1,0:T(4,128)}, u32[]{:S(2)}) copy-start(f32[3,16]{1,0:T(4,128)} %tables_a.1) | copy-start | bytes 580
  0.6 7.5 %copy-start.1 = (f32[3,16]{1,0:T(4,128)S(1)}, f32[3,16]{1,0:T(4,128)}, u32[]{:S(2)}) copy-start(f32[3,16]{1,0:T(4,128)} %tables_b.1) | copy-start | bytes 580
  1.9 27.2 %collective-permute-start = (f32[256,512]{1,0:T(8,128)S(1)}, f32[256,512]{1,0:T(8,128)S(1)}, u32[]{:S(2)}, u32[]{:S(2)}) collective-permute-start(f32[256,512]{1,0:T(8,128)S(1)} %get-tuple-element.43), channel_id=1, source_target_pairs={{0,2},{2,4},{4,6},{6,8},{8,10},{10,12},{12,14},{14,16},{16,18},{18... | collective-permute-start | bytes 1572872 | tf_op jit(solution)/shard_map/ppermute | solution.py:314
  6.8 24.3 %collective-permute-start.1 = (f32[256,512]{1,0:T(8,128)S(1)}, f32[256,512]{1,0:T(8,128)S(1)}, u32[]{:S(2)}, u32[]{:S(2)}) collective-permute-start(f32[256,512]{1,0:T(8,128)S(1)} %get-tuple-element.42), channel_id=1, source_target_pairs={{2,0},{4,2},{6,4},{8,6},{10,8},{12,10},{14,12},{16,14},{18,16},{20... | collective-permute-start | bytes 1572872 | tf_op jit(solution)/shard_map/ppermute | solution.py:314
  31.1 9.4 %collective-permute-start.8 = (f32[16,256,128]{2,1,0:T(8,128)S(1)}, f32[16,256,128]{2,1,0:T(8,128)S(1)}, u32[]{:S(2)}, u32[]{:S(2)}) collective-permute-start(f32[16,256,128]{2,1,0:T(8,128)S(1)} %get-tuple-element.30), channel_id=1, source_target_pairs={{0,1},{1,0},{2,3},{3,2},{4,5},{5,4},{6,7},{7,6},{8,9},{9,8},{10,11... | collective-permute-start | bytes 6291464 | tf_op jit(solution)/shard_map/ppermute | solution.py:378
  36.9 24.9 %collective-permute-start.4 = (f32[4,6,16,256]{3,2,1,0:T(8,128)S(1)}, f32[4,6,16,256]{3,2,1,0:T(8,128)S(1)}, u32[]{:S(2)}, u32[]{:S(2)}) collective-permute-start(f32[4,6,16,256]{3,2,1,0:T(8,128)S(1)} %get-tuple-element.27), channel_id=1, source_target_pairs={{0,2},{2,0},{4,6},{6,4},{8,10},{10,8},{12,14},{14,12},{16,18},{18,... | collective-permute-start | bytes 1179656 | tf_op jit(solution)/shard_map/ppermute | solution.py:328
  38.5 23.3 %collective-permute-start.3 = (f32[4,6,16,256]{3,2,1,0:T(8,128)S(1)}, f32[4,6,16,256]{3,2,1,0:T(8,128)S(1)}, u32[]{:S(2)}, u32[]{:S(2)}) collective-permute-start(f32[4,6,16,256]{3,2,1,0:T(8,128)S(1)} %get-tuple-element.26), channel_id=1, source_target_pairs={{0,4},{2,6},{4,0},{6,2},{8,12},{10,14},{12,8},{14,10},{16,20},{18,... | collective-permute-start | bytes 1179656 | tf_op jit(solution)/shard_map/ppermute | solution.py:328
  38.5 23.3 %collective-permute-start.2 = (f32[4,6,16,256]{3,2,1,0:T(8,128)S(1)}, f32[4,6,16,256]{3,2,1,0:T(8,128)S(1)}, u32[]{:S(2)}, u32[]{:S(2)}) collective-permute-start(f32[4,6,16,256]{3,2,1,0:T(8,128)S(1)} %get-tuple-element.25), channel_id=1, source_target_pairs={{0,6},{2,4},{4,2},{6,0},{8,14},{10,12},{12,10},{14,8},{16,22},{18,... | collective-permute-start | bytes 1179656 | tf_op jit(solution)/shard_map/ppermute | solution.py:328
  61.8 3.6 %copy-start.2 = (f32[4,6,16,256]{3,2,1,0:T(8,128)}, f32[4,6,16,256]{3,2,1,0:T(8,128)S(1)}, u32[]{:S(2)}) copy-start(f32[4,6,16,256]{3,2,1,0:T(8,128)S(1)} %collective-permute-done.2) | copy-start | bytes 1179652
  61.8 19.2 %collective-permute-start.10 = (f32[4,6,16,256]{3,2,1,0:T(8,128)S(1)}, f32[4,6,16,256]{3,2,1,0:T(8,128)S(1)}, u32[]{:S(2)}, u32[]{:S(2)}) collective-permute-start(f32[4,6,16,256]{3,2,1,0:T(8,128)S(1)} %get-tuple-element.39), channel_id=1, source_target_pairs={{0,4},{2,6},{4,0},{6,2},{8,12},{10,14},{12,8},{14,10},{16,20},{18,... | collective-permute-start | bytes 1179656 | tf_op jit(solution)/shard_map/ppermute | solution.py:328
  61.9 20.7 %collective-permute-start.9 = (f32[4,6,16,256]{3,2,1,0:T(8,128)S(1)}, f32[4,6,16,256]{3,2,1,0:T(8,128)S(1)}, u32[]{:S(2)}, u32[]{:S(2)}) collective-permute-start(f32[4,6,16,256]{3,2,1,0:T(8,128)S(1)} %get-tuple-element.38), channel_id=1, source_target_pairs={{0,6},{2,4},{4,2},{6,0},{8,14},{10,12},{12,10},{14,8},{16,22},{18,... | collective-permute-start | bytes 1179656 | tf_op jit(solution)/shard_map/ppermute | solution.py:328
  64.9 17.7 %collective-permute-start.11 = (f32[4,6,16,256]{3,2,1,0:T(8,128)S(1)}, f32[4,6,16,256]{3,2,1,0:T(8,128)}, u32[]{:S(2)}, u32[]{:S(2)}) collective-permute-start(f32[4,6,16,256]{3,2,1,0:T(8,128)S(1)} %get-tuple-element.40), channel_id=1, source_target_pairs={{0,2},{2,0},{4,6},{6,4},{8,10},{10,8},{12,14},{14,12},{16,18},{18,... | collective-permute-start | bytes 1179656 | tf_op jit(solution)/shard_map/ppermute | solution.py:328
  66.7 21.0 %collective-permute-start.6 = (f32[1,6,16,256]{3,2,1,0:T(8,128)S(1)}, f32[1,6,16,256]{3,2,1,0:T(8,128)S(1)}, u32[]{:S(2)}, u32[]{:S(2)}) collective-permute-start(f32[1,6,16,256]{3,2,1,0:T(8,128)S(1)} %get-tuple-element.53), channel_id=1, source_target_pairs={{0,16},{2,18},{4,20},{6,22},{8,24},{10,26},{12,28},{14,30},{16,0},... | collective-permute-start | bytes 294920 | tf_op jit(solution)/shard_map/ppermute | solution.py:328
  69.3 18.5 %collective-permute-start.5 = (f32[1,6,16,256]{3,2,1,0:T(8,128)S(1)}, f32[1,6,16,256]{3,2,1,0:T(8,128)S(1)}, u32[]{:S(2)}, u32[]{:S(2)}) collective-permute-start(f32[1,6,16,256]{3,2,1,0:T(8,128)S(1)} %get-tuple-element.52), channel_id=1, source_target_pairs={{0,24},{2,26},{4,28},{6,30},{8,16},{10,18},{12,20},{14,22},{16,8},... | collective-permute-start | bytes 294920 | tf_op jit(solution)/shard_map/ppermute | solution.py:328
  81.0 6.8 %collective-permute-start.7 = (f32[1,6,16,256]{3,2,1,0:T(8,128)S(1)}, f32[1,6,16,256]{3,2,1,0:T(8,128)S(1)}, u32[]{:S(2)}, u32[]{:S(2)}) collective-permute-start(f32[1,6,16,256]{3,2,1,0:T(8,128)S(1)} %get-tuple-element.54), channel_id=1, source_target_pairs={{0,8},{2,10},{4,12},{6,14},{8,0},{10,2},{12,4},{14,6},{16,24},{18,... | collective-permute-start | bytes 294920 | tf_op jit(solution)/shard_map/ppermute | solution.py:328
  83.9 9.9 %collective-permute-start.13 = (f32[1,6,16,256]{3,2,1,0:T(8,128)S(1)}, f32[1,6,16,256]{3,2,1,0:T(8,128)S(1)}, u32[]{:S(2)}, u32[]{:S(2)}) collective-permute-start(f32[1,6,16,256]{3,2,1,0:T(8,128)S(1)} %get-tuple-element.57), channel_id=1, source_target_pairs={{0,16},{2,18},{4,20},{6,22},{8,24},{10,26},{12,28},{14,30},{16,0},... | collective-permute-start | bytes 294920 | tf_op jit(solution)/shard_map/ppermute | solution.py:328
  86.5 7.2 %collective-permute-start.12 = (f32[1,6,16,256]{3,2,1,0:T(8,128)S(1)}, f32[1,6,16,256]{3,2,1,0:T(8,128)S(1)}, u32[]{:S(2)}, u32[]{:S(2)}) collective-permute-start(f32[1,6,16,256]{3,2,1,0:T(8,128)S(1)} %get-tuple-element.56), channel_id=1, source_target_pairs={{0,24},{2,26},{4,28},{6,30},{8,16},{10,18},{12,20},{14,22},{16,8},... | collective-permute-start | bytes 294920 | tf_op jit(solution)/shard_map/ppermute | solution.py:328
  87.6 6.5 %collective-permute-start.14 = (f32[1,6,16,256]{3,2,1,0:T(8,128)S(1)}, f32[1,6,16,256]{3,2,1,0:T(8,128)S(1)}, u32[]{:S(2)}, u32[]{:S(2)}) collective-permute-start(f32[1,6,16,256]{3,2,1,0:T(8,128)S(1)} %get-tuple-element.58), channel_id=1, source_target_pairs={{0,8},{2,10},{4,12},{6,14},{8,0},{10,2},{12,4},{14,6},{16,24},{18,... | collective-permute-start | bytes 294920 | tf_op jit(solution)/shard_map/ppermute | solution.py:328

commit v14 on v12

--- a/solution.py
+++ b/solution.py
@@ -135,7 +135,7 @@
         for copy in incoming(piece):
             copy.wait()
 
-    for piece in range(min(2, in_pieces)):
+    for piece in range(in_pieces):
         start(piece)
     if mode == "middle":
         first = pl.multiple_of((1 - core) * (width - LANES), LANES)
@@ -215,10 +215,6 @@
 
     @pl.loop(0, pieces)
     def _(piece):
-        @pl.when(piece + 2 < in_pieces)
-        def _():
-            start(piece + 2)
-
         @pl.loop(0, piece_rows // (SUBLANES * unroll))
         def _(step):
             last_step = step == piece_rows // (SUBLANES * unroll) - 1

time: 91.8 us -> 91.6 us (level)
  transfers between devices with their start and end apart: 15 -> 15, of which waited for: 5 -> 5; matrix products, arithmetic and copies ran while one was open for 3% -> 3% of each run, Pallas kernels for 44% -> 43%
where the time goes in v14:
time: 91.6 us; the launch traced here: 91.3 us
  Pallas kernels  39.7 us (43%)
  waiting for transfers between devices  23.5 us (26%)
  starting transfers between devices  22.8 us (25%)
  other arithmetic  3.27 us (4%)
  local copies, waits for them, and re-layouts  1.29 us (1%)
    pallas_call x3, Pallas kernels, march(): pl.pallas_call(functools.partial(march_kernel, mode, depth_total, group,...  39.7 us
    ppermute x12, starting transfers between devices, exchange(): lax.ppermute(part, 'slab', [(i, i ^ change << shift) for i in range(count)])  16.7 us
    ppermute x12, waiting for transfers between devices, exchange(): lax.ppermute(part, 'slab', [(i, i ^ change << shift) for i in range(count)])  16.6 us
    ppermute x1, waiting for transfers between devices, plane_halos(): lax.ppermute(last, 'slab', forward)  4.94 us
    ppermute x1, starting transfers between devices, plane_halos(): lax.ppermute(last, 'slab', forward)  4.88 us
    mul x2, other arithmetic, ordered(): return [near[0] + near[1] * far[0], near[1] * far[1]]  2.41 us
    ppermute x1, waiting for transfers between devices, plane_halos(): lax.ppermute(first, 'slab', backward)  1.95 us
  transfers between devices with their start and end apart: 15, of which 5 were waited for; matrix products, arithmetic and copies ran while one was open for 3% of the time, Pallas kernels for 43%

profile of v14, /device:TPU:0, one launch (start us, length us, event | category | flops | bytes accessed | tf_op | source)
XLA Modules:
  0.0 91.3 jit_solution(1830081667648642475)
XLA Ops:
  0.6 0.0 copy-start
  0.6 0.0 copy-start.1
  0.6 1.3 %slice_bitcast_fusion = (f32[256,512]{1,0:T(8,128)S(1)}, f32[256,512]{1,0:T(8,128)S(1)}) fusion(f32[16,256,512]{2,1,0:T(8,128)} %refs_0_.5), kind=kLoop, calls=%fused_computation.16 | loop fusion | bytes 2097152 | tf_op jit(solution)/shard_map/squeeze | solution.py:369
  1.9 4.9 %collective-permute-start = (f32[256,512]{1,0:T(8,128)S(1)}, f32[256,512]{1,0:T(8,128)S(1)}, u32[]{:S(2)}, u32[]{:S(2)}) collective-permute-start(f32[256,512]{1,0:T(8,128)S(1)} %get-tuple-element.43), channel_id=1, source_target_pairs={{0,2},{2,4},{4,6},{6,8},{8,10},{10,12},{12,14},{14,16},{16,18},{18... | collective-permute-start | bytes 1572872 | tf_op jit(solution)/shard_map/ppermute | solution.py:311
  6.8 1.3 %collective-permute-start.1 = (f32[256,512]{1,0:T(8,128)S(1)}, f32[256,512]{1,0:T(8,128)S(1)}, u32[]{:S(2)}, u32[]{:S(2)}) collective-permute-start(f32[256,512]{1,0:T(8,128)S(1)} %get-tuple-element.42), channel_id=1, source_target_pairs={{2,0},{4,2},{6,4},{8,6},{10,8},{12,10},{14,12},{16,14},{18,16},{20... | collective-permute-start | bytes 1572872 | tf_op jit(solution)/shard_map/ppermute | solution.py:311
  8.1 0.0 copy-done
  8.1 0.0 copy-done.1
  8.1 16.1 %march_middle.1 = (f32[6,256,256]{2,1,0:T(8,128)S(1)}, f32[16,256,128]{2,1,0:T(8,128)S(1)}, s32[6,8,128]{2,1,0:T(8,128)S(1)}, f32[6,8,128]{2,1,0:T(8,128)S(1)}) custom-call(f32[3,16]{1,0:T(4,128)S(1)} %copy-done, f32[3,16]{1,0:T(4,128)S(1)} %copy-done.1, f32[16,256,512]{2,1,0:T(8,128)} %refs_0_.5), custom_call_target="tpu_custom_call" | custom-call | tf_op jit(solution)/shard_map/march_middle/pallas_call | solution.py:290
  24.2 4.9 %collective-permute-done.refs_1_.refs_2_ = f32[256,512]{1,0:T(8,128)S(1)} collective-permute-done((f32[256,512]{1,0:T(8,128)S(1)}, f32[256,512]{1,0:T(8,128)S(1)}, u32[]{:S(2)}, u32[]{:S(2)}) %collective-permute-start) | collective-permute-done | bytes 524320 | tf_op jit(solution)/shard_map/ppermute | solution.py:311
  29.2 1.9 %collective-permute-done.1.refs_2_.refs_3_ = f32[256,512]{1,0:T(8,128)S(1)} collective-permute-done((f32[256,512]{1,0:T(8,128)S(1)}, f32[256,512]{1,0:T(8,128)S(1)}, u32[]{:S(2)}, u32[]{:S(2)}) %collective-permute-start.1) | collective-permute-done | bytes 524320 | tf_op jit(solution)/shard_map/ppermute | solution.py:311
  31.1 0.0 collective-permute-start.8
  31.1 5.8 %march_rim.1 = (f32[4,6,16,256]{3,2,1,0:T(8,128)S(1)}, f32[4,6,16,256]{3,2,1,0:T(8,128)S(1)}, f32[4,6,16,256]{3,2,1,0:T(8,128)S(1)}, f32[4,6,16,256]{3,2,1,0:T(8,128)S(1)}) custom-call(s32[6,8,128]{2,1,0:T(8,128)S(1)} %get-tuple-element.22.tables_a, f32[6,8,128]{2,1,0:T(8,128)S(1)} %get-tuple-element.23.tables_b, f32[16,256,512]{2,1,0:T(8,128)} %refs_0_.5, ...), custom_call_target="tpu_custom_call" | custom-call | tf_op jit(solution)/shard_map/march_rim/pallas_call | solution.py:290
  37.0 1.6 %collective-permute-start.4 = (f32[4,6,16,256]{3,2,1,0:T(8,128)S(1)}, f32[4,6,16,256]{3,2,1,0:T(8,128)S(1)}, u32[]{:S(2)}, u32[]{:S(2)}) collective-permute-start(f32[4,6,16,256]{3,2,1,0:T(8,128)S(1)} %get-tuple-element.27), channel_id=1, source_target_pairs={{0,2},{2,0},{4,6},{6,4},{8,10},{10,8},{12,14},{14,12},{16,18},{18,... | collective-permute-start | bytes 1179656 | tf_op jit(solution)/shard_map/ppermute | solution.py:325
  38.5 0.0 collective-permute-start.3
  38.5 2.0 %collective-permute-start.2 = (f32[4,6,16,256]{3,2,1,0:T(8,128)S(1)}, f32[4,6,16,256]{3,2,1,0:T(8,128)S(1)}, u32[]{:S(2)}, u32[]{:S(2)}) collective-permute-start(f32[4,6,16,256]{3,2,1,0:T(8,128)S(1)} %get-tuple-element.25), channel_id=1, source_target_pairs={{0,6},{2,4},{4,2},{6,0},{8,14},{10,12},{12,10},{14,8},{16,22},{18,... | collective-permute-start | bytes 1179656 | tf_op jit(solution)/shard_map/ppermute | solution.py:325
  40.5 0.0 collective-permute-done.8.refs_1_
  40.5 17.7 %march_outer.1 = (f32[4,6,16,256]{3,2,1,0:T(8,128)S(1)}, f32[4,6,16,256]{3,2,1,0:T(8,128)S(1)}, f32[4,6,16,256]{3,2,1,0:T(8,128)S(1)}, f32[4,6,16,256]{3,2,1,0:T(8,128)S(1)}) custom-call(s32[6,8,128]{2,1,0:T(8,128)S(1)} %get-tuple-element.22.tables_a, f32[6,8,128]{2,1,0:T(8,128)S(1)} %get-tuple-element.23.tables_b, f32[16,256,512]{2,1,0:T(8,128)} %refs_0_.5, ...), custom_call_target="tpu_custom_call" | custom-call | flops 20971520000 | bytes 327680000 | tf_op jit(solution)/shard_map/march_outer/pallas_call | solution.py:290
  58.3 0.0 collective-permute-done.4
  58.3 0.0 collective-permute-done.3
  58.3 0.0 collective-permute-done.2
  58.3 0.0 copy-start.2
  58.3 0.2 collective-permute-start.10
  58.5 2.9 %collective-permute-start.9 = (f32[4,6,16,256]{3,2,1,0:T(8,128)S(1)}, f32[4,6,16,256]{3,2,1,0:T(8,128)S(1)}, u32[]{:S(2)}, u32[]{:S(2)}) collective-permute-start(f32[4,6,16,256]{3,2,1,0:T(8,128)S(1)} %get-tuple-element.38), channel_id=1, source_target_pairs={{0,6},{2,4},{4,2},{6,0},{8,14},{10,12},{12,10},{14,8},{16,22},{18,... | collective-permute-start | bytes 1179656 | tf_op jit(solution)/shard_map/ppermute | solution.py:325
  61.3 0.5 collective-permute-start.11
  61.9 0.0 copy-done.2
  61.9 1.2 %select_multiply_fusion.3 = (f32[4,3,16,256]{3,2,1,0:T(8,128)S(1)}, f32[4,3,16,256]{3,2,1,0:T(8,128)S(1)}) fusion(pred[]{:T(512)S(6)} %eq.22, f32[4,6,16,256]{3,2,1,0:T(8,128)S(1)} %collective-permute-done.3, f32[4,6,16,256]{3,2,1,0:T(8,128)} %copy-done.2, pred[]{:T(512)S(6)} %eq.23, f32[4,6,16,256]{3,2,1,0:T(8,128)S(1)} %get-tuple-element.28, ...), kind=kLoop, calls=%fused_computation.22 | loop fusion | flops 1032192 | bytes 1966082 | tf_op jit(solution)/shard_map/mul | solution.py:317
  63.1 2.7 %collective-permute-start.6 = (f32[1,6,16,256]{3,2,1,0:T(8,128)S(1)}, f32[1,6,16,256]{3,2,1,0:T(8,128)S(1)}, u32[]{:S(2)}, u32[]{:S(2)}) collective-permute-start(f32[1,6,16,256]{3,2,1,0:T(8,128)S(1)} %get-tuple-element.53), channel_id=1, source_target_pairs={{0,16},{2,18},{4,20},{6,22},{8,24},{10,26},{12,28},{14,30},{16,0},... | collective-permute-start | bytes 294920 | tf_op jit(solution)/shard_map/ppermute | solution.py:325
  65.8 1.3 %collective-permute-start.5 = (f32[1,6,16,256]{3,2,1,0:T(8,128)S(1)}, f32[1,6,16,256]{3,2,1,0:T(8,128)S(1)}, u32[]{:S(2)}, u32[]{:S(2)}) collective-permute-start(f32[1,6,16,256]{3,2,1,0:T(8,128)S(1)} %get-tuple-element.52), channel_id=1, source_target_pairs={{0,24},{2,26},{4,28},{6,30},{8,16},{10,18},{12,20},{14,22},{16,8},... | collective-permute-start | bytes 294920 | tf_op jit(solution)/shard_map/ppermute | solution.py:325
  67.1 10.4 %collective-permute-done.10 = f32[4,6,16,256]{3,2,1,0:T(8,128)S(1)} collective-permute-done((f32[4,6,16,256]{3,2,1,0:T(8,128)S(1)}, f32[4,6,16,256]{3,2,1,0:T(8,128)S(1)}, u32[]{:S(2)}, u32[]{:S(2)}) %collective-permute-start.10) | collective-permute-done | bytes 393248 | tf_op jit(solution)/shard_map/ppermute | solution.py:325
  77.5 1.6 %collective-permute-start.7 = (f32[1,6,16,256]{3,2,1,0:T(8,128)S(1)}, f32[1,6,16,256]{3,2,1,0:T(8,128)S(1)}, u32[]{:S(2)}, u32[]{:S(2)}) collective-permute-start(f32[1,6,16,256]{3,2,1,0:T(8,128)S(1)} %get-tuple-element.54), channel_id=1, source_target_pairs={{0,8},{2,10},{4,12},{6,14},{8,0},{10,2},{12,4},{14,6},{16,24},{18,... | collective-permute-start | bytes 294920 | tf_op jit(solution)/shard_map/ppermute | solution.py:325
  79.1 0.0 collective-permute-done.9
  79.1 0.0 collective-permute-done.11
  79.1 1.2 %select_multiply_fusion = (f32[4,3,16,256]{3,2,1,0:T(8,128)S(1)}, f32[4,3,16,256]{3,2,1,0:T(8,128)S(1)}) fusion(pred[]{:T(512)S(6)} %eq.22, f32[4,6,16,256]{3,2,1,0:T(8,128)S(1)} %collective-permute-done.10, f32[4,6,16,256]{3,2,1,0:T(8,128)S(1)} %collective-permute-done.9, pred[]{:T(512)S(6)} %eq.23, f32[4,6,16,256]{3,2,1,0:T(8,128)S(1)} %get-tuple-element.41, ...), kind=kLoop, calls=%fused_computation.18 | loop fusion | flops 1032192 | bytes 1966082 | tf_op jit(solution)/shard_map/mul | solution.py:317
  80.3 2.7 %collective-permute-start.13 = (f32[1,6,16,256]{3,2,1,0:T(8,128)S(1)}, f32[1,6,16,256]{3,2,1,0:T(8,128)S(1)}, u32[]{:S(2)}, u32[]{:S(2)}) collective-permute-start(f32[1,6,16,256]{3,2,1,0:T(8,128)S(1)} %get-tuple-element.57), channel_id=1, source_target_pairs={{0,16},{2,18},{4,20},{6,22},{8,24},{10,26},{12,28},{14,30},{16,0},... | collective-permute-start | bytes 294920 | tf_op jit(solution)/shard_map/ppermute | solution.py:325
  83.0 1.1 %collective-permute-start.12 = (f32[1,6,16,256]{3,2,1,0:T(8,128)S(1)}, f32[1,6,16,256]{3,2,1,0:T(8,128)S(1)}, u32[]{:S(2)}, u32[]{:S(2)}) collective-permute-start(f32[1,6,16,256]{3,2,1,0:T(8,128)S(1)} %get-tuple-element.56), channel_id=1, source_target_pairs={{0,24},{2,26},{4,28},{6,30},{8,16},{10,18},{12,20},{14,22},{16,8},... | collective-permute-start | bytes 294920 | tf_op jit(solution)/shard_map/ppermute | solution.py:325
  84.1 0.0 collective-permute-done.6
  84.1 0.2 collective-permute-start.14
  84.3 0.0 collective-permute-done.5
  84.3 0.0 collective-permute-done.7
  84.4 5.8 %collective-permute-done.13 = f32[1,6,16,256]{3,2,1,0:T(8,128)S(1)} collective-permute-done((f32[1,6,16,256]{3,2,1,0:T(8,128)S(1)}, f32[1,6,16,256]{3,2,1,0:T(8,128)S(1)}, u32[]{:S(2)}, u32[]{:S(2)}) %collective-permute-start.13) | collective-permute-done | bytes 98336 | tf_op jit(solution)/shard_map/ppermute | solution.py:325
  90.2 0.0 collective-permute-done.12
  90.2 0.4 collective-permute-done.14
  90.6 0.7 maximum_select_fusion
  (4 shorter events, 0.2 us)
Async XLA Ops:
  0.6 7.5 %copy-start = (f32[3,16]{1,0:T(4,128)S(1)}, f32[3,16]{1,0:T(4,128)}, u32[]{:S(2)}) copy-start(f32[3,16]{1,0:T(4,128)} %tables_a.1) | copy-start | bytes 580
  0.6 7.5 %copy-start.1 = (f32[3,16]{1,0:T(4,128)S(1)}, f32[3,16]{1,0:T(4,128)}, u32[]{:S(2)}) copy-start(f32[3,16]{1,0:T(4,128)} %tables_b.1) | copy-start | bytes 580
  1.9 27.2 %collective-permute-start = (f32[256,512]{1,0:T(8,128)S(1)}, f32[256,512]{1,0:T(8,128)S(1)}, u32[]{:S(2)}, u32[]{:S(2)}) collective-permute-start(f32[256,512]{1,0:T(8,128)S(1)} %get-tuple-element.43), channel_id=1, source_target_pairs={{0,2},{2,4},{4,6},{6,8},{8,10},{10,12},{12,14},{14,16},{16,18},{18... | collective-permute-start | bytes 1572872 | tf_op jit(solution)/shard_map/ppermute | solution.py:311
  6.8 24.3 %collective-permute-start.1 = (f32[256,512]{1,0:T(8,128)S(1)}, f32[256,512]{1,0:T(8,128)S(1)}, u32[]{:S(2)}, u32[]{:S(2)}) collective-permute-start(f32[256,512]{1,0:T(8,128)S(1)} %get-tuple-element.42), channel_id=1, source_target_pairs={{2,0},{4,2},{6,4},{8,6},{10,8},{12,10},{14,12},{16,14},{18,16},{20... | collective-permute-start | bytes 1572872 | tf_op jit(solution)/shard_map/ppermute | solution.py:311
  31.1 9.4 %collective-permute-start.8 = (f32[16,256,128]{2,1,0:T(8,128)S(1)}, f32[16,256,128]{2,1,0:T(8,128)S(1)}, u32[]{:S(2)}, u32[]{:S(2)}) collective-permute-start(f32[16,256,128]{2,1,0:T(8,128)S(1)} %get-tuple-element.30), channel_id=1, source_target_pairs={{0,1},{1,0},{2,3},{3,2},{4,5},{5,4},{6,7},{7,6},{8,9},{9,8},{10,11... | collective-permute-start | bytes 6291464 | tf_op jit(solution)/shard_map/ppermute | solution.py:375
  37.0 21.3 %collective-permute-start.4 = (f32[4,6,16,256]{3,2,1,0:T(8,128)S(1)}, f32[4,6,16,256]{3,2,1,0:T(8,128)S(1)}, u32[]{:S(2)}, u32[]{:S(2)}) collective-permute-start(f32[4,6,16,256]{3,2,1,0:T(8,128)S(1)} %get-tuple-element.27), channel_id=1, source_target_pairs={{0,2},{2,0},{4,6},{6,4},{8,10},{10,8},{12,14},{14,12},{16,18},{18,... | collective-permute-start | bytes 1179656 | tf_op jit(solution)/shard_map/ppermute | solution.py:325
  38.5 19.8 %collective-permute-start.3 = (f32[4,6,16,256]{3,2,1,0:T(8,128)S(1)}, f32[4,6,16,256]{3,2,1,0:T(8,128)S(1)}, u32[]{:S(2)}, u32[]{:S(2)}) collective-permute-start(f32[4,6,16,256]{3,2,1,0:T(8,128)S(1)} %get-tuple-element.26), channel_id=1, source_target_pairs={{0,4},{2,6},{4,0},{6,2},{8,12},{10,14},{12,8},{14,10},{16,20},{18,... | collective-permute-start | bytes 1179656 | tf_op jit(solution)/shard_map/ppermute | solution.py:325
  38.5 19.8 %collective-permute-start.2 = (f32[4,6,16,256]{3,2,1,0:T(8,128)S(1)}, f32[4,6,16,256]{3,2,1,0:T(8,128)S(1)}, u32[]{:S(2)}, u32[]{:S(2)}) collective-permute-start(f32[4,6,16,256]{3,2,1,0:T(8,128)S(1)} %get-tuple-element.25), channel_id=1, source_target_pairs={{0,6},{2,4},{4,2},{6,0},{8,14},{10,12},{12,10},{14,8},{16,22},{18,... | collective-permute-start | bytes 1179656 | tf_op jit(solution)/shard_map/ppermute | solution.py:325
  58.3 3.6 %copy-start.2 = (f32[4,6,16,256]{3,2,1,0:T(8,128)}, f32[4,6,16,256]{3,2,1,0:T(8,128)S(1)}, u32[]{:S(2)}) copy-start(f32[4,6,16,256]{3,2,1,0:T(8,128)S(1)} %collective-permute-done.2) | copy-start | bytes 1179652
  58.3 19.2 %collective-permute-start.10 = (f32[4,6,16,256]{3,2,1,0:T(8,128)S(1)}, f32[4,6,16,256]{3,2,1,0:T(8,128)S(1)}, u32[]{:S(2)}, u32[]{:S(2)}) collective-permute-start(f32[4,6,16,256]{3,2,1,0:T(8,128)S(1)} %get-tuple-element.39), channel_id=1, source_target_pairs={{0,4},{2,6},{4,0},{6,2},{8,12},{10,14},{12,8},{14,10},{16,20},{18,... | collective-permute-start | bytes 1179656 | tf_op jit(solution)/shard_map/ppermute | solution.py:325
  58.5 20.6 %collective-permute-start.9 = (f32[4,6,16,256]{3,2,1,0:T(8,128)S(1)}, f32[4,6,16,256]{3,2,1,0:T(8,128)S(1)}, u32[]{:S(2)}, u32[]{:S(2)}) collective-permute-start(f32[4,6,16,256]{3,2,1,0:T(8,128)S(1)} %get-tuple-element.38), channel_id=1, source_target_pairs={{0,6},{2,4},{4,2},{6,0},{8,14},{10,12},{12,10},{14,8},{16,22},{18,... | collective-permute-start | bytes 1179656 | tf_op jit(solution)/shard_map/ppermute | solution.py:325
  61.3 17.7 %collective-permute-start.11 = (f32[4,6,16,256]{3,2,1,0:T(8,128)S(1)}, f32[4,6,16,256]{3,2,1,0:T(8,128)}, u32[]{:S(2)}, u32[]{:S(2)}) collective-permute-start(f32[4,6,16,256]{3,2,1,0:T(8,128)S(1)} %get-tuple-element.40), channel_id=1, source_target_pairs={{0,2},{2,0},{4,6},{6,4},{8,10},{10,8},{12,14},{14,12},{16,18},{18,... | collective-permute-start | bytes 1179656 | tf_op jit(solution)/shard_map/ppermute | solution.py:325
  63.1 21.0 %collective-permute-start.6 = (f32[1,6,16,256]{3,2,1,0:T(8,128)S(1)}, f32[1,6,16,256]{3,2,1,0:T(8,128)S(1)}, u32[]{:S(2)}, u32[]{:S(2)}) collective-permute-start(f32[1,6,16,256]{3,2,1,0:T(8,128)S(1)} %get-tuple-element.53), channel_id=1, source_target_pairs={{0,16},{2,18},{4,20},{6,22},{8,24},{10,26},{12,28},{14,30},{16,0},... | collective-permute-start | bytes 294920 | tf_op jit(solution)/shard_map/ppermute | solution.py:325
  65.8 18.5 %collective-permute-start.5 = (f32[1,6,16,256]{3,2,1,0:T(8,128)S(1)}, f32[1,6,16,256]{3,2,1,0:T(8,128)S(1)}, u32[]{:S(2)}, u32[]{:S(2)}) collective-permute-start(f32[1,6,16,256]{3,2,1,0:T(8,128)S(1)} %get-tuple-element.52), channel_id=1, source_target_pairs={{0,24},{2,26},{4,28},{6,30},{8,16},{10,18},{12,20},{14,22},{16,8},... | collective-permute-start | bytes 294920 | tf_op jit(solution)/shard_map/ppermute | solution.py:325
  77.5 6.8 %collective-permute-start.7 = (f32[1,6,16,256]{3,2,1,0:T(8,128)S(1)}, f32[1,6,16,256]{3,2,1,0:T(8,128)S(1)}, u32[]{:S(2)}, u32[]{:S(2)}) collective-permute-start(f32[1,6,16,256]{3,2,1,0:T(8,128)S(1)} %get-tuple-element.54), channel_id=1, source_target_pairs={{0,8},{2,10},{4,12},{6,14},{8,0},{10,2},{12,4},{14,6},{16,24},{18,... | collective-permute-start | bytes 294920 | tf_op jit(solution)/shard_map/ppermute | solution.py:325
  80.3 9.9 %collective-permute-start.13 = (f32[1,6,16,256]{3,2,1,0:T(8,128)S(1)}, f32[1,6,16,256]{3,2,1,0:T(8,128)S(1)}, u32[]{:S(2)}, u32[]{:S(2)}) collective-permute-start(f32[1,6,16,256]{3,2,1,0:T(8,128)S(1)} %get-tuple-element.57), channel_id=1, source_target_pairs={{0,16},{2,18},{4,20},{6,22},{8,24},{10,26},{12,28},{14,30},{16,0},... | collective-permute-start | bytes 294920 | tf_op jit(solution)/shard_map/ppermute | solution.py:325
  83.0 7.2 %collective-permute-start.12 = (f32[1,6,16,256]{3,2,1,0:T(8,128)S(1)}, f32[1,6,16,256]{3,2,1,0:T(8,128)S(1)}, u32[]{:S(2)}, u32[]{:S(2)}) collective-permute-start(f32[1,6,16,256]{3,2,1,0:T(8,128)S(1)} %get-tuple-element.56), channel_id=1, source_target_pairs={{0,24},{2,26},{4,28},{6,30},{8,16},{10,18},{12,20},{14,22},{16,8},... | collective-permute-start | bytes 294920 | tf_op jit(solution)/shard_map/ppermute | solution.py:325
  84.1 6.5 %collective-permute-start.14 = (f32[1,6,16,256]{3,2,1,0:T(8,128)S(1)}, f32[1,6,16,256]{3,2,1,0:T(8,128)S(1)}, u32[]{:S(2)}, u32[]{:S(2)}) collective-permute-start(f32[1,6,16,256]{3,2,1,0:T(8,128)S(1)} %get-tuple-element.58), channel_id=1, source_target_pairs={{0,8},{2,10},{4,12},{6,14},{8,0},{10,2},{12,4},{14,6},{16,24},{18,... | collective-permute-start | bytes 294920 | tf_op jit(solution)/shard_map/ppermute | solution.py:325
